TPU v7x, 256 devices: a whole 4x4x8 slice. The times are simulated.
256 devices in a mesh: inst: 8 (over y_lo, x), space: 32 (over z, y_hi, core).
Axes of the slice: x: 4, y: 4 (y_hi: 2, y_lo: 2; y = y_hi * 2 + y_lo), z: 8, core: 2. Of those that a mesh axis runs over, the one named last changes fastest.
Arguments:
- fluid_init: float32 [48, 5, 256, 1024], P('inst', None, 'space'), may hold values from -6 to 6
- source_term: float32 [48, 5, 256, 1024], P('inst', None, 'space'), may hold values from -6 to 6
- pseudo_step: float32 [256, 1024], P('space'), may hold values from 0.05 to 0.15
- jacobian_x: float32 [5, 5], replicated, may hold values from -2.5 to 2.5
- jacobian_z: float32 [5, 5], replicated, may hold values from -2.5 to 2.5
- metal_init: float32 [2, 4, 256, 512], P(None, None, 'space'), may hold values from -6 to 6
- conductivity: float32 [256, 512], P('space'), may hold values from 0.2 to 1
- face_coeff: float32 [16384], P('space'), may hold values from 0.5 to 2
- fluid_face: int32 [16384], P('space'), may hold values from 0 to 8191
- metal_face: int32 [16384], P('space'), may hold values from 0 to 4095
Outputs:
- fluid_out: float32 [48, 5, 256, 1024], P('inst', None, 'space')
- metal_out: float32 [2, 4, 256, 512], P(None, None, 'space')
All inputs are finite; a program needn't handle non-finite values.
Results may differ from a plain program's by a relative error of at most 0.0001.
Values sent between devices are 32-bit elements; how exact they have to be, the bound alone decides.
No kernel may reach another device: no remote copies, remote signals or barrier semaphores. Data moves between devices by JAX's collectives and lax.ppermute only.
A program may use at most 128 MiB of HBM per device.

v0:
```python
import math

import jax
import jax.numpy as jnp
from jax import lax
from jax.sharding import PartitionSpec as P

NH = 4
SWEEPS = 2


damping_fourth = 1.0 / 32.0
viscous_coef = 0.1
omega_base = 1.0
sigma_fluid = 0.5
metal_step = 0.2
sigma_metal = 0.5
heat_capacity = 0.5
flux_scale = 4.0
highest = lax.Precision.HIGHEST


def with_halo(array, sides, width):
    for axis, dim in sides:
        devices, length = (lax.axis_size(axis), array.shape[dim])
        up = [(i, (i + 1) % devices) for i in range(devices)]
        down = [(j, i) for i, j in up]
        last = lax.slice_in_dim(array, length - width, length, axis=dim)
        initial = lax.slice_in_dim(array, 0, width, axis=dim)
        before = lax.ppermute(last, axis, up)
        after = lax.ppermute(initial, axis, down)
        array = jnp.concatenate([before, array, after], axis=dim)
    return array


def spectral_matrix(instances):
    position = jnp.arange(instances, dtype=jnp.int32)
    offset = position[:, None] - position[None, :]
    parity = 1.0 - 2.0 * (offset % 2).astype(jnp.float32)
    angle_value = math.pi * offset.astype(jnp.float32) / instances
    safe_angle = jnp.where(offset == 0, 0.5, angle_value)
    entries = 0.5 * parity * jnp.cos(safe_angle) / jnp.sin(safe_angle)
    return jnp.where(offset == 0, 0.0, entries)


def harmonic_tables(instance_ids, instances):
    harmonic = jnp.arange(NH, dtype=jnp.int32)
    phase_angle = (
        2.0
        * math.pi
        * (harmonic[:, None] * instance_ids[None, :] % instances).astype(jnp.float32)
        / instances
    )
    return (jnp.cos(phase_angle), jnp.sin(phase_angle))


def padded_sides(adjoint):
    north_side = jnp.pad(adjoint[..., 1:], ((0, 0), (0, 0), (0, 0), (0, 1)))
    south_side = jnp.pad(adjoint[..., :-1], ((0, 0), (0, 0), (0, 0), (1, 0)))
    return (north_side, south_side)


def fluid_update(
    adjoint,
    east_one,
    west_one,
    east_two,
    west_two,
    north_side,
    south_side,
    derivative,
    source_term,
    pseudo_step,
    jacobian_x,
    jacobian_z,
    energy,
):
    central_x = 0.5 * (east_one - west_one)
    fourth = east_two - 4.0 * east_one + 6.0 * adjoint - 4.0 * west_one + west_two
    central_z = 0.5 * (north_side - south_side)
    second_z = north_side - 2.0 * adjoint + south_side
    convect = jnp.einsum("uv,tvxz->tuxz", jacobian_x, central_x, precision=highest)
    convect = convect + jnp.einsum("uv,tvxz->tuxz", jacobian_z, central_z, precision=highest)
    residual = (
        source_term
        - convect
        - damping_fourth * fourth
        + viscous_coef * second_z
        - omega_base * derivative
        - sigma_fluid * adjoint
    )
    residual = residual.at[:, adjoint.shape[1] - 1].add(energy)
    return adjoint + pseudo_step[None, None] * residual


def metal_update(metal_state, east_side, west_side, conductivity, heat_source):
    north_side = jnp.pad(metal_state[..., 1:], ((0, 0), (0, 0), (0, 0), (0, 1)))
    south_side = jnp.pad(metal_state[..., :-1], ((0, 0), (0, 0), (0, 0), (1, 0)))
    laplace = east_side + west_side + north_side + south_side - 4.0 * metal_state
    harmonic = jnp.arange(metal_state.shape[1], dtype=jnp.float32)[:, None, None]
    rotate = jnp.stack(
        [-heat_capacity * harmonic * metal_state[1], heat_capacity * harmonic * metal_state[0]]
    )
    change = heat_source + conductivity[None, None] * laplace - sigma_metal * metal_state - rotate
    return metal_state + metal_step * change


def local(
    fluid_init,
    source_term,
    pseudo_step,
    jacobian_x,
    jacobian_z,
    metal_init,
    conductivity,
    face_coeff,
    fluid_face,
    metal_face,
):
    local_count = fluid_init.shape[0]
    total_count = local_count * lax.axis_size("inst")
    rows_dev = fluid_init.shape[2]
    cell_span = fluid_init.shape[3]
    metal_span = metal_init.shape[3]
    harmonics = metal_init.shape[1]
    first_time = lax.axis_index("inst") * local_count
    spectral = spectral_matrix(total_count)
    local_rows = lax.dynamic_slice_in_dim(spectral, first_time, local_count, 0)
    adjoint = fluid_init
    instance_ids = first_time + jnp.arange(local_count, dtype=jnp.int32)
    cosine_table, sine_table = harmonic_tables(instance_ids, total_count)
    metal_state = metal_init
    for sweep_index in range(SWEEPS):
        at_faces = metal_state.reshape(2, harmonics, rows_dev * metal_span)[:, :, metal_face]
        synthesis = jnp.dot(cosine_table.T, at_faces[0], precision=highest) - jnp.dot(
            sine_table.T, at_faces[1], precision=highest
        )
        synthesis = synthesis * face_coeff[None]
        energy = (
            jnp.zeros((local_count, rows_dev * cell_span), jnp.float32)
            .at[:, fluid_face]
            .add(synthesis)
            .reshape(local_count, rows_dev, cell_span)
        )
        padded = with_halo(adjoint, (("space", 2),), 2)
        east_one = padded[:, :, 3 : 3 + rows_dev]
        west_one = padded[:, :, 1 : 1 + rows_dev]
        east_two = padded[:, :, 4 : 4 + rows_dev]
        west_two = padded[:, :, 0:rows_dev]
        north_side, south_side = padded_sides(adjoint)
        derivative = jnp.einsum(
            "ts,svxz->tvxz",
            local_rows,
            lax.all_gather(adjoint, "inst", axis=0, tiled=True),
            precision=highest,
        )
        adjoint = fluid_update(
            adjoint,
            east_one,
            west_one,
            east_two,
            west_two,
            north_side,
            south_side,
            derivative,
            source_term,
            pseudo_step,
            jacobian_x,
            jacobian_z,
            energy,
        )
        face_flux = (
            adjoint[:, adjoint.shape[1] - 1].reshape(local_count, rows_dev * cell_span)[
                :, fluid_face
            ]
            * face_coeff[None]
        )
        partial_value = jnp.stack(
            [
                jnp.dot(cosine_table, face_flux, precision=highest),
                -jnp.dot(sine_table, face_flux, precision=highest),
            ]
        ) * (flux_scale / total_count)
        heat_terms = lax.psum(partial_value, "inst")
        heat_source = (
            jnp.zeros((2, harmonics, rows_dev * metal_span), jnp.float32)
            .at[:, :, metal_face]
            .add(heat_terms)
            .reshape(2, harmonics, rows_dev, metal_span)
        )
        metal_padded = with_halo(metal_state, (("space", 2),), 1)
        metal_state = metal_update(
            metal_state, metal_padded[:, :, 2:], metal_padded[:, :, :-2], conductivity, heat_source
        )
    return (adjoint, metal_state)


def solution(mesh):
    return jax.shard_map(
        local,
        mesh=mesh,
        in_specs=(
            P("inst", None, "space", None),
            P("inst", None, "space", None),
            P("space", None),
            P(),
            P(),
            P(None, None, "space", None),
            P("space", None),
            P("space"),
            P("space"),
            P("space"),
        ),
        out_specs=(P("inst", None, "space", None), P(None, None, "space", None)),
        check_vma=False,
    )
```

profile of v0, /device:TPU:8, one launch (start us, length us, event | category | flops | bytes accessed | tf_op | source)
XLA Modules:
  0.0 372.0 jit_solution(9363541896420658755)
XLA Ops:
  10.6 7.0 %collective-permute-start = (f32[6,5,2,1024]{3,2,1,0:T(2,128)}, f32[6,5,2,1024]{3,2,1,0:T(2,128)}, u32[]{:S(2)}, u32[]{:S(2)}) collective-permute-start(f32[6,5,2,1024]{3,2,1,0:T(2,128)} %get-tuple-element.38), channel_id=1, source_target_pairs={{1,0},{2,1},{3,2},{4,3},{5,4},{6,5},{7,6},{8,7},{9,8},{10,9},{11,1... | collective-permute-start | bytes 737288 | tf_op jit(solution)/shard_map/ppermute | solution.py:31
  20.9 3.7 gather_fusion
  26.0 4.6 %scatter_custom_fusion = f32[6,8192]{0,1:T(8,128)} fusion(s32[512]{0:T(512)S(1)} %compare_select_fusion.1, f32[512,6]{1,0:T(8,128)S(1)} %copy.105, f32[]{:T(128)} %constant.108.clone.1), kind=kCustom, calls=%fused_computation.14 | custom fusion | flops 3072 | bytes 196612 | tf_op jit(solution)/shard_map/scatter-add | solution.py:142
  30.7 3.6 copy.125
  35.1 3.2 fusion.12
  41.3 3.3 fusion.14
  44.6 56.7 %all-gather.3.cloned.1.call-done = f32[48,5,8,1024]{3,2,1,0:T(8,128)} async-done(((f32[6,5,8,1024]{3,2,1,0:T(8,128)}), f32[48,5,8,1024]{3,2,1,0:T(8,128)}) %all-gather.3.cloned.1.call-update) | async-done | bytes 7864336 | tf_op jit(solution)/shard_map/all_gather | solution.py:154
  101.3 12.0 %fusion.2 = f32[6,5,8,1024]{3,0,2,1:T(8,128)S(1)} fusion(f32[6,48,1,1]{1,0,3,2:T(8,128)S(1)} %fusion.81, f32[48,5,8,1024]{3,2,1,0:T(8,128)} %all-gather.3.cloned.1.call-done), kind=kOutput, calls=%fused_computation.10 | convolution fusion | flops 141557760 | bytes 8848512 | tf_op jit(solution)/shard_map/ts,svxz->tvxz/dot_general | solution.py:151
  117.4 4.7 %collective-permute-start.4 = (f32[2,4,1,512]{3,2,1,0:T(1,128)S(1)}, f32[2,4,1,512]{3,2,1,0:T(1,128)S(1)}, u32[]{:S(2)}, u32[]{:S(2)}) collective-permute-start(f32[2,4,1,512]{3,2,1,0:T(1,128)S(1)} %get-tuple-element.54), channel_id=1, source_target_pairs={{1,0},{2,1},{3,2},{4,3},{5,4},{6,5},{7,6},{8,7},{9,8},{10,9},{11,1... | collective-permute-start | bytes 49160 | tf_op jit(solution)/shard_map/ppermute | solution.py:31
  123.3 5.3 %collective-permute-start.2 = (f32[6,5,2,1024]{3,2,1,0:T(2,128)}, f32[6,5,2,1024]{3,2,1,0:T(2,128)S(1)}, u32[]{:S(2)}, u32[]{:S(2)}) collective-permute-start(f32[6,5,2,1024]{3,2,1,0:T(2,128)} %get-tuple-element.34), channel_id=1, source_target_pairs={{1,0},{2,1},{3,2},{4,3},{5,4},{6,5},{7,6},{8,7},{9,8},{10,9},{11,1... | collective-permute-start | bytes 737288 | tf_op jit(solution)/shard_map/ppermute | solution.py:31
  131.4 3.2 gather_fusion.1
  135.4 33.0 %psum.14 = f32[2,4,512]{2,1,0:T(4,128)S(1)} all-reduce(f32[2,4,512]{2,1,0:T(4,128)S(1)} %maximum_multiply_fusion), channel_id=1, replica_groups=mesh['inst'=8,'space'=32] {'inst'}, use_global_device_ids=true, to_apply=%region_1.2 | all-reduce | flops 4096 | bytes 32768 | tf_op jit(solution)/shard_map/psum | solution.py:184
  171.6 48.7 %scatter_fusion = f32[2,4,4096]{1,0,2:T(2,128)} fusion(f32[2,4,4096]{1,0,2:T(2,128)} %broadcast.142.clone, s32[512]{0:T(512)S(1)} %compare_select_fusion, f32[512,2,4]{2,1,0:T(2,128)S(1)} %copy.114), kind=kCustom, calls=%fused_computation.5 | custom fusion | flops 4096 | bytes 51200 | tf_op jit(solution)/shard_map/scatter-add | solution.py:188
  220.4 3.6 copy.115
  228.9 4.4 %gather_fusion.2 = f32[512,2,4]{2,1,0:T(2,128)} fusion(f32[2,4,4096]{1,0,2:T(2,128)} %bitcast.66, s32[1024]{0:T(1024)S(1)} %get-tuple-element.59), kind=kCustom, calls=%fused_computation.2 | custom fusion | bytes 34816 | tf_op jit(solution)/shard_map/gather | solution.py:134
  235.9 3.3 fusion.8
  240.5 5.0 %scatter_custom_fusion.2 = f32[6,8192]{0,1:T(8,128)} fusion(s32[512]{0:T(512)} %copy-done.28, f32[512,6]{1,0:T(8,128)} %copy.117, f32[]{:T(128)} %constant.108.clone.1), kind=kCustom, calls=%fused_computation.12 | custom fusion | flops 3072 | bytes 197120 | tf_op jit(solution)/shard_map/scatter-add | solution.py:142
  245.5 3.5 copy.127
  251.1 3.3 fusion.10
  254.4 11.7 %fusion = f32[6,5,8,1024]{3,0,2,1:T(8,128)S(1)} fusion(f32[6,48,1,1]{1,0,3,2:T(8,128)S(1)} %fusion.81, f32[48,5,8,1024]{3,2,1,0:T(8,128)} %all-gather.5.cloned.1.call-done), kind=kOutput, calls=%fused_computation.8 | convolution fusion | flops 141557760 | bytes 8848512 | tf_op jit(solution)/shard_map/ts,svxz->tvxz/dot_general | solution.py:151
  266.2 3.8 %fusion.30 = f32[6,5,8,1024]{3,2,1,0:T(8,128)S(1)} fusion(f32[6,5,8,1024]{3,2,1,0:T(8,128)S(1)} %copy-done.1, f32[6,5,2,1024]{3,2,1,0:T(2,128)} %collective-permute-done.3, f32[6,5,2,1024]{3,2,1,0:T(2,128)S(1)} %collective-permute-done.2, f32[6,5,8,1024]{3,2,1,0:T(8,128)S(1)} %copy-done.10, f32[6,5,8,1024]{3,0,2,1:T(8,128)S(1)} %fusion, ...), kind=kLoop, calls=%fused_computation.51 | loop fusion | flops 5652480 | bytes 8353920 | tf_op jit(solution)/shard_map/sub | solution.py:85
  277.1 30.7 %psum.15 = f32[2,4,512]{2,1,0:T(4,128)S(1)} all-reduce(f32[2,4,512]{2,1,0:T(4,128)S(1)} %maximum_multiply_fusion.1), channel_id=1, replica_groups=mesh['inst'=8,'space'=32] {'inst'}, use_global_device_ids=true, to_apply=%region_4.5 | all-reduce | flops 4096 | bytes 32768 | tf_op jit(solution)/shard_map/psum | solution.py:184
  311.0 48.8 %scatter_fusion.1 = f32[2,4,4096]{1,0,2:T(2,128)} fusion(f32[2,4,4096]{1,0,2:T(2,128)} %broadcast.142, s32[512]{0:T(512)S(1)} %copy-done.23, f32[512,2,4]{2,1,0:T(2,128)S(1)} %copy.120), kind=kCustom, calls=%fused_computation.7 | custom fusion | flops 4096 | bytes 51200 | tf_op jit(solution)/shard_map/scatter-add | solution.py:188
  359.8 3.6 copy.121
  (144 shorter events, 46.3 us)
Async XLA Ops:
  7.2 27.9 %copy-start = (f32[5,5]{1,0:T(8,128)S(1)}, f32[5,5]{1,0:T(8,128)}, u32[]{:S(2)}) copy-start(f32[5,5]{1,0:T(8,128)} %param.18) | copy-start | bytes 304
  7.2 10.5 %copy-start.11 = (f32[2,4,8,512]{3,2,1,0:T(8,128)S(1)}, f32[2,4,8,512]{3,2,1,0:T(8,128)}, u32[]{:S(2)}) copy-start(f32[2,4,8,512]{3,2,1,0:T(8,128)} %param.19) | copy-start | bytes 393220
  7.2 94.1 %all-gather.3.cloned.1.call-start = ((), (), s32[]{:S(2)}) async-start(), calls=%async_computation | async-start | bytes 8847360 | tf_op jit(solution)/shard_map/all_gather | solution.py:154
  7.9 246.5 %all-gather.5.cloned.1.call-start = ((), (), s32[]{:S(2)}) async-start(), calls=%async_computation.1 | async-start | bytes 8847360 | tf_op jit(solution)/shard_map/all_gather | solution.py:154
  10.6 27.9 %collective-permute-start = (f32[6,5,2,1024]{3,2,1,0:T(2,128)}, f32[6,5,2,1024]{3,2,1,0:T(2,128)}, u32[]{:S(2)}, u32[]{:S(2)}) collective-permute-start(f32[6,5,2,1024]{3,2,1,0:T(2,128)} %get-tuple-element.38), channel_id=1, source_target_pairs={{1,0},{2,1},{3,2},{4,3},{5,4},{6,5},{7,6},{8,7},{9,8},{10,9},{11,1... | collective-permute-start | bytes 737288 | tf_op jit(solution)/shard_map/ppermute | solution.py:31
  17.6 21.9 %collective-permute-start.1 = (f32[6,5,2,1024]{3,2,1,0:T(2,128)}, f32[6,5,2,1024]{3,2,1,0:T(2,128)S(1)}, u32[]{:S(2)}, u32[]{:S(2)}) collective-permute-start(f32[6,5,2,1024]{3,2,1,0:T(2,128)} %get-tuple-element.39), channel_id=1, source_target_pairs={{0,1},{1,2},{2,3},{3,4},{4,5},{5,6},{6,7},{7,8},{8,9},{9,10},{10,1... | collective-permute-start | bytes 737288 | tf_op jit(solution)/shard_map/ppermute | solution.py:30
  20.9 9.8 %copy-start.28 = (s32[512]{0:T(512)}, s32[512]{0:T(512)S(1)}, u32[]{:S(2)}) copy-start(s32[512]{0:T(512)S(1)} %compare_select_fusion.1) | copy-start | bytes 6148
  20.9 150.8 %copy-start.22 = (s32[512]{0:T(512)}, s32[512]{0:T(512)S(1)}, u32[]{:S(2)}) copy-start(s32[512]{0:T(512)S(1)} %compare_select_fusion) | copy-start | bytes 6148
  20.9 110.5 %copy-start.26 = (s32[1024]{0:T(1024)}, s32[1024]{0:T(1024)S(1)}, u32[]{:S(2)}) copy-start(s32[1024]{0:T(1024)S(1)} %get-tuple-element.58) | copy-start | bytes 12292
  101.3 12.0 %copy-start.4 = (f32[6,5,10,1024]{3,2,1,0:T(8,128)S(1)}, f32[6,5,10,1024]{3,2,1,0:T(8,128)}, u32[]{:S(2)}) copy-start(f32[6,5,10,1024]{3,2,1,0:T(8,128)} %copy-done.3) | copy-start | bytes 3686404
  101.3 12.0 %copy-start.7 = (f32[6,8,1024,5]{2,3,1,0:T(8,128)S(1)}, f32[6,8,1024,5]{2,3,1,0:T(8,128)}, u32[]{:S(2)}) copy-start(f32[6,8,1024,5]{2,3,1,0:T(8,128)} %fusion.12) | copy-start | bytes 2949124
  101.3 12.0 %copy-start.8 = (f32[6,8,1024,5]{2,3,1,0:T(8,128)S(1)}, f32[6,8,1024,5]{2,3,1,0:T(8,128)}, u32[]{:S(2)}) copy-start(f32[6,8,1024,5]{2,3,1,0:T(8,128)} %fusion.14) | copy-start | bytes 2949124
  101.3 12.0 %copy-start.9 = (f32[6,5,8,1024]{3,2,1,0:T(8,128)S(1)}, f32[6,5,8,1024]{3,2,1,0:T(8,128)}, u32[]{:S(2)}) copy-start(f32[6,5,8,1024]{3,2,1,0:T(8,128)} %param.15) | copy-start | bytes 2949124
  117.4 106.5 %collective-permute-start.4 = (f32[2,4,1,512]{3,2,1,0:T(1,128)S(1)}, f32[2,4,1,512]{3,2,1,0:T(1,128)S(1)}, u32[]{:S(2)}, u32[]{:S(2)}) collective-permute-start(f32[2,4,1,512]{3,2,1,0:T(1,128)S(1)} %get-tuple-element.54), channel_id=1, source_target_pairs={{1,0},{2,1},{3,2},{4,3},{5,4},{6,5},{7,6},{8,7},{9,8},{10,9},{11,1... | collective-permute-start | bytes 49160 | tf_op jit(solution)/shard_map/ppermute | solution.py:31
  122.1 101.9 %collective-permute-start.5 = (f32[2,4,1,512]{3,2,1,0:T(1,128)S(1)}, f32[2,4,1,512]{3,2,1,0:T(1,128)S(1)}, u32[]{:S(2)}, u32[]{:S(2)}) collective-permute-start(f32[2,4,1,512]{3,2,1,0:T(1,128)S(1)} %get-tuple-element.55), channel_id=1, source_target_pairs={{0,1},{1,2},{2,3},{3,4},{4,5},{5,6},{6,7},{7,8},{8,9},{9,10},{10,1... | collective-permute-start | bytes 49160 | tf_op jit(solution)/shard_map/ppermute | solution.py:30
  122.1 9.2 %copy-start.29 = (f32[4]{0:T(128)}, f32[4]{0:T(128)S(1)}, u32[]{:S(2)}) copy-start(f32[4]{0:T(128)S(1)} %get-tuple-element.60) | copy-start | bytes 52
  122.1 9.2 %copy-start.31 = (f32[4]{0:T(128)}, f32[4]{0:T(128)S(1)}, u32[]{:S(2)}) copy-start(f32[4]{0:T(128)S(1)} %get-tuple-element.61) | copy-start | bytes 52
  123.3 126.4 %collective-permute-start.2 = (f32[6,5,2,1024]{3,2,1,0:T(2,128)}, f32[6,5,2,1024]{3,2,1,0:T(2,128)S(1)}, u32[]{:S(2)}, u32[]{:S(2)}) collective-permute-start(f32[6,5,2,1024]{3,2,1,0:T(2,128)} %get-tuple-element.34), channel_id=1, source_target_pairs={{1,0},{2,1},{3,2},{4,3},{5,4},{6,5},{7,6},{8,7},{9,8},{10,9},{11,1... | collective-permute-start | bytes 737288 | tf_op jit(solution)/shard_map/ppermute | solution.py:31
  128.6 121.0 %collective-permute-start.3 = (f32[6,5,2,1024]{3,2,1,0:T(2,128)}, f32[6,5,2,1024]{3,2,1,0:T(2,128)}, u32[]{:S(2)}, u32[]{:S(2)}) collective-permute-start(f32[6,5,2,1024]{3,2,1,0:T(2,128)} %get-tuple-element.35), channel_id=1, source_target_pairs={{0,1},{1,2},{2,3},{3,4},{4,5},{5,6},{6,7},{7,8},{8,9},{9,10},{10,1... | collective-permute-start | bytes 737288 | tf_op jit(solution)/shard_map/ppermute | solution.py:30
  227.9 135.5 %collective-permute-start.6 = (f32[2,4,1,512]{3,2,1,0:T(1,128)}, f32[2,4,1,512]{3,2,1,0:T(1,128)}, u32[]{:S(2)}, u32[]{:S(2)}) collective-permute-start(f32[2,4,1,512]{3,2,1,0:T(1,128)} %get-tuple-element.48), channel_id=1, source_target_pairs={{1,0},{2,1},{3,2},{4,3},{5,4},{6,5},{7,6},{8,7},{9,8},{10,9},{11,1... | collective-permute-start | bytes 49160 | tf_op jit(solution)/shard_map/ppermute | solution.py:31
  228.4 135.0 %collective-permute-start.7 = (f32[2,4,1,512]{3,2,1,0:T(1,128)}, f32[2,4,1,512]{3,2,1,0:T(1,128)}, u32[]{:S(2)}, u32[]{:S(2)}) collective-permute-start(f32[2,4,1,512]{3,2,1,0:T(1,128)} %get-tuple-element.49), channel_id=1, source_target_pairs={{0,1},{1,2},{2,3},{3,4},{4,5},{5,6},{6,7},{7,8},{8,9},{9,10},{10,1... | collective-permute-start | bytes 49160 | tf_op jit(solution)/shard_map/ppermute | solution.py:30
  254.4 11.8 %copy-start.5 = (f32[6,8,1024,5]{2,3,1,0:T(8,128)S(1)}, f32[6,8,1024,5]{2,3,1,0:T(8,128)}, u32[]{:S(2)}) copy-start(f32[6,8,1024,5]{2,3,1,0:T(8,128)} %fusion.8) | copy-start | bytes 2949124
  254.4 11.8 %copy-start.6 = (f32[6,8,1024,5]{2,3,1,0:T(8,128)S(1)}, f32[6,8,1024,5]{2,3,1,0:T(8,128)}, u32[]{:S(2)}) copy-start(f32[6,8,1024,5]{2,3,1,0:T(8,128)} %fusion.10) | copy-start | bytes 2949124
  254.4 11.8 %copy-start.10 = (f32[6,5,8,1024]{3,2,1,0:T(8,128)S(1)}, f32[6,5,8,1024]{3,2,1,0:T(8,128)}, u32[]{:S(2)}) copy-start(f32[6,5,8,1024]{3,2,1,0:T(8,128)} %param.15) | copy-start | bytes 2949124
  (21 other events, 64.3 us)
Sparse Core Ops, SparseCore 0:
  9.8 91.4 all-gather.2
  117.5 89.3 all-gather.4
where the time goes:
time: 379 us; the launch traced here: 372 us
  other arithmetic  120 us (32%)
  blocking collectives  63.7 us (17%)
  local copies, waits for them, and re-layouts  57.6 us (15%)
  waiting for transfers between devices  57.5 us (15%)
  matrix products  40.1 us (11%)
  starting transfers between devices  18.1 us (5%)
  between operations  14.9 us (4%)
    scatter-add x2, other arithmetic, local(): heat_source = jnp.zeros((2, harmonics, rows_dev * metal_span), jnp.float3...  97.6 us
    psum x2, blocking collectives, local(): heat_terms = lax.psum(partial_value, 'inst')  63.7 us
    all_gather x2, waiting for transfers between devices, local(): lax.all_gather(adjoint, 'inst', axis=0, tiled=True)  56.7 us
    dot_general x2, matrix products, local(): jnp.einsum('ts,svxz->tvxz', local_rows, lax.all_gather(adjoint, 'inst', a...  23.7 us
    ppermute x4, starting transfers between devices, with_halo(): after = lax.ppermute(initial, axis, down)  17.6 us
    another operation x4, local copies, waits for them, and re-layouts  13 us
    scatter-add x2, other arithmetic, local(): energy = jnp.zeros((local_count, rows_dev * cell_span), jnp.float32).at[:...  9.59 us
    gather x2, local copies, waits for them, and re-layouts, local(): metal_state.reshape(2, harmonics, rows_dev * metal_span)[:, :, metal_face]  8.11 us
  transfers between devices with their start and end apart: 10, of which 1 were waited for; matrix products, arithmetic and copies ran while one was open for 53% of the time, Pallas kernels for 0%

commit v1 on v0

v1 whole, which is shorter than its diff:
```python
import functools
import math

import jax
import jax.numpy as jnp
import ml_dtypes
import numpy as np
from jax import lax
from jax.experimental import pallas as pl
from jax.experimental.pallas import tpu as pltpu
from jax.sharding import PartitionSpec as P

NT, NV, NH = 48, 5, 4
ROWS, SPAN, MSPAN, NF = 8, 1024, 512, 512
CHUNK = 128
CH = 2 * NH
F32, BF16 = jnp.float32, jnp.bfloat16
VMEM = pl.BlockSpec(memory_space=pltpu.VMEM)
SMEM = pl.BlockSpec(memory_space=pltpu.SMEM)

damping_fourth = 1.0 / 32.0
viscous_coef = 0.1
sigma_fluid = 0.5
metal_step = 0.2
sigma_metal = 0.5
heat_capacity = 0.5
flux_scale = 4.0


def tables():
    t = np.arange(NT)
    offset = t[:, None] - t[None, :]
    angle = np.where(offset == 0, 0.5, math.pi * offset / NT)
    spectral = np.where(
        offset == 0, 0.0, 0.5 * (1.0 - 2.0 * (offset % 2)) * np.cos(angle) / np.sin(angle)
    )
    phase = 2.0 * math.pi * ((np.arange(NH)[:, None] * t[None, :]) % NT) / NT
    synth = np.concatenate([np.cos(phase), -np.sin(phase)])
    w0 = synth * (flux_scale / NT)
    w1 = w0 @ spectral
    w2 = w1 @ spectral
    high = spectral.astype(np.float32).astype(ml_dtypes.bfloat16)
    low = (spectral - high.astype(np.float64)).astype(np.float32).astype(ml_dtypes.bfloat16)
    eye = np.eye(ROWS, dtype=np.float32)
    kron_high = np.kron(high.astype(np.float32), eye)
    kron_low = np.kron(low.astype(np.float32), eye)
    kron = np.concatenate([kron_high, kron_high, kron_low], axis=1).astype(ml_dtypes.bfloat16)
    flat = np.concatenate([m.T.reshape(-1) for m in (synth, w0, w1, w2)]).astype(np.float32)
    return kron, flat


KRON, FLAT = tables()
SYNTH, W0, W1, W2 = (i * NT * CH for i in range(4))


def call(body, outs, n_in, smem=(), scratch=(), flops=1 << 20, moved=1 << 21):
    return pl.pallas_call(
        body,
        out_shape=outs,
        in_specs=[SMEM if i in smem else VMEM for i in range(n_in)],
        out_specs=[VMEM] * len(outs),
        scratch_shapes=list(scratch),
        compiler_params=pltpu.CompilerParams(vmem_limit_bytes=24 << 20),
        cost_estimate=pl.CostEstimate(flops=flops, bytes_accessed=moved, transcendentals=0),
    )


def shape(*dims):
    return jax.ShapeDtypeStruct(dims, F32)


def row_index(n=SPAN):
    return lax.broadcasted_iota(jnp.int32, (ROWS, n), 0)


def split(x):
    high = x.astype(BF16)
    return high, (x - high.astype(F32)).astype(BF16)


def one_hot(index, n):
    cell = lax.broadcasted_iota(jnp.int32, (n, NF), 0)
    return jnp.where(cell == index, 1.0, 0.0).astype(BF16)


def at_faces(field, span_hot, row_hot):
    n = field.shape[-1]
    both = jnp.concatenate(split(field.reshape(CH * ROWS, n)), axis=0)
    picked = jnp.dot(both, span_hot, preferred_element_type=F32)
    picked = (picked[: CH * ROWS] + picked[CH * ROWS :]).reshape(CH, ROWS, NF)
    return jnp.sum(picked * row_hot[None], axis=1)


def onto_cells(values, span_hot, row_hot):
    spread = (values[:, None, :] * row_hot[None]).reshape(CH * ROWS, NF)
    both = jnp.concatenate(split(spread), axis=0)
    out = lax.dot_general(both, span_hot, (((1,), (1,)), ((), ())), preferred_element_type=F32)
    return (out[: CH * ROWS] + out[CH * ROWS :]).reshape(CH, ROWS, span_hot.shape[0])


def fluid_hots(ff_ref):
    cell = ff_ref[...]
    span = one_hot(cell & (SPAN - 1), SPAN)
    rows = jnp.where(row_index(NF) == (cell >> 10), 1.0, 0.0)
    return span, rows


def metal_hots(mf_ref):
    cell = mf_ref[...]
    span = one_hot(cell & (MSPAN - 1), MSPAN)
    rows = jnp.where(row_index(NF) == (cell >> 9), 1.0, 0.0)
    return span, rows


def span_sides(a):
    n = a.shape[-1]
    lane = lax.broadcasted_iota(jnp.int32, a.shape, a.ndim - 1)
    north = jnp.where(lane == n - 1, 0.0, pltpu.roll(a, n - 1, a.ndim - 1))
    south = jnp.where(lane == 0, 0.0, pltpu.roll(a, 1, a.ndim - 1))
    return north, south


def stencil_parts(a, before, after):
    row = row_index(a.shape[-1])
    east_one = pltpu.roll(jnp.where(row == 0, after, a), 7, 0)
    east_two = pltpu.roll(jnp.where(row < 2, after, a), 6, 0)
    west_one = pltpu.roll(jnp.where(row == 7, before, a), 1, 0)
    west_two = pltpu.roll(jnp.where(row >= 6, before, a), 2, 0)
    north, south = span_sides(a)
    rest = (
        (4.0 * damping_fourth) * (east_one + west_one)
        - damping_fourth * (east_two + west_two)
        + viscous_coef * (north + south)
        - (6.0 * damping_fourth + 2.0 * viscous_coef + sigma_fluid) * a
    )
    return east_one - west_one, north - south, rest


def halo_pair(up_ref, down_ref, t, v):
    if v < 4:
        tile, slot = t, v
        before = pltpu.roll(up_ref[tile], (6 - 2 * slot) % 8, 0)
        after = pltpu.roll(down_ref[tile], (8 - 2 * slot) % 8, 0)
        return before, after
    tile, slot = 6 + t // 4, t % 4
    before = pltpu.roll(up_ref[tile], (6 - 2 * slot) % 8, 0)
    after = pltpu.roll(down_ref[tile], (8 - 2 * slot) % 8, 0)
    return before, after


def pack_edges(get, up_ref, down_ref, extra):
    row = row_index()
    groups = [[get(t, v) for v in range(4)] for t in range(6)]
    groups += [[get(t, 4) for t in range(4)], [get(4, 4), get(5, 4), extra, extra]]
    for tile, blocks in enumerate(groups):
        up = down = None
        for slot, a in enumerate(blocks):
            u = pltpu.roll(a, (2 * slot + 2) % 8, 0) if (2 * slot + 2) % 8 else a
            d = pltpu.roll(a, 2 * slot, 0) if slot else a
            mine = (row >> 1) == slot
            up = u if up is None else jnp.where(mine, u, up)
            down = d if down is None else jnp.where(mine, d, down)
        up_ref[tile] = up
        down_ref[tile] = down


def edges_kernel(a_ref, ps_ref, up_ref, down_ref):
    pack_edges(lambda t, v: a_ref[t, v], up_ref, down_ref, ps_ref[...])


def blocks_kernel(a_ref, out_ref):
    for i in range(8):
        for t in range(6):
            for v in range(NV):
                out_ref[i, t * NV + v] = a_ref[t, v, :, i * CHUNK : (i + 1) * CHUNK]


def energy_kernel(tab_ref, m_ref, fc_ref, ff_ref, mf_ref, e_ref):
    first = lax.axis_index("inst") * 6
    m_hot, m_row = metal_hots(mf_ref)
    f_hot, f_row = fluid_hots(ff_ref)
    values = at_faces(m_ref[...], m_hot, m_row) * fc_ref[...]
    cells = onto_cells(values, f_hot, f_row)
    for t in range(6):
        e_ref[t] = combine(tab_ref, SYNTH, first + t, cells)


def combine(tab_ref, base, t, fields):
    total = tab_ref[base + t * CH] * fields[0]
    for ch in range(1, CH):
        if ch != NH:
            total += tab_ref[base + t * CH + ch] * fields[ch]
    return total


def convect(jx_ref, jz_ref, dx, dz, rest, u):
    out = rest
    for v in range(NV):
        out = out - (0.5 * jx_ref[u, v]) * dx[v] - (0.5 * jz_ref[u, v]) * dz[v]
    return out


def first_kernel(
    tab_ref, jx_ref, jz_ref, a_ref, s_ref, ps_ref, up_ref, down_ref, e_ref, fc_ref, ff_ref,
    q_ref, b_ref, bup_ref, bdown_ref, hq_ref,
    parts,
):
    first = lax.axis_index("inst") * 6
    step = ps_ref[...]
    step_before = pltpu.roll(up_ref[7], 2, 0)
    step_after = pltpu.roll(down_ref[7], 4, 0)
    for t in range(6):
        for v in range(NV):
            a = a_ref[t, v]
            before, after = halo_pair(up_ref, down_ref, t, v)
            dx, dz, rest = stencil_parts(a, before, after)
            parts[0, v], parts[1, v], parts[2, v] = dx, dz, rest
            dx, dz, rest = stencil_parts(step * a, step_before * before, step_after * after)
            parts[3, v], parts[4, v], parts[5, v] = dx, dz, rest
        for i in range(8):
            cut = pl.ds(i * CHUNK, CHUNK)
            dx = [parts[0, v, :, cut] for v in range(NV)]
            dz = [parts[1, v, :, cut] for v in range(NV)]
            px = [parts[3, v, :, cut] for v in range(NV)]
            pz = [parts[4, v, :, cut] for v in range(NV)]
            for u in range(NV):
                a = a_ref[t, u, :, cut]
                space = convect(jx_ref, jz_ref, dx, dz, parts[2, u, :, cut], u)
                source = s_ref[t, u, :, cut] + space
                if u == NV - 1:
                    source = source + e_ref[t, :, cut]
                b = a + ps_ref[:, cut] * source
                b_ref[t, u, :, cut] = b
                q_ref[i, t * NV + u] = a + b + convect(jx_ref, jz_ref, px, pz, parts[5, u, :, cut], u)
    pack_edges(lambda t, v: b_ref[t, v], bup_ref, bdown_ref, step)
    f_hot, f_row = fluid_hots(ff_ref)
    heat = []
    for ch in range(CH):
        h0 = h1 = h2 = h3 = None
        for t in range(6):
            at = (first + t) * CH + ch
            q = jnp.concatenate([q_ref[i, t * NV + NV - 1] for i in range(8)], axis=1)
            a, b = a_ref[t, NV - 1], b_ref[t, NV - 1]
            x0 = tab_ref[W0 + at] * b
            x1 = tab_ref[W1 + at] * a
            x2 = tab_ref[W1 + at] * q
            x3 = tab_ref[W2 + at] * a
            h0, h1, h2, h3 = (
                (x0, x1, x2, x3) if t == 0 else (h0 + x0, h1 + x1, h2 + x2, h3 + x3)
            )
        heat.append(h0 - step * h1)
        hq_ref[ch] = step * (step * h3 - h2)
    values = at_faces(jnp.stack(heat), f_hot, f_row) * fc_ref[...]
    for i in range(8):
        for k in range(4):
            q_ref[i, 30 + k] = values[:, k * CHUNK : (k + 1) * CHUNK]


def rotate_time(kron_ref, x):
    high, low = split(x)
    return jnp.dot(
        kron_ref[...], jnp.concatenate([high, low, high], axis=0), preferred_element_type=F32
    )


def local_step(ps_ref):
    start = pl.multiple_of(lax.axis_index("inst") * CHUNK, CHUNK)
    return ps_ref[:, pl.ds(start, CHUNK)]


def turned(ref):
    return jnp.concatenate(
        [
            jnp.concatenate(
                [ref[j, t * NV + v] for j in range(8) for t in range(6)], axis=0
            )
            for v in range(NV)
        ],
        axis=1,
    )


def derive_kernel(kron_ref, a_ref, ps_ref, g_ref):
    step = local_step(ps_ref)
    wide = jnp.concatenate([step] * NV, axis=1)
    d = rotate_time(kron_ref, turned(a_ref))
    g_ref[...] = (d.reshape(NT, ROWS, NV * CHUNK) * wide[None]).reshape(NT * ROWS, NV * CHUNK)


def middle_kernel(jx_ref, jz_ref, tab_ref, b_ref, s_ref, ps_ref, up_ref, down_ref, hq_ref, c_ref, hc_ref, parts):
    first = lax.axis_index("inst") * 6
    for t in range(6):
        for v in range(NV):
            before, after = halo_pair(up_ref, down_ref, t, v)
            dx, dz, rest = stencil_parts(b_ref[t, v], before, after)
            parts[0, v], parts[1, v], parts[2, v] = dx, dz, rest
        for i in range(8):
            cut = pl.ds(i * CHUNK, CHUNK)
            dx = [parts[0, v, :, cut] for v in range(NV)]
            dz = [parts[1, v, :, cut] for v in range(NV)]
            for u in range(NV):
                space = convect(jx_ref, jz_ref, dx, dz, parts[2, u, :, cut], u)
                c_ref[t, u, :, cut] = b_ref[t, u, :, cut] + ps_ref[:, cut] * (s_ref[t, u, :, cut] + space)
    for ch in range(CH):
        total = hq_ref[ch]
        for t in range(6):
            total += tab_ref[W0 + (first + t) * CH + ch] * c_ref[t, NV - 1]
        hc_ref[ch] = total


def metal_update(m, before, after, cond, heat):
    row = row_index(MSPAN)
    out = []
    for ch in range(CH):
        a = m[ch]
        east = pltpu.roll(jnp.where(row == 0, after[ch], a), 7, 0)
        west = pltpu.roll(jnp.where(row == 7, before[ch], a), 1, 0)
        north, south = span_sides(a)
        laplace = east + west + north + south - 4.0 * a
        h = ch % NH
        turn = -heat_capacity * h * m[ch + NH] if ch < NH else heat_capacity * h * m[ch - NH]
        out.append(a + metal_step * (heat[ch] + cond * laplace - sigma_metal * a - turn))
    return out


def metal_edges(m, up_ref, down_ref):
    up_ref[...] = jnp.concatenate([m[ch][7:8] for ch in range(CH)], axis=0)
    down_ref[...] = jnp.concatenate([m[ch][0:1] for ch in range(CH)], axis=0)


def metal_sides(up_ref, down_ref):
    before = [jnp.broadcast_to(up_ref[ch : ch + 1], (ROWS, MSPAN)) for ch in range(CH)]
    after = [jnp.broadcast_to(down_ref[ch : ch + 1], (ROWS, MSPAN)) for ch in range(CH)]
    return before, after


def heat_sum(blocks_ref, lead):
    tiles = []
    for k in range(4):
        total = blocks_ref[0, lead + k]
        for j in range(1, 8):
            total += blocks_ref[j, lead + k]
        tiles.append(total)
    return jnp.concatenate(tiles, axis=1)


def second_kernel(
    kron_ref, tab_ref, q_ref, g_ref, ps_ref, m_ref, mup_ref, mdown_ref, cond_ref, fc_ref, ff_ref, mf_ref, hc_ref,
    v_ref, m_out, mup_out, mdown_out, e_ref,
):
    first = lax.axis_index("inst") * 6
    step = ps_ref[...]
    coeff = fc_ref[...]
    m_hot, m_row = metal_hots(mf_ref)
    f_hot, f_row = fluid_hots(ff_ref)
    source = onto_cells(heat_sum(q_ref, 30), m_hot, m_row)
    before, after = metal_sides(mup_ref, mdown_ref)
    m = metal_update(m_ref[...], before, after, cond_ref[...], source)
    for ch in range(CH):
        m_out[ch] = m[ch]
    metal_edges(m, mup_out, mdown_out)
    cells = onto_cells(at_faces(jnp.stack(m), m_hot, m_row) * coeff, f_hot, f_row)
    for t in range(6):
        e_ref[t] = step * combine(tab_ref, SYNTH, first + t, cells)
    heat = []
    for ch in range(CH):
        total = hc_ref[ch]
        for t in range(6):
            total += tab_ref[W0 + (first + t) * CH + ch] * e_ref[t]
        heat.append(total)
    values = at_faces(jnp.stack(heat), f_hot, f_row) * coeff
    for i in range(8):
        for k in range(4):
            v_ref[i, 30 + k] = values[:, k * CHUNK : (k + 1) * CHUNK]
    d = rotate_time(kron_ref, turned(q_ref) - g_ref[...])
    minus = -local_step(ps_ref)
    for j in range(8):
        for t in range(6):
            at = (j * 6 + t) * ROWS
            for v in range(NV):
                v_ref[j, t * NV + v] = minus * d[at : at + ROWS, v * CHUNK : (v + 1) * CHUNK]


def last_kernel(v_ref, c_ref, e_ref, m_ref, mup_ref, mdown_ref, cond_ref, mf_ref, out_ref, m_out):
    for i in range(8):
        cut = pl.ds(i * CHUNK, CHUNK)
        for t in range(6):
            for v in range(NV):
                total = c_ref[t, v, :, cut] + v_ref[i, t * NV + v]
                if v == NV - 1:
                    total = total + e_ref[t, :, cut]
                out_ref[t, v, :, cut] = total
    m_hot, m_row = metal_hots(mf_ref)
    source = onto_cells(heat_sum(v_ref, 30), m_hot, m_row)
    before, after = metal_sides(mup_ref, mdown_ref)
    m = metal_update(m_ref[...], before, after, cond_ref[...], source)
    for ch in range(CH):
        m_out[ch] = m[ch]


def exchange(up, down):
    n = lax.axis_size("space")
    forward = [(i, (i + 1) % n) for i in range(n)]
    back = [(j, i) for i, j in forward]
    return lax.ppermute(up, "space", forward), lax.ppermute(down, "space", back)


def turn(x):
    return lax.all_to_all(x, "inst", 0, 0, tiled=True)


def local(a0, source, ps, jx, jz, metal, cond, coeff, ff, mf):
    kron = jnp.asarray(KRON)
    tab = jnp.asarray(FLAT)
    coeff, ff, mf = (x.reshape(1, NF) for x in (coeff, ff, mf))
    metal = metal.reshape(CH, ROWS, MSPAN)
    up, down = call(edges_kernel, [shape(8, ROWS, SPAN)] * 2, 2)(a0, ps)
    up, down = exchange(up, down)
    (blocks,) = call(blocks_kernel, [shape(8, 30, ROWS, CHUNK)], 1)(a0)
    a_turned = turn(blocks)
    mup, mdown = exchange(metal[:, ROWS - 1], metal[:, 0])
    (e0,) = call(energy_kernel, [shape(6, ROWS, SPAN)], 5, smem=(0,))(tab, metal, coeff, ff, mf)
    parts = pltpu.VMEM((6, NV, ROWS, SPAN), F32)
    q, b, bup, bdown, hq = call(
        first_kernel,
        [shape(8, 34, ROWS, CHUNK), shape(6, NV, ROWS, SPAN)] + [shape(8, ROWS, SPAN)] * 3,
        11,
        smem=(0, 1, 2),
        scratch=[parts],
    )(tab, jx, jz, a0, source, ps, up, down, e0, coeff, ff)
    q_turned = turn(q)
    bup, bdown = exchange(bup, bdown)
    (g,) = call(derive_kernel, [shape(NT * ROWS, NV * CHUNK)], 3)(kron, a_turned, ps)
    c, hc = call(
        middle_kernel,
        [shape(6, NV, ROWS, SPAN), shape(CH, ROWS, SPAN)],
        9,
        smem=(0, 1, 2),
        scratch=[pltpu.VMEM((3, NV, ROWS, SPAN), F32)],
    )(jx, jz, tab, b, source, ps, bup, bdown, hq)
    v, metal, mup, mdown, e1 = call(
        second_kernel,
        [shape(8, 34, ROWS, CHUNK), shape(CH, ROWS, MSPAN)]
        + [shape(CH, MSPAN)] * 2
        + [shape(6, ROWS, SPAN)],
        13,
        smem=(1,),
    )(kron, tab, q_turned, g, ps, metal, mup, mdown, cond, coeff, ff, mf, hc)
    v = turn(v)
    mup, mdown = exchange(mup, mdown)
    out, metal = call(
        last_kernel, [shape(6, NV, ROWS, SPAN), shape(CH, ROWS, MSPAN)], 8
    )(v, c, e1, metal, mup, mdown, cond, mf)
    return out, metal.reshape(2, NH, ROWS, MSPAN)


def solution(mesh):
    return jax.shard_map(
        local,
        mesh=mesh,
        in_specs=(
            P("inst", None, "space", None),
            P("inst", None, "space", None),
            P("space", None),
            P(),
            P(),
            P(None, None, "space", None),
            P("space", None),
            P("space"),
            P("space"),
            P("space"),
        ),
        out_specs=(P("inst", None, "space", None), P(None, None, "space", None)),
        check_vma=False,
    )
```

time: 379 us -> 92.1 us (0.24)
  the two profiles are of different devices: /device:TPU:8 before, /device:TPU:112 now
where the time goes in v1:
time: 92.1 us; the launch traced here: 90.8 us
  waiting for transfers between devices  31.7 us (34%)
  starting transfers between devices  29 us (31%)
  Pallas kernels  14.9 us (16%)
  local copies, waits for them, and re-layouts  14.2 us (15%)
  between operations  0.93 us (1%)
    ppermute x4, waiting for transfers between devices, exchange(): lax.ppermute(up, 'space', forward)  27.7 us
    all_to_all x3, starting transfers between devices, turn(): return lax.all_to_all(x, 'inst', 0, 0, tiled=True)  15.8 us
    unnamed x72, local copies, waits for them, and re-layouts  14.2 us
    ppermute x4, starting transfers between devices, exchange(): lax.ppermute(down, 'space', back)  12.9 us
    pallas_call x1, Pallas kernels, local(): call(first_kernel, [shape(8, 34, ROWS, CHUNK), shape(6, NV, ROWS, SPAN)]...  4.83 us
    all_to_all x3, waiting for transfers between devices, turn(): return lax.all_to_all(x, 'inst', 0, 0, tiled=True)  3.94 us
    pallas_call x1, Pallas kernels, local(): call(second_kernel, [shape(8, 34, ROWS, CHUNK), shape(CH, ROWS, MSPAN)] +...  2.77 us
    pallas_call x1, Pallas kernels, local(): call(middle_kernel, [shape(6, NV, ROWS, SPAN), shape(CH, ROWS, SPAN)], 9,...  2.5 us
  transfers between devices with their start and end apart: 11, of which 4 were waited for; matrix products, arithmetic and copies ran while one was open for 0% of the time, Pallas kernels for 11%

profile of v1, /device:TPU:112, one launch (start us, length us, event | category | flops | bytes accessed | tf_op | source)
XLA Modules:
  0.0 90.8 jit_solution(1404178811020946732)
XLA Ops:
  0.6 1.2 %copy-done = f32[6,5,8,1024]{3,2,1,0:T(8,128)S(1)} copy-done((f32[6,5,8,1024]{3,2,1,0:T(8,128)S(1)}, f32[6,5,8,1024]{3,2,1,0:T(8,128)}, u32[]{:S(2)}) %copy-start) | copy-done | bytes 983064
  1.8 1.0 %shard_map.134 = f32[8,30,8,128]{3,2,1,0:T(8,128)} custom-call(f32[6,5,8,1024]{3,2,1,0:T(8,128)S(1)} %copy-done), custom_call_target="tpu_custom_call" | custom-call | flops 1048576 | bytes 2097152 | tf_op jit(solution)/shard_map/pallas_call | solution.py:419
  2.9 5.2 %all-to-all-start.1 = ((f32[8,30,8,128]{3,2,1,0:T(8,128)}), f32[8,30,8,128]{3,2,1,0:T(8,128)S(1)}, u32[]{:S(2)}, u32[]{:S(2)}) async-start(f32[8,30,8,128]{3,2,1,0:T(8,128)} %shard_map.134), calls=%async_computation.1 | async-start | bytes 1966080 | tf_op jit(solution)/shard_map/all_to_all | solution.py:409
  8.3 3.2 %collective-permute-start.1 = (f32[8,8,1024]{2,1,0:T(8,128)S(1)}, f32[8,8,1024]{2,1,0:T(8,128)S(1)}, u32[]{:S(2)}, u32[]{:S(2)}) collective-permute-start(f32[8,8,1024]{2,1,0:T(8,128)S(1)} %get-tuple-element.19), channel_id=1, source_target_pairs={{1,0},{2,1},{3,2},{4,3},{5,4},{6,5},{7,6},{8,7},{9,8},{10,9},{11,1... | collective-permute-start | bytes 786440 | tf_op jit(solution)/shard_map/ppermute | solution.py:405
  11.6 1.3 %shard_map.132.e_ref = f32[6,8,1024]{2,1,0:T(8,128)S(1)} custom-call(f32[1536]{0:T(1024)S(1)} %copy-done.17, f32[8,8,512]{2,1,0:T(8,128)S(1)} %bitcast.11, f32[1,512]{1,0:T(1,128)S(1)} %bitcast.14, s32[1,512]{1,0:T(1,128)S(1)} %bitcast.17, s32[1,512]{1,0:T(1,128)S(1)} %bitcast.20), custom_call_target="tpu_custom_call" | custom-call | flops 1048576 | bytes 2097152 | tf_op jit(solution)/shard_map/pallas_call | solution.py:422
  12.9 12.8 %collective-permute-done.up_ref = f32[8,8,1024]{2,1,0:T(8,128)S(1)} collective-permute-done((f32[8,8,1024]{2,1,0:T(8,128)S(1)}, f32[8,8,1024]{2,1,0:T(8,128)S(1)}, u32[]{:S(2)}, u32[]{:S(2)}) %collective-permute-start) | collective-permute-done | bytes 262176 | tf_op jit(solution)/shard_map/ppermute | solution.py:405
  25.8 4.8 %shard_map.133 = (f32[8,34,8,128]{3,2,1,0:T(8,128)S(1)}, f32[6,5,8,1024]{3,2,1,0:T(8,128)S(1)}, f32[8,8,1024]{2,1,0:T(8,128)S(1)}, f32[8,8,1024]{2,1,0:T(8,128)S(1)}, f32[8,8,1024]{2,1,0:T(8,128)S(1)}) custom-call(f32[1536]{0:T(1024)S(1)} %copy-done.17, f32[5,5]{1,0:T(8,128)S(1)} %copy-done.28, f32[5,5]{1,0:T(8,128)S(1)} %copy-done.29, ...), custom_call_target="tpu_custom_call" | custom-call | flops 1048576 | bytes 2097152 | tf_op jit(solution)/shard_map/pallas_call | solution.py:424
  30.6 1.0 %copy-done.5 = f32[8,34,8,128]{3,2,1,0:T(8,128)} copy-done((f32[8,34,8,128]{3,2,1,0:T(8,128)}, f32[8,34,8,128]{3,2,1,0:T(8,128)S(1)}, u32[]{:S(2)}) %copy-start.5) | copy-done | bytes 1114136
  31.6 1.0 %copy-done.9 = f32[6,5,8,1024]{3,2,1,0:T(8,128)} copy-done((f32[6,5,8,1024]{3,2,1,0:T(8,128)}, f32[6,5,8,1024]{3,2,1,0:T(8,128)S(1)}, u32[]{:S(2)}) %copy-start.9) | copy-done | bytes 983064
  34.0 5.7 %all-to-all-start = ((f32[8,34,8,128]{3,2,1,0:T(8,128)}), f32[8,34,8,128]{3,2,1,0:T(8,128)S(1)}, u32[]{:S(2)}, u32[]{:S(2)}) async-start(f32[8,34,8,128]{3,2,1,0:T(8,128)} %copy-done.5), calls=%async_computation | async-start | bytes 2228224 | tf_op jit(solution)/shard_map/all_to_all | solution.py:409
  39.8 3.2 %collective-permute-start.5 = (f32[8,8,1024]{2,1,0:T(8,128)S(1)}, f32[8,8,1024]{2,1,0:T(8,128)S(1)}, u32[]{:S(2)}, u32[]{:S(2)}) collective-permute-start(f32[8,8,1024]{2,1,0:T(8,128)S(1)} %get-tuple-element.23), channel_id=1, source_target_pairs={{1,0},{2,1},{3,2},{4,3},{5,4},{6,5},{7,6},{8,7},{9,8},{10,9},{11,1... | collective-permute-start | bytes 786440 | tf_op jit(solution)/shard_map/ppermute | solution.py:405
  43.2 3.2 %collective-permute-start.3 = (f32[8,512]{1,0:T(8,128)S(1)}, f32[8,512]{1,0:T(8,128)S(1)}, u32[]{:S(2)}, u32[]{:S(2)}) collective-permute-start(f32[8,512]{1,0:T(8,128)S(1)} %bitcast.24), channel_id=1, source_target_pairs={{1,0},{2,1},{3,2},{4,3},{5,4},{6,5},{7,6},{8,7},{9,8},{10,9},{11,1... | collective-permute-start | bytes 49160 | tf_op jit(solution)/shard_map/ppermute | solution.py:405
  46.4 10.4 %collective-permute-done.4.up_ref = f32[8,8,1024]{2,1,0:T(8,128)S(1)} collective-permute-done((f32[8,8,1024]{2,1,0:T(8,128)}, f32[8,8,1024]{2,1,0:T(8,128)S(1)}, u32[]{:S(2)}, u32[]{:S(2)}) %collective-permute-start.4) | collective-permute-done | bytes 262176 | tf_op jit(solution)/shard_map/ppermute | solution.py:405
  56.8 1.2 %copy-done.10 = f32[6,5,8,1024]{3,2,1,0:T(8,128)S(1)} copy-done((f32[6,5,8,1024]{3,2,1,0:T(8,128)S(1)}, f32[6,5,8,1024]{3,2,1,0:T(8,128)}, u32[]{:S(2)}) %copy-start.10) | copy-done | bytes 983064
  58.0 0.9 %copy-done.14 = f32[8,8,1024]{2,1,0:T(8,128)S(1)} copy-done((f32[8,8,1024]{2,1,0:T(8,128)S(1)}, f32[8,8,1024]{2,1,0:T(8,128)}, u32[]{:S(2)}) %copy-start.14) | copy-done | bytes 262168
  58.9 2.5 %shard_map.136 = (f32[6,5,8,1024]{3,2,1,0:T(8,128)S(1)}, f32[8,8,1024]{2,1,0:T(8,128)S(1)}) custom-call(f32[5,5]{1,0:T(8,128)S(1)} %copy-done.28, f32[5,5]{1,0:T(8,128)S(1)} %copy-done.29, f32[1536]{0:T(1024)S(1)} %copy-done.17, f32[6,5,8,1024]{3,2,1,0:T(8,128)S(1)} %copy-done.10, f32[6,5,8,1024]{3,2,1,0:T(8,128)S(1)} %copy-done.2, ...), custom_call_target="tpu_custom_call" | custom-call | flops 1048576 | bytes 2097152 | tf_op jit(solution)/shard_map/pallas_call | solution.py:434
  63.6 1.2 %copy-done.4 = bf16[384,1152]{1,0:T(8,128)(2,1)S(1)} copy-done((bf16[384,1152]{1,0:T(8,128)(2,1)S(1)}, bf16[384,1152]{1,0:T(8,128)(2,1)}, u32[]{:S(2)}) %copy-start.4) | copy-done | bytes 884760
  66.2 2.8 %shard_map.137 = (f32[8,34,8,128]{3,2,1,0:T(8,128)S(1)}, f32[8,8,512]{2,1,0:T(8,128)S(1)}, f32[8,512]{1,0:T(8,128)S(1)}, f32[8,512]{1,0:T(8,128)S(1)}, f32[6,8,1024]{2,1,0:T(8,128)S(1)}) custom-call(bf16[384,1152]{1,0:T(8,128)(2,1)S(1)} %copy-done.4, f32[1536]{0:T(1024)S(1)} %copy-done.17, f32[8,34,8,128]{3,2,1,0:T(8,128)S(1)} %all-to-all-done.q_ref, ...), custom_call_target="tpu_custom_call" | custom-call | flops 1048576 | bytes 2097152 | tf_op jit(solution)/shard_map/pallas_call | solution.py:441
  69.0 1.0 %copy-done.6 = f32[8,34,8,128]{3,2,1,0:T(8,128)} copy-done((f32[8,34,8,128]{3,2,1,0:T(8,128)}, f32[8,34,8,128]{3,2,1,0:T(8,128)S(1)}, u32[]{:S(2)}) %copy-start.6) | copy-done | bytes 1114136
  72.6 4.9 %all-to-all-start.2 = ((f32[8,34,8,128]{3,2,1,0:T(8,128)}), f32[8,34,8,128]{3,2,1,0:T(8,128)S(1)}, u32[]{:S(2)}, u32[]{:S(2)}) async-start(f32[8,34,8,128]{3,2,1,0:T(8,128)} %copy-done.6), calls=%async_computation.2 | async-start | bytes 2228224 | tf_op jit(solution)/shard_map/all_to_all | solution.py:409
  77.6 3.2 %collective-permute-start.7 = (f32[8,512]{1,0:T(8,128)S(1)}, f32[8,512]{1,0:T(8,128)S(1)}, u32[]{:S(2)}, u32[]{:S(2)}) collective-permute-start(f32[8,512]{1,0:T(8,128)S(1)} %copy-done.32), channel_id=1, source_target_pairs={{1,0},{2,1},{3,2},{4,3},{5,4},{6,5},{7,6},{8,7},{9,8},{10,9},{11,1... | collective-permute-start | bytes 49160 | tf_op jit(solution)/shard_map/ppermute | solution.py:405
  80.8 4.6 %collective-permute-done.6.mup_ref = f32[8,512]{1,0:T(8,128)S(1)} collective-permute-done((f32[8,512]{1,0:T(8,128)S(1)}, f32[8,512]{1,0:T(8,128)S(1)}, u32[]{:S(2)}, u32[]{:S(2)}) %collective-permute-start.6) | collective-permute-done | bytes 16416 | tf_op jit(solution)/shard_map/ppermute | solution.py:405
  85.4 3.9 %all-to-all-done.2.v_ref = f32[8,34,8,128]{3,2,1,0:T(8,128)S(1)} async-done(((f32[8,34,8,128]{3,2,1,0:T(8,128)}), f32[8,34,8,128]{3,2,1,0:T(8,128)S(1)}, u32[]{:S(2)}, u32[]{:S(2)}) %all-to-all-start.2) | async-done | bytes 1114144 | tf_op jit(solution)/shard_map/all_to_all | solution.py:409
  89.4 1.5 %shard_map.138 = (f32[6,5,8,1024]{3,2,1,0:T(8,128)}, f32[8,8,512]{2,1,0:T(8,128)}) custom-call(f32[8,34,8,128]{3,2,1,0:T(8,128)S(1)} %all-to-all-done.2.v_ref, f32[6,5,8,1024]{3,2,1,0:T(8,128)S(1)} %copy-done.8, f32[6,8,1024]{2,1,0:T(8,128)S(1)} %copy-done.16, f32[8,8,512]{2,1,0:T(8,128)S(1)} %copy-done.19, f32[8,512]{1,0:T(8,128)S(1)} %collective-permute-done.6.mup_ref, ...), custom_call_target="tpu_custom_call" | custom-call | flops 1048576 | bytes 2097152 | tf_op jit(solution)/shard_map/pallas_call | solution.py:451
  (79 shorter events, 8.0 us)
Async XLA Ops:
  2.8 5.2 %copy-start.1 = (f32[6,5,8,1024]{3,2,1,0:T(8,128)S(1)}, f32[6,5,8,1024]{3,2,1,0:T(8,128)}, u32[]{:S(2)}) copy-start(f32[6,5,8,1024]{3,2,1,0:T(8,128)} %a_ref.5) | copy-start | bytes 2949124
  2.9 5.2 %copy-start.11 = (f32[8,1024]{1,0:T(8,128)S(1)}, f32[8,1024]{1,0:T(8,128)}, u32[]{:S(2)}) copy-start(f32[8,1024]{1,0:T(8,128)} %ps_ref.9) | copy-start | bytes 98308
  2.9 8.7 %copy-start.12 = (f32[2,4,8,512]{3,2,1,0:T(8,128)S(1)}, f32[2,4,8,512]{3,2,1,0:T(8,128)}, u32[]{:S(2)}) copy-start(f32[2,4,8,512]{3,2,1,0:T(8,128)} %param.17) | copy-start | bytes 393220
  2.9 8.7 %copy-start.17 = (f32[1536]{0:T(1024)S(1)}, f32[1536]{0:T(1024)}, u32[]{:S(2)}) copy-start(f32[1536]{0:T(1024)} %constant.5.clone.tab_ref) | copy-start | bytes 18436
  2.9 8.7 %copy-start.21 = (f32[512]{0:T(512)S(1)}, f32[512]{0:T(512)}, u32[]{:S(2)}) copy-start(f32[512]{0:T(512)} %param.19) | copy-start | bytes 6148
  2.9 8.7 %copy-start.22 = (s32[512]{0:T(512)S(1)}, s32[512]{0:T(512)}, u32[]{:S(2)}) copy-start(s32[512]{0:T(512)} %param.20) | copy-start | bytes 6148
  2.9 8.7 %copy-start.23 = (s32[512]{0:T(512)S(1)}, s32[512]{0:T(512)}, u32[]{:S(2)}) copy-start(s32[512]{0:T(512)} %param.21) | copy-start | bytes 6148
  2.9 31.1 %all-to-all-start.1 = ((f32[8,30,8,128]{3,2,1,0:T(8,128)}), f32[8,30,8,128]{3,2,1,0:T(8,128)S(1)}, u32[]{:S(2)}, u32[]{:S(2)}) async-start(f32[8,30,8,128]{3,2,1,0:T(8,128)} %shard_map.134), calls=%async_computation.1 | async-start | bytes 1966080 | tf_op jit(solution)/shard_map/all_to_all | solution.py:409
  8.1 17.7 %copy-start.2 = (f32[6,5,8,1024]{3,2,1,0:T(8,128)S(1)}, f32[6,5,8,1024]{3,2,1,0:T(8,128)}, u32[]{:S(2)}) copy-start(f32[6,5,8,1024]{3,2,1,0:T(8,128)} %s_ref.3) | copy-start | bytes 2949124
  8.1 17.7 %copy-start.28 = (f32[5,5]{1,0:T(8,128)S(1)}, f32[5,5]{1,0:T(8,128)}, u32[]{:S(2)}) copy-start(f32[5,5]{1,0:T(8,128)} %jx_ref.3) | copy-start | bytes 304
  8.1 17.6 %copy-start.29 = (f32[5,5]{1,0:T(8,128)S(1)}, f32[5,5]{1,0:T(8,128)}, u32[]{:S(2)}) copy-start(f32[5,5]{1,0:T(8,128)} %jz_ref.3) | copy-start | bytes 304
  8.2 17.5 %collective-permute-start = (f32[8,8,1024]{2,1,0:T(8,128)S(1)}, f32[8,8,1024]{2,1,0:T(8,128)S(1)}, u32[]{:S(2)}, u32[]{:S(2)}) collective-permute-start(f32[8,8,1024]{2,1,0:T(8,128)S(1)} %get-tuple-element.18), channel_id=1, source_target_pairs={{0,1},{1,2},{2,3},{3,4},{4,5},{5,6},{6,7},{7,8},{8,9},{9,10},{10,1... | collective-permute-start | bytes 786440 | tf_op jit(solution)/shard_map/ppermute | solution.py:405
  8.3 17.4 %collective-permute-start.1 = (f32[8,8,1024]{2,1,0:T(8,128)S(1)}, f32[8,8,1024]{2,1,0:T(8,128)S(1)}, u32[]{:S(2)}, u32[]{:S(2)}) collective-permute-start(f32[8,8,1024]{2,1,0:T(8,128)S(1)} %get-tuple-element.19), channel_id=1, source_target_pairs={{1,0},{2,1},{3,2},{4,3},{5,4},{6,5},{7,6},{8,7},{9,8},{10,9},{11,1... | collective-permute-start | bytes 786440 | tf_op jit(solution)/shard_map/ppermute | solution.py:405
  34.0 29.6 %all-to-all-start = ((f32[8,34,8,128]{3,2,1,0:T(8,128)}), f32[8,34,8,128]{3,2,1,0:T(8,128)S(1)}, u32[]{:S(2)}, u32[]{:S(2)}) async-start(f32[8,34,8,128]{3,2,1,0:T(8,128)} %copy-done.5), calls=%async_computation | async-start | bytes 2228224 | tf_op jit(solution)/shard_map/all_to_all | solution.py:409
  39.8 17.0 %collective-permute-start.4 = (f32[8,8,1024]{2,1,0:T(8,128)}, f32[8,8,1024]{2,1,0:T(8,128)S(1)}, u32[]{:S(2)}, u32[]{:S(2)}) collective-permute-start(f32[8,8,1024]{2,1,0:T(8,128)} %copy-done.30), channel_id=1, source_target_pairs={{0,1},{1,2},{2,3},{3,4},{4,5},{5,6},{6,7},{7,8},{8,9},{9,10},{10,1... | collective-permute-start | bytes 786440 | tf_op jit(solution)/shard_map/ppermute | solution.py:405
  39.8 17.0 %collective-permute-start.5 = (f32[8,8,1024]{2,1,0:T(8,128)S(1)}, f32[8,8,1024]{2,1,0:T(8,128)S(1)}, u32[]{:S(2)}, u32[]{:S(2)}) collective-permute-start(f32[8,8,1024]{2,1,0:T(8,128)S(1)} %get-tuple-element.23), channel_id=1, source_target_pairs={{1,0},{2,1},{3,2},{4,3},{5,4},{6,5},{7,6},{8,7},{9,8},{10,9},{11,1... | collective-permute-start | bytes 786440 | tf_op jit(solution)/shard_map/ppermute | solution.py:405
  43.1 19.3 %collective-permute-start.2 = (f32[8,512]{1,0:T(8,128)S(1)}, f32[8,512]{1,0:T(8,128)S(1)}, u32[]{:S(2)}, u32[]{:S(2)}) collective-permute-start(f32[8,512]{1,0:T(8,128)S(1)} %bitcast.23), channel_id=1, source_target_pairs={{0,1},{1,2},{2,3},{3,4},{4,5},{5,6},{6,7},{7,8},{8,9},{9,10},{10,1... | collective-permute-start | bytes 49160 | tf_op jit(solution)/shard_map/ppermute | solution.py:405
  43.2 19.8 %collective-permute-start.3 = (f32[8,512]{1,0:T(8,128)S(1)}, f32[8,512]{1,0:T(8,128)S(1)}, u32[]{:S(2)}, u32[]{:S(2)}) collective-permute-start(f32[8,512]{1,0:T(8,128)S(1)} %bitcast.24), channel_id=1, source_target_pairs={{1,0},{2,1},{3,2},{4,3},{5,4},{6,5},{7,6},{8,7},{9,8},{10,9},{11,1... | collective-permute-start | bytes 49160 | tf_op jit(solution)/shard_map/ppermute | solution.py:405
  72.6 16.8 %copy-start.8 = (f32[6,5,8,1024]{3,2,1,0:T(8,128)S(1)}, f32[6,5,8,1024]{3,2,1,0:T(8,128)}, u32[]{:S(2)}) copy-start(f32[6,5,8,1024]{3,2,1,0:T(8,128)} %copy-done.7) | copy-start | bytes 2949124
  72.6 16.8 %copy-start.16 = (f32[6,8,1024]{2,1,0:T(8,128)S(1)}, f32[6,8,1024]{2,1,0:T(8,128)}, u32[]{:S(2)}) copy-start(f32[6,8,1024]{2,1,0:T(8,128)} %copy-done.15) | copy-start | bytes 589828
  72.6 16.8 %copy-start.19 = (f32[8,8,512]{2,1,0:T(8,128)S(1)}, f32[8,8,512]{2,1,0:T(8,128)}, u32[]{:S(2)}) copy-start(f32[8,8,512]{2,1,0:T(8,128)} %copy-done.18) | copy-start | bytes 393220
  72.6 16.8 %all-to-all-start.2 = ((f32[8,34,8,128]{3,2,1,0:T(8,128)}), f32[8,34,8,128]{3,2,1,0:T(8,128)S(1)}, u32[]{:S(2)}, u32[]{:S(2)}) async-start(f32[8,34,8,128]{3,2,1,0:T(8,128)} %copy-done.6), calls=%async_computation.2 | async-start | bytes 2228224 | tf_op jit(solution)/shard_map/all_to_all | solution.py:409
  77.5 7.9 %collective-permute-start.6 = (f32[8,512]{1,0:T(8,128)S(1)}, f32[8,512]{1,0:T(8,128)S(1)}, u32[]{:S(2)}, u32[]{:S(2)}) collective-permute-start(f32[8,512]{1,0:T(8,128)S(1)} %copy-done.34), channel_id=1, source_target_pairs={{0,1},{1,2},{2,3},{3,4},{4,5},{5,6},{6,7},{7,8},{8,9},{9,10},{10,1... | collective-permute-start | bytes 49160 | tf_op jit(solution)/shard_map/ppermute | solution.py:405
  77.6 7.8 %collective-permute-start.7 = (f32[8,512]{1,0:T(8,128)S(1)}, f32[8,512]{1,0:T(8,128)S(1)}, u32[]{:S(2)}, u32[]{:S(2)}) collective-permute-start(f32[8,512]{1,0:T(8,128)S(1)} %copy-done.32), channel_id=1, source_target_pairs={{1,0},{2,1},{3,2},{4,3},{5,4},{6,5},{7,6},{8,7},{9,8},{10,9},{11,1... | collective-permute-start | bytes 49160 | tf_op jit(solution)/shard_map/ppermute | solution.py:405
  (22 other events, 29.8 us)

commit v2 on v1

v2 whole, which is shorter than its diff:
```python
import math

import jax
import jax.numpy as jnp
import ml_dtypes
import numpy as np
from jax import lax
from jax.experimental import pallas as pl
from jax.experimental.pallas import tpu as pltpu
from jax.sharding import PartitionSpec as P

NT, NV, NH = 48, 5, 4
ROWS, SPAN, MSPAN, NF = 8, 1024, 512, 512
CHUNK = 128
CH = 2 * NH
F32, BF16 = jnp.float32, jnp.bfloat16

damping_fourth = 1.0 / 32.0
viscous_coef = 0.1
sigma_fluid = 0.5
metal_step = 0.2
sigma_metal = 0.5
heat_capacity = 0.5
flux_scale = 4.0


def tables():
    t = np.arange(NT)
    offset = t[:, None] - t[None, :]
    angle = np.where(offset == 0, 0.5, math.pi * offset / NT)
    spectral = np.where(
        offset == 0, 0.0, 0.5 * (1.0 - 2.0 * (offset % 2)) * np.cos(angle) / np.sin(angle)
    )
    phase = 2.0 * math.pi * ((np.arange(NH)[:, None] * t[None, :]) % NT) / NT
    synth = np.concatenate([np.cos(phase), -np.sin(phase)])
    w0 = synth * (flux_scale / NT)
    w1 = w0 @ spectral
    w2 = w1 @ spectral
    high = spectral.astype(np.float32).astype(ml_dtypes.bfloat16)
    low = (spectral - high.astype(np.float64)).astype(np.float32).astype(ml_dtypes.bfloat16)
    eye = np.eye(ROWS, dtype=np.float32)
    kron_high = np.kron(high.astype(np.float32), eye)
    kron_low = np.kron(low.astype(np.float32), eye)
    kron = np.concatenate([kron_high, kron_high, kron_low], axis=1).astype(ml_dtypes.bfloat16)
    flat = np.concatenate([m.T.reshape(-1) for m in (synth, w0, w1, w2)]).astype(np.float32)
    return kron, flat


KRON, FLAT = tables()
SYNTH, W0, W1, W2 = (i * NT * CH for i in range(4))


class Loaded:
    def __init__(self, source, buffer, sems, cut):
        self.buffer, self.copies = buffer, []
        for i, index in enumerate(cut):
            self.copies.append(pltpu.make_async_copy(source.at[index], buffer.at[index], sems.at[i]))
        self.waiting = set(range(len(cut)))

    def start(self, i):
        self.copies[i].start()

    def piece(self, i):
        if i in self.waiting:
            self.waiting.remove(i)
            self.copies[i].wait()
        return self.buffer

    def whole(self):
        for i in range(len(self.copies)):
            self.piece(i)
        return self.buffer


class Stored:
    def __init__(self, target, buffer, sems):
        self.target, self.buffer, self.sems, self.copies = target, buffer, sems, []

    def put(self, index):
        copy = pltpu.make_async_copy(
            self.buffer.at[index], self.target.at[index], self.sems.at[len(self.copies)]
        )
        copy.start()
        self.copies.append(copy)

    def finish(self):
        for copy in self.copies:
            copy.wait()


WHOLE = (slice(None),)


def by_piece(n):
    return tuple(pl.ds(i, 1) for i in range(n))


def call(body, operands, results, scratch=(), flops=1 << 22, moved=1 << 22):
    space = {"smem": pltpu.SMEM, "vmem": pltpu.VMEM}
    modes = [mode for _, mode in operands]
    here = [isinstance(mode, str) for mode in modes]
    in_specs = [
        pl.BlockSpec(memory_space=space[m] if h else pltpu.HBM) for m, h in zip(modes, here)
    ]
    out_specs = [pl.BlockSpec(memory_space=pltpu.HBM if n else pltpu.VMEM) for _, n in results]
    buffers = []
    for array, mode in operands:
        if not isinstance(mode, str):
            buffers += [pltpu.VMEM(array.shape, array.dtype), pltpu.SemaphoreType.DMA((len(mode),))]
    for dims, n in results:
        if n > 0:
            buffers += [pltpu.VMEM(dims, F32), pltpu.SemaphoreType.DMA((n,))]

    def kernel(*refs):
        ins, refs = refs[: len(modes)], refs[len(modes) :]
        outs, refs = refs[: len(results)], list(refs[len(results) :])
        args, loads = [], []
        for ref, mode, h in zip(ins, modes, here):
            if h:
                args.append(ref)
            else:
                args.append(Loaded(ref, refs.pop(0), refs.pop(0), mode))
                loads.append(args[-1])
        for i in range(max([len(x.copies) for x in loads], default=0)):
            for x in loads:
                if i < len(x.copies):
                    x.start(i)
        stores = []
        for ref, (_, n) in zip(outs, results):
            if n > 0:
                args.append(Stored(ref, refs.pop(0), refs.pop(0)))
                stores.append(args[-1])
            else:
                args.append(ref)
        body(*args, *refs)
        for x in loads:
            x.whole()
        for x in stores:
            x.finish()

    return pl.pallas_call(
        kernel,
        out_shape=[pltpu.HBM(dims, F32) if n else shape(*dims) for dims, n in results],
        in_specs=in_specs,
        out_specs=out_specs,
        scratch_shapes=buffers + list(scratch),
        compiler_params=pltpu.CompilerParams(vmem_limit_bytes=24 << 20),
        cost_estimate=pl.CostEstimate(flops=flops, bytes_accessed=moved, transcendentals=0),
    )(
        *[a if h else pltpu.with_memory_space_constraint(a, pltpu.HBM) for (a, _), h in zip(operands, here)]
    )


def shape(*dims):
    return jax.ShapeDtypeStruct(dims, F32)


def row_index(n=SPAN):
    return lax.broadcasted_iota(jnp.int32, (ROWS, n), 0)


def split(x):
    high = x.astype(BF16)
    return high, (x - high.astype(F32)).astype(BF16)


def one_hot(index, n):
    cell = lax.broadcasted_iota(jnp.int32, (n, NF), 0)
    return jnp.where(cell == index, 1.0, 0.0).astype(BF16)


def at_faces(field, span_hot, row_hot):
    n = field.shape[-1]
    both = jnp.concatenate(split(field.reshape(CH * ROWS, n)), axis=0)
    picked = jnp.dot(both, span_hot, preferred_element_type=F32)
    picked = (picked[: CH * ROWS] + picked[CH * ROWS :]).reshape(CH, ROWS, NF)
    return jnp.sum(picked * row_hot[None], axis=1)


def onto_cells(values, span_hot, row_hot):
    spread = (values[:, None, :] * row_hot[None]).reshape(CH * ROWS, NF)
    both = jnp.concatenate(split(spread), axis=0)
    out = lax.dot_general(both, span_hot, (((1,), (1,)), ((), ())), preferred_element_type=F32)
    return (out[: CH * ROWS] + out[CH * ROWS :]).reshape(CH, ROWS, span_hot.shape[0])


def fluid_hots(ff_ref):
    cell = ff_ref[...]
    span = one_hot(cell & (SPAN - 1), SPAN)
    rows = jnp.where(row_index(NF) == (cell >> 10), 1.0, 0.0)
    return span, rows


def metal_hots(mf_ref):
    cell = mf_ref[...]
    span = one_hot(cell & (MSPAN - 1), MSPAN)
    rows = jnp.where(row_index(NF) == (cell >> 9), 1.0, 0.0)
    return span, rows


def span_sides(a):
    n = a.shape[-1]
    lane = lax.broadcasted_iota(jnp.int32, a.shape, a.ndim - 1)
    north = jnp.where(lane == n - 1, 0.0, pltpu.roll(a, n - 1, a.ndim - 1))
    south = jnp.where(lane == 0, 0.0, pltpu.roll(a, 1, a.ndim - 1))
    return north, south


def stencil_parts(a, before, after):
    row = row_index(a.shape[-1])
    east_one = pltpu.roll(jnp.where(row == 0, after, a), 7, 0)
    east_two = pltpu.roll(jnp.where(row < 2, after, a), 6, 0)
    west_one = pltpu.roll(jnp.where(row == 7, before, a), 1, 0)
    west_two = pltpu.roll(jnp.where(row >= 6, before, a), 2, 0)
    north, south = span_sides(a)
    rest = (
        (4.0 * damping_fourth) * (east_one + west_one)
        - damping_fourth * (east_two + west_two)
        + viscous_coef * (north + south)
        - (6.0 * damping_fourth + 2.0 * viscous_coef + sigma_fluid) * a
    )
    return east_one - west_one, north - south, rest


def edge_tile(ref, tile):
    return jnp.concatenate([ref[2 * tile], ref[2 * tile + 1]], axis=1)


def halo_pair(up_ref, down_ref, t, v):
    tile, slot = (t, v) if v < 4 else (6 + t // 4, t % 4)
    before = pltpu.roll(edge_tile(up_ref, tile), (6 - 2 * slot) % 8, 0)
    after = pltpu.roll(edge_tile(down_ref, tile), (8 - 2 * slot) % 8, 0)
    return before, after


def pack_tile(blocks, tile, up_ref, down_ref):
    row = row_index()
    up = down = None
    for slot, a in enumerate(blocks):
        u = pltpu.roll(a, (2 * slot + 2) % 8, 0) if (2 * slot + 2) % 8 else a
        d = pltpu.roll(a, 2 * slot, 0) if slot else a
        mine = (row >> 1) == slot
        up = u if up is None else jnp.where(mine, u, up)
        down = d if down is None else jnp.where(mine, d, down)
    for half in range(2):
        cut = slice(half * 512, half * 512 + 512)
        up_ref[2 * tile + half] = up[:, cut]
        down_ref[2 * tile + half] = down[:, cut]


def pack_last(get, extra, up_ref, down_ref):
    pack_tile([get(t) for t in range(4)], 6, up_ref, down_ref)
    pack_tile([get(4), get(5), extra, extra], 7, up_ref, down_ref)


def prepare_kernel(a, ps, m_ref, up, down, blocks, sems):
    copies = []
    for t in range(6):
        ref = a.piece(t)
        pack_tile([ref[t, v] for v in range(4)], t, up.buffer, down.buffer)
    pack_last(lambda t: a.buffer[t, NV - 1], ps[...], up.buffer, down.buffer)
    metal_edges(m_ref, up.buffer.at[16], down.buffer.at[16])
    up.put(slice(None))
    down.put(slice(None))
    for i in range(8):
        copies.append(
            pltpu.make_async_copy(
                a.buffer.at[:, :, :, pl.ds(i * CHUNK, CHUNK)], blocks.at[i], sems.at[i]
            )
        )
        copies[-1].start()
    for copy in copies:
        copy.wait()


def energy_kernel(tab_ref, m_ref, fc_ref, ff_ref, mf_ref, e):
    first = lax.axis_index("inst") * 6
    m_hot, m_row = metal_hots(mf_ref)
    f_hot, f_row = fluid_hots(ff_ref)
    values = at_faces(m_ref[...], m_hot, m_row) * fc_ref[...]
    cells = onto_cells(values, f_hot, f_row)
    for t in range(6):
        e.buffer[t] = combine(tab_ref, SYNTH, first + t, cells)
        e.put(pl.ds(t, 1))


def combine(tab_ref, base, t, fields):
    total = tab_ref[base + t * CH] * fields[0]
    for ch in range(1, CH):
        if ch != NH:
            total += tab_ref[base + t * CH + ch] * fields[ch]
    return total


def convect(jx_ref, jz_ref, dx, dz, rest, u):
    out = rest
    for v in range(NV):
        out = out - (0.5 * jx_ref[u, v]) * dx[v] - (0.5 * jz_ref[u, v]) * dz[v]
    return out


def first_kernel(
    tab_ref, jx_ref, jz_ref, a_in, s_in, ps_ref, up_ref, down_ref, e_in, fc_ref, ff_ref, m_ref, cond_ref,
    q, b_out, bup, bdown, hq, m_out,
    parts,
):
    first = lax.axis_index("inst") * 6
    step = ps_ref[...]
    step_before = pltpu.roll(edge_tile(up_ref, 7), 2, 0)
    step_after = pltpu.roll(edge_tile(down_ref, 7), 4, 0)
    q_ref, b_ref = q.buffer, b_out.buffer
    for t in range(6):
        a_ref, s_ref, e_ref = a_in.piece(t), s_in.piece(t), e_in.piece(t)
        for v in range(NV):
            a = a_ref[t, v]
            before, after = halo_pair(up_ref, down_ref, t, v)
            dx, dz, rest = stencil_parts(a, before, after)
            parts[0, v], parts[1, v], parts[2, v] = dx, dz, rest
            dx, dz, rest = stencil_parts(step * a, step_before * before, step_after * after)
            parts[3, v], parts[4, v], parts[5, v] = dx, dz, rest
        for i in range(8):
            cut = pl.ds(i * CHUNK, CHUNK)
            dx = [parts[0, v, :, cut] for v in range(NV)]
            dz = [parts[1, v, :, cut] for v in range(NV)]
            px = [parts[3, v, :, cut] for v in range(NV)]
            pz = [parts[4, v, :, cut] for v in range(NV)]
            for u in range(NV):
                a = a_ref[t, u, :, cut]
                space = convect(jx_ref, jz_ref, dx, dz, parts[2, u, :, cut], u)
                source = s_ref[t, u, :, cut] + space
                if u == NV - 1:
                    source = source + e_ref[t, :, cut]
                b = a + ps_ref[:, cut] * source
                b_ref[t, u, :, cut] = b
                q_ref[i, t * NV + u] = a + b + convect(jx_ref, jz_ref, px, pz, parts[5, u, :, cut], u)
        q.put((slice(None), pl.ds(t * NV, NV)))
        b_out.put(pl.ds(t, 1))
        pack_tile([b_ref[t, v] for v in range(4)], t, bup.buffer, bdown.buffer)
    pack_last(lambda t: b_ref[t, NV - 1], step, bup.buffer, bdown.buffer)
    bup.put(slice(None))
    bdown.put(slice(None))
    f_hot, f_row = fluid_hots(ff_ref)
    heat = []
    for ch in range(CH):
        h0 = h1 = h2 = h3 = None
        for t in range(6):
            at = (first + t) * CH + ch
            q4 = jnp.concatenate([q_ref[i, t * NV + NV - 1] for i in range(8)], axis=1)
            a, b = a_in.buffer[t, NV - 1], b_ref[t, NV - 1]
            x0 = tab_ref[W0 + at] * b
            x1 = tab_ref[W1 + at] * a
            x2 = tab_ref[W1 + at] * q4
            x3 = tab_ref[W2 + at] * a
            h0, h1, h2, h3 = (
                (x0, x1, x2, x3) if t == 0 else (h0 + x0, h1 + x1, h2 + x2, h3 + x3)
            )
        heat.append(h0 - step * h1)
        hq.buffer[ch] = step * (step * h3 - h2)
    hq.put(slice(None))
    values = at_faces(jnp.stack(heat), f_hot, f_row) * fc_ref[...]
    for i in range(8):
        for k in range(4):
            q_ref[i, 30 + k] = values[:, k * CHUNK : (k + 1) * CHUNK]
    q.put((slice(None), pl.ds(30, 4)))
    before, after = metal_sides(up_ref.at[16], down_ref.at[16])
    m = metal_update(m_ref, before, after, cond_ref[...])
    for ch in range(CH):
        m_out.buffer[ch] = m[ch]
    m_out.put(slice(None))


def rotate_time(kron, x):
    high, low = split(x)
    return jnp.dot(kron, jnp.concatenate([high, low, high], axis=0), preferred_element_type=F32)


def local_step(ps_ref):
    start = pl.multiple_of(lax.axis_index("inst") * CHUNK, CHUNK)
    return ps_ref[:, pl.ds(start, CHUNK)]


def turned(get):
    return jnp.concatenate(
        [
            jnp.concatenate([get(j, t, v) for j in range(8) for t in range(6)], axis=0)
            for v in range(NV)
        ],
        axis=1,
    )


def derive_kernel(kron, a, ps_ref, g):
    wide = jnp.concatenate([local_step(ps_ref)] * NV, axis=1)
    a_ref = a.whole()
    x = turned(lambda j, t, v: a_ref[j, t, v])
    d = rotate_time(kron.whole()[...], x)
    g.buffer[...] = (d.reshape(NT, ROWS, NV * CHUNK) * wide[None]).reshape(NT * ROWS, NV * CHUNK)
    g.put(slice(None))


def middle_kernel(tab_ref, jx_ref, jz_ref, b_in, s_in, ps_ref, up_ref, down_ref, hq_in, c_out, hc, parts):
    first = lax.axis_index("inst") * 6
    c_ref = c_out.buffer
    for t in range(6):
        b_ref, s_ref = b_in.piece(t), s_in.piece(t)
        for v in range(NV):
            before, after = halo_pair(up_ref, down_ref, t, v)
            dx, dz, rest = stencil_parts(b_ref[t, v], before, after)
            parts[0, v], parts[1, v], parts[2, v] = dx, dz, rest
        for i in range(8):
            cut = pl.ds(i * CHUNK, CHUNK)
            dx = [parts[0, v, :, cut] for v in range(NV)]
            dz = [parts[1, v, :, cut] for v in range(NV)]
            for u in range(NV):
                space = convect(jx_ref, jz_ref, dx, dz, parts[2, u, :, cut], u)
                c_ref[t, u, :, cut] = b_ref[t, u, :, cut] + ps_ref[:, cut] * (s_ref[t, u, :, cut] + space)
        c_out.put(pl.ds(t, 1))
    hq_ref = hq_in.whole()
    for ch in range(CH):
        total = hq_ref[ch]
        for t in range(6):
            total += tab_ref[W0 + (first + t) * CH + ch] * c_ref[t, NV - 1]
        hc.buffer[ch] = total
    hc.put(slice(None))


def metal_update(m, before, after, cond):
    row = row_index(MSPAN)
    out = []
    for ch in range(CH):
        a = m[ch]
        east = pltpu.roll(jnp.where(row == 0, after[ch], a), 7, 0)
        west = pltpu.roll(jnp.where(row == 7, before[ch], a), 1, 0)
        north, south = span_sides(a)
        laplace = east + west + north + south - 4.0 * a
        h = ch % NH
        turn = -heat_capacity * h * m[ch + NH] if ch < NH else heat_capacity * h * m[ch - NH]
        out.append(a + metal_step * (cond * laplace - sigma_metal * a - turn))
    return out


def metal_edges(m, up_ref, down_ref):
    up_ref[...] = jnp.concatenate([m[ch][7:8] for ch in range(CH)], axis=0)
    down_ref[...] = jnp.concatenate([m[ch][0:1] for ch in range(CH)], axis=0)


def metal_sides(up_ref, down_ref):
    before = [jnp.broadcast_to(up_ref[ch : ch + 1], (ROWS, MSPAN)) for ch in range(CH)]
    after = [jnp.broadcast_to(down_ref[ch : ch + 1], (ROWS, MSPAN)) for ch in range(CH)]
    return before, after


def heat_sum(blocks_ref):
    tiles = []
    for k in range(4):
        total = blocks_ref[0, 30 + k]
        for j in range(1, 8):
            total += blocks_ref[j, 30 + k]
        tiles.append(total)
    return jnp.concatenate(tiles, axis=1)


def second_kernel(
    tab_ref, q, g, kron, ps_ref, m_in, fc_ref, ff_ref, mf_ref, hc,
    v, m_out, mup, mdown, e,
):
    first = lax.axis_index("inst") * 6
    step = ps_ref[...]
    coeff = fc_ref[...]
    m_hot, m_row = metal_hots(mf_ref)
    f_hot, f_row = fluid_hots(ff_ref)
    q_ref, v_ref = q.whole(), v.buffer
    source = onto_cells(heat_sum(q_ref), m_hot, m_row)
    m_ref = m_in.whole()
    m = [m_ref[ch] + metal_step * source[ch] for ch in range(CH)]
    for ch in range(CH):
        m_out.buffer[ch] = m[ch]
    m_out.put(slice(None))
    metal_edges(m, mup.buffer, mdown.buffer)
    mup.put(slice(None))
    mdown.put(slice(None))
    cells = onto_cells(at_faces(jnp.stack(m), m_hot, m_row) * coeff, f_hot, f_row)
    for t in range(6):
        e.buffer[t] = step * combine(tab_ref, SYNTH, first + t, cells)
    e.put(slice(None))
    hc_ref = hc.whole()
    heat = []
    for ch in range(CH):
        total = hc_ref[ch]
        for t in range(6):
            total += tab_ref[W0 + (first + t) * CH + ch] * e.buffer[t]
        heat.append(total)
    values = at_faces(jnp.stack(heat), f_hot, f_row) * coeff
    for i in range(8):
        for k in range(4):
            v_ref[i, 30 + k] = values[:, k * CHUNK : (k + 1) * CHUNK]
    x = turned(lambda j, t, u: q_ref[j, t * NV + u]) - g.whole()[...]
    kron_ref = kron.whole()
    minus = -local_step(ps_ref)
    for half in range(2):
        d = rotate_time(kron_ref[pl.ds(half * 192, 192), :], x)
        for j in range(4):
            for t in range(6):
                at = (j * 6 + t) * ROWS
                for u in range(NV):
                    v_ref[half * 4 + j, t * NV + u] = minus * d[at : at + ROWS, u * CHUNK : (u + 1) * CHUNK]
        v.put(pl.ds(half * 4, 4))


def last_kernel(v, c, e, m_in, mup_ref, mdown_ref, cond_ref, mf_ref, out, m_out):
    for t in range(6):
        v_ref, c_ref, e_ref = v.piece(t), c.piece(t), e.whole()
        for i in range(8):
            cut = pl.ds(i * CHUNK, CHUNK)
            for u in range(NV):
                total = c_ref[t, u, :, cut] + v_ref[i, t * NV + u]
                if u == NV - 1:
                    total = total + e_ref[t, :, cut]
                out.buffer[t, u, :, cut] = total
        out.put(pl.ds(t, 1))
    m_hot, m_row = metal_hots(mf_ref)
    source = onto_cells(heat_sum(v.whole()), m_hot, m_row)
    before, after = metal_sides(mup_ref, mdown_ref)
    m = metal_update(m_in.whole(), before, after, cond_ref[...])
    for ch in range(CH):
        m_out.buffer[ch] = m[ch] + metal_step * source[ch]
    m_out.put(slice(None))


def exchange(up, down):
    n = lax.axis_size("space")
    forward = [(i, (i + 1) % n) for i in range(n)]
    back = [(j, i) for i, j in forward]
    return lax.ppermute(up, "space", forward), lax.ppermute(down, "space", back)


def turn(x):
    return lax.all_to_all(x, "inst", 0, 0, tiled=True)


SIX = by_piece(6)
EDGES = (17, ROWS, 512)
FLUID = (6, NV, ROWS, SPAN)
METAL = (CH, ROWS, MSPAN)
BLOCKS = (8, 34, ROWS, CHUNK)


def local(a0, source, ps, jx, jz, metal, cond, coeff, ff, mf):
    kron = jnp.asarray(KRON)
    tab = jnp.asarray(FLAT)
    coeff, ff, mf = (x.reshape(1, NF) for x in (coeff, ff, mf))
    metal = metal.reshape(CH, ROWS, MSPAN)
    up, down, blocks = call(
        prepare_kernel,
        [(a0, SIX), (ps, "vmem"), (metal, "vmem")],
        [(EDGES, 1), (EDGES, 1), ((8, 6, NV, ROWS, CHUNK), -1)],
        scratch=[pltpu.SemaphoreType.DMA((8,))],
    )
    up, down = exchange(up, down)
    a_turned = turn(blocks)
    (e0,) = call(
        energy_kernel,
        [(tab, "smem"), (metal, "vmem"), (coeff, "vmem"), (ff, "vmem"), (mf, "vmem")],
        [((6, ROWS, SPAN), 6)],
    )
    jacobians = [(tab, "smem"), (jx, "smem"), (jz, "smem")]
    q, b, bup, bdown, hq, metal = call(
        first_kernel,
        jacobians
        + [(a0, SIX), (source, SIX), (ps, "vmem"), (up, "vmem"), (down, "vmem"), (e0, SIX)]
        + [(coeff, "vmem"), (ff, "vmem"), (metal, "vmem"), (cond, "vmem")],
        [(BLOCKS, 7), (FLUID, 6), (EDGES, 1), (EDGES, 1), ((CH, ROWS, SPAN), 1), (METAL, 1)],
        scratch=[pltpu.VMEM((6, NV, ROWS, SPAN), F32)],
    )
    q_turned = turn(q)
    bup, bdown = exchange(bup, bdown)
    (g,) = call(
        derive_kernel,
        [(kron, WHOLE), (a_turned, WHOLE), (ps, "vmem")],
        [((NT * ROWS, NV * CHUNK), 1)],
    )
    c, hc = call(
        middle_kernel,
        jacobians
        + [(b, SIX), (source, SIX), (ps, "vmem"), (bup, "vmem"), (bdown, "vmem"), (hq, WHOLE)],
        [(FLUID, 6), ((CH, ROWS, SPAN), 1)],
        scratch=[pltpu.VMEM((3, NV, ROWS, SPAN), F32)],
    )
    v, metal, mup, mdown, e1 = call(
        second_kernel,
        [(tab, "smem"), (q_turned, WHOLE), (g, WHOLE), (kron, WHOLE), (ps, "vmem"), (metal, WHOLE)]
        + [(coeff, "vmem"), (ff, "vmem"), (mf, "vmem"), (hc, WHOLE)],
        [(BLOCKS, 2), (METAL, 1), ((CH, MSPAN), 1), ((CH, MSPAN), 1), ((6, ROWS, SPAN), 1)],
    )
    v = turn(v)
    mup, mdown = exchange(mup, mdown)
    pieces = tuple((slice(None), pl.ds(t * NV, NV)) for t in range(6)) + ((slice(None), pl.ds(30, 4)),)
    out, metal = call(
        last_kernel,
        [(v, pieces), (c, SIX), (e1, WHOLE), (metal, WHOLE), (mup, "vmem"), (mdown, "vmem")]
        + [(cond, "vmem"), (mf, "vmem")],
        [(FLUID, 6), (METAL, 1)],
    )
    return out, metal.reshape(2, NH, ROWS, MSPAN)


def solution(mesh):
    return jax.shard_map(
        local,
        mesh=mesh,
        in_specs=(
            P("inst", None, "space", None),
            P("inst", None, "space", None),
            P("space", None),
            P(),
            P(),
            P(None, None, "space", None),
            P("space", None),
            P("space"),
            P("space"),
            P("space"),
        ),
        out_specs=(P("inst", None, "space", None), P(None, None, "space", None)),
        check_vma=False,
    )
```

time: 92.1 us -> 96.3 us (1.046)
  Pallas kernels: 14.9 us -> 28.8 us
  local copies, waits for them, and re-layouts: 14.2 us -> 4.64 us
  starting transfers between devices: 29 us -> 25.8 us
  waiting for transfers between devices: 31.7 us -> 34.7 us
    pallas_call x8 -> x7, Pallas kernels: 14.9 us -> 28.8 us  [call(): pl.pallas_call(kernel, out_shape=[pltpu.HBM(dims, F32) if n else shape(*d...]
    unnamed x72 -> x40, local copies, waits for them, and re-layouts: 14.2 us -> 4.64 us
    ppermute x4 -> x3, starting transfers between devices: 12.9 us -> 9.69 us  [exchange(): lax.ppermute(down, 'space', back)]
    ppermute x4 -> x3, waiting for transfers between devices: 27.7 us -> 30.8 us  [exchange(): lax.ppermute(up, 'space', forward)]
  transfers between devices with their start and end apart: 11 -> 9, of which waited for: 4 -> 4; matrix products, arithmetic and copies ran while one was open for 0% -> 0% of each run, Pallas kernels for 11% -> 18%
where the time goes in v2:
time: 96.3 us; the launch traced here: 95.1 us
  waiting for transfers between devices  34.7 us (36%)
  Pallas kernels  28.8 us (30%)
  starting transfers between devices  25.8 us (27%)
  local copies, waits for them, and re-layouts  4.64 us (5%)
  between operations  1.09 us (1%)
    ppermute x3, waiting for transfers between devices, exchange(): lax.ppermute(up, 'space', forward)  30.8 us
    pallas_call x7, Pallas kernels, call(): pl.pallas_call(kernel, out_shape=[pltpu.HBM(dims, F32) if n else shape(*d...  28.8 us
    all_to_all x3, starting transfers between devices, turn(): return lax.all_to_all(x, 'inst', 0, 0, tiled=True)  15.9 us
    ppermute x3, starting transfers between devices, exchange(): lax.ppermute(down, 'space', back)  9.69 us
    unnamed x40, local copies, waits for them, and re-layouts  4.64 us
    all_to_all x3, waiting for transfers between devices, turn(): return lax.all_to_all(x, 'inst', 0, 0, tiled=True)  3.94 us
  transfers between devices with their start and end apart: 9, of which 4 were waited for; matrix products, arithmetic and copies ran while one was open for 0% of the time, Pallas kernels for 18%

profile of v2, /device:TPU:112, one launch (start us, length us, event | category | flops | bytes accessed | tf_op | source)
XLA Modules:
  0.0 95.1 jit_solution(4394104612942777438)
XLA Ops:
  0.6 0.9 copy-done
  1.5 0.8 copy-done.2
  2.3 2.5 %shard_map.131 = (f32[17,8,512]{2,1,0:T(8,128)}, f32[17,8,512]{2,1,0:T(8,128)}, f32[8,6,5,8,128]{4,3,2,1,0:T(8,128)}) custom-call(f32[6,5,8,1024]{3,2,1,0:T(8,128)} %refs_3_.2, f32[8,1024]{1,0:T(8,128)S(1)} %copy-done.2, f32[8,8,512]{2,1,0:T(8,128)S(1)} %bitcast.5), custom_call_target="tpu_custom_call" | custom-call | flops 4194304 | bytes 4194304 | tf_op jit(solution)/shard_map/pallas_call | solution.py:141
  5.0 5.2 %all-to-all-start.1 = ((f32[8,6,5,8,128]{4,3,2,1,0:T(8,128)}), f32[8,6,5,8,128]{4,3,2,1,0:T(8,128)S(1)}, u32[]{:S(2)}, u32[]{:S(2)}) async-start(f32[8,6,5,8,128]{4,3,2,1,0:T(8,128)} %get-tuple-element.23), calls=%async_computation.1 | async-start | bytes 1966080 | tf_op jit(solution)/shard_map/all_to_all | solution.py:538
  10.1 0.1 collective-permute-start
  10.2 3.2 %collective-permute-start.1 = (f32[17,8,512]{2,1,0:T(8,128)S(1)}, f32[17,8,512]{2,1,0:T(8,128)S(1)}, u32[]{:S(2)}, u32[]{:S(2)}) collective-permute-start(f32[17,8,512]{2,1,0:T(8,128)S(1)} %copy-done.16), channel_id=1, source_target_pairs={{1,0},{2,1},{3,2},{4,3},{5,4},{6,5},{7,6},{8,7},{9,8},{10,9},{11,1... | collective-permute-start | bytes 835592 | tf_op jit(solution)/shard_map/ppermute | solution.py:534
  13.5 2.1 %shard_map.132.refs_8_ = f32[6,8,1024]{2,1,0:T(8,128)} custom-call(f32[1536]{0:T(1024)S(1)} %copy-done.4, f32[8,8,512]{2,1,0:T(8,128)S(1)} %bitcast.6, f32[1,512]{1,0:T(1,128)S(1)} %bitcast.8, s32[1,512]{1,0:T(1,128)S(1)} %bitcast.11, s32[1,512]{1,0:T(1,128)S(1)} %bitcast.14), custom_call_target="tpu_custom_call" | custom-call | flops 4194304 | bytes 4194304 | tf_op jit(solution)/shard_map/pallas_call | solution.py:141
  15.6 12.5 %collective-permute-done.refs_6_ = f32[17,8,512]{2,1,0:T(8,128)S(1)} collective-permute-done((f32[17,8,512]{2,1,0:T(8,128)S(1)}, f32[17,8,512]{2,1,0:T(8,128)S(1)}, u32[]{:S(2)}, u32[]{:S(2)}) %collective-permute-start) | collective-permute-done | bytes 278560 | tf_op jit(solution)/shard_map/ppermute | solution.py:534
  28.1 7.4 %shard_map.133 = (f32[8,34,8,128]{3,2,1,0:T(8,128)}, f32[6,5,8,1024]{3,2,1,0:T(8,128)}, f32[17,8,512]{2,1,0:T(8,128)}, f32[17,8,512]{2,1,0:T(8,128)}, f32[8,8,1024]{2,1,0:T(8,128)}, /*index=5*/f32[8,8,512]{2,1,0:T(8,128)}) custom-call(f32[1536]{0:T(1024)S(1)} %copy-done.4, f32[5,5]{1,0:T(8,128)S(1)} %copy-done.9, f32[5,5]{1,0:T(8,128)S(1)} %copy-done.10, ...), custom_call_target="tpu_custom_call" | custom-call | flops 4194304 | bytes 4194304 | tf_op jit(solution)/shard_map/pallas_call | solution.py:141
  35.5 0.9 copy-done.13
  36.4 5.8 %all-to-all-start = ((f32[8,34,8,128]{3,2,1,0:T(8,128)}), f32[8,34,8,128]{3,2,1,0:T(8,128)S(1)}, u32[]{:S(2)}, u32[]{:S(2)}) async-start(f32[8,34,8,128]{3,2,1,0:T(8,128)} %get-tuple-element.22), calls=%async_computation | async-start | bytes 2228224 | tf_op jit(solution)/shard_map/all_to_all | solution.py:538
  42.3 0.1 collective-permute-start.2
  42.4 3.2 %collective-permute-start.3 = (f32[17,8,512]{2,1,0:T(8,128)S(1)}, f32[17,8,512]{2,1,0:T(8,128)S(1)}, u32[]{:S(2)}, u32[]{:S(2)}) collective-permute-start(f32[17,8,512]{2,1,0:T(8,128)S(1)} %copy-done.14), channel_id=1, source_target_pairs={{1,0},{2,1},{3,2},{4,3},{5,4},{6,5},{7,6},{8,7},{9,8},{10,9},{11,1... | collective-permute-start | bytes 835592 | tf_op jit(solution)/shard_map/ppermute | solution.py:534
  45.6 13.7 %collective-permute-done.2.refs_6_ = f32[17,8,512]{2,1,0:T(8,128)S(1)} collective-permute-done((f32[17,8,512]{2,1,0:T(8,128)S(1)}, f32[17,8,512]{2,1,0:T(8,128)S(1)}, u32[]{:S(2)}, u32[]{:S(2)}) %collective-permute-start.2) | collective-permute-done | bytes 278560 | tf_op jit(solution)/shard_map/ppermute | solution.py:534
  59.3 4.6 %shard_map.135 = (f32[6,5,8,1024]{3,2,1,0:T(8,128)}, f32[8,8,1024]{2,1,0:T(8,128)}) custom-call(f32[1536]{0:T(1024)S(1)} %copy-done.4, f32[5,5]{1,0:T(8,128)S(1)} %copy-done.9, f32[5,5]{1,0:T(8,128)S(1)} %copy-done.10, f32[6,5,8,1024]{3,2,1,0:T(8,128)} %get-tuple-element.25.refs_3_, f32[6,5,8,1024]{3,2,1,0:T(8,128)} %refs_4_.4, f32[8,1024]{1,0:T(8,128)S(1)} %copy-done.3, ...), custom_call_target="tpu_custom_call" | custom-call | flops 4194304 | bytes 4194304 | tf_op jit(solution)/shard_map/pallas_call | solution.py:141
  63.9 3.4 %shard_map.134.refs_2_ = f32[384,640]{1,0:T(8,128)} custom-call(bf16[384,1152]{1,0:T(8,128)(2,1)} %constant.4.clone.refs_0_.refs_3_, f32[8,6,5,8,128]{4,3,2,1,0:T(8,128)} %copy-done.13, f32[8,1024]{1,0:T(8,128)S(1)} %copy-done.3), custom_call_target="tpu_custom_call" | custom-call | flops 4194304 | bytes 4194304 | tf_op jit(solution)/shard_map/pallas_call | solution.py:141
  67.4 1.0 %copy-done.11 = f32[8,34,8,128]{3,2,1,0:T(8,128)} copy-done((f32[8,34,8,128]{3,2,1,0:T(8,128)}, f32[8,34,8,128]{3,2,1,0:T(8,128)S(1)}, u32[]{:S(2)}) %copy-start.11) | copy-done | bytes 1114136
  68.4 5.6 %shard_map.136 = (f32[8,34,8,128]{3,2,1,0:T(8,128)}, f32[8,8,512]{2,1,0:T(8,128)}, f32[8,512]{1,0:T(8,128)}, f32[8,512]{1,0:T(8,128)}, f32[6,8,1024]{2,1,0:T(8,128)}) custom-call(f32[1536]{0:T(1024)S(1)} %copy-done.4, f32[8,34,8,128]{3,2,1,0:T(8,128)} %copy-done.11, f32[384,640]{1,0:T(8,128)} %shard_map.134.refs_2_, ...), custom_call_target="tpu_custom_call" | custom-call | flops 4194304 | bytes 4194304 | tf_op jit(solution)/shard_map/pallas_call | solution.py:141
  74.0 4.9 %all-to-all-start.2 = ((f32[8,34,8,128]{3,2,1,0:T(8,128)}), f32[8,34,8,128]{3,2,1,0:T(8,128)S(1)}, u32[]{:S(2)}, u32[]{:S(2)}) async-start(f32[8,34,8,128]{3,2,1,0:T(8,128)} %get-tuple-element.30), calls=%async_computation.2 | async-start | bytes 2228224 | tf_op jit(solution)/shard_map/all_to_all | solution.py:538
  79.0 3.2 %collective-permute-start.5 = (f32[8,512]{1,0:T(8,128)S(1)}, f32[8,512]{1,0:T(8,128)S(1)}, u32[]{:S(2)}, u32[]{:S(2)}) collective-permute-start(f32[8,512]{1,0:T(8,128)S(1)} %copy-done.18), channel_id=1, source_target_pairs={{1,0},{2,1},{3,2},{4,3},{5,4},{6,5},{7,6},{8,7},{9,8},{10,9},{11,1... | collective-permute-start | bytes 49160 | tf_op jit(solution)/shard_map/ppermute | solution.py:534
  82.3 4.6 %collective-permute-done.4.refs_4_ = f32[8,512]{1,0:T(8,128)S(1)} collective-permute-done((f32[8,512]{1,0:T(8,128)S(1)}, f32[8,512]{1,0:T(8,128)S(1)}, u32[]{:S(2)}, u32[]{:S(2)}) %collective-permute-start.4) | collective-permute-done | bytes 16416 | tf_op jit(solution)/shard_map/ppermute | solution.py:534
  86.8 3.9 %all-to-all-done.2.refs_0_ = f32[8,34,8,128]{3,2,1,0:T(8,128)S(1)} async-done(((f32[8,34,8,128]{3,2,1,0:T(8,128)}), f32[8,34,8,128]{3,2,1,0:T(8,128)S(1)}, u32[]{:S(2)}, u32[]{:S(2)}) %all-to-all-start.2) | async-done | bytes 1114144 | tf_op jit(solution)/shard_map/all_to_all | solution.py:538
  90.8 1.0 %copy-done.12 = f32[8,34,8,128]{3,2,1,0:T(8,128)} copy-done((f32[8,34,8,128]{3,2,1,0:T(8,128)}, f32[8,34,8,128]{3,2,1,0:T(8,128)S(1)}, u32[]{:S(2)}) %copy-start.12) | copy-done | bytes 1114136
  91.8 3.2 %shard_map.137 = (f32[6,5,8,1024]{3,2,1,0:T(8,128)}, f32[8,8,512]{2,1,0:T(8,128)}) custom-call(f32[8,34,8,128]{3,2,1,0:T(8,128)} %copy-done.12, f32[6,5,8,1024]{3,2,1,0:T(8,128)} %get-tuple-element.31.refs_1_, f32[6,8,1024]{2,1,0:T(8,128)} %get-tuple-element.32.refs_2_, f32[8,8,512]{2,1,0:T(8,128)} %get-tuple-element.33.refs_3_, ...), custom_call_target="tpu_custom_call" | custom-call | flops 4194304 | bytes 4194304 | tf_op jit(solution)/shard_map/pallas_call | solution.py:141
  (41 shorter events, 0.2 us)
Async XLA Ops:
  4.8 5.3 %copy-start.17 = (f32[17,8,512]{2,1,0:T(8,128)S(1)}, f32[17,8,512]{2,1,0:T(8,128)}, u32[]{:S(2)}) copy-start(f32[17,8,512]{2,1,0:T(8,128)} %get-tuple-element.20) | copy-start | bytes 835588
  4.9 5.4 %copy-start.16 = (f32[17,8,512]{2,1,0:T(8,128)S(1)}, f32[17,8,512]{2,1,0:T(8,128)}, u32[]{:S(2)}) copy-start(f32[17,8,512]{2,1,0:T(8,128)} %get-tuple-element.21) | copy-start | bytes 835588
  4.9 8.6 %copy-start.1 = (f32[2,4,8,512]{3,2,1,0:T(8,128)S(1)}, f32[2,4,8,512]{3,2,1,0:T(8,128)}, u32[]{:S(2)}) copy-start(f32[2,4,8,512]{3,2,1,0:T(8,128)} %param.17) | copy-start | bytes 393220
  4.9 8.6 %copy-start.4 = (f32[1536]{0:T(1024)S(1)}, f32[1536]{0:T(1024)}, u32[]{:S(2)}) copy-start(f32[1536]{0:T(1024)} %constant.5.clone.refs_0_) | copy-start | bytes 18436
  4.9 8.6 %copy-start.6 = (f32[512]{0:T(512)S(1)}, f32[512]{0:T(512)}, u32[]{:S(2)}) copy-start(f32[512]{0:T(512)} %param.19) | copy-start | bytes 6148
  4.9 8.6 %copy-start.7 = (s32[512]{0:T(512)S(1)}, s32[512]{0:T(512)}, u32[]{:S(2)}) copy-start(s32[512]{0:T(512)} %param.20) | copy-start | bytes 6148
  4.9 8.6 %copy-start.8 = (s32[512]{0:T(512)S(1)}, s32[512]{0:T(512)}, u32[]{:S(2)}) copy-start(s32[512]{0:T(512)} %param.21) | copy-start | bytes 6148
  4.9 23.2 %copy-start.3 = (f32[8,1024]{1,0:T(8,128)S(1)}, f32[8,1024]{1,0:T(8,128)}, u32[]{:S(2)}) copy-start(f32[8,1024]{1,0:T(8,128)} %refs_4_.5) | copy-start | bytes 98308
  4.9 23.2 %copy-start.5 = (f32[8,512]{1,0:T(8,128)S(1)}, f32[8,512]{1,0:T(8,128)}, u32[]{:S(2)}) copy-start(f32[8,512]{1,0:T(8,128)} %refs_6_.1) | copy-start | bytes 49156
  4.9 23.1 %copy-start.9 = (f32[5,5]{1,0:T(8,128)S(1)}, f32[5,5]{1,0:T(8,128)}, u32[]{:S(2)}) copy-start(f32[5,5]{1,0:T(8,128)} %refs_1_.5) | copy-start | bytes 304
  5.0 23.1 %copy-start.10 = (f32[5,5]{1,0:T(8,128)S(1)}, f32[5,5]{1,0:T(8,128)}, u32[]{:S(2)}) copy-start(f32[5,5]{1,0:T(8,128)} %refs_2_.5) | copy-start | bytes 304
  5.0 30.5 %all-to-all-start.1 = ((f32[8,6,5,8,128]{4,3,2,1,0:T(8,128)}), f32[8,6,5,8,128]{4,3,2,1,0:T(8,128)S(1)}, u32[]{:S(2)}, u32[]{:S(2)}) async-start(f32[8,6,5,8,128]{4,3,2,1,0:T(8,128)} %get-tuple-element.23), calls=%async_computation.1 | async-start | bytes 1966080 | tf_op jit(solution)/shard_map/all_to_all | solution.py:538
  10.1 17.9 %collective-permute-start = (f32[17,8,512]{2,1,0:T(8,128)S(1)}, f32[17,8,512]{2,1,0:T(8,128)S(1)}, u32[]{:S(2)}, u32[]{:S(2)}) collective-permute-start(f32[17,8,512]{2,1,0:T(8,128)S(1)} %copy-done.17), channel_id=1, source_target_pairs={{0,1},{1,2},{2,3},{3,4},{4,5},{5,6},{6,7},{7,8},{8,9},{9,10},{10,1... | collective-permute-start | bytes 835592 | tf_op jit(solution)/shard_map/ppermute | solution.py:534
  10.2 17.8 %collective-permute-start.1 = (f32[17,8,512]{2,1,0:T(8,128)S(1)}, f32[17,8,512]{2,1,0:T(8,128)S(1)}, u32[]{:S(2)}, u32[]{:S(2)}) collective-permute-start(f32[17,8,512]{2,1,0:T(8,128)S(1)} %copy-done.16), channel_id=1, source_target_pairs={{1,0},{2,1},{3,2},{4,3},{5,4},{6,5},{7,6},{8,7},{9,8},{10,9},{11,1... | collective-permute-start | bytes 835592 | tf_op jit(solution)/shard_map/ppermute | solution.py:534
  35.5 6.8 %copy-start.15 = (f32[17,8,512]{2,1,0:T(8,128)S(1)}, f32[17,8,512]{2,1,0:T(8,128)}, u32[]{:S(2)}) copy-start(f32[17,8,512]{2,1,0:T(8,128)} %get-tuple-element.26) | copy-start | bytes 835588
  35.5 6.8 %copy-start.14 = (f32[17,8,512]{2,1,0:T(8,128)S(1)}, f32[17,8,512]{2,1,0:T(8,128)}, u32[]{:S(2)}) copy-start(f32[17,8,512]{2,1,0:T(8,128)} %get-tuple-element.27) | copy-start | bytes 835588
  36.4 30.9 %all-to-all-start = ((f32[8,34,8,128]{3,2,1,0:T(8,128)}), f32[8,34,8,128]{3,2,1,0:T(8,128)S(1)}, u32[]{:S(2)}, u32[]{:S(2)}) async-start(f32[8,34,8,128]{3,2,1,0:T(8,128)} %get-tuple-element.22), calls=%async_computation | async-start | bytes 2228224 | tf_op jit(solution)/shard_map/all_to_all | solution.py:538
  42.3 17.0 %collective-permute-start.2 = (f32[17,8,512]{2,1,0:T(8,128)S(1)}, f32[17,8,512]{2,1,0:T(8,128)S(1)}, u32[]{:S(2)}, u32[]{:S(2)}) collective-permute-start(f32[17,8,512]{2,1,0:T(8,128)S(1)} %copy-done.15), channel_id=1, source_target_pairs={{0,1},{1,2},{2,3},{3,4},{4,5},{5,6},{6,7},{7,8},{8,9},{9,10},{10,1... | collective-permute-start | bytes 835592 | tf_op jit(solution)/shard_map/ppermute | solution.py:534
  42.4 16.9 %collective-permute-start.3 = (f32[17,8,512]{2,1,0:T(8,128)S(1)}, f32[17,8,512]{2,1,0:T(8,128)S(1)}, u32[]{:S(2)}, u32[]{:S(2)}) collective-permute-start(f32[17,8,512]{2,1,0:T(8,128)S(1)} %copy-done.14), channel_id=1, source_target_pairs={{1,0},{2,1},{3,2},{4,3},{5,4},{6,5},{7,6},{8,7},{9,8},{10,9},{11,1... | collective-permute-start | bytes 835592 | tf_op jit(solution)/shard_map/ppermute | solution.py:534
  74.0 4.9 %copy-start.19 = (f32[8,512]{1,0:T(8,128)S(1)}, f32[8,512]{1,0:T(8,128)}, u32[]{:S(2)}) copy-start(f32[8,512]{1,0:T(8,128)} %get-tuple-element.34) | copy-start | bytes 49156
  74.0 5.0 %copy-start.18 = (f32[8,512]{1,0:T(8,128)S(1)}, f32[8,512]{1,0:T(8,128)}, u32[]{:S(2)}) copy-start(f32[8,512]{1,0:T(8,128)} %get-tuple-element.35) | copy-start | bytes 49156
  74.0 16.8 %all-to-all-start.2 = ((f32[8,34,8,128]{3,2,1,0:T(8,128)}), f32[8,34,8,128]{3,2,1,0:T(8,128)S(1)}, u32[]{:S(2)}, u32[]{:S(2)}) async-start(f32[8,34,8,128]{3,2,1,0:T(8,128)} %get-tuple-element.30), calls=%async_computation.2 | async-start | bytes 2228224 | tf_op jit(solution)/shard_map/all_to_all | solution.py:538
  78.9 7.9 %collective-permute-start.4 = (f32[8,512]{1,0:T(8,128)S(1)}, f32[8,512]{1,0:T(8,128)S(1)}, u32[]{:S(2)}, u32[]{:S(2)}) collective-permute-start(f32[8,512]{1,0:T(8,128)S(1)} %copy-done.19), channel_id=1, source_target_pairs={{0,1},{1,2},{2,3},{3,4},{4,5},{5,6},{6,7},{7,8},{8,9},{9,10},{10,1... | collective-permute-start | bytes 49160 | tf_op jit(solution)/shard_map/ppermute | solution.py:534
  79.0 7.8 %collective-permute-start.5 = (f32[8,512]{1,0:T(8,128)S(1)}, f32[8,512]{1,0:T(8,128)S(1)}, u32[]{:S(2)}, u32[]{:S(2)}) collective-permute-start(f32[8,512]{1,0:T(8,128)S(1)} %copy-done.18), channel_id=1, source_target_pairs={{1,0},{2,1},{3,2},{4,3},{5,4},{6,5},{7,6},{8,7},{9,8},{10,9},{11,1... | collective-permute-start | bytes 49160 | tf_op jit(solution)/shard_map/ppermute | solution.py:534
  (5 other events, 4.6 us)

commit v3 on v1

v3 whole, which is shorter than its diff:
```python
import math

import jax
import jax.numpy as jnp
import ml_dtypes
import numpy as np
from jax import lax
from jax.experimental import pallas as pl
from jax.experimental.pallas import tpu as pltpu
from jax.sharding import PartitionSpec as P

NT, NV, NH = 48, 5, 4
ROWS, SPAN, MSPAN, NF = 8, 1024, 512, 512
CHUNK = 128
CH = 2 * NH
F32, BF16 = jnp.float32, jnp.bfloat16

damping_fourth = 1.0 / 32.0
viscous_coef = 0.1
sigma_fluid = 0.5
metal_step = 0.2
sigma_metal = 0.5
heat_capacity = 0.5
flux_scale = 4.0


def tables():
    t = np.arange(NT)
    offset = t[:, None] - t[None, :]
    angle = np.where(offset == 0, 0.5, math.pi * offset / NT)
    spectral = np.where(
        offset == 0, 0.0, 0.5 * (1.0 - 2.0 * (offset % 2)) * np.cos(angle) / np.sin(angle)
    )
    phase = 2.0 * math.pi * ((np.arange(NH)[:, None] * t[None, :]) % NT) / NT
    synth = np.concatenate([np.cos(phase), -np.sin(phase)])
    w0 = synth * (flux_scale / NT)
    w1 = w0 @ spectral
    w2 = w1 @ spectral
    block, inner = np.divmod(t, 6)
    relative = spectral[(6 * (block[:, None] + block[None, :]) + inner[:, None]) % NT, inner[None, :]]
    high = relative.astype(np.float32).astype(ml_dtypes.bfloat16)
    low = (relative - high.astype(np.float64)).astype(np.float32).astype(ml_dtypes.bfloat16)
    eye = np.eye(ROWS, dtype=np.float32)
    kron_high = np.kron(high.astype(np.float32), eye)
    kron_low = np.kron(low.astype(np.float32), eye)
    kron = np.concatenate([kron_high, kron_high, kron_low], axis=1).astype(ml_dtypes.bfloat16)
    flat = np.concatenate([m.T.reshape(-1) for m in (synth, w0, w1, w2)]).astype(np.float32)
    return kron, flat


KRON, FLAT = tables()
SYNTH, W0, W1, W2 = (i * NT * CH for i in range(4))


def call(body, operands, results, scratch=(), flops=1 << 22, moved=1 << 22):
    return pl.pallas_call(
        body,
        out_shape=[shape(*dims) for dims in results],
        in_specs=[pl.BlockSpec(memory_space=pltpu.SMEM if m else pltpu.VMEM) for _, m in operands],
        out_specs=[pl.BlockSpec(memory_space=pltpu.VMEM)] * len(results),
        scratch_shapes=list(scratch),
        compiler_params=pltpu.CompilerParams(vmem_limit_bytes=24 << 20),
        cost_estimate=pl.CostEstimate(flops=flops, bytes_accessed=moved, transcendentals=0),
    )(*[array for array, _ in operands])


def shape(*dims):
    return jax.ShapeDtypeStruct(dims, F32)


def row_index(n=SPAN):
    return lax.broadcasted_iota(jnp.int32, (ROWS, n), 0)


def split(x):
    high = x.astype(BF16)
    return high, (x - high.astype(F32)).astype(BF16)


def one_hot(index, n):
    cell = lax.broadcasted_iota(jnp.int32, (n, NF), 0)
    return jnp.where(cell == index, 1.0, 0.0).astype(BF16)


def at_faces(field, span_hot, row_hot):
    n = field.shape[-1]
    both = jnp.concatenate(split(field.reshape(CH * ROWS, n)), axis=0)
    picked = jnp.dot(both, span_hot, preferred_element_type=F32)
    picked = (picked[: CH * ROWS] + picked[CH * ROWS :]).reshape(CH, ROWS, NF)
    return jnp.sum(picked * row_hot[None], axis=1)


def onto_cells(values, span_hot, row_hot):
    spread = (values[:, None, :] * row_hot[None]).reshape(CH * ROWS, NF)
    both = jnp.concatenate(split(spread), axis=0)
    out = lax.dot_general(both, span_hot, (((1,), (1,)), ((), ())), preferred_element_type=F32)
    return (out[: CH * ROWS] + out[CH * ROWS :]).reshape(CH, ROWS, span_hot.shape[0])


def fluid_hots(ff_ref):
    cell = ff_ref[...]
    span = one_hot(cell & (SPAN - 1), SPAN)
    rows = jnp.where(row_index(NF) == (cell >> 10), 1.0, 0.0)
    return span, rows


def metal_hots(mf_ref):
    cell = mf_ref[...]
    span = one_hot(cell & (MSPAN - 1), MSPAN)
    rows = jnp.where(row_index(NF) == (cell >> 9), 1.0, 0.0)
    return span, rows


def span_sides(a):
    n = a.shape[-1]
    lane = lax.broadcasted_iota(jnp.int32, a.shape, a.ndim - 1)
    north = jnp.where(lane == n - 1, 0.0, pltpu.roll(a, n - 1, a.ndim - 1))
    south = jnp.where(lane == 0, 0.0, pltpu.roll(a, 1, a.ndim - 1))
    return north, south


def stencil_parts(a, before, after):
    row = row_index(a.shape[-1])
    east_one = pltpu.roll(jnp.where(row == 0, after, a), 7, 0)
    east_two = pltpu.roll(jnp.where(row < 2, after, a), 6, 0)
    west_one = pltpu.roll(jnp.where(row == 7, before, a), 1, 0)
    west_two = pltpu.roll(jnp.where(row >= 6, before, a), 2, 0)
    north, south = span_sides(a)
    rest = (
        (4.0 * damping_fourth) * (east_one + west_one)
        - damping_fourth * (east_two + west_two)
        + viscous_coef * (north + south)
        - (6.0 * damping_fourth + 2.0 * viscous_coef + sigma_fluid) * a
    )
    return east_one - west_one, north - south, rest


def edge_tile(ref, tile):
    return jnp.concatenate([ref[2 * tile], ref[2 * tile + 1]], axis=1)


def halo_pair(up_ref, down_ref, t, v):
    tile, slot = (t, v) if v < 4 else (6 + t // 4, t % 4)
    before = pltpu.roll(edge_tile(up_ref, tile), (6 - 2 * slot) % 8, 0)
    after = pltpu.roll(edge_tile(down_ref, tile), (8 - 2 * slot) % 8, 0)
    return before, after


def pack_tile(blocks, tile, up_ref, down_ref):
    row = row_index()
    up = down = None
    for slot, a in enumerate(blocks):
        u = pltpu.roll(a, (2 * slot + 2) % 8, 0) if (2 * slot + 2) % 8 else a
        d = pltpu.roll(a, 2 * slot, 0) if slot else a
        mine = (row >> 1) == slot
        up = u if up is None else jnp.where(mine, u, up)
        down = d if down is None else jnp.where(mine, d, down)
    for half in range(2):
        cut = slice(half * 512, half * 512 + 512)
        up_ref[2 * tile + half] = up[:, cut]
        down_ref[2 * tile + half] = down[:, cut]


def pack_last(get, extra, up_ref, down_ref):
    pack_tile([get(t) for t in range(4)], 6, up_ref, down_ref)
    pack_tile([get(4), get(5), extra, extra], 7, up_ref, down_ref)


def prepare_kernel(a_ref, ps_ref, m_ref, up_ref, down_ref):
    for t in range(6):
        pack_tile([a_ref[t, v] for v in range(4)], t, up_ref, down_ref)
    pack_last(lambda t: a_ref[t, NV - 1], ps_ref[...], up_ref, down_ref)
    metal_edges(m_ref, up_ref.at[16], down_ref.at[16])


def chunk_of(k):
    return pl.ds(pl.multiple_of(lax.rem(lax.axis_index("inst") + k, 8) * CHUNK, CHUNK), CHUNK)


def blocks_kernel(a_ref, *out_refs):
    for k, out_ref in enumerate(out_refs):
        cut = chunk_of(k)
        for t in range(6):
            for v in range(NV):
                out_ref[t * NV + v] = a_ref[t, v, :, cut]


def energy_kernel(tab_ref, m_ref, fc_ref, ff_ref, mf_ref, e_ref):
    first = lax.axis_index("inst") * 6
    m_hot, m_row = metal_hots(mf_ref)
    f_hot, f_row = fluid_hots(ff_ref)
    values = at_faces(m_ref[...], m_hot, m_row) * fc_ref[...]
    cells = onto_cells(values, f_hot, f_row)
    for t in range(6):
        e_ref[t] = combine(tab_ref, SYNTH, first + t, cells)


def combine(tab_ref, base, t, fields):
    total = tab_ref[base + t * CH] * fields[0]
    for ch in range(1, CH):
        if ch != NH:
            total += tab_ref[base + t * CH + ch] * fields[ch]
    return total


def convect(jx_ref, jz_ref, dx, dz, rest, u):
    out = rest
    for v in range(NV):
        out = out - (0.5 * jx_ref[u, v]) * dx[v] - (0.5 * jz_ref[u, v]) * dz[v]
    return out


def first_kernel(
    tab_ref, jx_ref, jz_ref, a_ref, s_ref, ps_ref, up_ref, down_ref, e_ref, fc_ref, ff_ref, m_ref, cond_ref,
    *refs,
):
    q_refs, (b_ref, bup_ref, bdown_ref, hq_ref, m_out, parts, q4_ref) = refs[:8], refs[8:]
    first = lax.axis_index("inst") * 6
    step = ps_ref[...]
    step_before = pltpu.roll(edge_tile(up_ref, 7), 2, 0)
    step_after = pltpu.roll(edge_tile(down_ref, 7), 4, 0)
    cuts = [chunk_of(k) for k in range(8)]
    for t in range(6):
        for v in range(NV):
            a = a_ref[t, v]
            before, after = halo_pair(up_ref, down_ref, t, v)
            dx, dz, rest = stencil_parts(a, before, after)
            parts[0, v], parts[1, v], parts[2, v] = dx, dz, rest
            dx, dz, rest = stencil_parts(step * a, step_before * before, step_after * after)
            parts[3, v], parts[4, v], parts[5, v] = dx, dz, rest
        for i in range(8):
            cut = cuts[i]
            dx = [parts[0, v, :, cut] for v in range(NV)]
            dz = [parts[1, v, :, cut] for v in range(NV)]
            px = [parts[3, v, :, cut] for v in range(NV)]
            pz = [parts[4, v, :, cut] for v in range(NV)]
            for u in range(NV):
                a = a_ref[t, u, :, cut]
                space = convect(jx_ref, jz_ref, dx, dz, parts[2, u, :, cut], u)
                source = s_ref[t, u, :, cut] + space
                if u == NV - 1:
                    source = source + e_ref[t, :, cut]
                b = a + ps_ref[:, cut] * source
                b_ref[t, u, :, cut] = b
                q = a + b + convect(jx_ref, jz_ref, px, pz, parts[5, u, :, cut], u)
                q_refs[i][t * NV + u] = q
                if u == NV - 1:
                    q4_ref[t, :, cut] = q
        pack_tile([b_ref[t, v] for v in range(4)], t, bup_ref, bdown_ref)
    pack_last(lambda t: b_ref[t, NV - 1], step, bup_ref, bdown_ref)
    f_hot, f_row = fluid_hots(ff_ref)
    heat = []
    for ch in range(CH):
        h0 = h1 = h2 = h3 = None
        for t in range(6):
            at = (first + t) * CH + ch
            a, b = a_ref[t, NV - 1], b_ref[t, NV - 1]
            x0 = tab_ref[W0 + at] * b
            x1 = tab_ref[W1 + at] * a
            x2 = tab_ref[W1 + at] * q4_ref[t]
            x3 = tab_ref[W2 + at] * a
            h0, h1, h2, h3 = (
                (x0, x1, x2, x3) if t == 0 else (h0 + x0, h1 + x1, h2 + x2, h3 + x3)
            )
        heat.append(h0 - step * h1)
        hq_ref[ch] = step * (step * h3 - h2)
    values = at_faces(jnp.stack(heat), f_hot, f_row) * fc_ref[...]
    put_heat(q_refs, values)
    before, after = metal_sides(up_ref.at[16], down_ref.at[16])
    m = metal_update(m_ref, before, after, cond_ref[...])
    for ch in range(CH):
        m_out[ch] = m[ch]


def put_heat(refs, values):
    for ref in refs:
        for k in range(4):
            ref[30 + k] = values[:, k * CHUNK : (k + 1) * CHUNK]


def rotate_time(kron, x):
    high, low = split(x)
    return jnp.dot(kron, jnp.concatenate([high, low, high], axis=0), preferred_element_type=F32)


def local_step(ps_ref):
    start = pl.multiple_of(lax.axis_index("inst") * CHUNK, CHUNK)
    return ps_ref[:, pl.ds(start, CHUNK)]


def turned(get):
    return jnp.concatenate(
        [
            jnp.concatenate([get(j, t, v) for j in range(8) for t in range(6)], axis=0)
            for v in range(NV)
        ],
        axis=1,
    )


def derive_kernel(kron_ref, ps_ref, *refs):
    a_refs, g_ref = refs[:8], refs[8]
    wide = jnp.concatenate([local_step(ps_ref)] * NV, axis=1)
    x = turned(lambda j, t, v: a_refs[j][t * NV + v])
    d = rotate_time(kron_ref[...], x)
    d = (d.reshape(NT, ROWS, NV * CHUNK) * wide[None]).reshape(NT * ROWS, NV * CHUNK)
    for k in range(8):
        at = ((8 - k) % 8) * 6 * ROWS
        g_ref[pl.ds(k * 6 * ROWS, 6 * ROWS), :] = d[at : at + 6 * ROWS]


def middle_kernel(tab_ref, jx_ref, jz_ref, b_ref, s_ref, ps_ref, up_ref, down_ref, hq_ref, g_ref, c_ref, hc_ref, parts):
    first = lax.axis_index("inst") * 6
    for t in range(6):
        for v in range(NV):
            before, after = halo_pair(up_ref, down_ref, t, v)
            dx, dz, rest = stencil_parts(b_ref[t, v], before, after)
            parts[0, v], parts[1, v], parts[2, v] = dx, dz, rest
        for i in range(8):
            cut = pl.ds(i * CHUNK, CHUNK)
            dx = [parts[0, v, :, cut] for v in range(NV)]
            dz = [parts[1, v, :, cut] for v in range(NV)]
            for u in range(NV):
                space = convect(jx_ref, jz_ref, dx, dz, parts[2, u, :, cut], u)
                c_ref[t, u, :, cut] = b_ref[t, u, :, cut] + ps_ref[:, cut] * (s_ref[t, u, :, cut] + space)
    for ch in range(CH):
        total = hq_ref[ch]
        for t in range(6):
            total += tab_ref[W0 + (first + t) * CH + ch] * c_ref[t, NV - 1]
        hc_ref[ch] = total


def metal_update(m, before, after, cond):
    row = row_index(MSPAN)
    out = []
    for ch in range(CH):
        a = m[ch]
        east = pltpu.roll(jnp.where(row == 0, after[ch], a), 7, 0)
        west = pltpu.roll(jnp.where(row == 7, before[ch], a), 1, 0)
        north, south = span_sides(a)
        laplace = east + west + north + south - 4.0 * a
        h = ch % NH
        turn = -heat_capacity * h * m[ch + NH] if ch < NH else heat_capacity * h * m[ch - NH]
        out.append(a + metal_step * (cond * laplace - sigma_metal * a - turn))
    return out


def metal_edges(m, up_ref, down_ref):
    up_ref[...] = jnp.concatenate([m[ch][7:8] for ch in range(CH)], axis=0)
    down_ref[...] = jnp.concatenate([m[ch][0:1] for ch in range(CH)], axis=0)


def metal_sides(up_ref, down_ref):
    before = [jnp.broadcast_to(up_ref[ch : ch + 1], (ROWS, MSPAN)) for ch in range(CH)]
    after = [jnp.broadcast_to(down_ref[ch : ch + 1], (ROWS, MSPAN)) for ch in range(CH)]
    return before, after


def heat_sum(refs):
    tiles = []
    for k in range(4):
        total = refs[0][30 + k]
        for ref in refs[1:]:
            total += ref[30 + k]
        tiles.append(total)
    return jnp.concatenate(tiles, axis=1)


def second_kernel(
    tab_ref, g_ref, kron_ref, ps_ref, m_ref, fc_ref, ff_ref, mf_ref, hc_ref,
    *refs,
):
    q_refs, v_refs, (m_out, mup_ref, mdown_ref, e_ref) = refs[:8], refs[8:16], refs[16:]
    first = lax.axis_index("inst") * 6
    step = ps_ref[...]
    coeff = fc_ref[...]
    m_hot, m_row = metal_hots(mf_ref)
    f_hot, f_row = fluid_hots(ff_ref)
    source = onto_cells(heat_sum(q_refs), m_hot, m_row)
    m = [m_ref[ch] + metal_step * source[ch] for ch in range(CH)]
    for ch in range(CH):
        m_out[ch] = m[ch]
    metal_edges(m, mup_ref, mdown_ref)
    cells = onto_cells(at_faces(jnp.stack(m), m_hot, m_row) * coeff, f_hot, f_row)
    for t in range(6):
        e_ref[t] = step * combine(tab_ref, SYNTH, first + t, cells)
    heat = []
    for ch in range(CH):
        total = hc_ref[ch]
        for t in range(6):
            total += tab_ref[W0 + (first + t) * CH + ch] * e_ref[t]
        heat.append(total)
    put_heat(v_refs, at_faces(jnp.stack(heat), f_hot, f_row) * coeff)
    x = turned(lambda j, t, u: q_refs[j][t * NV + u]) - g_ref[...]
    d = rotate_time(kron_ref[...], x)
    minus = -local_step(ps_ref)
    for j in range(8):
        for t in range(6):
            at = (j * 6 + t) * ROWS
            for u in range(NV):
                v_refs[j][t * NV + u] = minus * d[at : at + ROWS, u * CHUNK : (u + 1) * CHUNK]


def last_kernel(c_ref, e_ref, m_ref, mup_ref, mdown_ref, cond_ref, mf_ref, *refs):
    v_refs, (out_ref, m_out) = refs[:8], refs[8:]
    for k in range(8):
        cut = chunk_of(8 - k)
        for t in range(6):
            for u in range(NV):
                total = c_ref[t, u, :, cut] + v_refs[k][t * NV + u]
                if u == NV - 1:
                    total = total + e_ref[t, :, cut]
                out_ref[t, u, :, cut] = total
    m_hot, m_row = metal_hots(mf_ref)
    source = onto_cells(heat_sum(v_refs), m_hot, m_row)
    before, after = metal_sides(mup_ref, mdown_ref)
    m = metal_update(m_ref, before, after, cond_ref[...])
    for ch in range(CH):
        m_out[ch] = m[ch] + metal_step * source[ch]


def exchange(up, down):
    n = lax.axis_size("space")
    forward = [(i, (i + 1) % n) for i in range(n)]
    back = [(j, i) for i, j in forward]
    return lax.ppermute(up, "space", forward), lax.ppermute(down, "space", back)


def turn(blocks):
    n = len(blocks)
    return [blocks[0]] + [
        lax.ppermute(blocks[k], "inst", [(i, (i + k) % n) for i in range(n)]) for k in range(1, n)
    ]


EDGES = (17, ROWS, 512)
FLUID = (6, NV, ROWS, SPAN)
ONE = (6, ROWS, SPAN)
METAL = (CH, ROWS, MSPAN)
HARMONICS = (CH, ROWS, SPAN)
BLOCK = (34, ROWS, CHUNK)


def plain(*arrays):
    return [(array, False) for array in arrays]


def local(a0, source, ps, jx, jz, metal, cond, coeff, ff, mf):
    kron = jnp.asarray(KRON)
    tab = jnp.asarray(FLAT)
    coeff, ff, mf = (x.reshape(1, NF) for x in (coeff, ff, mf))
    metal = metal.reshape(METAL)
    up, down = call(prepare_kernel, plain(a0, ps, metal), [EDGES] * 2)
    up, down = exchange(up, down)
    a_turned = turn(call(blocks_kernel, plain(a0), [(30, ROWS, CHUNK)] * 8))
    (e0,) = call(energy_kernel, [(tab, True)] + plain(metal, coeff, ff, mf), [ONE])
    scalars = [(tab, True), (jx, True), (jz, True)]
    *q, b, bup, bdown, hq, metal = call(
        first_kernel,
        scalars + plain(a0, source, ps, up, down, e0, coeff, ff, metal, cond),
        [BLOCK] * 8 + [FLUID, EDGES, EDGES, HARMONICS, METAL],
        scratch=[pltpu.VMEM((6, NV, ROWS, SPAN), F32), pltpu.VMEM(ONE, F32)],
    )
    q_turned = turn(q)
    bup, bdown = exchange(bup, bdown)
    (g,) = call(derive_kernel, plain(kron, ps, *a_turned), [(NT * ROWS, NV * CHUNK)])
    c, hc = call(
        middle_kernel,
        scalars + plain(b, source, ps, bup, bdown, hq, g),
        [FLUID, HARMONICS],
        scratch=[pltpu.VMEM((3, NV, ROWS, SPAN), F32)],
    )
    *v, metal, mup, mdown, e1 = call(
        second_kernel,
        [(tab, True)] + plain(g, kron, ps, metal, coeff, ff, mf, hc, *q_turned),
        [BLOCK] * 8 + [METAL, (CH, MSPAN), (CH, MSPAN), ONE],
    )
    v = turn(v)
    mup, mdown = exchange(mup, mdown)
    out, metal = call(last_kernel, plain(c, e1, metal, mup, mdown, cond, mf, *v), [FLUID, METAL])
    return out, metal.reshape(2, NH, ROWS, MSPAN)


def solution(mesh):
    return jax.shard_map(
        local,
        mesh=mesh,
        in_specs=(
            P("inst", None, "space", None),
            P("inst", None, "space", None),
            P("space", None),
            P(),
            P(),
            P(None, None, "space", None),
            P("space", None),
            P("space"),
            P("space"),
            P("space"),
        ),
        out_specs=(P("inst", None, "space", None), P(None, None, "space", None)),
        check_vma=False,
    )
```

time: 92.1 us -> 96.1 us (1.043)
  the two profiles are of different devices: /device:TPU:112 before, /device:TPU:1 now
where the time goes in v3:
time: 96.1 us; the launch traced here: 95.9 us
  starting transfers between devices  39.6 us (41%)
  waiting for transfers between devices  36.7 us (38%)
  Pallas kernels  15.2 us (16%)
  local copies, waits for them, and re-layouts  3.56 us (4%)
    ppermute x21, starting transfers between devices, turn(): lax.ppermute(blocks[k], 'inst', [(i, (i + k) % n) for i in range(n)])  32 us
    ppermute x21, waiting for transfers between devices, turn(): lax.ppermute(blocks[k], 'inst', [(i, (i + k) % n) for i in range(n)])  22.9 us
    pallas_call x8, Pallas kernels, call(): pl.pallas_call(body, out_shape=[shape(*dims) for dims in results], in_spe...  15.2 us
    ppermute x3, waiting for transfers between devices, exchange(): lax.ppermute(down, 'space', back)  13.8 us
    ppermute x3, starting transfers between devices, exchange(): lax.ppermute(up, 'space', forward)  7.11 us
    unnamed x30, local copies, waits for them, and re-layouts  3.56 us
  transfers between devices with their start and end apart: 27, of which 8 were waited for; matrix products, arithmetic and copies ran while one was open for 0% of the time, Pallas kernels for 11%

profile of v3, /device:TPU:1, one launch (start us, length us, event | category | flops | bytes accessed | tf_op | source)
XLA Modules:
  0.0 95.9 jit_solution(12969413394683417580)
XLA Ops:
  3.6 4.4 %collective-permute-start = (f32[17,8,512]{2,1,0:T(8,128)S(1)}, f32[17,8,512]{2,1,0:T(8,128)S(1)}, u32[]{:S(2)}, u32[]{:S(2)}) collective-permute-start(f32[17,8,512]{2,1,0:T(8,128)S(1)} %get-tuple-element.41), channel_id=1, source_target_pairs={{0,1},{1,2},{2,3},{3,4},{4,5},{5,6},{6,7},{7,8},{8,9},{9,10},{10,1... | collective-permute-start | bytes 835592 | tf_op jit(solution)/shard_map/ppermute | solution.py:426
  8.2 1.3 %collective-permute-start.4 = (f32[30,8,128]{2,1,0:T(8,128)S(1)}, f32[30,8,128]{2,1,0:T(8,128)S(1)}, u32[]{:S(2)}, u32[]{:S(2)}) collective-permute-start(f32[30,8,128]{2,1,0:T(8,128)S(1)} %get-tuple-element.48), channel_id=1, source_target_pairs={{0,32},{32,64},{64,96},{96,128},{128,160},{160,192},{192,224},{224... | collective-permute-start | bytes 368648 | tf_op jit(solution)/shard_map/ppermute | solution.py:432
  9.5 2.5 %collective-permute-start.5 = (f32[30,8,128]{2,1,0:T(8,128)S(1)}, f32[30,8,128]{2,1,0:T(8,128)S(1)}, u32[]{:S(2)}, u32[]{:S(2)}) collective-permute-start(f32[30,8,128]{2,1,0:T(8,128)S(1)} %get-tuple-element.49), channel_id=1, source_target_pairs={{0,64},{32,96},{64,128},{96,160},{128,192},{160,224},{192,0},{224,... | collective-permute-start | bytes 368648 | tf_op jit(solution)/shard_map/ppermute | solution.py:432
  11.9 1.3 %collective-permute-start.6 = (f32[30,8,128]{2,1,0:T(8,128)S(1)}, f32[30,8,128]{2,1,0:T(8,128)S(1)}, u32[]{:S(2)}, u32[]{:S(2)}) collective-permute-start(f32[30,8,128]{2,1,0:T(8,128)S(1)} %get-tuple-element.50), channel_id=1, source_target_pairs={{0,96},{32,128},{64,160},{96,192},{128,224},{160,0},{192,32},{224,... | collective-permute-start | bytes 368648 | tf_op jit(solution)/shard_map/ppermute | solution.py:432
  13.9 1.4 %shard_map.132.e_ref = f32[6,8,1024]{2,1,0:T(8,128)S(1)} custom-call(f32[1536]{0:T(1024)S(1)} %copy-done.8, f32[8,8,512]{2,1,0:T(8,128)S(1)} %bitcast.6, f32[1,512]{1,0:T(1,128)S(1)} %bitcast.8, s32[1,512]{1,0:T(1,128)S(1)} %bitcast.11, s32[1,512]{1,0:T(1,128)S(1)} %bitcast.14), custom_call_target="tpu_custom_call" | custom-call | flops 4194304 | bytes 4194304 | tf_op jit(solution)/shard_map/pallas_call | solution.py:56
  15.3 11.1 %collective-permute-done.1.down_ref = f32[17,8,512]{2,1,0:T(8,128)S(1)} collective-permute-done((f32[17,8,512]{2,1,0:T(8,128)S(1)}, f32[17,8,512]{2,1,0:T(8,128)S(1)}, u32[]{:S(2)}, u32[]{:S(2)}) %collective-permute-start.1) | collective-permute-done | bytes 278560 | tf_op jit(solution)/shard_map/ppermute | solution.py:426
  26.4 5.7 %shard_map.133 = (f32[34,8,128]{2,1,0:T(8,128)S(1)}, f32[34,8,128]{2,1,0:T(8,128)S(1)}, f32[34,8,128]{2,1,0:T(8,128)S(1)}, f32[34,8,128]{2,1,0:T(8,128)S(1)}, f3...) custom-call(f32[1536]{0:T(1024)S(1)} %copy-done.8, ...), custom_call_target="tpu_custom_call" | custom-call | flops 4194304 | bytes 4194304 | tf_op jit(solution)/shard_map/pallas_call | solution.py:56
  33.2 9.1 %collective-permute-done.7.refs_4_ = f32[30,8,128]{2,1,0:T(8,128)S(1)} collective-permute-done((f32[30,8,128]{2,1,0:T(8,128)S(1)}, f32[30,8,128]{2,1,0:T(8,128)S(1)}, u32[]{:S(2)}, u32[]{:S(2)}) %collective-permute-start.7) | collective-permute-done | bytes 122912 | tf_op jit(solution)/shard_map/ppermute | solution.py:432
  43.4 1.8 %collective-permute-start.12 = (f32[34,8,128]{2,1,0:T(8,128)S(1)}, f32[34,8,128]{2,1,0:T(8,128)S(1)}, u32[]{:S(2)}, u32[]{:S(2)}) collective-permute-start(f32[34,8,128]{2,1,0:T(8,128)S(1)} %get-tuple-element.60), channel_id=1, source_target_pairs={{0,64},{32,96},{64,128},{96,160},{128,192},{160,224},{192,0},{224,... | collective-permute-start | bytes 417800 | tf_op jit(solution)/shard_map/ppermute | solution.py:432
  45.2 3.0 %collective-permute-start.10 = (f32[30,8,128]{2,1,0:T(8,128)S(1)}, f32[30,8,128]{2,1,0:T(8,128)S(1)}, u32[]{:S(2)}, u32[]{:S(2)}) collective-permute-start(f32[30,8,128]{2,1,0:T(8,128)S(1)} %get-tuple-element.54), channel_id=1, source_target_pairs={{0,224},{32,0},{64,32},{96,64},{128,96},{160,128},{192,160},{224,1... | collective-permute-start | bytes 368648 | tf_op jit(solution)/shard_map/ppermute | solution.py:432
  48.2 3.2 %collective-permute-done.10.refs_7_ = f32[30,8,128]{2,1,0:T(8,128)S(1)} collective-permute-done((f32[30,8,128]{2,1,0:T(8,128)S(1)}, f32[30,8,128]{2,1,0:T(8,128)S(1)}, u32[]{:S(2)}, u32[]{:S(2)}) %collective-permute-start.10) | collective-permute-done | bytes 122912 | tf_op jit(solution)/shard_map/ppermute | solution.py:432
  51.4 3.4 %collective-permute-start.13 = (f32[34,8,128]{2,1,0:T(8,128)S(1)}, f32[34,8,128]{2,1,0:T(8,128)S(1)}, u32[]{:S(2)}, u32[]{:S(2)}) collective-permute-start(f32[34,8,128]{2,1,0:T(8,128)S(1)} %get-tuple-element.61), channel_id=1, source_target_pairs={{0,96},{32,128},{64,160},{96,192},{128,224},{160,0},{192,32},{224,... | collective-permute-start | bytes 417800 | tf_op jit(solution)/shard_map/ppermute | solution.py:432
  55.8 2.3 %collective-permute-start.16 = (f32[34,8,128]{2,1,0:T(8,128)S(1)}, f32[34,8,128]{2,1,0:T(8,128)S(1)}, u32[]{:S(2)}, u32[]{:S(2)}) collective-permute-start(f32[34,8,128]{2,1,0:T(8,128)S(1)} %get-tuple-element.64), channel_id=1, source_target_pairs={{0,192},{32,224},{64,0},{96,32},{128,64},{160,96},{192,128},{224,1... | collective-permute-start | bytes 417800 | tf_op jit(solution)/shard_map/ppermute | solution.py:432
  60.0 2.6 %shard_map.136 = (f32[6,5,8,1024]{3,2,1,0:T(8,128)S(1)}, f32[8,8,1024]{2,1,0:T(8,128)S(1)}) custom-call(f32[1536]{0:T(1024)S(1)} %copy-done.8, f32[5,5]{1,0:T(8,128)S(1)} %copy-done.13, f32[5,5]{1,0:T(8,128)S(1)} %copy-done.14, f32[6,5,8,1024]{3,2,1,0:T(8,128)S(1)} %get-tuple-element.43.b_ref, f32[6,5,8,1024]{3,2,1,0:T(8,128)S(1)} %copy-done.2, ...), custom_call_target="tpu_custom_call" | custom-call | flops 4194304 | bytes 4194304 | tf_op jit(solution)/shard_map/pallas_call | solution.py:56
  62.7 1.4 %collective-permute-done.16.refs_6_ = f32[34,8,128]{2,1,0:T(8,128)S(1)} collective-permute-done((f32[34,8,128]{2,1,0:T(8,128)S(1)}, f32[34,8,128]{2,1,0:T(8,128)S(1)}, u32[]{:S(2)}, u32[]{:S(2)}) %collective-permute-start.16) | collective-permute-done | bytes 139296 | tf_op jit(solution)/shard_map/ppermute | solution.py:432
  64.1 1.7 %collective-permute-done.17.refs_7_ = f32[34,8,128]{2,1,0:T(8,128)S(1)} collective-permute-done((f32[34,8,128]{2,1,0:T(8,128)S(1)}, f32[34,8,128]{2,1,0:T(8,128)S(1)}, u32[]{:S(2)}, u32[]{:S(2)}) %collective-permute-start.17) | collective-permute-done | bytes 139296 | tf_op jit(solution)/shard_map/ppermute | solution.py:432
  65.8 2.8 %shard_map.137 = (f32[34,8,128]{2,1,0:T(8,128)S(1)}, f32[34,8,128]{2,1,0:T(8,128)S(1)}, f32[34,8,128]{2,1,0:T(8,128)S(1)}, f32[34,8,128]{2,1,0:T(8,128)S(1)}, f3...) custom-call(f32[1536]{0:T(1024)S(1)} %copy-done.8, ...), custom_call_target="tpu_custom_call" | custom-call | flops 4194304 | bytes 4194304 | tf_op jit(solution)/shard_map/pallas_call | solution.py:56
  69.7 3.6 %collective-permute-start.21 = (f32[34,8,128]{2,1,0:T(8,128)S(1)}, f32[34,8,128]{2,1,0:T(8,128)S(1)}, u32[]{:S(2)}, u32[]{:S(2)}) collective-permute-start(f32[34,8,128]{2,1,0:T(8,128)S(1)} %get-tuple-element.72), channel_id=1, source_target_pairs={{0,64},{32,96},{64,128},{96,160},{128,192},{160,224},{192,0},{224,... | collective-permute-start | bytes 417800 | tf_op jit(solution)/shard_map/ppermute | solution.py:432
  73.3 2.6 %collective-permute-start.18 = (f32[8,512]{1,0:T(8,128)S(1)}, f32[8,512]{1,0:T(8,128)S(1)}, u32[]{:S(2)}, u32[]{:S(2)}) collective-permute-start(f32[8,512]{1,0:T(8,128)S(1)} %get-tuple-element.68), channel_id=1, source_target_pairs={{0,1},{1,2},{2,3},{3,4},{4,5},{5,6},{6,7},{7,8},{8,9},{9,10},{10,1... | collective-permute-start | bytes 49160 | tf_op jit(solution)/shard_map/ppermute | solution.py:426
  78.2 2.7 %collective-permute-done.19.mdown_ref = f32[8,512]{1,0:T(8,128)S(1)} collective-permute-done((f32[8,512]{1,0:T(8,128)S(1)}, f32[8,512]{1,0:T(8,128)S(1)}, u32[]{:S(2)}, u32[]{:S(2)}) %collective-permute-start.19) | collective-permute-done | bytes 16416 | tf_op jit(solution)/shard_map/ppermute | solution.py:426
  82.0 2.1 %collective-permute-start.25 = (f32[34,8,128]{2,1,0:T(8,128)S(1)}, f32[34,8,128]{2,1,0:T(8,128)S(1)}, u32[]{:S(2)}, u32[]{:S(2)}) collective-permute-start(f32[34,8,128]{2,1,0:T(8,128)S(1)} %get-tuple-element.76), channel_id=1, source_target_pairs={{0,192},{32,224},{64,0},{96,32},{128,64},{160,96},{192,128},{224,1... | collective-permute-start | bytes 417800 | tf_op jit(solution)/shard_map/ppermute | solution.py:432
  84.0 2.9 %collective-permute-start.26 = (f32[34,8,128]{2,1,0:T(8,128)S(1)}, f32[34,8,128]{2,1,0:T(8,128)S(1)}, u32[]{:S(2)}, u32[]{:S(2)}) collective-permute-start(f32[34,8,128]{2,1,0:T(8,128)S(1)} %get-tuple-element.77), channel_id=1, source_target_pairs={{0,224},{32,0},{64,32},{96,64},{128,96},{160,128},{192,160},{224,1... | collective-permute-start | bytes 417800 | tf_op jit(solution)/shard_map/ppermute | solution.py:432
  87.5 6.9 %collective-permute-done.26.refs_7_ = f32[34,8,128]{2,1,0:T(8,128)S(1)} collective-permute-done((f32[34,8,128]{2,1,0:T(8,128)S(1)}, f32[34,8,128]{2,1,0:T(8,128)S(1)}, u32[]{:S(2)}, u32[]{:S(2)}) %collective-permute-start.26) | collective-permute-done | bytes 139296 | tf_op jit(solution)/shard_map/ppermute | solution.py:432
  94.4 1.5 %shard_map.138 = (f32[6,5,8,1024]{3,2,1,0:T(8,128)}, f32[8,8,512]{2,1,0:T(8,128)}) custom-call(f32[6,5,8,1024]{3,2,1,0:T(8,128)S(1)} %get-tuple-element.55.c_ref, f32[6,8,1024]{2,1,0:T(8,128)S(1)} %get-tuple-element.66.e_ref, f32[8,8,512]{2,1,0:T(8,128)S(1)} %get-tuple-element.67.m_ref, f32[8,512]{1,0:T(8,128)S(1)} %collective-permute-done.18.mup_ref, ...), custom_call_target="tpu_custom_call" | custom-call | flops 4194304 | bytes 4194304 | tf_op jit(solution)/shard_map/pallas_call | solution.py:56
  (68 shorter events, 13.7 us)
Async XLA Ops:
  3.6 11.6 %collective-permute-start = (f32[17,8,512]{2,1,0:T(8,128)S(1)}, f32[17,8,512]{2,1,0:T(8,128)S(1)}, u32[]{:S(2)}, u32[]{:S(2)}) collective-permute-start(f32[17,8,512]{2,1,0:T(8,128)S(1)} %get-tuple-element.41), channel_id=1, source_target_pairs={{0,1},{1,2},{2,3},{3,4},{4,5},{5,6},{6,7},{7,8},{8,9},{9,10},{10,1... | collective-permute-start | bytes 835592 | tf_op jit(solution)/shard_map/ppermute | solution.py:426
  8.0 18.4 %collective-permute-start.1 = (f32[17,8,512]{2,1,0:T(8,128)S(1)}, f32[17,8,512]{2,1,0:T(8,128)S(1)}, u32[]{:S(2)}, u32[]{:S(2)}) collective-permute-start(f32[17,8,512]{2,1,0:T(8,128)S(1)} %get-tuple-element.42), channel_id=1, source_target_pairs={{1,0},{2,1},{3,2},{4,3},{5,4},{6,5},{7,6},{8,7},{9,8},{10,9},{11,1... | collective-permute-start | bytes 835592 | tf_op jit(solution)/shard_map/ppermute | solution.py:426
  8.2 24.5 %collective-permute-start.4 = (f32[30,8,128]{2,1,0:T(8,128)S(1)}, f32[30,8,128]{2,1,0:T(8,128)S(1)}, u32[]{:S(2)}, u32[]{:S(2)}) collective-permute-start(f32[30,8,128]{2,1,0:T(8,128)S(1)} %get-tuple-element.48), channel_id=1, source_target_pairs={{0,32},{32,64},{64,96},{96,128},{128,160},{160,192},{192,224},{224... | collective-permute-start | bytes 368648 | tf_op jit(solution)/shard_map/ppermute | solution.py:432
  9.5 23.6 %collective-permute-start.5 = (f32[30,8,128]{2,1,0:T(8,128)S(1)}, f32[30,8,128]{2,1,0:T(8,128)S(1)}, u32[]{:S(2)}, u32[]{:S(2)}) collective-permute-start(f32[30,8,128]{2,1,0:T(8,128)S(1)} %get-tuple-element.49), channel_id=1, source_target_pairs={{0,64},{32,96},{64,128},{96,160},{128,192},{160,224},{192,0},{224,... | collective-permute-start | bytes 368648 | tf_op jit(solution)/shard_map/ppermute | solution.py:432
  11.9 21.2 %collective-permute-start.6 = (f32[30,8,128]{2,1,0:T(8,128)S(1)}, f32[30,8,128]{2,1,0:T(8,128)S(1)}, u32[]{:S(2)}, u32[]{:S(2)}) collective-permute-start(f32[30,8,128]{2,1,0:T(8,128)S(1)} %get-tuple-element.50), channel_id=1, source_target_pairs={{0,96},{32,128},{64,160},{96,192},{128,224},{160,0},{192,32},{224,... | collective-permute-start | bytes 368648 | tf_op jit(solution)/shard_map/ppermute | solution.py:432
  32.1 23.7 %collective-permute-start.2 = (f32[17,8,512]{2,1,0:T(8,128)S(1)}, f32[17,8,512]{2,1,0:T(8,128)S(1)}, u32[]{:S(2)}, u32[]{:S(2)}) collective-permute-start(f32[17,8,512]{2,1,0:T(8,128)S(1)} %get-tuple-element.44), channel_id=1, source_target_pairs={{0,1},{1,2},{2,3},{3,4},{4,5},{5,6},{6,7},{7,8},{8,9},{9,10},{10,1... | collective-permute-start | bytes 835592 | tf_op jit(solution)/shard_map/ppermute | solution.py:426
  32.2 25.9 %collective-permute-start.3 = (f32[17,8,512]{2,1,0:T(8,128)S(1)}, f32[17,8,512]{2,1,0:T(8,128)S(1)}, u32[]{:S(2)}, u32[]{:S(2)}) collective-permute-start(f32[17,8,512]{2,1,0:T(8,128)S(1)} %get-tuple-element.45), channel_id=1, source_target_pairs={{1,0},{2,1},{3,2},{4,3},{5,4},{6,5},{7,6},{8,7},{9,8},{10,9},{11,1... | collective-permute-start | bytes 835592 | tf_op jit(solution)/shard_map/ppermute | solution.py:426
  32.7 9.6 %collective-permute-start.7 = (f32[30,8,128]{2,1,0:T(8,128)S(1)}, f32[30,8,128]{2,1,0:T(8,128)S(1)}, u32[]{:S(2)}, u32[]{:S(2)}) collective-permute-start(f32[30,8,128]{2,1,0:T(8,128)S(1)} %get-tuple-element.51), channel_id=1, source_target_pairs={{0,128},{32,160},{64,192},{96,224},{128,0},{160,32},{192,64},{224,... | collective-permute-start | bytes 368648 | tf_op jit(solution)/shard_map/ppermute | solution.py:432
  33.1 10.3 %collective-permute-start.8 = (f32[30,8,128]{2,1,0:T(8,128)S(1)}, f32[30,8,128]{2,1,0:T(8,128)S(1)}, u32[]{:S(2)}, u32[]{:S(2)}) collective-permute-start(f32[30,8,128]{2,1,0:T(8,128)S(1)} %get-tuple-element.52), channel_id=1, source_target_pairs={{0,160},{32,192},{64,224},{96,0},{128,32},{160,64},{192,96},{224,1... | collective-permute-start | bytes 368648 | tf_op jit(solution)/shard_map/ppermute | solution.py:432
  33.1 12.1 %collective-permute-start.9 = (f32[30,8,128]{2,1,0:T(8,128)S(1)}, f32[30,8,128]{2,1,0:T(8,128)S(1)}, u32[]{:S(2)}, u32[]{:S(2)}) collective-permute-start(f32[30,8,128]{2,1,0:T(8,128)S(1)} %get-tuple-element.53), channel_id=1, source_target_pairs={{0,192},{32,224},{64,0},{96,32},{128,64},{160,96},{192,128},{224,1... | collective-permute-start | bytes 368648 | tf_op jit(solution)/shard_map/ppermute | solution.py:432
  42.3 12.5 %collective-permute-start.11 = (f32[34,8,128]{2,1,0:T(8,128)S(1)}, f32[34,8,128]{2,1,0:T(8,128)S(1)}, u32[]{:S(2)}, u32[]{:S(2)}) collective-permute-start(f32[34,8,128]{2,1,0:T(8,128)S(1)} %get-tuple-element.59), channel_id=1, source_target_pairs={{0,32},{32,64},{64,96},{96,128},{128,160},{160,192},{192,224},{224... | collective-permute-start | bytes 417800 | tf_op jit(solution)/shard_map/ppermute | solution.py:432
  43.4 12.4 %collective-permute-start.12 = (f32[34,8,128]{2,1,0:T(8,128)S(1)}, f32[34,8,128]{2,1,0:T(8,128)S(1)}, u32[]{:S(2)}, u32[]{:S(2)}) collective-permute-start(f32[34,8,128]{2,1,0:T(8,128)S(1)} %get-tuple-element.60), channel_id=1, source_target_pairs={{0,64},{32,96},{64,128},{96,160},{128,192},{160,224},{192,0},{224,... | collective-permute-start | bytes 417800 | tf_op jit(solution)/shard_map/ppermute | solution.py:432
  45.2 6.2 %collective-permute-start.10 = (f32[30,8,128]{2,1,0:T(8,128)S(1)}, f32[30,8,128]{2,1,0:T(8,128)S(1)}, u32[]{:S(2)}, u32[]{:S(2)}) collective-permute-start(f32[30,8,128]{2,1,0:T(8,128)S(1)} %get-tuple-element.54), channel_id=1, source_target_pairs={{0,224},{32,0},{64,32},{96,64},{128,96},{160,128},{192,160},{224,1... | collective-permute-start | bytes 368648 | tf_op jit(solution)/shard_map/ppermute | solution.py:432
  51.4 11.3 %collective-permute-start.13 = (f32[34,8,128]{2,1,0:T(8,128)S(1)}, f32[34,8,128]{2,1,0:T(8,128)S(1)}, u32[]{:S(2)}, u32[]{:S(2)}) collective-permute-start(f32[34,8,128]{2,1,0:T(8,128)S(1)} %get-tuple-element.61), channel_id=1, source_target_pairs={{0,96},{32,128},{64,160},{96,192},{128,224},{160,0},{192,32},{224,... | collective-permute-start | bytes 417800 | tf_op jit(solution)/shard_map/ppermute | solution.py:432
  54.8 7.8 %collective-permute-start.14 = (f32[34,8,128]{2,1,0:T(8,128)S(1)}, f32[34,8,128]{2,1,0:T(8,128)S(1)}, u32[]{:S(2)}, u32[]{:S(2)}) collective-permute-start(f32[34,8,128]{2,1,0:T(8,128)S(1)} %get-tuple-element.62), channel_id=1, source_target_pairs={{0,128},{32,160},{64,192},{96,224},{128,0},{160,32},{192,64},{224,... | collective-permute-start | bytes 417800 | tf_op jit(solution)/shard_map/ppermute | solution.py:432
  55.8 6.9 %collective-permute-start.15 = (f32[34,8,128]{2,1,0:T(8,128)S(1)}, f32[34,8,128]{2,1,0:T(8,128)S(1)}, u32[]{:S(2)}, u32[]{:S(2)}) collective-permute-start(f32[34,8,128]{2,1,0:T(8,128)S(1)} %get-tuple-element.63), channel_id=1, source_target_pairs={{0,160},{32,192},{64,224},{96,0},{128,32},{160,64},{192,96},{224,1... | collective-permute-start | bytes 417800 | tf_op jit(solution)/shard_map/ppermute | solution.py:432
  55.8 8.3 %collective-permute-start.16 = (f32[34,8,128]{2,1,0:T(8,128)S(1)}, f32[34,8,128]{2,1,0:T(8,128)S(1)}, u32[]{:S(2)}, u32[]{:S(2)}) collective-permute-start(f32[34,8,128]{2,1,0:T(8,128)S(1)} %get-tuple-element.64), channel_id=1, source_target_pairs={{0,192},{32,224},{64,0},{96,32},{128,64},{160,96},{192,128},{224,1... | collective-permute-start | bytes 417800 | tf_op jit(solution)/shard_map/ppermute | solution.py:432
  58.1 7.7 %collective-permute-start.17 = (f32[34,8,128]{2,1,0:T(8,128)S(1)}, f32[34,8,128]{2,1,0:T(8,128)S(1)}, u32[]{:S(2)}, u32[]{:S(2)}) collective-permute-start(f32[34,8,128]{2,1,0:T(8,128)S(1)} %get-tuple-element.65), channel_id=1, source_target_pairs={{0,224},{32,0},{64,32},{96,64},{128,96},{160,128},{192,160},{224,1... | collective-permute-start | bytes 417800 | tf_op jit(solution)/shard_map/ppermute | solution.py:432
  68.7 13.3 %collective-permute-start.20 = (f32[34,8,128]{2,1,0:T(8,128)S(1)}, f32[34,8,128]{2,1,0:T(8,128)S(1)}, u32[]{:S(2)}, u32[]{:S(2)}) collective-permute-start(f32[34,8,128]{2,1,0:T(8,128)S(1)} %get-tuple-element.71), channel_id=1, source_target_pairs={{0,32},{32,64},{64,96},{96,128},{128,160},{160,192},{192,224},{224... | collective-permute-start | bytes 417800 | tf_op jit(solution)/shard_map/ppermute | solution.py:432
  69.7 14.4 %collective-permute-start.21 = (f32[34,8,128]{2,1,0:T(8,128)S(1)}, f32[34,8,128]{2,1,0:T(8,128)S(1)}, u32[]{:S(2)}, u32[]{:S(2)}) collective-permute-start(f32[34,8,128]{2,1,0:T(8,128)S(1)} %get-tuple-element.72), channel_id=1, source_target_pairs={{0,64},{32,96},{64,128},{96,160},{128,192},{160,224},{192,0},{224,... | collective-permute-start | bytes 417800 | tf_op jit(solution)/shard_map/ppermute | solution.py:432
  75.9 11.1 %collective-permute-start.22 = (f32[34,8,128]{2,1,0:T(8,128)S(1)}, f32[34,8,128]{2,1,0:T(8,128)S(1)}, u32[]{:S(2)}, u32[]{:S(2)}) collective-permute-start(f32[34,8,128]{2,1,0:T(8,128)S(1)} %get-tuple-element.73), channel_id=1, source_target_pairs={{0,96},{32,128},{64,160},{96,192},{128,224},{160,0},{192,32},{224,... | collective-permute-start | bytes 417800 | tf_op jit(solution)/shard_map/ppermute | solution.py:432
  77.0 10.0 %collective-permute-start.23 = (f32[34,8,128]{2,1,0:T(8,128)S(1)}, f32[34,8,128]{2,1,0:T(8,128)S(1)}, u32[]{:S(2)}, u32[]{:S(2)}) collective-permute-start(f32[34,8,128]{2,1,0:T(8,128)S(1)} %get-tuple-element.74), channel_id=1, source_target_pairs={{0,128},{32,160},{64,192},{96,224},{128,0},{160,32},{192,64},{224,... | collective-permute-start | bytes 417800 | tf_op jit(solution)/shard_map/ppermute | solution.py:432
  80.9 6.6 %collective-permute-start.24 = (f32[34,8,128]{2,1,0:T(8,128)S(1)}, f32[34,8,128]{2,1,0:T(8,128)S(1)}, u32[]{:S(2)}, u32[]{:S(2)}) collective-permute-start(f32[34,8,128]{2,1,0:T(8,128)S(1)} %get-tuple-element.75), channel_id=1, source_target_pairs={{0,160},{32,192},{64,224},{96,0},{128,32},{160,64},{192,96},{224,1... | collective-permute-start | bytes 417800 | tf_op jit(solution)/shard_map/ppermute | solution.py:432
  84.0 10.3 %collective-permute-start.26 = (f32[34,8,128]{2,1,0:T(8,128)S(1)}, f32[34,8,128]{2,1,0:T(8,128)S(1)}, u32[]{:S(2)}, u32[]{:S(2)}) collective-permute-start(f32[34,8,128]{2,1,0:T(8,128)S(1)} %get-tuple-element.77), channel_id=1, source_target_pairs={{0,224},{32,0},{64,32},{96,64},{128,96},{160,128},{192,160},{224,1... | collective-permute-start | bytes 417800 | tf_op jit(solution)/shard_map/ppermute | solution.py:432
  (18 other events, 178.0 us)

commit v4 on v2

--- a/solution.py
+++ b/solution.py
@@ -72,6 +72,20 @@
         return self.buffer
 
 
+class Held:
+    def __init__(self, ref):
+        self.buffer = ref
+
+    def piece(self, i):
+        return self.buffer
+
+    def whole(self):
+        return self.buffer
+
+    def put(self, index):
+        pass
+
+
 class Stored:
     def __init__(self, target, buffer, sems):
         self.target, self.buffer, self.sems, self.copies = target, buffer, sems, []
@@ -95,8 +109,8 @@
     return tuple(pl.ds(i, 1) for i in range(n))
 
 
-def call(body, operands, results, scratch=(), flops=1 << 22, moved=1 << 22):
-    space = {"smem": pltpu.SMEM, "vmem": pltpu.VMEM}
+def call(body, operands, results, scratch=(), flops=1 << 20, moved=1 << 20):
+    space = {"smem": pltpu.SMEM, "vmem": pltpu.VMEM, "held": pltpu.VMEM}
     modes = [mode for _, mode in operands]
     here = [isinstance(mode, str) for mode in modes]
     in_specs = [
@@ -117,7 +131,7 @@
         args, loads = [], []
         for ref, mode, h in zip(ins, modes, here):
             if h:
-                args.append(ref)
+                args.append(Held(ref) if mode == "held" else ref)
             else:
                 args.append(Loaded(ref, refs.pop(0), refs.pop(0), mode))
                 loads.append(args[-1])
@@ -131,7 +145,7 @@
                 args.append(Stored(ref, refs.pop(0), refs.pop(0)))
                 stores.append(args[-1])
             else:
-                args.append(ref)
+                args.append(ref if n else Held(ref))
         body(*args, *refs)
         for x in loads:
             x.whole()
@@ -253,22 +267,26 @@
     pack_tile([get(4), get(5), extra, extra], 7, up_ref, down_ref)
 
 
-def prepare_kernel(a, ps, m_ref, up, down, blocks, sems):
-    copies = []
+def prepare_kernel(a_ref, ps_ref, m_ref, up, down):
     for t in range(6):
-        ref = a.piece(t)
-        pack_tile([ref[t, v] for v in range(4)], t, up.buffer, down.buffer)
-    pack_last(lambda t: a.buffer[t, NV - 1], ps[...], up.buffer, down.buffer)
+        pack_tile([a_ref[t, v] for v in range(4)], t, up.buffer, down.buffer)
+        for x in (up, down):
+            x.put(pl.ds(2 * t, 2))
+    pack_last(lambda t: a_ref[t, NV - 1], ps_ref[...], up.buffer, down.buffer)
     metal_edges(m_ref, up.buffer.at[16], down.buffer.at[16])
-    up.put(slice(None))
-    down.put(slice(None))
-    for i in range(8):
-        copies.append(
-            pltpu.make_async_copy(
-                a.buffer.at[:, :, :, pl.ds(i * CHUNK, CHUNK)], blocks.at[i], sems.at[i]
-            )
+    for x in (up, down):
+        x.put(pl.ds(12, 5))
+
+
+def blocks_kernel(a_ref, blocks, sems):
+    copies = [
+        pltpu.make_async_copy(
+            a_ref.at[:, :, :, pl.ds(i * CHUNK, CHUNK)], blocks.at[i], sems.at[i]
         )
-        copies[-1].start()
+        for i in range(8)
+    ]
+    for copy in copies:
+        copy.start()
     for copy in copies:
         copy.wait()
 
@@ -389,16 +407,19 @@
     )
 
 
-def derive_kernel(kron, a, ps_ref, g):
+def derive_kernel(kron_ref, a_ref, ps_ref, g):
     wide = jnp.concatenate([local_step(ps_ref)] * NV, axis=1)
-    a_ref = a.whole()
     x = turned(lambda j, t, v: a_ref[j, t, v])
-    d = rotate_time(kron.whole()[...], x)
+    d = rotate_time(kron_ref[...], x)
     g.buffer[...] = (d.reshape(NT, ROWS, NV * CHUNK) * wide[None]).reshape(NT * ROWS, NV * CHUNK)
     g.put(slice(None))
 
 
-def middle_kernel(tab_ref, jx_ref, jz_ref, b_in, s_in, ps_ref, up_ref, down_ref, hq_in, c_out, hc, parts):
+def middle_kernel(
+    tab_ref, jx_ref, jz_ref, b_in, s_in, ps_ref, up_ref, down_ref, hq_in, g_ref,
+    c_out, hc,
+    parts,
+):
     first = lax.axis_index("inst") * 6
     c_ref = c_out.buffer
     for t in range(6):
@@ -545,61 +566,62 @@
 BLOCKS = (8, 34, ROWS, CHUNK)
 
 
+LONG = 1 << 36
+
+
+def plain(*arrays):
+    return [(array, "vmem") for array in arrays]
+
+
+def held(*arrays):
+    return [(array, "held") for array in arrays]
+
+
 def local(a0, source, ps, jx, jz, metal, cond, coeff, ff, mf):
     kron = jnp.asarray(KRON)
     tab = jnp.asarray(FLAT)
     coeff, ff, mf = (x.reshape(1, NF) for x in (coeff, ff, mf))
-    metal = metal.reshape(CH, ROWS, MSPAN)
-    up, down, blocks = call(
-        prepare_kernel,
-        [(a0, SIX), (ps, "vmem"), (metal, "vmem")],
-        [(EDGES, 1), (EDGES, 1), ((8, 6, NV, ROWS, CHUNK), -1)],
+    metal = metal.reshape(METAL)
+    up, down = call(prepare_kernel, plain(a0, ps, metal), [(EDGES, 7), (EDGES, 7)])
+    up, down = exchange(up, down)
+    (blocks,) = call(
+        blocks_kernel,
+        plain(a0),
+        [((8, 6, NV, ROWS, CHUNK), -1)],
         scratch=[pltpu.SemaphoreType.DMA((8,))],
     )
-    up, down = exchange(up, down)
     a_turned = turn(blocks)
+    scalars = [(tab, "smem"), (jx, "smem"), (jz, "smem")]
     (e0,) = call(
-        energy_kernel,
-        [(tab, "smem"), (metal, "vmem"), (coeff, "vmem"), (ff, "vmem"), (mf, "vmem")],
-        [((6, ROWS, SPAN), 6)],
-    )
-    jacobians = [(tab, "smem"), (jx, "smem"), (jz, "smem")]
+        energy_kernel, scalars[:1] + plain(metal, coeff, ff, mf), [((6, ROWS, SPAN), 6)]
+    )
     q, b, bup, bdown, hq, metal = call(
         first_kernel,
-        jacobians
-        + [(a0, SIX), (source, SIX), (ps, "vmem"), (up, "vmem"), (down, "vmem"), (e0, SIX)]
-        + [(coeff, "vmem"), (ff, "vmem"), (metal, "vmem"), (cond, "vmem")],
+        scalars + held(a0, source) + plain(ps, up, down) + held(e0) + plain(coeff, ff, metal, cond),
         [(BLOCKS, 7), (FLUID, 6), (EDGES, 1), (EDGES, 1), ((CH, ROWS, SPAN), 1), (METAL, 1)],
         scratch=[pltpu.VMEM((6, NV, ROWS, SPAN), F32)],
+        flops=LONG,
     )
     q_turned = turn(q)
     bup, bdown = exchange(bup, bdown)
-    (g,) = call(
-        derive_kernel,
-        [(kron, WHOLE), (a_turned, WHOLE), (ps, "vmem")],
-        [((NT * ROWS, NV * CHUNK), 1)],
-    )
+    (g,) = call(derive_kernel, plain(kron, a_turned, ps), [((NT * ROWS, NV * CHUNK), 0)])
     c, hc = call(
         middle_kernel,
-        jacobians
-        + [(b, SIX), (source, SIX), (ps, "vmem"), (bup, "vmem"), (bdown, "vmem"), (hq, WHOLE)],
-        [(FLUID, 6), ((CH, ROWS, SPAN), 1)],
+        scalars + held(b, source) + plain(ps, bup, bdown) + held(hq) + plain(g),
+        [(FLUID, 0), ((CH, ROWS, SPAN), 0)],
         scratch=[pltpu.VMEM((3, NV, ROWS, SPAN), F32)],
+        flops=LONG,
     )
     v, metal, mup, mdown, e1 = call(
         second_kernel,
-        [(tab, "smem"), (q_turned, WHOLE), (g, WHOLE), (kron, WHOLE), (ps, "vmem"), (metal, WHOLE)]
-        + [(coeff, "vmem"), (ff, "vmem"), (mf, "vmem"), (hc, WHOLE)],
+        scalars[:1] + held(q_turned, g) + [(kron, WHOLE)] + plain(ps) + held(metal)
+        + plain(coeff, ff, mf) + held(hc),
         [(BLOCKS, 2), (METAL, 1), ((CH, MSPAN), 1), ((CH, MSPAN), 1), ((6, ROWS, SPAN), 1)],
     )
     v = turn(v)
     mup, mdown = exchange(mup, mdown)
-    pieces = tuple((slice(None), pl.ds(t * NV, NV)) for t in range(6)) + ((slice(None), pl.ds(30, 4)),)
     out, metal = call(
-        last_kernel,
-        [(v, pieces), (c, SIX), (e1, WHOLE), (metal, WHOLE), (mup, "vmem"), (mdown, "vmem")]
-        + [(cond, "vmem"), (mf, "vmem")],
-        [(FLUID, 6), (METAL, 1)],
+        last_kernel, held(v, c, e1, metal) + plain(mup, mdown, cond, mf), [(FLUID, 6), (METAL, 1)]
     )
     return out, metal.reshape(2, NH, ROWS, MSPAN)
 

time: 96.3 us -> 85.6 us (0.89)
  the two profiles are of different devices: /device:TPU:112 before, /device:TPU:1 now
where the time goes in v4:
time: 85.6 us; the launch traced here: 85 us
  waiting for transfers between devices  30 us (35%)
  starting transfers between devices  26.9 us (31%)
  Pallas kernels  20.3 us (24%)
  local copies, waits for them, and re-layouts  6.7 us (8%)
  between operations  1.12 us (1%)
    all_to_all x3, starting transfers between devices, turn(): return lax.all_to_all(x, 'inst', 0, 0, tiled=True)  20.5 us
    pallas_call x8, Pallas kernels, call(): pl.pallas_call(kernel, out_shape=[pltpu.HBM(dims, F32) if n else shape(*d...  20.3 us
    all_to_all x3, waiting for transfers between devices, turn(): return lax.all_to_all(x, 'inst', 0, 0, tiled=True)  19.9 us
    ppermute x3, waiting for transfers between devices, exchange(): lax.ppermute(down, 'space', back)  7.32 us
    unnamed x52, local copies, waits for them, and re-layouts  6.7 us
    ppermute x3, starting transfers between devices, exchange(): lax.ppermute(up, 'space', forward)  4.89 us
    ppermute x3, waiting for transfers between devices, exchange(): lax.ppermute(up, 'space', forward)  2.73 us
  transfers between devices with their start and end apart: 9, of which 5 were waited for; matrix products, arithmetic and copies ran while one was open for 0% of the time, Pallas kernels for 16%

profile of v4, /device:TPU:1, one launch (start us, length us, event | category | flops | bytes accessed | tf_op | source)
XLA Modules:
  0.0 85.0 jit_solution(3668523116910277715)
XLA Ops:
  0.6 1.2 %copy-done = f32[6,5,8,1024]{3,2,1,0:T(8,128)S(1)} copy-done((f32[6,5,8,1024]{3,2,1,0:T(8,128)S(1)}, f32[6,5,8,1024]{3,2,1,0:T(8,128)}, u32[]{:S(2)}) %copy-start) | copy-done | bytes 983064
  1.8 0.9 %copy-done.3 = f32[2,4,8,512]{3,2,1,0:T(8,128)S(1)} copy-done((f32[2,4,8,512]{3,2,1,0:T(8,128)S(1)}, f32[2,4,8,512]{3,2,1,0:T(8,128)}, u32[]{:S(2)}) %copy-start.3) | copy-done | bytes 131096
  2.7 0.8 copy-done.5
  3.5 0.9 %shard_map.131 = (f32[17,8,512]{2,1,0:T(8,128)}, f32[17,8,512]{2,1,0:T(8,128)}) custom-call(f32[6,5,8,1024]{3,2,1,0:T(8,128)S(1)} %copy-done, f32[8,1024]{1,0:T(8,128)S(1)} %copy-done.5, f32[8,8,512]{2,1,0:T(8,128)S(1)} %bitcast.5), custom_call_target="tpu_custom_call" | custom-call | flops 1048576 | bytes 1048576 | tf_op jit(solution)/shard_map/pallas_call | solution.py:155
  4.4 4.4 %collective-permute-start = (f32[17,8,512]{2,1,0:T(8,128)}, f32[17,8,512]{2,1,0:T(8,128)S(1)}, u32[]{:S(2)}, u32[]{:S(2)}) collective-permute-start(f32[17,8,512]{2,1,0:T(8,128)} %get-tuple-element.19), channel_id=1, source_target_pairs={{0,1},{1,2},{2,3},{3,4},{4,5},{5,6},{6,7},{7,8},{8,9},{9,10},{10,1... | collective-permute-start | bytes 835592 | tf_op jit(solution)/shard_map/ppermute | solution.py:555
  8.8 1.0 %shard_map.134 = f32[8,6,5,8,128]{4,3,2,1,0:T(8,128)} custom-call(f32[6,5,8,1024]{3,2,1,0:T(8,128)S(1)} %copy-done), custom_call_target="tpu_custom_call" | custom-call | flops 1048576 | bytes 1048576 | tf_op jit(solution)/shard_map/pallas_call | solution.py:155
  10.0 4.3 %all-to-all-start.1 = ((f32[8,6,5,8,128]{4,3,2,1,0:T(8,128)}), f32[8,6,5,8,128]{4,3,2,1,0:T(8,128)S(1)}, u32[]{:S(2)}, u32[]{:S(2)}) async-start(f32[8,6,5,8,128]{4,3,2,1,0:T(8,128)} %shard_map.134), calls=%async_computation.1 | async-start | bytes 1966080 | tf_op jit(solution)/shard_map/all_to_all | solution.py:559
  14.3 2.1 %shard_map.132.refs_8_ = f32[6,8,1024]{2,1,0:T(8,128)} custom-call(f32[1536]{0:T(1024)S(1)} %copy-done.11, f32[8,8,512]{2,1,0:T(8,128)S(1)} %bitcast.6, f32[1,512]{1,0:T(1,128)S(1)} %bitcast.11, s32[1,512]{1,0:T(1,128)S(1)} %bitcast.14, s32[1,512]{1,0:T(1,128)S(1)} %bitcast.8), custom_call_target="tpu_custom_call" | custom-call | flops 1048576 | bytes 1048576 | tf_op jit(solution)/shard_map/pallas_call | solution.py:155
  16.4 4.3 %collective-permute-done.1.refs_7_ = f32[17,8,512]{2,1,0:T(8,128)} collective-permute-done((f32[17,8,512]{2,1,0:T(8,128)}, f32[17,8,512]{2,1,0:T(8,128)}, u32[]{:S(2)}, u32[]{:S(2)}) %collective-permute-start.1) | collective-permute-done | bytes 278560 | tf_op jit(solution)/shard_map/ppermute | solution.py:555
  20.7 0.9 %copy-done.8 = f32[6,8,1024]{2,1,0:T(8,128)S(1)} copy-done((f32[6,8,1024]{2,1,0:T(8,128)S(1)}, f32[6,8,1024]{2,1,0:T(8,128)}, u32[]{:S(2)}) %copy-start.8) | copy-done | bytes 196632
  21.6 6.3 %shard_map.133 = (f32[8,34,8,128]{3,2,1,0:T(8,128)}, f32[6,5,8,1024]{3,2,1,0:T(8,128)}, f32[17,8,512]{2,1,0:T(8,128)}, f32[17,8,512]{2,1,0:T(8,128)}, f32[8,8,1024]{2,1,0:T(8,128)}, /*index=5*/f32[8,8,512]{2,1,0:T(8,128)}) custom-call(f32[1536]{0:T(1024)S(1)} %copy-done.11, f32[5,5]{1,0:T(8,128)S(1)} %copy-done.20, f32[5,5]{1,0:T(8,128)S(1)} %copy-done.21, ...), custom_call_target="tpu_custom_call" | custom-call | flops 68719476736 | bytes 1048576 | tf_op jit(solution)/shard_map/pallas_call | solution.py:155
  28.1 1.3 %collective-permute-start.3 = (f32[17,8,512]{2,1,0:T(8,128)}, f32[17,8,512]{2,1,0:T(8,128)}, u32[]{:S(2)}, u32[]{:S(2)}) collective-permute-start(f32[17,8,512]{2,1,0:T(8,128)} %get-tuple-element.25), channel_id=1, source_target_pairs={{1,0},{2,1},{3,2},{4,3},{5,4},{6,5},{7,6},{8,7},{9,8},{10,9},{11,1... | collective-permute-start | bytes 835592 | tf_op jit(solution)/shard_map/ppermute | solution.py:555
  29.4 11.1 %all-to-all-start = ((f32[8,34,8,128]{3,2,1,0:T(8,128)}), f32[8,34,8,128]{3,2,1,0:T(8,128)S(1)}, u32[]{:S(2)}, u32[]{:S(2)}) async-start(f32[8,34,8,128]{3,2,1,0:T(8,128)} %get-tuple-element.21), calls=%async_computation | async-start | bytes 2228224 | tf_op jit(solution)/shard_map/all_to_all | solution.py:559
  40.5 1.2 %copy-done.2 = bf16[384,1152]{1,0:T(8,128)(2,1)S(1)} copy-done((bf16[384,1152]{1,0:T(8,128)(2,1)S(1)}, bf16[384,1152]{1,0:T(8,128)(2,1)}, u32[]{:S(2)}) %copy-start.2) | copy-done | bytes 884760
  41.6 0.9 %shard_map.135.refs_9_.refs_2_ = f32[384,640]{1,0:T(8,128)S(1)} custom-call(bf16[384,1152]{1,0:T(8,128)(2,1)S(1)} %copy-done.2, f32[8,6,5,8,128]{4,3,2,1,0:T(8,128)S(1)} %all-to-all-done.1.refs_1_, f32[8,1024]{1,0:T(8,128)S(1)} %copy-done.6), custom_call_target="tpu_custom_call" | custom-call | flops 1048576 | bytes 1048576 | tf_op jit(solution)/shard_map/pallas_call | solution.py:155
  43.3 0.9 %copy-done.19 = f32[17,8,512]{2,1,0:T(8,128)S(1)} copy-done((f32[17,8,512]{2,1,0:T(8,128)S(1)}, f32[17,8,512]{2,1,0:T(8,128)}, u32[]{:S(2)}) %copy-start.19) | copy-done | bytes 278552
  44.3 2.8 %shard_map.136 = (f32[6,5,8,1024]{3,2,1,0:T(8,128)S(1)}, f32[8,8,1024]{2,1,0:T(8,128)S(1)}) custom-call(f32[1536]{0:T(1024)S(1)} %copy-done.11, f32[5,5]{1,0:T(8,128)S(1)} %copy-done.20, f32[5,5]{1,0:T(8,128)S(1)} %copy-done.21, f32[6,5,8,1024]{3,2,1,0:T(8,128)S(1)} %copy-done.22, f32[6,5,8,1024]{3,2,1,0:T(8,128)S(1)} %copy-done.17, ...), custom_call_target="tpu_custom_call" | custom-call | flops 68719476736 | bytes 1048576 | tf_op jit(solution)/shard_map/pallas_call | solution.py:155
  47.1 9.9 %all-to-all-done.refs_1_ = f32[8,34,8,128]{3,2,1,0:T(8,128)S(1)} async-done(((f32[8,34,8,128]{3,2,1,0:T(8,128)}), f32[8,34,8,128]{3,2,1,0:T(8,128)S(1)}, u32[]{:S(2)}, u32[]{:S(2)}) %all-to-all-start) | async-done | bytes 1114144 | tf_op jit(solution)/shard_map/all_to_all | solution.py:559
  57.1 4.9 %shard_map.137 = (f32[8,34,8,128]{3,2,1,0:T(8,128)}, f32[8,8,512]{2,1,0:T(8,128)}, f32[8,512]{1,0:T(8,128)}, f32[8,512]{1,0:T(8,128)}, f32[6,8,1024]{2,1,0:T(8,128)}) custom-call(f32[1536]{0:T(1024)S(1)} %copy-done.11, f32[8,34,8,128]{3,2,1,0:T(8,128)S(1)} %all-to-all-done.refs_1_, f32[384,640]{1,0:T(8,128)S(1)} %shard_map.135.refs_9_.refs_2_, ...), custom_call_target="tpu_custom_call" | custom-call | flops 1048576 | bytes 1048576 | tf_op jit(solution)/shard_map/pallas_call | solution.py:155
  62.0 5.2 %all-to-all-start.2 = ((f32[8,34,8,128]{3,2,1,0:T(8,128)}), f32[8,34,8,128]{3,2,1,0:T(8,128)S(1)}, u32[]{:S(2)}, u32[]{:S(2)}) async-start(f32[8,34,8,128]{3,2,1,0:T(8,128)} %get-tuple-element.28), calls=%async_computation.2 | async-start | bytes 2228224 | tf_op jit(solution)/shard_map/all_to_all | solution.py:559
  67.8 2.7 %collective-permute-done.4.refs_4_ = f32[8,512]{1,0:T(8,128)S(1)} collective-permute-done((f32[8,512]{1,0:T(8,128)S(1)}, f32[8,512]{1,0:T(8,128)S(1)}, u32[]{:S(2)}, u32[]{:S(2)}) %collective-permute-start.4) | collective-permute-done | bytes 16416 | tf_op jit(solution)/shard_map/ppermute | solution.py:555
  70.5 3.0 %collective-permute-done.5.refs_5_ = f32[8,512]{1,0:T(8,128)S(1)} collective-permute-done((f32[8,512]{1,0:T(8,128)S(1)}, f32[8,512]{1,0:T(8,128)S(1)}, u32[]{:S(2)}, u32[]{:S(2)}) %collective-permute-start.5) | collective-permute-done | bytes 16416 | tf_op jit(solution)/shard_map/ppermute | solution.py:555
  73.5 10.0 %all-to-all-done.2.refs_0_ = f32[8,34,8,128]{3,2,1,0:T(8,128)S(1)} async-done(((f32[8,34,8,128]{3,2,1,0:T(8,128)}), f32[8,34,8,128]{3,2,1,0:T(8,128)S(1)}, u32[]{:S(2)}, u32[]{:S(2)}) %all-to-all-start.2) | async-done | bytes 1114144 | tf_op jit(solution)/shard_map/all_to_all | solution.py:559
  83.5 1.3 %shard_map.138 = (f32[6,5,8,1024]{3,2,1,0:T(8,128)}, f32[8,8,512]{2,1,0:T(8,128)}) custom-call(f32[8,34,8,128]{3,2,1,0:T(8,128)S(1)} %all-to-all-done.2.refs_0_, f32[6,5,8,1024]{3,2,1,0:T(8,128)S(1)} %get-tuple-element.29.refs_1_, f32[6,8,1024]{2,1,0:T(8,128)S(1)} %copy-done.7, f32[8,8,512]{2,1,0:T(8,128)S(1)} %copy-done.10, ...), custom_call_target="tpu_custom_call" | custom-call | flops 1048576 | bytes 1048576 | tf_op jit(solution)/shard_map/pallas_call | solution.py:155
  (54 shorter events, 1.5 us)
Async XLA Ops:
  4.4 12.0 %collective-permute-start = (f32[17,8,512]{2,1,0:T(8,128)}, f32[17,8,512]{2,1,0:T(8,128)S(1)}, u32[]{:S(2)}, u32[]{:S(2)}) collective-permute-start(f32[17,8,512]{2,1,0:T(8,128)} %get-tuple-element.19), channel_id=1, source_target_pairs={{0,1},{1,2},{2,3},{3,4},{4,5},{5,6},{6,7},{7,8},{8,9},{9,10},{10,1... | collective-permute-start | bytes 835592 | tf_op jit(solution)/shard_map/ppermute | solution.py:555
  8.8 11.9 %collective-permute-start.1 = (f32[17,8,512]{2,1,0:T(8,128)}, f32[17,8,512]{2,1,0:T(8,128)}, u32[]{:S(2)}, u32[]{:S(2)}) collective-permute-start(f32[17,8,512]{2,1,0:T(8,128)} %get-tuple-element.20), channel_id=1, source_target_pairs={{1,0},{2,1},{3,2},{4,3},{5,4},{6,5},{7,6},{8,7},{9,8},{10,9},{11,1... | collective-permute-start | bytes 835592 | tf_op jit(solution)/shard_map/ppermute | solution.py:555
  9.8 4.4 %copy-start.4 = (f32[2,4,8,512]{3,2,1,0:T(8,128)S(1)}, f32[2,4,8,512]{3,2,1,0:T(8,128)}, u32[]{:S(2)}) copy-start(f32[2,4,8,512]{3,2,1,0:T(8,128)} %param.17) | copy-start | bytes 393220
  9.8 4.4 %copy-start.11 = (f32[1536]{0:T(1024)S(1)}, f32[1536]{0:T(1024)}, u32[]{:S(2)}) copy-start(f32[1536]{0:T(1024)} %constant.5.clone.refs_0_) | copy-start | bytes 18436
  9.9 4.4 %copy-start.12 = (s32[512]{0:T(512)S(1)}, s32[512]{0:T(512)}, u32[]{:S(2)}) copy-start(s32[512]{0:T(512)} %param.21) | copy-start | bytes 6148
  9.9 4.4 %copy-start.14 = (f32[512]{0:T(512)S(1)}, f32[512]{0:T(512)}, u32[]{:S(2)}) copy-start(f32[512]{0:T(512)} %param.19) | copy-start | bytes 6148
  9.9 10.8 %copy-start.1 = (f32[6,5,8,1024]{3,2,1,0:T(8,128)S(1)}, f32[6,5,8,1024]{3,2,1,0:T(8,128)}, u32[]{:S(2)}) copy-start(f32[6,5,8,1024]{3,2,1,0:T(8,128)} %refs_0_.8) | copy-start | bytes 2949124
  9.9 10.8 %copy-start.6 = (f32[8,1024]{1,0:T(8,128)S(1)}, f32[8,1024]{1,0:T(8,128)}, u32[]{:S(2)}) copy-start(f32[8,1024]{1,0:T(8,128)} %refs_4_.5) | copy-start | bytes 98308
  9.9 10.8 %copy-start.13 = (f32[8,512]{1,0:T(8,128)S(1)}, f32[8,512]{1,0:T(8,128)}, u32[]{:S(2)}) copy-start(f32[8,512]{1,0:T(8,128)} %refs_6_.1) | copy-start | bytes 49156
  9.9 10.7 %copy-start.16 = (f32[6,5,8,1024]{3,2,1,0:T(8,128)S(1)}, f32[6,5,8,1024]{3,2,1,0:T(8,128)}, u32[]{:S(2)}) copy-start(f32[6,5,8,1024]{3,2,1,0:T(8,128)} %refs_4_.4) | copy-start | bytes 2949124
  9.9 10.7 %copy-start.20 = (f32[5,5]{1,0:T(8,128)S(1)}, f32[5,5]{1,0:T(8,128)}, u32[]{:S(2)}) copy-start(f32[5,5]{1,0:T(8,128)} %refs_1_.5) | copy-start | bytes 304
  10.0 10.7 %copy-start.21 = (f32[5,5]{1,0:T(8,128)S(1)}, f32[5,5]{1,0:T(8,128)}, u32[]{:S(2)}) copy-start(f32[5,5]{1,0:T(8,128)} %refs_2_.5) | copy-start | bytes 304
  10.0 19.4 %all-to-all-start.1 = ((f32[8,6,5,8,128]{4,3,2,1,0:T(8,128)}), f32[8,6,5,8,128]{4,3,2,1,0:T(8,128)S(1)}, u32[]{:S(2)}, u32[]{:S(2)}) async-start(f32[8,6,5,8,128]{4,3,2,1,0:T(8,128)} %shard_map.134), calls=%async_computation.1 | async-start | bytes 1966080 | tf_op jit(solution)/shard_map/all_to_all | solution.py:559
  28.0 14.6 %collective-permute-start.2 = (f32[17,8,512]{2,1,0:T(8,128)}, f32[17,8,512]{2,1,0:T(8,128)S(1)}, u32[]{:S(2)}, u32[]{:S(2)}) collective-permute-start(f32[17,8,512]{2,1,0:T(8,128)} %get-tuple-element.24), channel_id=1, source_target_pairs={{0,1},{1,2},{2,3},{3,4},{4,5},{5,6},{6,7},{7,8},{8,9},{9,10},{10,1... | collective-permute-start | bytes 835592 | tf_op jit(solution)/shard_map/ppermute | solution.py:555
  28.1 15.2 %collective-permute-start.3 = (f32[17,8,512]{2,1,0:T(8,128)}, f32[17,8,512]{2,1,0:T(8,128)}, u32[]{:S(2)}, u32[]{:S(2)}) collective-permute-start(f32[17,8,512]{2,1,0:T(8,128)} %get-tuple-element.25), channel_id=1, source_target_pairs={{1,0},{2,1},{3,2},{4,3},{5,4},{6,5},{7,6},{8,7},{9,8},{10,9},{11,1... | collective-permute-start | bytes 835592 | tf_op jit(solution)/shard_map/ppermute | solution.py:555
  29.4 27.7 %all-to-all-start = ((f32[8,34,8,128]{3,2,1,0:T(8,128)}), f32[8,34,8,128]{3,2,1,0:T(8,128)S(1)}, u32[]{:S(2)}, u32[]{:S(2)}) async-start(f32[8,34,8,128]{3,2,1,0:T(8,128)} %get-tuple-element.21), calls=%async_computation | async-start | bytes 2228224 | tf_op jit(solution)/shard_map/all_to_all | solution.py:559
  44.3 12.8 %copy-start.9 = (f32[8,8,512]{2,1,0:T(8,128)S(1)}, f32[8,8,512]{2,1,0:T(8,128)}, u32[]{:S(2)}) copy-start(f32[8,8,512]{2,1,0:T(8,128)} %get-tuple-element.22.refs_5_) | copy-start | bytes 393220
  61.9 5.2 %copy-start.25 = (f32[8,512]{1,0:T(8,128)S(1)}, f32[8,512]{1,0:T(8,128)}, u32[]{:S(2)}) copy-start(f32[8,512]{1,0:T(8,128)} %get-tuple-element.32) | copy-start | bytes 49156
  61.9 5.7 %copy-start.24 = (f32[8,512]{1,0:T(8,128)S(1)}, f32[8,512]{1,0:T(8,128)}, u32[]{:S(2)}) copy-start(f32[8,512]{1,0:T(8,128)} %get-tuple-element.33) | copy-start | bytes 49156
  61.9 21.6 %copy-start.7 = (f32[6,8,1024]{2,1,0:T(8,128)S(1)}, f32[6,8,1024]{2,1,0:T(8,128)}, u32[]{:S(2)}) copy-start(f32[6,8,1024]{2,1,0:T(8,128)} %get-tuple-element.30.refs_2_) | copy-start | bytes 589828
  62.0 21.6 %copy-start.10 = (f32[8,8,512]{2,1,0:T(8,128)S(1)}, f32[8,8,512]{2,1,0:T(8,128)}, u32[]{:S(2)}) copy-start(f32[8,8,512]{2,1,0:T(8,128)} %get-tuple-element.31.refs_3_) | copy-start | bytes 393220
  62.0 21.5 %all-to-all-start.2 = ((f32[8,34,8,128]{3,2,1,0:T(8,128)}), f32[8,34,8,128]{3,2,1,0:T(8,128)S(1)}, u32[]{:S(2)}, u32[]{:S(2)}) async-start(f32[8,34,8,128]{3,2,1,0:T(8,128)} %get-tuple-element.28), calls=%async_computation.2 | async-start | bytes 2228224 | tf_op jit(solution)/shard_map/all_to_all | solution.py:559
  67.2 3.3 %collective-permute-start.4 = (f32[8,512]{1,0:T(8,128)S(1)}, f32[8,512]{1,0:T(8,128)S(1)}, u32[]{:S(2)}, u32[]{:S(2)}) collective-permute-start(f32[8,512]{1,0:T(8,128)S(1)} %copy-done.25), channel_id=1, source_target_pairs={{0,1},{1,2},{2,3},{3,4},{4,5},{5,6},{6,7},{7,8},{8,9},{9,10},{10,1... | collective-permute-start | bytes 49160 | tf_op jit(solution)/shard_map/ppermute | solution.py:555
  67.6 5.9 %collective-permute-start.5 = (f32[8,512]{1,0:T(8,128)S(1)}, f32[8,512]{1,0:T(8,128)S(1)}, u32[]{:S(2)}, u32[]{:S(2)}) collective-permute-start(f32[8,512]{1,0:T(8,128)S(1)} %copy-done.24), channel_id=1, source_target_pairs={{1,0},{2,1},{3,2},{4,3},{5,4},{6,5},{7,6},{8,7},{9,8},{10,9},{11,1... | collective-permute-start | bytes 49160 | tf_op jit(solution)/shard_map/ppermute | solution.py:555
  (11 other events, 16.1 us)

commit v5 on v4

--- a/solution.py
+++ b/solution.py
@@ -267,28 +267,16 @@
     pack_tile([get(4), get(5), extra, extra], 7, up_ref, down_ref)
 
 
-def prepare_kernel(a_ref, ps_ref, m_ref, up, down):
+def prepare_kernel(a, ps, m_in, up, down):
     for t in range(6):
-        pack_tile([a_ref[t, v] for v in range(4)], t, up.buffer, down.buffer)
+        ref = a.piece(t)
+        pack_tile([ref[t, v] for v in range(4)], t, up.buffer, down.buffer)
         for x in (up, down):
             x.put(pl.ds(2 * t, 2))
-    pack_last(lambda t: a_ref[t, NV - 1], ps_ref[...], up.buffer, down.buffer)
-    metal_edges(m_ref, up.buffer.at[16], down.buffer.at[16])
+    pack_last(lambda t: a.buffer[t, NV - 1], ps.whole()[...], up.buffer, down.buffer)
+    metal_edges(m_in.whole(), up.buffer.at[16], down.buffer.at[16])
     for x in (up, down):
         x.put(pl.ds(12, 5))
-
-
-def blocks_kernel(a_ref, blocks, sems):
-    copies = [
-        pltpu.make_async_copy(
-            a_ref.at[:, :, :, pl.ds(i * CHUNK, CHUNK)], blocks.at[i], sems.at[i]
-        )
-        for i in range(8)
-    ]
-    for copy in copies:
-        copy.start()
-    for copy in copies:
-        copy.wait()
 
 
 def energy_kernel(tab_ref, m_ref, fc_ref, ff_ref, mf_ref, e):
@@ -317,24 +305,14 @@
     return out
 
 
-def first_kernel(
-    tab_ref, jx_ref, jz_ref, a_in, s_in, ps_ref, up_ref, down_ref, e_in, fc_ref, ff_ref, m_ref, cond_ref,
-    q, b_out, bup, bdown, hq, m_out,
-    parts,
-):
-    first = lax.axis_index("inst") * 6
+def inner_kernel(jx_ref, jz_ref, a_ref, s_ref, ps_ref, e_ref, b, q, parts):
     step = ps_ref[...]
-    step_before = pltpu.roll(edge_tile(up_ref, 7), 2, 0)
-    step_after = pltpu.roll(edge_tile(down_ref, 7), 4, 0)
-    q_ref, b_ref = q.buffer, b_out.buffer
     for t in range(6):
-        a_ref, s_ref, e_ref = a_in.piece(t), s_in.piece(t), e_in.piece(t)
         for v in range(NV):
             a = a_ref[t, v]
-            before, after = halo_pair(up_ref, down_ref, t, v)
-            dx, dz, rest = stencil_parts(a, before, after)
+            dx, dz, rest = stencil_parts(a, 0.0, 0.0)
             parts[0, v], parts[1, v], parts[2, v] = dx, dz, rest
-            dx, dz, rest = stencil_parts(step * a, step_before * before, step_after * after)
+            dx, dz, rest = stencil_parts(step * a, 0.0, 0.0)
             parts[3, v], parts[4, v], parts[5, v] = dx, dz, rest
         for i in range(8):
             cut = pl.ds(i * CHUNK, CHUNK)
@@ -348,10 +326,69 @@
                 source = s_ref[t, u, :, cut] + space
                 if u == NV - 1:
                     source = source + e_ref[t, :, cut]
-                b = a + ps_ref[:, cut] * source
-                b_ref[t, u, :, cut] = b
-                q_ref[i, t * NV + u] = a + b + convect(jx_ref, jz_ref, px, pz, parts[5, u, :, cut], u)
-        q.put((slice(None), pl.ds(t * NV, NV)))
+                inner = a + ps_ref[:, cut] * source
+                b.buffer[t, u, :, cut] = inner
+                q.buffer[t, u, :, cut] = a + inner + convect(jx_ref, jz_ref, px, pz, parts[5, u, :, cut], u)
+
+
+def edge_terms(up_ref, down_ref, half, t, v):
+    tile, slot = (t, v) if v < 4 else (6 + t // 4, t % 4)
+    row = row_index(512)
+    up, down = up_ref[2 * tile + half], down_ref[2 * tile + half]
+    east_one = pltpu.roll(down, (7 - 2 * slot) % 8, 0)
+    west_one = pltpu.roll(up, (7 - 2 * slot) % 8, 0)
+    east_two = pltpu.roll(down, (6 - 2 * slot) % 8, 0)
+    west_two = pltpu.roll(up, (8 - 2 * slot) % 8, 0)
+    one = jnp.where(row == 7, east_one, jnp.where(row == 0, west_one, 0.0))
+    two = jnp.where(row >= 6, east_two, jnp.where(row < 2, west_two, 0.0))
+    return one, two
+
+
+def first_kernel(
+    tab_ref, jx_ref, jz_ref, a_ref, bi_ref, qi_ref, ps_ref, up_ref, down_ref, fc_ref, ff_ref, m_ref, cond_ref,
+    q, b_out, bup, bdown, hq, m_out,
+    q4_ref, sems,
+):
+    first = lax.axis_index("inst") * 6
+    copies = [
+        pltpu.make_async_copy(
+            a_ref.at[:, :, :, pl.ds(i * CHUNK, CHUNK)], q.target.at[i, pl.ds(6, 6)], sems.at[i]
+        )
+        for i in range(8)
+    ]
+    for copy in copies:
+        copy.start()
+    step = ps_ref[...]
+    q_ref, b_ref = q.buffer, b_out.buffer
+    sign = jnp.where(row_index(512) == 0, 0.5, -0.5)
+    step_edges = []
+    for half in range(2):
+        tile = 14 + half
+        row = row_index(512)
+        up, down = up_ref[tile], down_ref[tile]
+        one = jnp.where(row == 7, pltpu.roll(down, 3, 0), pltpu.roll(up, 3, 0))
+        two = jnp.where(row >= 6, pltpu.roll(down, 2, 0), pltpu.roll(up, 4, 0))
+        step_edges.append((one, two))
+    for t in range(6):
+        for half in range(2):
+            wide = pl.ds(half * 512, 512)
+            here = ps_ref[:, wide]
+            step_one, step_two = step_edges[half]
+            edges = [edge_terms(up_ref, down_ref, half, t, v) for v in range(NV)]
+            for u in range(NV):
+                total = jx_ref[u, 0] * edges[0][0]
+                for v in range(1, NV):
+                    total += jx_ref[u, v] * edges[v][0]
+                one = sign * total + (4.0 * damping_fourth) * edges[u][0]
+                two = damping_fourth * edges[u][1]
+                change = here * (one - two)
+                b_ref[t, u, :, wide] = bi_ref[t, u, :, wide] + change
+                value = qi_ref[t, u, :, wide] + change + (step_one * one - step_two * two)
+                for i in range(4):
+                    q_ref[4 * half + i, t, u] = value[:, i * CHUNK : (i + 1) * CHUNK]
+                if u == NV - 1:
+                    q4_ref[t, :, wide] = value
+        q.put((slice(None), pl.ds(t, 1)))
         b_out.put(pl.ds(t, 1))
         pack_tile([b_ref[t, v] for v in range(4)], t, bup.buffer, bdown.buffer)
     pack_last(lambda t: b_ref[t, NV - 1], step, bup.buffer, bdown.buffer)
@@ -363,11 +400,10 @@
         h0 = h1 = h2 = h3 = None
         for t in range(6):
             at = (first + t) * CH + ch
-            q4 = jnp.concatenate([q_ref[i, t * NV + NV - 1] for i in range(8)], axis=1)
-            a, b = a_in.buffer[t, NV - 1], b_ref[t, NV - 1]
+            a, b = a_ref[t, NV - 1], b_ref[t, NV - 1]
             x0 = tab_ref[W0 + at] * b
             x1 = tab_ref[W1 + at] * a
-            x2 = tab_ref[W1 + at] * q4
+            x2 = tab_ref[W1 + at] * q4_ref[t]
             x3 = tab_ref[W2 + at] * a
             h0, h1, h2, h3 = (
                 (x0, x1, x2, x3) if t == 0 else (h0 + x0, h1 + x1, h2 + x2, h3 + x3)
@@ -378,13 +414,16 @@
     values = at_faces(jnp.stack(heat), f_hot, f_row) * fc_ref[...]
     for i in range(8):
         for k in range(4):
-            q_ref[i, 30 + k] = values[:, k * CHUNK : (k + 1) * CHUNK]
-    q.put((slice(None), pl.ds(30, 4)))
+            q_ref[i, 12, k] = values[:, k * CHUNK : (k + 1) * CHUNK]
+        q_ref[i, 12, 4] = jnp.zeros((ROWS, CHUNK), F32)
+    q.put((slice(None), pl.ds(12, 1)))
     before, after = metal_sides(up_ref.at[16], down_ref.at[16])
     m = metal_update(m_ref, before, after, cond_ref[...])
     for ch in range(CH):
         m_out.buffer[ch] = m[ch]
     m_out.put(slice(None))
+    for copy in copies:
+        copy.wait()
 
 
 def rotate_time(kron, x):
@@ -407,16 +446,8 @@
     )
 
 
-def derive_kernel(kron_ref, a_ref, ps_ref, g):
-    wide = jnp.concatenate([local_step(ps_ref)] * NV, axis=1)
-    x = turned(lambda j, t, v: a_ref[j, t, v])
-    d = rotate_time(kron_ref[...], x)
-    g.buffer[...] = (d.reshape(NT, ROWS, NV * CHUNK) * wide[None]).reshape(NT * ROWS, NV * CHUNK)
-    g.put(slice(None))
-
-
 def middle_kernel(
-    tab_ref, jx_ref, jz_ref, b_in, s_in, ps_ref, up_ref, down_ref, hq_in, g_ref,
+    tab_ref, jx_ref, jz_ref, b_in, s_in, ps_ref, up_ref, down_ref, hq_in,
     c_out, hc,
     parts,
 ):
@@ -471,28 +502,40 @@
     return before, after
 
 
-def heat_sum(blocks_ref):
+def heat_sum(get):
     tiles = []
     for k in range(4):
-        total = blocks_ref[0, 30 + k]
+        total = get(0, k)
         for j in range(1, 8):
-            total += blocks_ref[j, 30 + k]
+            total += get(j, k)
         tiles.append(total)
     return jnp.concatenate(tiles, axis=1)
 
 
 def second_kernel(
-    tab_ref, q, g, kron, ps_ref, m_in, fc_ref, ff_ref, mf_ref, hc,
+    tab_ref, q_ref, kron_ref, ps_ref, m_ref, fc_ref, ff_ref, mf_ref, hc_ref,
     v, m_out, mup, mdown, e,
 ):
     first = lax.axis_index("inst") * 6
+    v_ref = v.buffer
+    near = local_step(ps_ref)
+    wide = jnp.concatenate([near] * NV, axis=1)[None]
+    d = rotate_time(kron_ref[...], turned(lambda j, t, u: q_ref[j, 6 + t, u]))
+    d = (d.reshape(NT, ROWS, NV * CHUNK) * wide).reshape(NT * ROWS, NV * CHUNK)
+    x = turned(lambda j, t, u: q_ref[j, t, u]) - d
+    for half in range(2):
+        d = rotate_time(kron_ref[pl.ds(half * 192, 192), :], x)
+        for j in range(4):
+            for t in range(6):
+                at = (j * 6 + t) * ROWS
+                for u in range(NV):
+                    v_ref[half * 4 + j, t * NV + u] = -near * d[at : at + ROWS, u * CHUNK : (u + 1) * CHUNK]
+        v.put((pl.ds(half * 4, 4), pl.ds(0, 30)))
     step = ps_ref[...]
     coeff = fc_ref[...]
     m_hot, m_row = metal_hots(mf_ref)
     f_hot, f_row = fluid_hots(ff_ref)
-    q_ref, v_ref = q.whole(), v.buffer
-    source = onto_cells(heat_sum(q_ref), m_hot, m_row)
-    m_ref = m_in.whole()
+    source = onto_cells(heat_sum(lambda j, k: q_ref[j, 12, k]), m_hot, m_row)
     m = [m_ref[ch] + metal_step * source[ch] for ch in range(CH)]
     for ch in range(CH):
         m_out.buffer[ch] = m[ch]
@@ -504,7 +547,6 @@
     for t in range(6):
         e.buffer[t] = step * combine(tab_ref, SYNTH, first + t, cells)
     e.put(slice(None))
-    hc_ref = hc.whole()
     heat = []
     for ch in range(CH):
         total = hc_ref[ch]
@@ -515,17 +557,7 @@
     for i in range(8):
         for k in range(4):
             v_ref[i, 30 + k] = values[:, k * CHUNK : (k + 1) * CHUNK]
-    x = turned(lambda j, t, u: q_ref[j, t * NV + u]) - g.whole()[...]
-    kron_ref = kron.whole()
-    minus = -local_step(ps_ref)
-    for half in range(2):
-        d = rotate_time(kron_ref[pl.ds(half * 192, 192), :], x)
-        for j in range(4):
-            for t in range(6):
-                at = (j * 6 + t) * ROWS
-                for u in range(NV):
-                    v_ref[half * 4 + j, t * NV + u] = minus * d[at : at + ROWS, u * CHUNK : (u + 1) * CHUNK]
-        v.put(pl.ds(half * 4, 4))
+    v.put((slice(None), pl.ds(30, 4)))
 
 
 def last_kernel(v, c, e, m_in, mup_ref, mdown_ref, cond_ref, mf_ref, out, m_out):
@@ -540,7 +572,7 @@
                 out.buffer[t, u, :, cut] = total
         out.put(pl.ds(t, 1))
     m_hot, m_row = metal_hots(mf_ref)
-    source = onto_cells(heat_sum(v.whole()), m_hot, m_row)
+    source = onto_cells(heat_sum(lambda j, k: v.buffer[j, 30 + k]), m_hot, m_row)
     before, after = metal_sides(mup_ref, mdown_ref)
     m = metal_update(m_in.whole(), before, after, cond_ref[...])
     for ch in range(CH):
@@ -582,41 +614,39 @@
     tab = jnp.asarray(FLAT)
     coeff, ff, mf = (x.reshape(1, NF) for x in (coeff, ff, mf))
     metal = metal.reshape(METAL)
-    up, down = call(prepare_kernel, plain(a0, ps, metal), [(EDGES, 7), (EDGES, 7)])
+    up, down = call(
+        prepare_kernel, [(a0, SIX), (ps, WHOLE), (metal, WHOLE)], [(EDGES, 7), (EDGES, 7)]
+    )
     up, down = exchange(up, down)
-    (blocks,) = call(
-        blocks_kernel,
-        plain(a0),
-        [((8, 6, NV, ROWS, CHUNK), -1)],
-        scratch=[pltpu.SemaphoreType.DMA((8,))],
-    )
-    a_turned = turn(blocks)
     scalars = [(tab, "smem"), (jx, "smem"), (jz, "smem")]
     (e0,) = call(
-        energy_kernel, scalars[:1] + plain(metal, coeff, ff, mf), [((6, ROWS, SPAN), 6)]
+        energy_kernel, scalars[:1] + plain(metal, coeff, ff, mf), [((6, ROWS, SPAN), 0)]
+    )
+    b, q = call(
+        inner_kernel,
+        scalars[1:] + plain(a0, source, ps, e0),
+        [(FLUID, 0), (FLUID, 0)],
+        scratch=[pltpu.VMEM((6, NV, ROWS, SPAN), F32)],
     )
     q, b, bup, bdown, hq, metal = call(
         first_kernel,
-        scalars + held(a0, source) + plain(ps, up, down) + held(e0) + plain(coeff, ff, metal, cond),
-        [(BLOCKS, 7), (FLUID, 6), (EDGES, 1), (EDGES, 1), ((CH, ROWS, SPAN), 1), (METAL, 1)],
-        scratch=[pltpu.VMEM((6, NV, ROWS, SPAN), F32)],
-        flops=LONG,
+        scalars + plain(a0, b, q, ps, up, down, coeff, ff, metal, cond),
+        [((8, 13, NV, ROWS, CHUNK), 7), (FLUID, 6), (EDGES, 1), (EDGES, 1), ((CH, ROWS, SPAN), 1), (METAL, 1)],
+        scratch=[pltpu.VMEM((6, ROWS, SPAN), F32), pltpu.SemaphoreType.DMA((8,))],
     )
     q_turned = turn(q)
     bup, bdown = exchange(bup, bdown)
-    (g,) = call(derive_kernel, plain(kron, a_turned, ps), [((NT * ROWS, NV * CHUNK), 0)])
     c, hc = call(
         middle_kernel,
-        scalars + held(b, source) + plain(ps, bup, bdown) + held(hq) + plain(g),
+        scalars + held(b, source) + plain(ps, bup, bdown) + held(hq),
         [(FLUID, 0), ((CH, ROWS, SPAN), 0)],
         scratch=[pltpu.VMEM((3, NV, ROWS, SPAN), F32)],
         flops=LONG,
     )
     v, metal, mup, mdown, e1 = call(
         second_kernel,
-        scalars[:1] + held(q_turned, g) + [(kron, WHOLE)] + plain(ps) + held(metal)
-        + plain(coeff, ff, mf) + held(hc),
-        [(BLOCKS, 2), (METAL, 1), ((CH, MSPAN), 1), ((CH, MSPAN), 1), ((6, ROWS, SPAN), 1)],
+        scalars[:1] + plain(q_turned, kron, ps, metal, coeff, ff, mf, hc),
+        [(BLOCKS, 3), (METAL, 1), ((CH, MSPAN), 1), ((CH, MSPAN), 1), ((6, ROWS, SPAN), 1)],
     )
     v = turn(v)
     mup, mdown = exchange(mup, mdown)

time: 85.6 us -> 92.3 us (1.078)
  the two profiles are of different devices: /device:TPU:1 before, /device:TPU:16 now
where the time goes in v5:
time: 92.3 us; the launch traced here: 91.5 us
  waiting for transfers between devices  32.6 us (35%)
  starting transfers between devices  22.4 us (24%)
  Pallas kernels  20.4 us (22%)
  local copies, waits for them, and re-layouts  15 us (16%)
  between operations  1.08 us (1%)
    all_to_all x2, waiting for transfers between devices, turn(): return lax.all_to_all(x, 'inst', 0, 0, tiled=True)  29.2 us
    pallas_call x7, Pallas kernels, call(): pl.pallas_call(kernel, out_shape=[pltpu.HBM(dims, F32) if n else shape(*d...  20.4 us
    unnamed x68, local copies, waits for them, and re-layouts  15 us
    all_to_all x2, starting transfers between devices, turn(): return lax.all_to_all(x, 'inst', 0, 0, tiled=True)  12.5 us
    ppermute x3, starting transfers between devices, exchange(): lax.ppermute(down, 'space', back)  9.7 us
    ppermute x3, waiting for transfers between devices, exchange(): lax.ppermute(up, 'space', forward)  3.47 us
  transfers between devices with their start and end apart: 8, of which 3 were waited for; matrix products, arithmetic and copies ran while one was open for 0% of the time, Pallas kernels for 9%

profile of v5, /device:TPU:16, one launch (start us, length us, event | category | flops | bytes accessed | tf_op | source)
XLA Modules:
  0.0 91.5 jit_solution(13407085612075924478)
XLA Ops:
  0.7 2.3 %shard_map.133 = (f32[17,8,512]{2,1,0:T(8,128)}, f32[17,8,512]{2,1,0:T(8,128)}) custom-call(f32[6,5,8,1024]{3,2,1,0:T(8,128)} %refs_3_.4, f32[8,1024]{1,0:T(8,128)} %refs_3_.5, f32[8,8,512]{2,1,0:T(8,128)} %bitcast.5), custom_call_target="tpu_custom_call" | custom-call | flops 1048576 | bytes 1048576 | tf_op jit(solution)/shard_map/pallas_call | solution.py:155
  3.1 3.2 %collective-permute-start.1 = (f32[17,8,512]{2,1,0:T(8,128)}, f32[17,8,512]{2,1,0:T(8,128)S(1)}, u32[]{:S(2)}, u32[]{:S(2)}) collective-permute-start(f32[17,8,512]{2,1,0:T(8,128)} %get-tuple-element.24), channel_id=1, source_target_pairs={{1,0},{2,1},{3,2},{4,3},{5,4},{6,5},{7,6},{8,7},{9,8},{10,9},{11,1... | collective-permute-start | bytes 835592 | tf_op jit(solution)/shard_map/ppermute | solution.py:587
  6.3 0.9 copy-done.1
  7.2 0.7 copy-done.13
  10.0 1.3 %shard_map.131.refs_5_ = f32[6,8,1024]{2,1,0:T(8,128)S(1)} custom-call(f32[1536]{0:T(1024)S(1)} %copy-done.13, f32[8,8,512]{2,1,0:T(8,128)S(1)} %bitcast.6, f32[1,512]{1,0:T(1,128)S(1)} %bitcast.8, s32[1,512]{1,0:T(1,128)S(1)} %bitcast.11, s32[1,512]{1,0:T(1,128)S(1)} %bitcast.14), custom_call_target="tpu_custom_call" | custom-call | flops 1048576 | bytes 1048576 | tf_op jit(solution)/shard_map/pallas_call | solution.py:155
  11.3 1.2 %copy-done.3 = f32[6,5,8,1024]{3,2,1,0:T(8,128)S(1)} copy-done((f32[6,5,8,1024]{3,2,1,0:T(8,128)S(1)}, f32[6,5,8,1024]{3,2,1,0:T(8,128)}, u32[]{:S(2)}) %copy-start.3) | copy-done | bytes 983064
  12.5 0.8 copy-done.8
  14.7 3.8 %shard_map.132 = (f32[6,5,8,1024]{3,2,1,0:T(8,128)S(1)}, f32[6,5,8,1024]{3,2,1,0:T(8,128)S(1)}) custom-call(f32[5,5]{1,0:T(8,128)S(1)} %copy-done.24, f32[5,5]{1,0:T(8,128)S(1)} %copy-done.26, f32[6,5,8,1024]{3,2,1,0:T(8,128)S(1)} %copy-done, f32[6,5,8,1024]{3,2,1,0:T(8,128)S(1)} %copy-done.3, f32[8,1024]{1,0:T(8,128)S(1)} %copy-done.8, ...), custom_call_target="tpu_custom_call" | custom-call | flops 1048576 | bytes 1048576 | tf_op jit(solution)/shard_map/pallas_call | solution.py:155
  18.6 4.4 %shard_map.134 = (f32[8,13,5,8,128]{4,3,2,1,0:T(8,128)}, f32[6,5,8,1024]{3,2,1,0:T(8,128)}, f32[17,8,512]{2,1,0:T(8,128)}, f32[17,8,512]{2,1,0:T(8,128)}, f32[8,8,1024]{2,1,0:T(8,128)}, /*index=5*/f32[8,8,512]{2,1,0:T(8,128)}) custom-call(f32[1536]{0:T(1024)S(1)} %copy-done.13, f32[5,5]{1,0:T(8,128)S(1)} %copy-done.24, f32[5,5]{1,0:T(8,128)S(1)} %copy-done.26, ...), custom_call_target="tpu_custom_call" | custom-call | flops 1048576 | bytes 1048576 | tf_op jit(solution)/shard_map/pallas_call | solution.py:155
  23.0 3.2 %collective-permute-start.3 = (f32[17,8,512]{2,1,0:T(8,128)}, f32[17,8,512]{2,1,0:T(8,128)}, u32[]{:S(2)}, u32[]{:S(2)}) collective-permute-start(f32[17,8,512]{2,1,0:T(8,128)} %get-tuple-element.29), channel_id=1, source_target_pairs={{1,0},{2,1},{3,2},{4,3},{5,4},{6,5},{7,6},{8,7},{9,8},{10,9},{11,1... | collective-permute-start | bytes 835592 | tf_op jit(solution)/shard_map/ppermute | solution.py:587
  26.3 5.2 %all-to-all-start = ((f32[8,13,5,8,128]{4,3,2,1,0:T(8,128)}), f32[8,13,5,8,128]{4,3,2,1,0:T(8,128)S(1)}, u32[]{:S(2)}, u32[]{:S(2)}) async-start(f32[8,13,5,8,128]{4,3,2,1,0:T(8,128)} %get-tuple-element.25), calls=%async_computation | async-start | bytes 4259840 | tf_op jit(solution)/shard_map/all_to_all | solution.py:591
  33.5 1.2 %copy-done.28 = f32[6,5,8,1024]{3,2,1,0:T(8,128)S(1)} copy-done((f32[6,5,8,1024]{3,2,1,0:T(8,128)S(1)}, f32[6,5,8,1024]{3,2,1,0:T(8,128)}, u32[]{:S(2)}) %copy-start.28) | copy-done | bytes 983064
  34.7 1.0 %copy-done.30 = f32[17,8,512]{2,1,0:T(8,128)S(1)} copy-done((f32[17,8,512]{2,1,0:T(8,128)S(1)}, f32[17,8,512]{2,1,0:T(8,128)}, u32[]{:S(2)}) %copy-start.30) | copy-done | bytes 278552
  35.7 0.9 %copy-done.31 = f32[8,8,1024]{2,1,0:T(8,128)S(1)} copy-done((f32[8,8,1024]{2,1,0:T(8,128)S(1)}, f32[8,8,1024]{2,1,0:T(8,128)}, u32[]{:S(2)}) %copy-start.31) | copy-done | bytes 262168
  36.7 2.7 %shard_map.135 = (f32[6,5,8,1024]{3,2,1,0:T(8,128)S(1)}, f32[8,8,1024]{2,1,0:T(8,128)S(1)}) custom-call(f32[1536]{0:T(1024)S(1)} %copy-done.14, f32[5,5]{1,0:T(8,128)S(1)} %copy-done.25, f32[5,5]{1,0:T(8,128)S(1)} %copy-done.27, f32[6,5,8,1024]{3,2,1,0:T(8,128)S(1)} %copy-done.28, f32[6,5,8,1024]{3,2,1,0:T(8,128)S(1)} %copy-done.4, f32[8,1024]{1,0:T(8,128)S(1)} %copy-done.9, ...), custom_call_target="tpu_custom_call" | custom-call | flops 68719476736 | bytes 1048576 | tf_op jit(solution)/shard_map/pallas_call | solution.py:155
  39.4 0.9 %copy-done.5 = f32[6,5,8,1024]{3,2,1,0:T(8,128)} copy-done((f32[6,5,8,1024]{3,2,1,0:T(8,128)}, f32[6,5,8,1024]{3,2,1,0:T(8,128)S(1)}, u32[]{:S(2)}) %copy-start.5) | copy-done | bytes 983064
  40.3 20.2 %all-to-all-done.refs_1_ = f32[8,13,5,8,128]{4,3,2,1,0:T(8,128)S(1)} async-done(((f32[8,13,5,8,128]{4,3,2,1,0:T(8,128)}), f32[8,13,5,8,128]{4,3,2,1,0:T(8,128)S(1)}, u32[]{:S(2)}, u32[]{:S(2)}) %all-to-all-start) | async-done | bytes 2129952 | tf_op jit(solution)/shard_map/all_to_all | solution.py:591
  60.6 1.2 %copy-done.7 = bf16[384,1152]{1,0:T(8,128)(2,1)S(1)} copy-done((bf16[384,1152]{1,0:T(8,128)(2,1)S(1)}, bf16[384,1152]{1,0:T(8,128)(2,1)}, u32[]{:S(2)}) %copy-start.7) | copy-done | bytes 884760
  62.4 4.4 %shard_map.136 = (f32[8,34,8,128]{3,2,1,0:T(8,128)}, f32[8,8,512]{2,1,0:T(8,128)}, f32[8,512]{1,0:T(8,128)}, f32[8,512]{1,0:T(8,128)}, f32[6,8,1024]{2,1,0:T(8,128)}) custom-call(f32[1536]{0:T(1024)S(1)} %copy-done.14, f32[8,13,5,8,128]{4,3,2,1,0:T(8,128)S(1)} %all-to-all-done.refs_1_, bf16[384,1152]{1,0:T(8,128)(2,1)S(1)} %copy-done.7, ...), custom_call_target="tpu_custom_call" | custom-call | flops 1048576 | bytes 1048576 | tf_op jit(solution)/shard_map/pallas_call | solution.py:155
  66.9 7.3 %all-to-all-start.1 = ((f32[8,34,8,128]{3,2,1,0:T(8,128)}), f32[8,34,8,128]{3,2,1,0:T(8,128)S(1)}, u32[]{:S(2)}, u32[]{:S(2)}) async-start(f32[8,34,8,128]{3,2,1,0:T(8,128)} %get-tuple-element.32), calls=%async_computation.1 | async-start | bytes 2228224 | tf_op jit(solution)/shard_map/all_to_all | solution.py:591
  74.3 3.2 %collective-permute-start.5 = (f32[8,512]{1,0:T(8,128)S(1)}, f32[8,512]{1,0:T(8,128)S(1)}, u32[]{:S(2)}, u32[]{:S(2)}) collective-permute-start(f32[8,512]{1,0:T(8,128)S(1)} %copy-done.32), channel_id=1, source_target_pairs={{1,0},{2,1},{3,2},{4,3},{5,4},{6,5},{7,6},{8,7},{9,8},{10,9},{11,1... | collective-permute-start | bytes 49160 | tf_op jit(solution)/shard_map/ppermute | solution.py:587
  77.6 3.5 %collective-permute-done.4.refs_4_ = f32[8,512]{1,0:T(8,128)S(1)} collective-permute-done((f32[8,512]{1,0:T(8,128)S(1)}, f32[8,512]{1,0:T(8,128)S(1)}, u32[]{:S(2)}, u32[]{:S(2)}) %collective-permute-start.4) | collective-permute-done | bytes 16416 | tf_op jit(solution)/shard_map/ppermute | solution.py:587
  81.0 8.9 %all-to-all-done.1.refs_0_ = f32[8,34,8,128]{3,2,1,0:T(8,128)S(1)} async-done(((f32[8,34,8,128]{3,2,1,0:T(8,128)}), f32[8,34,8,128]{3,2,1,0:T(8,128)S(1)}, u32[]{:S(2)}, u32[]{:S(2)}) %all-to-all-start.1) | async-done | bytes 1114144 | tf_op jit(solution)/shard_map/all_to_all | solution.py:591
  90.0 1.3 %shard_map.137 = (f32[6,5,8,1024]{3,2,1,0:T(8,128)}, f32[8,8,512]{2,1,0:T(8,128)}) custom-call(f32[8,34,8,128]{3,2,1,0:T(8,128)S(1)} %all-to-all-done.1.refs_0_, f32[6,5,8,1024]{3,2,1,0:T(8,128)S(1)} %copy-done.6, f32[6,8,1024]{2,1,0:T(8,128)S(1)} %copy-done.10, f32[8,8,512]{2,1,0:T(8,128)S(1)} %copy-done.12, f32[8,512]{1,0:T(8,128)S(1)} %collective-permute-done.4.refs_4_, ...), custom_call_target="tpu_custom_call" | custom-call | flops 1048576 | bytes 1048576 | tf_op jit(solution)/shard_map/pallas_call | solution.py:155
  (67 shorter events, 6.5 us)
Async XLA Ops:
  0.6 10.7 %copy-start = (f32[6,5,8,1024]{3,2,1,0:T(8,128)S(1)}, f32[6,5,8,1024]{3,2,1,0:T(8,128)}, u32[]{:S(2)}) copy-start(f32[6,5,8,1024]{3,2,1,0:T(8,128)} %refs_3_.4) | copy-start | bytes 2949124
  0.6 17.9 %copy-start.2 = (f32[2,4,8,512]{3,2,1,0:T(8,128)S(1)}, f32[2,4,8,512]{3,2,1,0:T(8,128)}, u32[]{:S(2)}) copy-start(f32[2,4,8,512]{3,2,1,0:T(8,128)} %param.17) | copy-start | bytes 393220
  0.7 17.9 %copy-start.15 = (f32[8,512]{1,0:T(8,128)S(1)}, f32[8,512]{1,0:T(8,128)}, u32[]{:S(2)}) copy-start(f32[8,512]{1,0:T(8,128)} %refs_6_.3) | copy-start | bytes 49156
  3.0 15.5 %collective-permute-start = (f32[17,8,512]{2,1,0:T(8,128)}, f32[17,8,512]{2,1,0:T(8,128)S(1)}, u32[]{:S(2)}, u32[]{:S(2)}) collective-permute-start(f32[17,8,512]{2,1,0:T(8,128)} %get-tuple-element.23), channel_id=1, source_target_pairs={{0,1},{1,2},{2,3},{3,4},{4,5},{5,6},{6,7},{7,8},{8,9},{9,10},{10,1... | collective-permute-start | bytes 835592 | tf_op jit(solution)/shard_map/ppermute | solution.py:587
  3.1 15.4 %collective-permute-start.1 = (f32[17,8,512]{2,1,0:T(8,128)}, f32[17,8,512]{2,1,0:T(8,128)S(1)}, u32[]{:S(2)}, u32[]{:S(2)}) collective-permute-start(f32[17,8,512]{2,1,0:T(8,128)} %get-tuple-element.24), channel_id=1, source_target_pairs={{1,0},{2,1},{3,2},{4,3},{5,4},{6,5},{7,6},{8,7},{9,8},{10,9},{11,1... | collective-permute-start | bytes 835592 | tf_op jit(solution)/shard_map/ppermute | solution.py:587
  22.9 8.5 %collective-permute-start.2 = (f32[17,8,512]{2,1,0:T(8,128)}, f32[17,8,512]{2,1,0:T(8,128)S(1)}, u32[]{:S(2)}, u32[]{:S(2)}) collective-permute-start(f32[17,8,512]{2,1,0:T(8,128)} %get-tuple-element.28), channel_id=1, source_target_pairs={{0,1},{1,2},{2,3},{3,4},{4,5},{5,6},{6,7},{7,8},{8,9},{9,10},{10,1... | collective-permute-start | bytes 835592 | tf_op jit(solution)/shard_map/ppermute | solution.py:587
  23.0 9.1 %collective-permute-start.3 = (f32[17,8,512]{2,1,0:T(8,128)}, f32[17,8,512]{2,1,0:T(8,128)}, u32[]{:S(2)}, u32[]{:S(2)}) collective-permute-start(f32[17,8,512]{2,1,0:T(8,128)} %get-tuple-element.29), channel_id=1, source_target_pairs={{1,0},{2,1},{3,2},{4,3},{5,4},{6,5},{7,6},{8,7},{9,8},{10,9},{11,1... | collective-permute-start | bytes 835592 | tf_op jit(solution)/shard_map/ppermute | solution.py:587
  26.3 5.9 %copy-start.4 = (f32[6,5,8,1024]{3,2,1,0:T(8,128)S(1)}, f32[6,5,8,1024]{3,2,1,0:T(8,128)}, u32[]{:S(2)}) copy-start(f32[6,5,8,1024]{3,2,1,0:T(8,128)} %refs_4_.3) | copy-start | bytes 2949124
  26.3 5.9 %copy-start.9 = (f32[8,1024]{1,0:T(8,128)S(1)}, f32[8,1024]{1,0:T(8,128)}, u32[]{:S(2)}) copy-start(f32[8,1024]{1,0:T(8,128)} %refs_3_.5) | copy-start | bytes 98308
  26.3 5.9 %copy-start.14 = (f32[1536]{0:T(1024)S(1)}, f32[1536]{0:T(1024)}, u32[]{:S(2)}) copy-start(f32[1536]{0:T(1024)} %constant.5.clone.refs_0_) | copy-start | bytes 18436
  26.3 34.3 %all-to-all-start = ((f32[8,13,5,8,128]{4,3,2,1,0:T(8,128)}), f32[8,13,5,8,128]{4,3,2,1,0:T(8,128)S(1)}, u32[]{:S(2)}, u32[]{:S(2)}) async-start(f32[8,13,5,8,128]{4,3,2,1,0:T(8,128)} %get-tuple-element.25), calls=%async_computation | async-start | bytes 4259840 | tf_op jit(solution)/shard_map/all_to_all | solution.py:591
  36.6 23.9 %copy-start.11 = (f32[8,8,512]{2,1,0:T(8,128)S(1)}, f32[8,8,512]{2,1,0:T(8,128)}, u32[]{:S(2)}) copy-start(f32[8,8,512]{2,1,0:T(8,128)} %get-tuple-element.26.refs_4_) | copy-start | bytes 393220
  36.6 23.9 %copy-start.18 = (f32[512]{0:T(512)S(1)}, f32[512]{0:T(512)}, u32[]{:S(2)}) copy-start(f32[512]{0:T(512)} %param.19) | copy-start | bytes 6148
  36.6 23.9 %copy-start.20 = (s32[512]{0:T(512)S(1)}, s32[512]{0:T(512)}, u32[]{:S(2)}) copy-start(s32[512]{0:T(512)} %param.20) | copy-start | bytes 6148
  62.4 27.6 %copy-start.6 = (f32[6,5,8,1024]{3,2,1,0:T(8,128)S(1)}, f32[6,5,8,1024]{3,2,1,0:T(8,128)}, u32[]{:S(2)}) copy-start(f32[6,5,8,1024]{3,2,1,0:T(8,128)} %copy-done.5) | copy-start | bytes 2949124
  66.8 7.4 %copy-start.33 = (f32[8,512]{1,0:T(8,128)S(1)}, f32[8,512]{1,0:T(8,128)}, u32[]{:S(2)}) copy-start(f32[8,512]{1,0:T(8,128)} %get-tuple-element.36) | copy-start | bytes 49156
  66.9 7.5 %copy-start.32 = (f32[8,512]{1,0:T(8,128)S(1)}, f32[8,512]{1,0:T(8,128)}, u32[]{:S(2)}) copy-start(f32[8,512]{1,0:T(8,128)} %get-tuple-element.37) | copy-start | bytes 49156
  66.9 23.1 %copy-start.10 = (f32[6,8,1024]{2,1,0:T(8,128)S(1)}, f32[6,8,1024]{2,1,0:T(8,128)}, u32[]{:S(2)}) copy-start(f32[6,8,1024]{2,1,0:T(8,128)} %get-tuple-element.34.refs_2_) | copy-start | bytes 589828
  66.9 23.1 %copy-start.12 = (f32[8,8,512]{2,1,0:T(8,128)S(1)}, f32[8,8,512]{2,1,0:T(8,128)}, u32[]{:S(2)}) copy-start(f32[8,8,512]{2,1,0:T(8,128)} %get-tuple-element.35.refs_3_) | copy-start | bytes 393220
  66.9 23.1 %copy-start.16 = (f32[8,512]{1,0:T(8,128)S(1)}, f32[8,512]{1,0:T(8,128)}, u32[]{:S(2)}) copy-start(f32[8,512]{1,0:T(8,128)} %refs_6_.3) | copy-start | bytes 49156
  66.9 23.1 %copy-start.23 = (s32[512]{0:T(512)S(1)}, s32[512]{0:T(512)}, u32[]{:S(2)}) copy-start(s32[512]{0:T(512)} %param.21) | copy-start | bytes 6148
  66.9 23.1 %all-to-all-start.1 = ((f32[8,34,8,128]{3,2,1,0:T(8,128)}), f32[8,34,8,128]{3,2,1,0:T(8,128)S(1)}, u32[]{:S(2)}, u32[]{:S(2)}) async-start(f32[8,34,8,128]{3,2,1,0:T(8,128)} %get-tuple-element.32), calls=%async_computation.1 | async-start | bytes 2228224 | tf_op jit(solution)/shard_map/all_to_all | solution.py:591
  74.2 6.8 %collective-permute-start.4 = (f32[8,512]{1,0:T(8,128)S(1)}, f32[8,512]{1,0:T(8,128)S(1)}, u32[]{:S(2)}, u32[]{:S(2)}) collective-permute-start(f32[8,512]{1,0:T(8,128)S(1)} %copy-done.33), channel_id=1, source_target_pairs={{0,1},{1,2},{2,3},{3,4},{4,5},{5,6},{6,7},{7,8},{8,9},{9,10},{10,1... | collective-permute-start | bytes 49160 | tf_op jit(solution)/shard_map/ppermute | solution.py:587
  74.3 6.7 %collective-permute-start.5 = (f32[8,512]{1,0:T(8,128)S(1)}, f32[8,512]{1,0:T(8,128)S(1)}, u32[]{:S(2)}, u32[]{:S(2)}) collective-permute-start(f32[8,512]{1,0:T(8,128)S(1)} %copy-done.32), channel_id=1, source_target_pairs={{1,0},{2,1},{3,2},{4,3},{5,4},{6,5},{7,6},{8,7},{9,8},{10,9},{11,1... | collective-permute-start | bytes 49160 | tf_op jit(solution)/shard_map/ppermute | solution.py:587
  (18 other events, 15.0 us)

commit v6 on v5

--- a/solution.py
+++ b/solution.py
@@ -70,6 +70,9 @@
         for i in range(len(self.copies)):
             self.piece(i)
         return self.buffer
+
+    def __getitem__(self, index):
+        return self.whole()[index]
 
 
 class Held:
@@ -305,9 +308,15 @@
     return out
 
 
-def inner_kernel(jx_ref, jz_ref, a_ref, s_ref, ps_ref, e_ref, b, q, parts):
+def inner_kernel(jx_ref, jz_ref, a_in, s_in, ps_ref, e_ref, b, q, blocks, parts, sems):
     step = ps_ref[...]
+    copies = []
     for t in range(6):
+        a_ref, s_ref = a_in.piece(t), s_in.piece(t)
+        for i in range(8):
+            source = a_ref.at[t, :, :, pl.ds(i * CHUNK, CHUNK)]
+            copies.append(pltpu.make_async_copy(source, blocks.at[i, t], sems.at[8 * t + i]))
+            copies[-1].start()
         for v in range(NV):
             a = a_ref[t, v]
             dx, dz, rest = stencil_parts(a, 0.0, 0.0)
@@ -329,35 +338,29 @@
                 inner = a + ps_ref[:, cut] * source
                 b.buffer[t, u, :, cut] = inner
                 q.buffer[t, u, :, cut] = a + inner + convect(jx_ref, jz_ref, px, pz, parts[5, u, :, cut], u)
+        b.put(pl.ds(t, 1))
+        q.put(pl.ds(t, 1))
+    for copy in copies:
+        copy.wait()
 
 
 def edge_terms(up_ref, down_ref, half, t, v):
     tile, slot = (t, v) if v < 4 else (6 + t // 4, t % 4)
     row = row_index(512)
     up, down = up_ref[2 * tile + half], down_ref[2 * tile + half]
-    east_one = pltpu.roll(down, (7 - 2 * slot) % 8, 0)
-    west_one = pltpu.roll(up, (7 - 2 * slot) % 8, 0)
+    one = pltpu.roll(jnp.where(row == 2 * slot, down, up), (7 - 2 * slot) % 8, 0)
+    one = jnp.where((row == 0) | (row == 7), one, 0.0)
     east_two = pltpu.roll(down, (6 - 2 * slot) % 8, 0)
     west_two = pltpu.roll(up, (8 - 2 * slot) % 8, 0)
-    one = jnp.where(row == 7, east_one, jnp.where(row == 0, west_one, 0.0))
     two = jnp.where(row >= 6, east_two, jnp.where(row < 2, west_two, 0.0))
     return one, two
 
 
 def first_kernel(
     tab_ref, jx_ref, jz_ref, a_ref, bi_ref, qi_ref, ps_ref, up_ref, down_ref, fc_ref, ff_ref, m_ref, cond_ref,
-    q, b_out, bup, bdown, hq, m_out,
-    q4_ref, sems,
+    q, b_out, bup, bdown, q4, m_out,
 ):
     first = lax.axis_index("inst") * 6
-    copies = [
-        pltpu.make_async_copy(
-            a_ref.at[:, :, :, pl.ds(i * CHUNK, CHUNK)], q.target.at[i, pl.ds(6, 6)], sems.at[i]
-        )
-        for i in range(8)
-    ]
-    for copy in copies:
-        copy.start()
     step = ps_ref[...]
     q_ref, b_ref = q.buffer, b_out.buffer
     sign = jnp.where(row_index(512) == 0, 0.5, -0.5)
@@ -385,45 +388,35 @@
                 b_ref[t, u, :, wide] = bi_ref[t, u, :, wide] + change
                 value = qi_ref[t, u, :, wide] + change + (step_one * one - step_two * two)
                 for i in range(4):
-                    q_ref[4 * half + i, t, u] = value[:, i * CHUNK : (i + 1) * CHUNK]
+                    q_ref[4 * half + i, t * NV + u] = value[:, i * CHUNK : (i + 1) * CHUNK]
                 if u == NV - 1:
-                    q4_ref[t, :, wide] = value
-        q.put((slice(None), pl.ds(t, 1)))
+                    q4.buffer[t, :, wide] = value
+        q.put((slice(None), pl.ds(t * NV, NV)))
         b_out.put(pl.ds(t, 1))
         pack_tile([b_ref[t, v] for v in range(4)], t, bup.buffer, bdown.buffer)
     pack_last(lambda t: b_ref[t, NV - 1], step, bup.buffer, bdown.buffer)
+    q4.put(slice(None))
     bup.put(slice(None))
     bdown.put(slice(None))
     f_hot, f_row = fluid_hots(ff_ref)
     heat = []
     for ch in range(CH):
-        h0 = h1 = h2 = h3 = None
-        for t in range(6):
+        h0 = h1 = jnp.zeros((ROWS, SPAN), F32)
+        for t in range(6 if ch != NH else 0):
             at = (first + t) * CH + ch
-            a, b = a_ref[t, NV - 1], b_ref[t, NV - 1]
-            x0 = tab_ref[W0 + at] * b
-            x1 = tab_ref[W1 + at] * a
-            x2 = tab_ref[W1 + at] * q4_ref[t]
-            x3 = tab_ref[W2 + at] * a
-            h0, h1, h2, h3 = (
-                (x0, x1, x2, x3) if t == 0 else (h0 + x0, h1 + x1, h2 + x2, h3 + x3)
-            )
+            h0 += tab_ref[W0 + at] * b_ref[t, NV - 1]
+            h1 += tab_ref[W1 + at] * a_ref[t, NV - 1]
         heat.append(h0 - step * h1)
-        hq.buffer[ch] = step * (step * h3 - h2)
-    hq.put(slice(None))
     values = at_faces(jnp.stack(heat), f_hot, f_row) * fc_ref[...]
     for i in range(8):
         for k in range(4):
-            q_ref[i, 12, k] = values[:, k * CHUNK : (k + 1) * CHUNK]
-        q_ref[i, 12, 4] = jnp.zeros((ROWS, CHUNK), F32)
-    q.put((slice(None), pl.ds(12, 1)))
+            q_ref[i, 30 + k] = values[:, k * CHUNK : (k + 1) * CHUNK]
+    q.put((slice(None), pl.ds(30, 4)))
     before, after = metal_sides(up_ref.at[16], down_ref.at[16])
     m = metal_update(m_ref, before, after, cond_ref[...])
     for ch in range(CH):
         m_out.buffer[ch] = m[ch]
     m_out.put(slice(None))
-    for copy in copies:
-        copy.wait()
 
 
 def rotate_time(kron, x):
@@ -446,8 +439,16 @@
     )
 
 
+def derive_kernel(kron_ref, a_ref, ps_ref, g):
+    wide = jnp.concatenate([local_step(ps_ref)] * NV, axis=1)
+    x = turned(lambda j, t, v: a_ref[j, t, v])
+    d = rotate_time(kron_ref[...], x)
+    g.buffer[...] = (d.reshape(NT, ROWS, NV * CHUNK) * wide[None]).reshape(NT * ROWS, NV * CHUNK)
+    g.put(slice(None))
+
+
 def middle_kernel(
-    tab_ref, jx_ref, jz_ref, b_in, s_in, ps_ref, up_ref, down_ref, hq_in,
+    tab_ref, jx_ref, jz_ref, b_in, s_in, ps_ref, up_ref, down_ref, a_ref, q4_ref, g_ref,
     c_out, hc,
     parts,
 ):
@@ -467,12 +468,15 @@
                 space = convect(jx_ref, jz_ref, dx, dz, parts[2, u, :, cut], u)
                 c_ref[t, u, :, cut] = b_ref[t, u, :, cut] + ps_ref[:, cut] * (s_ref[t, u, :, cut] + space)
         c_out.put(pl.ds(t, 1))
-    hq_ref = hq_in.whole()
+    step = ps_ref[...]
     for ch in range(CH):
-        total = hq_ref[ch]
-        for t in range(6):
-            total += tab_ref[W0 + (first + t) * CH + ch] * c_ref[t, NV - 1]
-        hc.buffer[ch] = total
+        h0 = h2 = h3 = jnp.zeros((ROWS, SPAN), F32)
+        for t in range(6 if ch != NH else 0):
+            at = (first + t) * CH + ch
+            h0 += tab_ref[W0 + at] * c_ref[t, NV - 1]
+            h2 += tab_ref[W1 + at] * q4_ref[t]
+            h3 += tab_ref[W2 + at] * a_ref[t, NV - 1]
+        hc.buffer[ch] = h0 + step * (step * h3 - h2)
     hc.put(slice(None))
 
 
@@ -513,16 +517,13 @@
 
 
 def second_kernel(
-    tab_ref, q_ref, kron_ref, ps_ref, m_ref, fc_ref, ff_ref, mf_ref, hc_ref,
+    tab_ref, q_ref, g_ref, kron_ref, ps_ref, m_ref, fc_ref, ff_ref, mf_ref, hc_ref,
     v, m_out, mup, mdown, e,
 ):
     first = lax.axis_index("inst") * 6
     v_ref = v.buffer
     near = local_step(ps_ref)
-    wide = jnp.concatenate([near] * NV, axis=1)[None]
-    d = rotate_time(kron_ref[...], turned(lambda j, t, u: q_ref[j, 6 + t, u]))
-    d = (d.reshape(NT, ROWS, NV * CHUNK) * wide).reshape(NT * ROWS, NV * CHUNK)
-    x = turned(lambda j, t, u: q_ref[j, t, u]) - d
+    x = turned(lambda j, t, u: q_ref[j, t * NV + u]) - g_ref[...]
     for half in range(2):
         d = rotate_time(kron_ref[pl.ds(half * 192, 192), :], x)
         for j in range(4):
@@ -535,7 +536,7 @@
     coeff = fc_ref[...]
     m_hot, m_row = metal_hots(mf_ref)
     f_hot, f_row = fluid_hots(ff_ref)
-    source = onto_cells(heat_sum(lambda j, k: q_ref[j, 12, k]), m_hot, m_row)
+    source = onto_cells(heat_sum(lambda j, k: q_ref[j, 30 + k]), m_hot, m_row)
     m = [m_ref[ch] + metal_step * source[ch] for ch in range(CH)]
     for ch in range(CH):
         m_out.buffer[ch] = m[ch]
@@ -595,6 +596,7 @@
 EDGES = (17, ROWS, 512)
 FLUID = (6, NV, ROWS, SPAN)
 METAL = (CH, ROWS, MSPAN)
+ONE = (6, ROWS, SPAN)
 BLOCKS = (8, 34, ROWS, CHUNK)
 
 
@@ -603,6 +605,10 @@
 
 def plain(*arrays):
     return [(array, "vmem") for array in arrays]
+
+
+def late(*arrays):
+    return [(array, WHOLE) for array in arrays]
 
 
 def held(*arrays):
@@ -619,39 +625,41 @@
     )
     up, down = exchange(up, down)
     scalars = [(tab, "smem"), (jx, "smem"), (jz, "smem")]
-    (e0,) = call(
-        energy_kernel, scalars[:1] + plain(metal, coeff, ff, mf), [((6, ROWS, SPAN), 0)]
-    )
-    b, q = call(
+    last_variable = (a0, ((slice(None), pl.ds(NV - 1, 1)),))
+    (e0,) = call(energy_kernel, scalars[:1] + late(metal, coeff, ff, mf), [(ONE, 0)])
+    b, q, blocks = call(
         inner_kernel,
-        scalars[1:] + plain(a0, source, ps, e0),
-        [(FLUID, 0), (FLUID, 0)],
-        scratch=[pltpu.VMEM((6, NV, ROWS, SPAN), F32)],
-    )
-    q, b, bup, bdown, hq, metal = call(
+        scalars[1:] + [(a0, SIX), (source, SIX)] + late(ps) + plain(e0),
+        [(FLUID, 6), (FLUID, 6), ((8, 6, NV, ROWS, CHUNK), -1)],
+        scratch=[pltpu.VMEM((6, NV, ROWS, SPAN), F32), pltpu.SemaphoreType.DMA((48,))],
+    )
+    a_turned = turn(blocks)
+    q, b, bup, bdown, q4, metal = call(
         first_kernel,
-        scalars + plain(a0, b, q, ps, up, down, coeff, ff, metal, cond),
-        [((8, 13, NV, ROWS, CHUNK), 7), (FLUID, 6), (EDGES, 1), (EDGES, 1), ((CH, ROWS, SPAN), 1), (METAL, 1)],
-        scratch=[pltpu.VMEM((6, ROWS, SPAN), F32), pltpu.SemaphoreType.DMA((8,))],
+        scalars + [last_variable] + plain(b, q) + late(ps) + plain(up, down) + late(coeff, ff, metal, cond),
+        [(BLOCKS, 7), (FLUID, 6), (EDGES, 1), (EDGES, 1), (ONE, 1), (METAL, 1)],
+        flops=LONG,
     )
     q_turned = turn(q)
     bup, bdown = exchange(bup, bdown)
+    (g,) = call(derive_kernel, plain(kron, a_turned) + late(ps), [((NT * ROWS, NV * CHUNK), 0)])
     c, hc = call(
         middle_kernel,
-        scalars + held(b, source) + plain(ps, bup, bdown) + held(hq),
+        scalars + [(b, SIX), (source, SIX)] + late(ps) + plain(bup, bdown) + [last_variable] + late(q4)
+        + plain(g),
         [(FLUID, 0), ((CH, ROWS, SPAN), 0)],
         scratch=[pltpu.VMEM((3, NV, ROWS, SPAN), F32)],
         flops=LONG,
     )
     v, metal, mup, mdown, e1 = call(
         second_kernel,
-        scalars[:1] + plain(q_turned, kron, ps, metal, coeff, ff, mf, hc),
-        [(BLOCKS, 3), (METAL, 1), ((CH, MSPAN), 1), ((CH, MSPAN), 1), ((6, ROWS, SPAN), 1)],
+        scalars[:1] + plain(q_turned, g, kron) + late(ps, metal, coeff, ff, mf) + plain(hc),
+        [(BLOCKS, 3), (METAL, 1), ((CH, MSPAN), 1), ((CH, MSPAN), 1), (ONE, 1)],
     )
     v = turn(v)
     mup, mdown = exchange(mup, mdown)
     out, metal = call(
-        last_kernel, held(v, c, e1, metal) + plain(mup, mdown, cond, mf), [(FLUID, 6), (METAL, 1)]
+        last_kernel, held(v, c) + late(e1, metal) + plain(mup, mdown) + late(cond, mf), [(FLUID, 6), (METAL, 1)]
     )
     return out, metal.reshape(2, NH, ROWS, MSPAN)
 

time: 92.3 us -> 86.4 us (0.936)
  the two profiles are of different devices: /device:TPU:16 before, /device:TPU:112 now
where the time goes in v6:
time: 86.4 us; the launch traced here: 85.8 us
  waiting for transfers between devices  30.3 us (35%)
  Pallas kernels  29.8 us (34%)
  starting transfers between devices  22.6 us (26%)
  local copies, waits for them, and re-layouts  2.15 us (2%)
  between operations  1.05 us (1%)
    pallas_call x8, Pallas kernels, call(): pl.pallas_call(kernel, out_shape=[pltpu.HBM(dims, F32) if n else shape(*d...  29.8 us
    all_to_all x3, waiting for transfers between devices, turn(): return lax.all_to_all(x, 'inst', 0, 0, tiled=True)  26 us
    all_to_all x3, starting transfers between devices, turn(): return lax.all_to_all(x, 'inst', 0, 0, tiled=True)  12.6 us
    ppermute x3, starting transfers between devices, exchange(): lax.ppermute(down, 'space', back)  9.33 us
    ppermute x3, waiting for transfers between devices, exchange(): lax.ppermute(up, 'space', forward)  4.33 us
    unnamed x22, local copies, waits for them, and re-layouts  2.15 us
  transfers between devices with their start and end apart: 9, of which 4 were waited for; matrix products, arithmetic and copies ran while one was open for 0% of the time, Pallas kernels for 24%

profile of v6, /device:TPU:112, one launch (start us, length us, event | category | flops | bytes accessed | tf_op | source)
XLA Modules:
  0.0 85.8 jit_solution(11645817210015988968)
XLA Ops:
  0.6 0.0 copy-start.4
  0.7 2.3 %shard_map.133 = (f32[17,8,512]{2,1,0:T(8,128)}, f32[17,8,512]{2,1,0:T(8,128)}) custom-call(f32[6,5,8,1024]{3,2,1,0:T(8,128)} %refs_8_.1, f32[8,1024]{1,0:T(8,128)} %refs_4_.5, f32[8,8,512]{2,1,0:T(8,128)} %bitcast.5), custom_call_target="tpu_custom_call" | custom-call | flops 1048576 | bytes 1048576 | tf_op jit(solution)/shard_map/pallas_call | solution.py:158
  2.9 0.1 collective-permute-start
  3.0 3.2 %collective-permute-start.1 = (f32[17,8,512]{2,1,0:T(8,128)}, f32[17,8,512]{2,1,0:T(8,128)}, u32[]{:S(2)}, u32[]{:S(2)}) collective-permute-start(f32[17,8,512]{2,1,0:T(8,128)} %get-tuple-element.25), channel_id=1, source_target_pairs={{1,0},{2,1},{3,2},{4,3},{5,4},{6,5},{7,6},{8,7},{9,8},{10,9},{11,1... | collective-permute-start | bytes 835592 | tf_op jit(solution)/shard_map/ppermute | solution.py:588
  6.3 2.6 %shard_map.131.refs_5_ = f32[6,8,1024]{2,1,0:T(8,128)S(1)} custom-call(f32[1536]{0:T(1024)S(1)} %copy-done.4, f32[8,8,512]{2,1,0:T(8,128)} %bitcast.6, f32[1,512]{1,0:T(1,128)} %bitcast.11, s32[1,512]{1,0:T(1,128)} %bitcast.14, s32[1,512]{1,0:T(1,128)} %bitcast.8), custom_call_target="tpu_custom_call" | custom-call | flops 1048576 | bytes 1048576 | tf_op jit(solution)/shard_map/pallas_call | solution.py:158
  8.9 6.6 %shard_map.132 = (f32[6,5,8,1024]{3,2,1,0:T(8,128)}, f32[6,5,8,1024]{3,2,1,0:T(8,128)}, f32[8,6,5,8,128]{4,3,2,1,0:T(8,128)}) custom-call(f32[5,5]{1,0:T(8,128)S(1)} %copy-done.5, f32[5,5]{1,0:T(8,128)S(1)} %copy-done.6, f32[6,5,8,1024]{3,2,1,0:T(8,128)} %refs_8_.1, f32[6,5,8,1024]{3,2,1,0:T(8,128)} %refs_4_.4, f32[8,1024]{1,0:T(8,128)} %refs_4_.5, ...), custom_call_target="tpu_custom_call" | custom-call | flops 1048576 | bytes 1048576 | tf_op jit(solution)/shard_map/pallas_call | solution.py:158
  15.5 5.2 %all-to-all-start.1 = ((f32[8,6,5,8,128]{4,3,2,1,0:T(8,128)}), f32[8,6,5,8,128]{4,3,2,1,0:T(8,128)S(1)}, u32[]{:S(2)}, u32[]{:S(2)}) async-start(f32[8,6,5,8,128]{4,3,2,1,0:T(8,128)} %get-tuple-element.27), calls=%async_computation.1 | async-start | bytes 1966080 | tf_op jit(solution)/shard_map/all_to_all | solution.py:592
  20.7 4.8 %shard_map.134 = (f32[8,34,8,128]{3,2,1,0:T(8,128)}, f32[6,5,8,1024]{3,2,1,0:T(8,128)}, f32[17,8,512]{2,1,0:T(8,128)}, f32[17,8,512]{2,1,0:T(8,128)}, f32[6,8,1024]{2,1,0:T(8,128)}, /*index=5*/f32[8,8,512]{2,1,0:T(8,128)}) custom-call(f32[1536]{0:T(1024)S(1)} %copy-done.4, f32[5,5]{1,0:T(8,128)S(1)} %copy-done.5, f32[5,5]{1,0:T(8,128)S(1)} %copy-done.6, ...), custom_call_target="tpu_custom_call" | custom-call | flops 68719476736 | bytes 1048576 | tf_op jit(solution)/shard_map/pallas_call | solution.py:158
  25.6 0.5 collective-permute-start.2
  26.0 2.9 %collective-permute-start.3 = (f32[17,8,512]{2,1,0:T(8,128)}, f32[17,8,512]{2,1,0:T(8,128)}, u32[]{:S(2)}, u32[]{:S(2)}) collective-permute-start(f32[17,8,512]{2,1,0:T(8,128)} %get-tuple-element.31), channel_id=1, source_target_pairs={{1,0},{2,1},{3,2},{4,3},{5,4},{6,5},{7,6},{8,7},{9,8},{10,9},{11,1... | collective-permute-start | bytes 835592 | tf_op jit(solution)/shard_map/ppermute | solution.py:588
  28.9 9.5 %all-to-all-done.1.refs_1_ = f32[8,6,5,8,128]{4,3,2,1,0:T(8,128)S(1)} async-done(((f32[8,6,5,8,128]{4,3,2,1,0:T(8,128)}), f32[8,6,5,8,128]{4,3,2,1,0:T(8,128)S(1)}, u32[]{:S(2)}, u32[]{:S(2)}) %all-to-all-start.1) | async-done | bytes 983072 | tf_op jit(solution)/shard_map/all_to_all | solution.py:592
  38.4 3.7 %all-to-all-start = ((f32[8,34,8,128]{3,2,1,0:T(8,128)}), f32[8,34,8,128]{3,2,1,0:T(8,128)S(1)}, u32[]{:S(2)}, u32[]{:S(2)}) async-start(f32[8,34,8,128]{3,2,1,0:T(8,128)} %get-tuple-element.26), calls=%async_computation | async-start | bytes 2228224 | tf_op jit(solution)/shard_map/all_to_all | solution.py:592
  42.2 1.2 %copy-done = bf16[384,1152]{1,0:T(8,128)(2,1)S(1)} copy-done((bf16[384,1152]{1,0:T(8,128)(2,1)S(1)}, bf16[384,1152]{1,0:T(8,128)(2,1)}, u32[]{:S(2)}) %copy-start) | copy-done | bytes 884760
  43.3 1.7 %shard_map.135.refs_10_.refs_2_ = f32[384,640]{1,0:T(8,128)S(1)} custom-call(bf16[384,1152]{1,0:T(8,128)(2,1)S(1)} %copy-done, f32[8,6,5,8,128]{4,3,2,1,0:T(8,128)S(1)} %all-to-all-done.1.refs_1_, f32[8,1024]{1,0:T(8,128)} %refs_4_.5), custom_call_target="tpu_custom_call" | custom-call | flops 1048576 | bytes 1048576 | tf_op jit(solution)/shard_map/pallas_call | solution.py:158
  45.0 4.6 %shard_map.136 = (f32[6,5,8,1024]{3,2,1,0:T(8,128)S(1)}, f32[8,8,1024]{2,1,0:T(8,128)S(1)}) custom-call(f32[1536]{0:T(1024)S(1)} %copy-done.4, f32[5,5]{1,0:T(8,128)S(1)} %copy-done.5, f32[5,5]{1,0:T(8,128)S(1)} %copy-done.6, f32[6,5,8,1024]{3,2,1,0:T(8,128)} %get-tuple-element.29.refs_3_, f32[6,5,8,1024]{3,2,1,0:T(8,128)} %refs_4_.4, f32[8,1024]{1,0:T(8,128)} %refs_4_.5, ...), custom_call_target="tpu_custom_call" | custom-call | flops 68719476736 | bytes 1048576 | tf_op jit(solution)/shard_map/pallas_call | solution.py:158
  49.6 0.9 %copy-done.2 = f32[6,5,8,1024]{3,2,1,0:T(8,128)} copy-done((f32[6,5,8,1024]{3,2,1,0:T(8,128)}, f32[6,5,8,1024]{3,2,1,0:T(8,128)S(1)}, u32[]{:S(2)}) %copy-start.2) | copy-done | bytes 983064
  50.6 7.7 %all-to-all-done.refs_1_ = f32[8,34,8,128]{3,2,1,0:T(8,128)S(1)} async-done(((f32[8,34,8,128]{3,2,1,0:T(8,128)}), f32[8,34,8,128]{3,2,1,0:T(8,128)S(1)}, u32[]{:S(2)}, u32[]{:S(2)}) %all-to-all-start) | async-done | bytes 1114144 | tf_op jit(solution)/shard_map/all_to_all | solution.py:592
  58.3 4.9 %shard_map.137 = (f32[8,34,8,128]{3,2,1,0:T(8,128)}, f32[8,8,512]{2,1,0:T(8,128)}, f32[8,512]{1,0:T(8,128)}, f32[8,512]{1,0:T(8,128)}, f32[6,8,1024]{2,1,0:T(8,128)}) custom-call(f32[1536]{0:T(1024)S(1)} %copy-done.4, f32[8,34,8,128]{3,2,1,0:T(8,128)S(1)} %all-to-all-done.refs_1_, f32[384,640]{1,0:T(8,128)S(1)} %shard_map.135.refs_10_.refs_2_, ...), custom_call_target="tpu_custom_call" | custom-call | flops 1048576 | bytes 1048576 | tf_op jit(solution)/shard_map/pallas_call | solution.py:158
  63.2 3.7 %all-to-all-start.2 = ((f32[8,34,8,128]{3,2,1,0:T(8,128)}), f32[8,34,8,128]{3,2,1,0:T(8,128)S(1)}, u32[]{:S(2)}, u32[]{:S(2)}) async-start(f32[8,34,8,128]{3,2,1,0:T(8,128)} %get-tuple-element.34), calls=%async_computation.2 | async-start | bytes 2228224 | tf_op jit(solution)/shard_map/all_to_all | solution.py:592
  66.9 0.1 collective-permute-start.4
  67.0 3.2 %collective-permute-start.5 = (f32[8,512]{1,0:T(8,128)S(1)}, f32[8,512]{1,0:T(8,128)S(1)}, u32[]{:S(2)}, u32[]{:S(2)}) collective-permute-start(f32[8,512]{1,0:T(8,128)S(1)} %copy-done.9), channel_id=1, source_target_pairs={{1,0},{2,1},{3,2},{4,3},{5,4},{6,5},{7,6},{8,7},{9,8},{10,9},{11,1... | collective-permute-start | bytes 49160 | tf_op jit(solution)/shard_map/ppermute | solution.py:588
  70.3 4.3 %collective-permute-done.4.refs_4_ = f32[8,512]{1,0:T(8,128)S(1)} collective-permute-done((f32[8,512]{1,0:T(8,128)S(1)}, f32[8,512]{1,0:T(8,128)S(1)}, u32[]{:S(2)}, u32[]{:S(2)}) %collective-permute-start.4) | collective-permute-done | bytes 16416 | tf_op jit(solution)/shard_map/ppermute | solution.py:588
  74.6 8.8 %all-to-all-done.2.refs_0_ = f32[8,34,8,128]{3,2,1,0:T(8,128)S(1)} async-done(((f32[8,34,8,128]{3,2,1,0:T(8,128)}), f32[8,34,8,128]{3,2,1,0:T(8,128)S(1)}, u32[]{:S(2)}, u32[]{:S(2)}) %all-to-all-start.2) | async-done | bytes 1114144 | tf_op jit(solution)/shard_map/all_to_all | solution.py:592
  83.4 2.3 %shard_map.138 = (f32[6,5,8,1024]{3,2,1,0:T(8,128)}, f32[8,8,512]{2,1,0:T(8,128)}) custom-call(f32[8,34,8,128]{3,2,1,0:T(8,128)S(1)} %all-to-all-done.2.refs_0_, f32[6,5,8,1024]{3,2,1,0:T(8,128)S(1)} %copy-done.3, f32[6,8,1024]{2,1,0:T(8,128)} %get-tuple-element.36.refs_2_, f32[8,8,512]{2,1,0:T(8,128)} %get-tuple-element.37.refs_3_, ...), custom_call_target="tpu_custom_call" | custom-call | flops 1048576 | bytes 1048576 | tf_op jit(solution)/shard_map/pallas_call | solution.py:158
  (24 shorter events, 0.1 us)
Async XLA Ops:
  0.6 5.6 %copy-start.4 = (f32[1536]{0:T(1024)S(1)}, f32[1536]{0:T(1024)}, u32[]{:S(2)}) copy-start(f32[1536]{0:T(1024)} %constant.5.clone.refs_0_) | copy-start | bytes 18436
  0.6 8.3 %copy-start.6 = (f32[5,5]{1,0:T(8,128)S(1)}, f32[5,5]{1,0:T(8,128)}, u32[]{:S(2)}) copy-start(f32[5,5]{1,0:T(8,128)} %refs_2_.7) | copy-start | bytes 304
  0.7 8.3 %copy-start.5 = (f32[5,5]{1,0:T(8,128)S(1)}, f32[5,5]{1,0:T(8,128)}, u32[]{:S(2)}) copy-start(f32[5,5]{1,0:T(8,128)} %refs_1_.7) | copy-start | bytes 304
  2.9 17.8 %collective-permute-start = (f32[17,8,512]{2,1,0:T(8,128)}, f32[17,8,512]{2,1,0:T(8,128)}, u32[]{:S(2)}, u32[]{:S(2)}) collective-permute-start(f32[17,8,512]{2,1,0:T(8,128)} %get-tuple-element.24), channel_id=1, source_target_pairs={{0,1},{1,2},{2,3},{3,4},{4,5},{5,6},{6,7},{7,8},{8,9},{9,10},{10,1... | collective-permute-start | bytes 835592 | tf_op jit(solution)/shard_map/ppermute | solution.py:588
  3.0 17.7 %collective-permute-start.1 = (f32[17,8,512]{2,1,0:T(8,128)}, f32[17,8,512]{2,1,0:T(8,128)}, u32[]{:S(2)}, u32[]{:S(2)}) collective-permute-start(f32[17,8,512]{2,1,0:T(8,128)} %get-tuple-element.25), channel_id=1, source_target_pairs={{1,0},{2,1},{3,2},{4,3},{5,4},{6,5},{7,6},{8,7},{9,8},{10,9},{11,1... | collective-permute-start | bytes 835592 | tf_op jit(solution)/shard_map/ppermute | solution.py:588
  15.5 5.2 %copy-start.7 = (f32[6,5,8,1024]{3,2,1,0:T(8,128)S(1)}, f32[6,5,8,1024]{3,2,1,0:T(8,128)}, u32[]{:S(2)}) copy-start(f32[6,5,8,1024]{3,2,1,0:T(8,128)} %get-tuple-element.22.refs_4_) | copy-start | bytes 2949124
  15.5 5.2 %copy-start.8 = (f32[6,5,8,1024]{3,2,1,0:T(8,128)S(1)}, f32[6,5,8,1024]{3,2,1,0:T(8,128)}, u32[]{:S(2)}) copy-start(f32[6,5,8,1024]{3,2,1,0:T(8,128)} %get-tuple-element.23.refs_5_) | copy-start | bytes 2949124
  15.5 22.9 %all-to-all-start.1 = ((f32[8,6,5,8,128]{4,3,2,1,0:T(8,128)}), f32[8,6,5,8,128]{4,3,2,1,0:T(8,128)S(1)}, u32[]{:S(2)}, u32[]{:S(2)}) async-start(f32[8,6,5,8,128]{4,3,2,1,0:T(8,128)} %get-tuple-element.27), calls=%async_computation.1 | async-start | bytes 1966080 | tf_op jit(solution)/shard_map/all_to_all | solution.py:592
  25.6 19.4 %collective-permute-start.2 = (f32[17,8,512]{2,1,0:T(8,128)}, f32[17,8,512]{2,1,0:T(8,128)}, u32[]{:S(2)}, u32[]{:S(2)}) collective-permute-start(f32[17,8,512]{2,1,0:T(8,128)} %get-tuple-element.30), channel_id=1, source_target_pairs={{0,1},{1,2},{2,3},{3,4},{4,5},{5,6},{6,7},{7,8},{8,9},{9,10},{10,1... | collective-permute-start | bytes 835592 | tf_op jit(solution)/shard_map/ppermute | solution.py:588
  26.0 19.0 %collective-permute-start.3 = (f32[17,8,512]{2,1,0:T(8,128)}, f32[17,8,512]{2,1,0:T(8,128)}, u32[]{:S(2)}, u32[]{:S(2)}) collective-permute-start(f32[17,8,512]{2,1,0:T(8,128)} %get-tuple-element.31), channel_id=1, source_target_pairs={{1,0},{2,1},{3,2},{4,3},{5,4},{6,5},{7,6},{8,7},{9,8},{10,9},{11,1... | collective-permute-start | bytes 835592 | tf_op jit(solution)/shard_map/ppermute | solution.py:588
  38.4 19.9 %all-to-all-start = ((f32[8,34,8,128]{3,2,1,0:T(8,128)}), f32[8,34,8,128]{3,2,1,0:T(8,128)S(1)}, u32[]{:S(2)}, u32[]{:S(2)}) async-start(f32[8,34,8,128]{3,2,1,0:T(8,128)} %get-tuple-element.26), calls=%async_computation | async-start | bytes 2228224 | tf_op jit(solution)/shard_map/all_to_all | solution.py:592
  42.1 1.2 %copy-start = (bf16[384,1152]{1,0:T(8,128)(2,1)S(1)}, bf16[384,1152]{1,0:T(8,128)(2,1)}, u32[]{:S(2)}) copy-start(bf16[384,1152]{1,0:T(8,128)(2,1)} %constant.4.clone.refs_0_.refs_3_) | copy-start | bytes 2654212
  45.0 13.2 %copy-start.1 = (bf16[384,1152]{1,0:T(8,128)(2,1)S(1)}, bf16[384,1152]{1,0:T(8,128)(2,1)}, u32[]{:S(2)}) copy-start(bf16[384,1152]{1,0:T(8,128)(2,1)} %constant.4.clone.refs_0_.refs_3_) | copy-start | bytes 2654212
  49.6 0.9 %copy-start.2 = (f32[6,5,8,1024]{3,2,1,0:T(8,128)}, f32[6,5,8,1024]{3,2,1,0:T(8,128)S(1)}, u32[]{:S(2)}) copy-start(f32[6,5,8,1024]{3,2,1,0:T(8,128)S(1)} %get-tuple-element.35.refs_1_) | copy-start | bytes 2949124
  63.2 3.7 %copy-start.10 = (f32[8,512]{1,0:T(8,128)S(1)}, f32[8,512]{1,0:T(8,128)}, u32[]{:S(2)}) copy-start(f32[8,512]{1,0:T(8,128)} %get-tuple-element.38) | copy-start | bytes 49156
  63.2 3.8 %copy-start.9 = (f32[8,512]{1,0:T(8,128)S(1)}, f32[8,512]{1,0:T(8,128)}, u32[]{:S(2)}) copy-start(f32[8,512]{1,0:T(8,128)} %get-tuple-element.39) | copy-start | bytes 49156
  63.2 20.2 %copy-start.3 = (f32[6,5,8,1024]{3,2,1,0:T(8,128)S(1)}, f32[6,5,8,1024]{3,2,1,0:T(8,128)}, u32[]{:S(2)}) copy-start(f32[6,5,8,1024]{3,2,1,0:T(8,128)} %copy-done.2) | copy-start | bytes 2949124
  63.2 20.2 %all-to-all-start.2 = ((f32[8,34,8,128]{3,2,1,0:T(8,128)}), f32[8,34,8,128]{3,2,1,0:T(8,128)S(1)}, u32[]{:S(2)}, u32[]{:S(2)}) async-start(f32[8,34,8,128]{3,2,1,0:T(8,128)} %get-tuple-element.34), calls=%async_computation.2 | async-start | bytes 2228224 | tf_op jit(solution)/shard_map/all_to_all | solution.py:592
  66.9 7.7 %collective-permute-start.4 = (f32[8,512]{1,0:T(8,128)S(1)}, f32[8,512]{1,0:T(8,128)S(1)}, u32[]{:S(2)}, u32[]{:S(2)}) collective-permute-start(f32[8,512]{1,0:T(8,128)S(1)} %copy-done.10), channel_id=1, source_target_pairs={{0,1},{1,2},{2,3},{3,4},{4,5},{5,6},{6,7},{7,8},{8,9},{9,10},{10,1... | collective-permute-start | bytes 49160 | tf_op jit(solution)/shard_map/ppermute | solution.py:588
  67.0 7.6 %collective-permute-start.5 = (f32[8,512]{1,0:T(8,128)S(1)}, f32[8,512]{1,0:T(8,128)S(1)}, u32[]{:S(2)}, u32[]{:S(2)}) collective-permute-start(f32[8,512]{1,0:T(8,128)S(1)} %copy-done.9), channel_id=1, source_target_pairs={{1,0},{2,1},{3,2},{4,3},{5,4},{6,5},{7,6},{8,7},{9,8},{10,9},{11,1... | collective-permute-start | bytes 49160 | tf_op jit(solution)/shard_map/ppermute | solution.py:588

commit v7 on v6

--- a/solution.py
+++ b/solution.py
@@ -105,6 +105,14 @@
             copy.wait()
 
 
+class Into:
+    def __init__(self, result, cut):
+        self.result, self.cut = result, cut
+
+    def __len__(self):
+        return len(self.cut)
+
+
 WHOLE = (slice(None),)
 
 
@@ -121,9 +129,12 @@
     ]
     out_specs = [pl.BlockSpec(memory_space=pltpu.HBM if n else pltpu.VMEM) for _, n in results]
     buffers = []
+    kinds = {mode.result: array.dtype for array, mode in operands if isinstance(mode, Into)}
     for array, mode in operands:
+        if isinstance(mode, tuple):
+            buffers.append(pltpu.VMEM(array.shape, array.dtype))
         if not isinstance(mode, str):
-            buffers += [pltpu.VMEM(array.shape, array.dtype), pltpu.SemaphoreType.DMA((len(mode),))]
+            buffers.append(pltpu.SemaphoreType.DMA((len(mode),)))
     for dims, n in results:
         if n > 0:
             buffers += [pltpu.VMEM(dims, F32), pltpu.SemaphoreType.DMA((n,))]
@@ -136,7 +147,9 @@
             if h:
                 args.append(Held(ref) if mode == "held" else ref)
             else:
-                args.append(Loaded(ref, refs.pop(0), refs.pop(0), mode))
+                into = isinstance(mode, Into)
+                buffer = outs[mode.result] if into else refs.pop(0)
+                args.append(Loaded(ref, buffer, refs.pop(0), mode.cut if into else mode))
                 loads.append(args[-1])
         for i in range(max([len(x.copies) for x in loads], default=0)):
             for x in loads:
@@ -157,7 +170,7 @@
 
     return pl.pallas_call(
         kernel,
-        out_shape=[pltpu.HBM(dims, F32) if n else shape(*dims) for dims, n in results],
+        out_shape=[pltpu.HBM(dims, F32) if n else jax.ShapeDtypeStruct(dims, kinds.get(k, F32)) for k, (dims, n) in enumerate(results)],
         in_specs=in_specs,
         out_specs=out_specs,
         scratch_shapes=buffers + list(scratch),
@@ -270,7 +283,7 @@
     pack_tile([get(4), get(5), extra, extra], 7, up_ref, down_ref)
 
 
-def prepare_kernel(a, ps, m_in, up, down):
+def prepare_kernel(a, ps, m_in, fc, ff, mf, up, down, *copies):
     for t in range(6):
         ref = a.piece(t)
         pack_tile([ref[t, v] for v in range(4)], t, up.buffer, down.buffer)
@@ -282,7 +295,7 @@
         x.put(pl.ds(12, 5))
 
 
-def energy_kernel(tab_ref, m_ref, fc_ref, ff_ref, mf_ref, e):
+def energy_kernel(tab_ref, m_ref, fc_ref, ff_ref, mf_ref, source, e, copied):
     first = lax.axis_index("inst") * 6
     m_hot, m_row = metal_hots(mf_ref)
     f_hot, f_row = fluid_hots(ff_ref)
@@ -308,11 +321,10 @@
     return out
 
 
-def inner_kernel(jx_ref, jz_ref, a_in, s_in, ps_ref, e_ref, b, q, blocks, parts, sems):
+def inner_kernel(jx_ref, jz_ref, a_ref, s_ref, ps_ref, e_ref, b, q, blocks, parts, sems):
     step = ps_ref[...]
     copies = []
     for t in range(6):
-        a_ref, s_ref = a_in.piece(t), s_in.piece(t)
         for i in range(8):
             source = a_ref.at[t, :, :, pl.ds(i * CHUNK, CHUNK)]
             copies.append(pltpu.make_async_copy(source, blocks.at[i, t], sems.at[8 * t + i]))
@@ -620,29 +632,36 @@
     tab = jnp.asarray(FLAT)
     coeff, ff, mf = (x.reshape(1, NF) for x in (coeff, ff, mf))
     metal = metal.reshape(METAL)
-    up, down = call(
-        prepare_kernel, [(a0, SIX), (ps, WHOLE), (metal, WHOLE)], [(EDGES, 7), (EDGES, 7)]
+    small = [(x, Into(3 + i, WHOLE)) for i, x in enumerate((ps, metal, coeff, ff, mf))]
+    up, down, a_here, ps_here, metal_here, coeff_here, ff_here, mf_here = call(
+        prepare_kernel,
+        [(a0, Into(2, SIX))] + small,
+        [(EDGES, 7), (EDGES, 7), (FLUID, 0), ((ROWS, SPAN), 0), (METAL, 0)] + [((1, NF), 0)] * 3,
     )
     up, down = exchange(up, down)
     scalars = [(tab, "smem"), (jx, "smem"), (jz, "smem")]
     last_variable = (a0, ((slice(None), pl.ds(NV - 1, 1)),))
-    (e0,) = call(energy_kernel, scalars[:1] + late(metal, coeff, ff, mf), [(ONE, 0)])
+    e0, source_here = call(
+        energy_kernel,
+        scalars[:1] + plain(metal_here, coeff_here, ff_here, mf_here) + [(source, Into(1, WHOLE))],
+        [(ONE, 0), (FLUID, 0)],
+    )
     b, q, blocks = call(
         inner_kernel,
-        scalars[1:] + [(a0, SIX), (source, SIX)] + late(ps) + plain(e0),
+        scalars[1:] + plain(a_here, source_here, ps_here, e0),
         [(FLUID, 6), (FLUID, 6), ((8, 6, NV, ROWS, CHUNK), -1)],
         scratch=[pltpu.VMEM((6, NV, ROWS, SPAN), F32), pltpu.SemaphoreType.DMA((48,))],
     )
     a_turned = turn(blocks)
     q, b, bup, bdown, q4, metal = call(
         first_kernel,
-        scalars + [last_variable] + plain(b, q) + late(ps) + plain(up, down) + late(coeff, ff, metal, cond),
+        scalars + [last_variable] + plain(b, q, ps, up, down, coeff, ff, metal, cond),
         [(BLOCKS, 7), (FLUID, 6), (EDGES, 1), (EDGES, 1), (ONE, 1), (METAL, 1)],
         flops=LONG,
     )
     q_turned = turn(q)
     bup, bdown = exchange(bup, bdown)
-    (g,) = call(derive_kernel, plain(kron, a_turned) + late(ps), [((NT * ROWS, NV * CHUNK), 0)])
+    (g,) = call(derive_kernel, plain(kron, a_turned, ps), [((NT * ROWS, NV * CHUNK), 0)])
     c, hc = call(
         middle_kernel,
         scalars + [(b, SIX), (source, SIX)] + late(ps) + plain(bup, bdown) + [last_variable] + late(q4)
@@ -653,13 +672,13 @@
     )
     v, metal, mup, mdown, e1 = call(
         second_kernel,
-        scalars[:1] + plain(q_turned, g, kron) + late(ps, metal, coeff, ff, mf) + plain(hc),
+        scalars[:1] + plain(q_turned, g, kron, ps, metal, coeff, ff, mf, hc),
         [(BLOCKS, 3), (METAL, 1), ((CH, MSPAN), 1), ((CH, MSPAN), 1), (ONE, 1)],
     )
     v = turn(v)
     mup, mdown = exchange(mup, mdown)
     out, metal = call(
-        last_kernel, held(v, c) + late(e1, metal) + plain(mup, mdown) + late(cond, mf), [(FLUID, 6), (METAL, 1)]
+        last_kernel, held(v, c, e1, metal) + plain(mup, mdown, cond, mf), [(FLUID, 6), (METAL, 1)]
     )
     return out, metal.reshape(2, NH, ROWS, MSPAN)
 

time: 86.4 us -> 82.6 us (0.956)
  Pallas kernels: 29.8 us -> 24.3 us
  local copies, waits for them, and re-layouts: 2.15 us -> 5.06 us
  waiting for transfers between devices: 30.3 us -> 29 us
    pallas_call x8, Pallas kernels: 29.8 us -> 24.3 us  [call(): pl.pallas_call(kernel, out_shape=[pltpu.HBM(dims, F32) if n else jax.Shap...]
    unnamed x22 -> x46, local copies, waits for them, and re-layouts: 2.15 us -> 5.06 us
    ppermute x3, waiting for transfers between devices: 4.33 us -> 2.22 us  [exchange(): lax.ppermute(up, 'space', forward)]
  transfers between devices with their start and end apart: 9 -> 9, of which waited for: 4 -> 4; matrix products, arithmetic and copies ran while one was open for 0% -> 0% of each run, Pallas kernels for 24% -> 21%
where the time goes in v7:
time: 82.6 us; the launch traced here: 82.1 us
  waiting for transfers between devices  29 us (35%)
  Pallas kernels  24.3 us (29%)
  starting transfers between devices  22.6 us (27%)
  local copies, waits for them, and re-layouts  5.06 us (6%)
  between operations  1.15 us (1%)
    all_to_all x3, waiting for transfers between devices, turn(): return lax.all_to_all(x, 'inst', 0, 0, tiled=True)  26.8 us
    pallas_call x8, Pallas kernels, call(): pl.pallas_call(kernel, out_shape=[pltpu.HBM(dims, F32) if n else jax.Shap...  24.3 us
    all_to_all x3, starting transfers between devices, turn(): return lax.all_to_all(x, 'inst', 0, 0, tiled=True)  12.6 us
    ppermute x3, starting transfers between devices, exchange(): lax.ppermute(down, 'space', back)  9.33 us
    unnamed x46, local copies, waits for them, and re-layouts  5.06 us
    ppermute x3, waiting for transfers between devices, exchange(): lax.ppermute(up, 'space', forward)  2.22 us
  transfers between devices with their start and end apart: 9, of which 4 were waited for; matrix products, arithmetic and copies ran while one was open for 0% of the time, Pallas kernels for 21%

profile of v7, /device:TPU:112, one launch (start us, length us, event | category | flops | bytes accessed | tf_op | source)
XLA Modules:
  0.0 82.1 jit_solution(13025727657599285357)
XLA Ops:
  0.7 2.3 %shard_map.131 = (f32[17,8,512]{2,1,0:T(8,128)}, f32[17,8,512]{2,1,0:T(8,128)}, f32[6,5,8,1024]{3,2,1,0:T(8,128)S(1)}, f32[8,1024]{1,0:T(8,128)S(1)}, f32[8,8,51...) custom-call(f32[6,5,8,1024]{3,2,1,0:T(8,128)} %refs_8_.1, ...), custom_call_target="tpu_custom_call" | custom-call | flops 1048576 | bytes 1048576 | tf_op jit(solution)/shard_map/pallas_call | solution.py:171
  3.1 3.2 %collective-permute-start.1 = (f32[17,8,512]{2,1,0:T(8,128)}, f32[17,8,512]{2,1,0:T(8,128)S(1)}, u32[]{:S(2)}, u32[]{:S(2)}) collective-permute-start(f32[17,8,512]{2,1,0:T(8,128)} %get-tuple-element.41), channel_id=1, source_target_pairs={{1,0},{2,1},{3,2},{4,3},{5,4},{6,5},{7,6},{8,7},{9,8},{10,9},{11,1... | collective-permute-start | bytes 835592 | tf_op jit(solution)/shard_map/ppermute | solution.py:600
  6.3 2.4 %shard_map.132 = (f32[6,8,1024]{2,1,0:T(8,128)S(1)}, f32[6,5,8,1024]{3,2,1,0:T(8,128)S(1)}) custom-call(f32[1536]{0:T(1024)S(1)} %copy-done.10, f32[8,8,512]{2,1,0:T(8,128)S(1)} %get-tuple-element.31.refs_1_, f32[1,512]{1,0:T(1,128)S(1)} %get-tuple-element.32.refs_2_, s32[1,512]{1,0:T(1,128)S(1)} %get-tuple-element.33.refs_3_, ...), custom_call_target="tpu_custom_call" | custom-call | flops 1048576 | bytes 1048576 | tf_op jit(solution)/shard_map/pallas_call | solution.py:171
  8.7 5.3 %shard_map.133 = (f32[6,5,8,1024]{3,2,1,0:T(8,128)}, f32[6,5,8,1024]{3,2,1,0:T(8,128)}, f32[8,6,5,8,128]{4,3,2,1,0:T(8,128)}) custom-call(f32[5,5]{1,0:T(8,128)S(1)} %copy-done.15, f32[5,5]{1,0:T(8,128)S(1)} %copy-done.16, f32[6,5,8,1024]{3,2,1,0:T(8,128)S(1)} %get-tuple-element.30.refs_2_, f32[6,5,8,1024]{3,2,1,0:T(8,128)S(1)} %get-tuple-element.35.refs_3_, ...), custom_call_target="tpu_custom_call" | custom-call | flops 1048576 | bytes 1048576 | tf_op jit(solution)/shard_map/pallas_call | solution.py:171
  14.1 5.2 %all-to-all-start.1 = ((f32[8,6,5,8,128]{4,3,2,1,0:T(8,128)}), f32[8,6,5,8,128]{4,3,2,1,0:T(8,128)S(1)}, u32[]{:S(2)}, u32[]{:S(2)}) async-start(f32[8,6,5,8,128]{4,3,2,1,0:T(8,128)} %get-tuple-element.43), calls=%async_computation.1 | async-start | bytes 1966080 | tf_op jit(solution)/shard_map/all_to_all | solution.py:604
  19.3 1.2 %copy-done.18 = f32[6,5,8,1024]{3,2,1,0:T(8,128)S(1)} copy-done((f32[6,5,8,1024]{3,2,1,0:T(8,128)S(1)}, f32[6,5,8,1024]{3,2,1,0:T(8,128)}, u32[]{:S(2)}) %copy-start.18) | copy-done | bytes 983064
  20.5 4.1 %shard_map.134 = (f32[8,34,8,128]{3,2,1,0:T(8,128)}, f32[6,5,8,1024]{3,2,1,0:T(8,128)}, f32[17,8,512]{2,1,0:T(8,128)}, f32[17,8,512]{2,1,0:T(8,128)}, f32[6,8,1024]{2,1,0:T(8,128)}, /*index=5*/f32[8,8,512]{2,1,0:T(8,128)}) custom-call(f32[1536]{0:T(1024)S(1)} %copy-done.10, f32[5,5]{1,0:T(8,128)S(1)} %copy-done.15, f32[5,5]{1,0:T(8,128)S(1)} %copy-done.16, ...), custom_call_target="tpu_custom_call" | custom-call | flops 68719476736 | bytes 1048576 | tf_op jit(solution)/shard_map/pallas_call | solution.py:171
  24.6 0.5 collective-permute-start.2
  25.0 2.9 %collective-permute-start.3 = (f32[17,8,512]{2,1,0:T(8,128)}, f32[17,8,512]{2,1,0:T(8,128)}, u32[]{:S(2)}, u32[]{:S(2)}) collective-permute-start(f32[17,8,512]{2,1,0:T(8,128)} %get-tuple-element.47), channel_id=1, source_target_pairs={{1,0},{2,1},{3,2},{4,3},{5,4},{6,5},{7,6},{8,7},{9,8},{10,9},{11,1... | collective-permute-start | bytes 835592 | tf_op jit(solution)/shard_map/ppermute | solution.py:600
  27.9 9.0 %all-to-all-done.1.refs_1_ = f32[8,6,5,8,128]{4,3,2,1,0:T(8,128)S(1)} async-done(((f32[8,6,5,8,128]{4,3,2,1,0:T(8,128)}), f32[8,6,5,8,128]{4,3,2,1,0:T(8,128)S(1)}, u32[]{:S(2)}, u32[]{:S(2)}) %all-to-all-start.1) | async-done | bytes 983072 | tf_op jit(solution)/shard_map/all_to_all | solution.py:604
  36.9 3.7 %all-to-all-start = ((f32[8,34,8,128]{3,2,1,0:T(8,128)}), f32[8,34,8,128]{3,2,1,0:T(8,128)S(1)}, u32[]{:S(2)}, u32[]{:S(2)}) async-start(f32[8,34,8,128]{3,2,1,0:T(8,128)} %get-tuple-element.42), calls=%async_computation | async-start | bytes 2228224 | tf_op jit(solution)/shard_map/all_to_all | solution.py:604
  40.7 1.2 %copy-done = bf16[384,1152]{1,0:T(8,128)(2,1)S(1)} copy-done((bf16[384,1152]{1,0:T(8,128)(2,1)S(1)}, bf16[384,1152]{1,0:T(8,128)(2,1)}, u32[]{:S(2)}) %copy-start) | copy-done | bytes 884760
  41.9 0.9 %shard_map.135.refs_10_.refs_2_ = f32[384,640]{1,0:T(8,128)S(1)} custom-call(bf16[384,1152]{1,0:T(8,128)(2,1)S(1)} %copy-done, f32[8,6,5,8,128]{4,3,2,1,0:T(8,128)S(1)} %all-to-all-done.1.refs_1_, f32[8,1024]{1,0:T(8,128)S(1)} %copy-done.4), custom_call_target="tpu_custom_call" | custom-call | flops 1048576 | bytes 1048576 | tf_op jit(solution)/shard_map/pallas_call | solution.py:171
  42.8 0.7 copy-done.19
  43.5 1.0 %copy-done.20 = f32[17,8,512]{2,1,0:T(8,128)S(1)} copy-done((f32[17,8,512]{2,1,0:T(8,128)S(1)}, f32[17,8,512]{2,1,0:T(8,128)}, u32[]{:S(2)}) %copy-start.20) | copy-done | bytes 278552
  44.5 4.5 %shard_map.136 = (f32[6,5,8,1024]{3,2,1,0:T(8,128)S(1)}, f32[8,8,1024]{2,1,0:T(8,128)S(1)}) custom-call(f32[1536]{0:T(1024)S(1)} %copy-done.10, f32[5,5]{1,0:T(8,128)S(1)} %copy-done.15, f32[5,5]{1,0:T(8,128)S(1)} %copy-done.16, f32[6,5,8,1024]{3,2,1,0:T(8,128)} %get-tuple-element.45.refs_3_, f32[6,5,8,1024]{3,2,1,0:T(8,128)} %refs_4_.2, f32[8,1024]{1,0:T(8,128)} %refs_4_.3, ...), custom_call_target="tpu_custom_call" | custom-call | flops 68719476736 | bytes 1048576 | tf_op jit(solution)/shard_map/pallas_call | solution.py:171
  49.0 0.9 %copy-done.2 = f32[6,5,8,1024]{3,2,1,0:T(8,128)} copy-done((f32[6,5,8,1024]{3,2,1,0:T(8,128)}, f32[6,5,8,1024]{3,2,1,0:T(8,128)S(1)}, u32[]{:S(2)}) %copy-start.2) | copy-done | bytes 983064
  49.9 6.9 %all-to-all-done.refs_1_ = f32[8,34,8,128]{3,2,1,0:T(8,128)S(1)} async-done(((f32[8,34,8,128]{3,2,1,0:T(8,128)}), f32[8,34,8,128]{3,2,1,0:T(8,128)S(1)}, u32[]{:S(2)}, u32[]{:S(2)}) %all-to-all-start) | async-done | bytes 1114144 | tf_op jit(solution)/shard_map/all_to_all | solution.py:604
  56.8 3.5 %shard_map.137 = (f32[8,34,8,128]{3,2,1,0:T(8,128)}, f32[8,8,512]{2,1,0:T(8,128)}, f32[8,512]{1,0:T(8,128)}, f32[8,512]{1,0:T(8,128)}, f32[6,8,1024]{2,1,0:T(8,128)}) custom-call(f32[1536]{0:T(1024)S(1)} %copy-done.10, f32[8,34,8,128]{3,2,1,0:T(8,128)S(1)} %all-to-all-done.refs_1_, f32[384,640]{1,0:T(8,128)S(1)} %shard_map.135.refs_10_.refs_2_, ...), custom_call_target="tpu_custom_call" | custom-call | flops 1048576 | bytes 1048576 | tf_op jit(solution)/shard_map/pallas_call | solution.py:171
  60.4 3.7 %all-to-all-start.2 = ((f32[8,34,8,128]{3,2,1,0:T(8,128)}), f32[8,34,8,128]{3,2,1,0:T(8,128)S(1)}, u32[]{:S(2)}, u32[]{:S(2)}) async-start(f32[8,34,8,128]{3,2,1,0:T(8,128)} %get-tuple-element.50), calls=%async_computation.2 | async-start | bytes 2228224 | tf_op jit(solution)/shard_map/all_to_all | solution.py:604
  64.2 3.2 %collective-permute-start.5 = (f32[8,512]{1,0:T(8,128)S(1)}, f32[8,512]{1,0:T(8,128)S(1)}, u32[]{:S(2)}, u32[]{:S(2)}) collective-permute-start(f32[8,512]{1,0:T(8,128)S(1)} %copy-done.21), channel_id=1, source_target_pairs={{1,0},{2,1},{3,2},{4,3},{5,4},{6,5},{7,6},{8,7},{9,8},{10,9},{11,1... | collective-permute-start | bytes 49160 | tf_op jit(solution)/shard_map/ppermute | solution.py:600
  67.5 2.2 %collective-permute-done.4.refs_4_ = f32[8,512]{1,0:T(8,128)S(1)} collective-permute-done((f32[8,512]{1,0:T(8,128)S(1)}, f32[8,512]{1,0:T(8,128)S(1)}, u32[]{:S(2)}, u32[]{:S(2)}) %collective-permute-start.4) | collective-permute-done | bytes 16416 | tf_op jit(solution)/shard_map/ppermute | solution.py:600
  69.7 10.9 %all-to-all-done.2.refs_0_ = f32[8,34,8,128]{3,2,1,0:T(8,128)S(1)} async-done(((f32[8,34,8,128]{3,2,1,0:T(8,128)}), f32[8,34,8,128]{3,2,1,0:T(8,128)S(1)}, u32[]{:S(2)}, u32[]{:S(2)}) %all-to-all-start.2) | async-done | bytes 1114144 | tf_op jit(solution)/shard_map/all_to_all | solution.py:604
  80.6 1.3 %shard_map.138 = (f32[6,5,8,1024]{3,2,1,0:T(8,128)}, f32[8,8,512]{2,1,0:T(8,128)}) custom-call(f32[8,34,8,128]{3,2,1,0:T(8,128)S(1)} %all-to-all-done.2.refs_0_, f32[6,5,8,1024]{3,2,1,0:T(8,128)S(1)} %copy-done.3, f32[6,8,1024]{2,1,0:T(8,128)S(1)} %copy-done.6, f32[8,8,512]{2,1,0:T(8,128)S(1)} %copy-done.9, f32[8,512]{1,0:T(8,128)S(1)} %collective-permute-done.4.refs_4_, ...), custom_call_target="tpu_custom_call" | custom-call | flops 1048576 | bytes 1048576 | tf_op jit(solution)/shard_map/pallas_call | solution.py:171
  (48 shorter events, 0.3 us)
Async XLA Ops:
  0.6 5.7 %copy-start.10 = (f32[1536]{0:T(1024)S(1)}, f32[1536]{0:T(1024)}, u32[]{:S(2)}) copy-start(f32[1536]{0:T(1024)} %constant.5.clone.refs_0_) | copy-start | bytes 18436
  0.6 8.0 %copy-start.15 = (f32[5,5]{1,0:T(8,128)S(1)}, f32[5,5]{1,0:T(8,128)}, u32[]{:S(2)}) copy-start(f32[5,5]{1,0:T(8,128)} %refs_1_.7) | copy-start | bytes 304
  0.7 8.0 %copy-start.16 = (f32[5,5]{1,0:T(8,128)S(1)}, f32[5,5]{1,0:T(8,128)}, u32[]{:S(2)}) copy-start(f32[5,5]{1,0:T(8,128)} %refs_2_.5) | copy-start | bytes 304
  3.0 16.3 %collective-permute-start = (f32[17,8,512]{2,1,0:T(8,128)}, f32[17,8,512]{2,1,0:T(8,128)S(1)}, u32[]{:S(2)}, u32[]{:S(2)}) collective-permute-start(f32[17,8,512]{2,1,0:T(8,128)} %get-tuple-element.40), channel_id=1, source_target_pairs={{0,1},{1,2},{2,3},{3,4},{4,5},{5,6},{6,7},{7,8},{8,9},{9,10},{10,1... | collective-permute-start | bytes 835592 | tf_op jit(solution)/shard_map/ppermute | solution.py:600
  3.1 16.2 %collective-permute-start.1 = (f32[17,8,512]{2,1,0:T(8,128)}, f32[17,8,512]{2,1,0:T(8,128)S(1)}, u32[]{:S(2)}, u32[]{:S(2)}) collective-permute-start(f32[17,8,512]{2,1,0:T(8,128)} %get-tuple-element.41), channel_id=1, source_target_pairs={{1,0},{2,1},{3,2},{4,3},{5,4},{6,5},{7,6},{8,7},{9,8},{10,9},{11,1... | collective-permute-start | bytes 835592 | tf_op jit(solution)/shard_map/ppermute | solution.py:600
  14.0 5.3 %copy-start.4 = (f32[8,1024]{1,0:T(8,128)S(1)}, f32[8,1024]{1,0:T(8,128)}, u32[]{:S(2)}) copy-start(f32[8,1024]{1,0:T(8,128)} %refs_4_.3) | copy-start | bytes 98308
  14.0 5.2 %copy-start.7 = (f32[2,4,8,512]{3,2,1,0:T(8,128)S(1)}, f32[2,4,8,512]{3,2,1,0:T(8,128)}, u32[]{:S(2)}) copy-start(f32[2,4,8,512]{3,2,1,0:T(8,128)} %param.17) | copy-start | bytes 393220
  14.0 5.2 %copy-start.12 = (f32[8,512]{1,0:T(8,128)S(1)}, f32[8,512]{1,0:T(8,128)}, u32[]{:S(2)}) copy-start(f32[8,512]{1,0:T(8,128)} %refs_6_.3) | copy-start | bytes 49156
  14.0 5.2 %copy-start.13 = (f32[512]{0:T(512)S(1)}, f32[512]{0:T(512)}, u32[]{:S(2)}) copy-start(f32[512]{0:T(512)} %param.19) | copy-start | bytes 6148
  14.0 5.2 %copy-start.14 = (s32[512]{0:T(512)S(1)}, s32[512]{0:T(512)}, u32[]{:S(2)}) copy-start(s32[512]{0:T(512)} %param.20) | copy-start | bytes 6148
  14.1 22.9 %all-to-all-start.1 = ((f32[8,6,5,8,128]{4,3,2,1,0:T(8,128)}), f32[8,6,5,8,128]{4,3,2,1,0:T(8,128)S(1)}, u32[]{:S(2)}, u32[]{:S(2)}) async-start(f32[8,6,5,8,128]{4,3,2,1,0:T(8,128)} %get-tuple-element.43), calls=%async_computation.1 | async-start | bytes 1966080 | tf_op jit(solution)/shard_map/all_to_all | solution.py:604
  24.6 18.2 %collective-permute-start.2 = (f32[17,8,512]{2,1,0:T(8,128)}, f32[17,8,512]{2,1,0:T(8,128)S(1)}, u32[]{:S(2)}, u32[]{:S(2)}) collective-permute-start(f32[17,8,512]{2,1,0:T(8,128)} %get-tuple-element.46), channel_id=1, source_target_pairs={{0,1},{1,2},{2,3},{3,4},{4,5},{5,6},{6,7},{7,8},{8,9},{9,10},{10,1... | collective-permute-start | bytes 835592 | tf_op jit(solution)/shard_map/ppermute | solution.py:600
  25.0 18.5 %collective-permute-start.3 = (f32[17,8,512]{2,1,0:T(8,128)}, f32[17,8,512]{2,1,0:T(8,128)}, u32[]{:S(2)}, u32[]{:S(2)}) collective-permute-start(f32[17,8,512]{2,1,0:T(8,128)} %get-tuple-element.47), channel_id=1, source_target_pairs={{1,0},{2,1},{3,2},{4,3},{5,4},{6,5},{7,6},{8,7},{9,8},{10,9},{11,1... | collective-permute-start | bytes 835592 | tf_op jit(solution)/shard_map/ppermute | solution.py:600
  36.9 19.9 %all-to-all-start = ((f32[8,34,8,128]{3,2,1,0:T(8,128)}), f32[8,34,8,128]{3,2,1,0:T(8,128)S(1)}, u32[]{:S(2)}, u32[]{:S(2)}) async-start(f32[8,34,8,128]{3,2,1,0:T(8,128)} %get-tuple-element.42), calls=%async_computation | async-start | bytes 2228224 | tf_op jit(solution)/shard_map/all_to_all | solution.py:604
  44.5 12.3 %copy-start.1 = (bf16[384,1152]{1,0:T(8,128)(2,1)S(1)}, bf16[384,1152]{1,0:T(8,128)(2,1)}, u32[]{:S(2)}) copy-start(bf16[384,1152]{1,0:T(8,128)(2,1)} %constant.4.clone.refs_0_.refs_3_) | copy-start | bytes 2654212
  44.5 12.3 %copy-start.5 = (f32[8,1024]{1,0:T(8,128)S(1)}, f32[8,1024]{1,0:T(8,128)}, u32[]{:S(2)}) copy-start(f32[8,1024]{1,0:T(8,128)} %refs_4_.3) | copy-start | bytes 98308
  44.5 12.3 %copy-start.8 = (f32[8,8,512]{2,1,0:T(8,128)S(1)}, f32[8,8,512]{2,1,0:T(8,128)}, u32[]{:S(2)}) copy-start(f32[8,8,512]{2,1,0:T(8,128)} %get-tuple-element.44.refs_5_) | copy-start | bytes 393220
  44.5 12.3 %copy-start.11 = (s32[512]{0:T(512)S(1)}, s32[512]{0:T(512)}, u32[]{:S(2)}) copy-start(s32[512]{0:T(512)} %param.21) | copy-start | bytes 6148
  60.4 20.2 %copy-start.3 = (f32[6,5,8,1024]{3,2,1,0:T(8,128)S(1)}, f32[6,5,8,1024]{3,2,1,0:T(8,128)}, u32[]{:S(2)}) copy-start(f32[6,5,8,1024]{3,2,1,0:T(8,128)} %copy-done.2) | copy-start | bytes 2949124
  60.4 20.2 %copy-start.6 = (f32[6,8,1024]{2,1,0:T(8,128)S(1)}, f32[6,8,1024]{2,1,0:T(8,128)}, u32[]{:S(2)}) copy-start(f32[6,8,1024]{2,1,0:T(8,128)} %get-tuple-element.52.refs_2_) | copy-start | bytes 589828
  60.4 20.2 %copy-start.9 = (f32[8,8,512]{2,1,0:T(8,128)S(1)}, f32[8,8,512]{2,1,0:T(8,128)}, u32[]{:S(2)}) copy-start(f32[8,8,512]{2,1,0:T(8,128)} %get-tuple-element.53.refs_3_) | copy-start | bytes 393220
  60.4 20.2 %all-to-all-start.2 = ((f32[8,34,8,128]{3,2,1,0:T(8,128)}), f32[8,34,8,128]{3,2,1,0:T(8,128)S(1)}, u32[]{:S(2)}, u32[]{:S(2)}) async-start(f32[8,34,8,128]{3,2,1,0:T(8,128)} %get-tuple-element.50), calls=%async_computation.2 | async-start | bytes 2228224 | tf_op jit(solution)/shard_map/all_to_all | solution.py:604
  64.1 5.5 %collective-permute-start.4 = (f32[8,512]{1,0:T(8,128)S(1)}, f32[8,512]{1,0:T(8,128)S(1)}, u32[]{:S(2)}, u32[]{:S(2)}) collective-permute-start(f32[8,512]{1,0:T(8,128)S(1)} %copy-done.22), channel_id=1, source_target_pairs={{0,1},{1,2},{2,3},{3,4},{4,5},{5,6},{6,7},{7,8},{8,9},{9,10},{10,1... | collective-permute-start | bytes 49160 | tf_op jit(solution)/shard_map/ppermute | solution.py:600
  64.2 5.4 %collective-permute-start.5 = (f32[8,512]{1,0:T(8,128)S(1)}, f32[8,512]{1,0:T(8,128)S(1)}, u32[]{:S(2)}, u32[]{:S(2)}) collective-permute-start(f32[8,512]{1,0:T(8,128)S(1)} %copy-done.21), channel_id=1, source_target_pairs={{1,0},{2,1},{3,2},{4,3},{5,4},{6,5},{7,6},{8,7},{9,8},{10,9},{11,1... | collective-permute-start | bytes 49160 | tf_op jit(solution)/shard_map/ppermute | solution.py:600
  (8 other events, 17.9 us)

commit v8 on v7

--- a/solution.py
+++ b/solution.py
@@ -121,7 +121,7 @@
 
 
 def call(body, operands, results, scratch=(), flops=1 << 20, moved=1 << 20):
-    space = {"smem": pltpu.SMEM, "vmem": pltpu.VMEM, "held": pltpu.VMEM}
+    space = {"idle": pltpu.HBM, "smem": pltpu.SMEM, "vmem": pltpu.VMEM, "held": pltpu.VMEM}
     modes = [mode for _, mode in operands]
     here = [isinstance(mode, str) for mode in modes]
     in_specs = [
@@ -177,7 +177,10 @@
         compiler_params=pltpu.CompilerParams(vmem_limit_bytes=24 << 20),
         cost_estimate=pl.CostEstimate(flops=flops, bytes_accessed=moved, transcendentals=0),
     )(
-        *[a if h else pltpu.with_memory_space_constraint(a, pltpu.HBM) for (a, _), h in zip(operands, here)]
+        *[
+            a if h and m != "idle" else pltpu.with_memory_space_constraint(a, pltpu.HBM)
+            for (a, m), h in zip(operands, here)
+        ]
     )
 
 
@@ -283,7 +286,7 @@
     pack_tile([get(4), get(5), extra, extra], 7, up_ref, down_ref)
 
 
-def prepare_kernel(a, ps, m_in, fc, ff, mf, up, down, *copies):
+def prepare_kernel(a, ps, m_in, up, down, a_copy, ps_copy):
     for t in range(6):
         ref = a.piece(t)
         pack_tile([ref[t, v] for v in range(4)], t, up.buffer, down.buffer)
@@ -295,7 +298,7 @@
         x.put(pl.ds(12, 5))
 
 
-def energy_kernel(tab_ref, m_ref, fc_ref, ff_ref, mf_ref, source, e, copied):
+def energy_kernel(tab_ref, m_ref, fc_ref, ff_ref, mf_ref, after, e):
     first = lax.axis_index("inst") * 6
     m_hot, m_row = metal_hots(mf_ref)
     f_hot, f_row = fluid_hots(ff_ref)
@@ -321,14 +324,17 @@
     return out
 
 
-def inner_kernel(jx_ref, jz_ref, a_ref, s_ref, ps_ref, e_ref, b, q, blocks, parts, sems):
+def inner_kernel(jx_ref, jz_ref, a_ref, s_ref, ps_ref, b, q, blocks, parts, sems):
     step = ps_ref[...]
-    copies = []
+    copies = [
+        pltpu.make_async_copy(
+            a_ref.at[:, :, :, pl.ds(i * CHUNK, CHUNK)], blocks.at[i], sems.at[i]
+        )
+        for i in range(8)
+    ]
+    for copy in copies:
+        copy.start()
     for t in range(6):
-        for i in range(8):
-            source = a_ref.at[t, :, :, pl.ds(i * CHUNK, CHUNK)]
-            copies.append(pltpu.make_async_copy(source, blocks.at[i, t], sems.at[8 * t + i]))
-            copies[-1].start()
         for v in range(NV):
             a = a_ref[t, v]
             dx, dz, rest = stencil_parts(a, 0.0, 0.0)
@@ -345,8 +351,6 @@
                 a = a_ref[t, u, :, cut]
                 space = convect(jx_ref, jz_ref, dx, dz, parts[2, u, :, cut], u)
                 source = s_ref[t, u, :, cut] + space
-                if u == NV - 1:
-                    source = source + e_ref[t, :, cut]
                 inner = a + ps_ref[:, cut] * source
                 b.buffer[t, u, :, cut] = inner
                 q.buffer[t, u, :, cut] = a + inner + convect(jx_ref, jz_ref, px, pz, parts[5, u, :, cut], u)
@@ -369,7 +373,7 @@
 
 
 def first_kernel(
-    tab_ref, jx_ref, jz_ref, a_ref, bi_ref, qi_ref, ps_ref, up_ref, down_ref, fc_ref, ff_ref, m_ref, cond_ref,
+    tab_ref, jx_ref, jz_ref, a_ref, bi_ref, qi_ref, e_ref, ps_ref, up_ref, down_ref, fc_ref, ff_ref, m_ref, cond_ref,
     q, b_out, bup, bdown, q4, m_out,
 ):
     first = lax.axis_index("inst") * 6
@@ -396,7 +400,10 @@
                     total += jx_ref[u, v] * edges[v][0]
                 one = sign * total + (4.0 * damping_fourth) * edges[u][0]
                 two = damping_fourth * edges[u][1]
-                change = here * (one - two)
+                change = one - two
+                if u == NV - 1:
+                    change = change + e_ref[t, :, wide]
+                change = here * change
                 b_ref[t, u, :, wide] = bi_ref[t, u, :, wide] + change
                 value = qi_ref[t, u, :, wide] + change + (step_one * one - step_two * two)
                 for i in range(4):
@@ -632,32 +639,31 @@
     tab = jnp.asarray(FLAT)
     coeff, ff, mf = (x.reshape(1, NF) for x in (coeff, ff, mf))
     metal = metal.reshape(METAL)
-    small = [(x, Into(3 + i, WHOLE)) for i, x in enumerate((ps, metal, coeff, ff, mf))]
-    up, down, a_here, ps_here, metal_here, coeff_here, ff_here, mf_here = call(
+    up, down, a_here, ps_here = call(
         prepare_kernel,
-        [(a0, Into(2, SIX))] + small,
-        [(EDGES, 7), (EDGES, 7), (FLUID, 0), ((ROWS, SPAN), 0), (METAL, 0)] + [((1, NF), 0)] * 3,
+        [(a0, Into(2, SIX)), (ps, Into(3, WHOLE))] + late(metal),
+        [(EDGES, 7), (EDGES, 7), (FLUID, 0), ((ROWS, SPAN), 0)],
     )
     up, down = exchange(up, down)
     scalars = [(tab, "smem"), (jx, "smem"), (jz, "smem")]
     last_variable = (a0, ((slice(None), pl.ds(NV - 1, 1)),))
-    e0, source_here = call(
-        energy_kernel,
-        scalars[:1] + plain(metal_here, coeff_here, ff_here, mf_here) + [(source, Into(1, WHOLE))],
-        [(ONE, 0), (FLUID, 0)],
-    )
     b, q, blocks = call(
         inner_kernel,
-        scalars[1:] + plain(a_here, source_here, ps_here, e0),
+        scalars[1:] + plain(a_here, source, ps_here),
         [(FLUID, 6), (FLUID, 6), ((8, 6, NV, ROWS, CHUNK), -1)],
-        scratch=[pltpu.VMEM((6, NV, ROWS, SPAN), F32), pltpu.SemaphoreType.DMA((48,))],
+        scratch=[pltpu.VMEM((6, NV, ROWS, SPAN), F32), pltpu.SemaphoreType.DMA((8,))],
+    )
+    (e0,) = call(
+        energy_kernel,
+        scalars[:1] + plain(metal, coeff, ff, mf) + [(blocks, "idle")],
+        [(ONE, 0)],
+        flops=LONG,
     )
     a_turned = turn(blocks)
     q, b, bup, bdown, q4, metal = call(
         first_kernel,
-        scalars + [last_variable] + plain(b, q, ps, up, down, coeff, ff, metal, cond),
+        scalars + [last_variable] + plain(b, q, e0, ps, up, down, coeff, ff, metal, cond),
         [(BLOCKS, 7), (FLUID, 6), (EDGES, 1), (EDGES, 1), (ONE, 1), (METAL, 1)],
-        flops=LONG,
     )
     q_turned = turn(q)
     bup, bdown = exchange(bup, bdown)

time: 82.6 us -> 79.8 us (0.966)
  Pallas kernels: 24.3 us -> 23 us
  local copies, waits for them, and re-layouts: 5.06 us -> 3.94 us
    pallas_call x8, Pallas kernels: 24.3 us -> 23 us  [call(): pl.pallas_call(kernel, out_shape=[pltpu.HBM(dims, F32) if n else jax.Shap...]
    unnamed x46 -> x48, local copies, waits for them, and re-layouts: 5.06 us -> 3.94 us
  transfers between devices with their start and end apart: 9 -> 9, of which waited for: 4 -> 4; matrix products, arithmetic and copies ran while one was open for 0% -> 0% of each run, Pallas kernels for 21% -> 20%
where the time goes in v8:
time: 79.8 us; the launch traced here: 79.3 us
  waiting for transfers between devices  28.7 us (36%)
  Pallas kernels  23 us (29%)
  starting transfers between devices  22.6 us (28%)
  local copies, waits for them, and re-layouts  3.94 us (5%)
  between operations  1.14 us (1%)
    all_to_all x3, waiting for transfers between devices, turn(): return lax.all_to_all(x, 'inst', 0, 0, tiled=True)  27 us
    pallas_call x8, Pallas kernels, call(): pl.pallas_call(kernel, out_shape=[pltpu.HBM(dims, F32) if n else jax.Shap...  23 us
    all_to_all x3, starting transfers between devices, turn(): return lax.all_to_all(x, 'inst', 0, 0, tiled=True)  12.6 us
    ppermute x3, starting transfers between devices, exchange(): lax.ppermute(down, 'space', back)  9.32 us
    unnamed x48, local copies, waits for them, and re-layouts  3.94 us
    ppermute x3, waiting for transfers between devices, exchange(): lax.ppermute(up, 'space', forward)  1.67 us
  transfers between devices with their start and end apart: 9, of which 4 were waited for; matrix products, arithmetic and copies ran while one was open for 0% of the time, Pallas kernels for 20%

profile of v8, /device:TPU:112, one launch (start us, length us, event | category | flops | bytes accessed | tf_op | source)
XLA Modules:
  0.0 79.3 jit_solution(419142587390232841)
XLA Ops:
  0.7 2.3 %shard_map.131 = (f32[17,8,512]{2,1,0:T(8,128)}, f32[17,8,512]{2,1,0:T(8,128)}, f32[6,5,8,1024]{3,2,1,0:T(8,128)S(1)}, f32[8,1024]{1,0:T(8,128)S(1)}) custom-call(f32[6,5,8,1024]{3,2,1,0:T(8,128)} %refs_8_.1, f32[8,1024]{1,0:T(8,128)} %refs_4_.3, f32[8,8,512]{2,1,0:T(8,128)} %bitcast.5), custom_call_target="tpu_custom_call" | custom-call | flops 1048576 | bytes 1048576 | tf_op jit(solution)/shard_map/pallas_call | solution.py:171
  3.1 3.2 %collective-permute-start.1 = (f32[17,8,512]{2,1,0:T(8,128)}, f32[17,8,512]{2,1,0:T(8,128)S(1)}, u32[]{:S(2)}, u32[]{:S(2)}) collective-permute-start(f32[17,8,512]{2,1,0:T(8,128)} %get-tuple-element.30), channel_id=1, source_target_pairs={{1,0},{2,1},{3,2},{4,3},{5,4},{6,5},{7,6},{8,7},{9,8},{10,9},{11,1... | collective-permute-start | bytes 835592 | tf_op jit(solution)/shard_map/ppermute | solution.py:607
  6.3 4.9 %shard_map.132 = (f32[6,5,8,1024]{3,2,1,0:T(8,128)}, f32[6,5,8,1024]{3,2,1,0:T(8,128)}, f32[8,6,5,8,128]{4,3,2,1,0:T(8,128)}) custom-call(f32[5,5]{1,0:T(8,128)S(1)} %copy-done.15, f32[5,5]{1,0:T(8,128)S(1)} %copy-done.16, f32[6,5,8,1024]{3,2,1,0:T(8,128)S(1)} %get-tuple-element.24.refs_2_, f32[6,5,8,1024]{3,2,1,0:T(8,128)S(1)} %copy-done.2, ...), custom_call_target="tpu_custom_call" | custom-call | flops 1048576 | bytes 1048576 | tf_op jit(solution)/shard_map/pallas_call | solution.py:171
  11.3 5.2 %all-to-all-start.1 = ((f32[8,6,5,8,128]{4,3,2,1,0:T(8,128)}), f32[8,6,5,8,128]{4,3,2,1,0:T(8,128)S(1)}, u32[]{:S(2)}, u32[]{:S(2)}) async-start(f32[8,6,5,8,128]{4,3,2,1,0:T(8,128)} %get-tuple-element.28.refs_5_), calls=%async_computation.1 | async-start | bytes 1966080 | tf_op jit(solution)/shard_map/all_to_all | solution.py:611
  16.5 1.4 %shard_map.133.refs_6_ = f32[6,8,1024]{2,1,0:T(8,128)S(1)} custom-call(f32[1536]{0:T(1024)S(1)} %copy-done.14, f32[8,8,512]{2,1,0:T(8,128)S(1)} %bitcast.6, f32[1,512]{1,0:T(1,128)S(1)} %bitcast.8, s32[1,512]{1,0:T(1,128)S(1)} %bitcast.11, s32[1,512]{1,0:T(1,128)S(1)} %bitcast.14, f32[8,6,5,8,128]{4,3,2,1,0:T(8,128)} %get-tuple-element.28.refs_5_), custom_call_target="tpu_custom_call" | custom-call | flops 68719476736 | bytes 1048576 | tf_op jit(solution)/shard_map/pallas_call | solution.py:171
  18.0 4.1 %shard_map.134 = (f32[8,34,8,128]{3,2,1,0:T(8,128)}, f32[6,5,8,1024]{3,2,1,0:T(8,128)}, f32[17,8,512]{2,1,0:T(8,128)}, f32[17,8,512]{2,1,0:T(8,128)}, f32[6,8,1024]{2,1,0:T(8,128)}, /*index=5*/f32[8,8,512]{2,1,0:T(8,128)}) custom-call(f32[1536]{0:T(1024)S(1)} %copy-done.14, f32[5,5]{1,0:T(8,128)S(1)} %copy-done.15, f32[5,5]{1,0:T(8,128)S(1)} %copy-done.16, ...), custom_call_target="tpu_custom_call" | custom-call | flops 1048576 | bytes 1048576 | tf_op jit(solution)/shard_map/pallas_call | solution.py:171
  22.1 0.5 collective-permute-start.2
  22.6 2.8 %collective-permute-start.3 = (f32[17,8,512]{2,1,0:T(8,128)}, f32[17,8,512]{2,1,0:T(8,128)}, u32[]{:S(2)}, u32[]{:S(2)}) collective-permute-start(f32[17,8,512]{2,1,0:T(8,128)} %get-tuple-element.35), channel_id=1, source_target_pairs={{1,0},{2,1},{3,2},{4,3},{5,4},{6,5},{7,6},{8,7},{9,8},{10,9},{11,1... | collective-permute-start | bytes 835592 | tf_op jit(solution)/shard_map/ppermute | solution.py:607
  25.5 8.7 %all-to-all-done.1.refs_1_ = f32[8,6,5,8,128]{4,3,2,1,0:T(8,128)S(1)} async-done(((f32[8,6,5,8,128]{4,3,2,1,0:T(8,128)}), f32[8,6,5,8,128]{4,3,2,1,0:T(8,128)S(1)}, u32[]{:S(2)}, u32[]{:S(2)}) %all-to-all-start.1) | async-done | bytes 983072 | tf_op jit(solution)/shard_map/all_to_all | solution.py:611
  34.2 3.7 %all-to-all-start = ((f32[8,34,8,128]{3,2,1,0:T(8,128)}), f32[8,34,8,128]{3,2,1,0:T(8,128)S(1)}, u32[]{:S(2)}, u32[]{:S(2)}) async-start(f32[8,34,8,128]{3,2,1,0:T(8,128)} %get-tuple-element.31), calls=%async_computation | async-start | bytes 2228224 | tf_op jit(solution)/shard_map/all_to_all | solution.py:611
  37.9 1.2 %copy-done = bf16[384,1152]{1,0:T(8,128)(2,1)S(1)} copy-done((bf16[384,1152]{1,0:T(8,128)(2,1)S(1)}, bf16[384,1152]{1,0:T(8,128)(2,1)}, u32[]{:S(2)}) %copy-start) | copy-done | bytes 884760
  39.1 0.9 %shard_map.135.refs_10_.refs_2_ = f32[384,640]{1,0:T(8,128)S(1)} custom-call(bf16[384,1152]{1,0:T(8,128)(2,1)S(1)} %copy-done, f32[8,6,5,8,128]{4,3,2,1,0:T(8,128)S(1)} %all-to-all-done.1.refs_1_, f32[8,1024]{1,0:T(8,128)S(1)} %copy-done.7), custom_call_target="tpu_custom_call" | custom-call | flops 1048576 | bytes 1048576 | tf_op jit(solution)/shard_map/pallas_call | solution.py:171
  40.0 0.7 copy-done.20
  40.8 1.0 %copy-done.21 = f32[17,8,512]{2,1,0:T(8,128)S(1)} copy-done((f32[17,8,512]{2,1,0:T(8,128)S(1)}, f32[17,8,512]{2,1,0:T(8,128)}, u32[]{:S(2)}) %copy-start.21) | copy-done | bytes 278552
  41.7 4.5 %shard_map.136 = (f32[6,5,8,1024]{3,2,1,0:T(8,128)S(1)}, f32[8,8,1024]{2,1,0:T(8,128)S(1)}) custom-call(f32[1536]{0:T(1024)S(1)} %copy-done.14, f32[5,5]{1,0:T(8,128)S(1)} %copy-done.15, f32[5,5]{1,0:T(8,128)S(1)} %copy-done.16, f32[6,5,8,1024]{3,2,1,0:T(8,128)} %get-tuple-element.33.refs_3_, f32[6,5,8,1024]{3,2,1,0:T(8,128)} %refs_4_.2, f32[8,1024]{1,0:T(8,128)} %refs_4_.3, ...), custom_call_target="tpu_custom_call" | custom-call | flops 68719476736 | bytes 1048576 | tf_op jit(solution)/shard_map/pallas_call | solution.py:171
  46.2 0.9 %copy-done.3 = f32[6,5,8,1024]{3,2,1,0:T(8,128)} copy-done((f32[6,5,8,1024]{3,2,1,0:T(8,128)}, f32[6,5,8,1024]{3,2,1,0:T(8,128)S(1)}, u32[]{:S(2)}) %copy-start.3) | copy-done | bytes 983064
  47.2 6.9 %all-to-all-done.refs_1_ = f32[8,34,8,128]{3,2,1,0:T(8,128)S(1)} async-done(((f32[8,34,8,128]{3,2,1,0:T(8,128)}), f32[8,34,8,128]{3,2,1,0:T(8,128)S(1)}, u32[]{:S(2)}, u32[]{:S(2)}) %all-to-all-start) | async-done | bytes 1114144 | tf_op jit(solution)/shard_map/all_to_all | solution.py:611
  54.1 3.5 %shard_map.137 = (f32[8,34,8,128]{3,2,1,0:T(8,128)}, f32[8,8,512]{2,1,0:T(8,128)}, f32[8,512]{1,0:T(8,128)}, f32[8,512]{1,0:T(8,128)}, f32[6,8,1024]{2,1,0:T(8,128)}) custom-call(f32[1536]{0:T(1024)S(1)} %copy-done.14, f32[8,34,8,128]{3,2,1,0:T(8,128)S(1)} %all-to-all-done.refs_1_, f32[384,640]{1,0:T(8,128)S(1)} %shard_map.135.refs_10_.refs_2_, ...), custom_call_target="tpu_custom_call" | custom-call | flops 1048576 | bytes 1048576 | tf_op jit(solution)/shard_map/pallas_call | solution.py:171
  57.7 3.7 %all-to-all-start.2 = ((f32[8,34,8,128]{3,2,1,0:T(8,128)}), f32[8,34,8,128]{3,2,1,0:T(8,128)S(1)}, u32[]{:S(2)}, u32[]{:S(2)}) async-start(f32[8,34,8,128]{3,2,1,0:T(8,128)} %get-tuple-element.38), calls=%async_computation.2 | async-start | bytes 2228224 | tf_op jit(solution)/shard_map/all_to_all | solution.py:611
  61.4 0.1 collective-permute-start.4
  61.5 3.2 %collective-permute-start.5 = (f32[8,512]{1,0:T(8,128)S(1)}, f32[8,512]{1,0:T(8,128)S(1)}, u32[]{:S(2)}, u32[]{:S(2)}) collective-permute-start(f32[8,512]{1,0:T(8,128)S(1)} %copy-done.22), channel_id=1, source_target_pairs={{1,0},{2,1},{3,2},{4,3},{5,4},{6,5},{7,6},{8,7},{9,8},{10,9},{11,1... | collective-permute-start | bytes 49160 | tf_op jit(solution)/shard_map/ppermute | solution.py:607
  64.7 1.7 %collective-permute-done.4.refs_4_ = f32[8,512]{1,0:T(8,128)S(1)} collective-permute-done((f32[8,512]{1,0:T(8,128)S(1)}, f32[8,512]{1,0:T(8,128)S(1)}, u32[]{:S(2)}, u32[]{:S(2)}) %collective-permute-start.4) | collective-permute-done | bytes 16416 | tf_op jit(solution)/shard_map/ppermute | solution.py:607
  66.4 11.4 %all-to-all-done.2.refs_0_ = f32[8,34,8,128]{3,2,1,0:T(8,128)S(1)} async-done(((f32[8,34,8,128]{3,2,1,0:T(8,128)}), f32[8,34,8,128]{3,2,1,0:T(8,128)S(1)}, u32[]{:S(2)}, u32[]{:S(2)}) %all-to-all-start.2) | async-done | bytes 1114144 | tf_op jit(solution)/shard_map/all_to_all | solution.py:611
  77.8 1.3 %shard_map.138 = (f32[6,5,8,1024]{3,2,1,0:T(8,128)}, f32[8,8,512]{2,1,0:T(8,128)}) custom-call(f32[8,34,8,128]{3,2,1,0:T(8,128)S(1)} %all-to-all-done.2.refs_0_, f32[6,5,8,1024]{3,2,1,0:T(8,128)S(1)} %copy-done.4, f32[6,8,1024]{2,1,0:T(8,128)S(1)} %copy-done.10, f32[8,8,512]{2,1,0:T(8,128)S(1)} %copy-done.12, f32[8,512]{1,0:T(8,128)S(1)} %collective-permute-done.4.refs_4_, ...), custom_call_target="tpu_custom_call" | custom-call | flops 1048576 | bytes 1048576 | tf_op jit(solution)/shard_map/pallas_call | solution.py:171
  (50 shorter events, 0.3 us)
Async XLA Ops:
  0.6 5.7 %copy-start.16 = (f32[5,5]{1,0:T(8,128)S(1)}, f32[5,5]{1,0:T(8,128)}, u32[]{:S(2)}) copy-start(f32[5,5]{1,0:T(8,128)} %refs_2_.5) | copy-start | bytes 304
  0.6 5.7 %copy-start.15 = (f32[5,5]{1,0:T(8,128)S(1)}, f32[5,5]{1,0:T(8,128)}, u32[]{:S(2)}) copy-start(f32[5,5]{1,0:T(8,128)} %refs_1_.7) | copy-start | bytes 304
  0.6 5.7 %copy-start.2 = (f32[6,5,8,1024]{3,2,1,0:T(8,128)S(1)}, f32[6,5,8,1024]{3,2,1,0:T(8,128)}, u32[]{:S(2)}) copy-start(f32[6,5,8,1024]{3,2,1,0:T(8,128)} %refs_4_.2) | copy-start | bytes 2949124
  3.0 14.9 %collective-permute-start = (f32[17,8,512]{2,1,0:T(8,128)}, f32[17,8,512]{2,1,0:T(8,128)S(1)}, u32[]{:S(2)}, u32[]{:S(2)}) collective-permute-start(f32[17,8,512]{2,1,0:T(8,128)} %get-tuple-element.29), channel_id=1, source_target_pairs={{0,1},{1,2},{2,3},{3,4},{4,5},{5,6},{6,7},{7,8},{8,9},{9,10},{10,1... | collective-permute-start | bytes 835592 | tf_op jit(solution)/shard_map/ppermute | solution.py:607
  3.1 14.8 %collective-permute-start.1 = (f32[17,8,512]{2,1,0:T(8,128)}, f32[17,8,512]{2,1,0:T(8,128)S(1)}, u32[]{:S(2)}, u32[]{:S(2)}) collective-permute-start(f32[17,8,512]{2,1,0:T(8,128)} %get-tuple-element.30), channel_id=1, source_target_pairs={{1,0},{2,1},{3,2},{4,3},{5,4},{6,5},{7,6},{8,7},{9,8},{10,9},{11,1... | collective-permute-start | bytes 835592 | tf_op jit(solution)/shard_map/ppermute | solution.py:607
  11.2 5.2 %copy-start.9 = (f32[2,4,8,512]{3,2,1,0:T(8,128)S(1)}, f32[2,4,8,512]{3,2,1,0:T(8,128)}, u32[]{:S(2)}) copy-start(f32[2,4,8,512]{3,2,1,0:T(8,128)} %param.17) | copy-start | bytes 393220
  11.2 5.2 %copy-start.14 = (f32[1536]{0:T(1024)S(1)}, f32[1536]{0:T(1024)}, u32[]{:S(2)}) copy-start(f32[1536]{0:T(1024)} %constant.5.clone.refs_0_) | copy-start | bytes 18436
  11.2 5.2 %copy-start.17 = (f32[512]{0:T(512)S(1)}, f32[512]{0:T(512)}, u32[]{:S(2)}) copy-start(f32[512]{0:T(512)} %param.19) | copy-start | bytes 6148
  11.3 5.2 %copy-start.18 = (s32[512]{0:T(512)S(1)}, s32[512]{0:T(512)}, u32[]{:S(2)}) copy-start(s32[512]{0:T(512)} %param.20) | copy-start | bytes 6148
  11.3 5.2 %copy-start.19 = (s32[512]{0:T(512)S(1)}, s32[512]{0:T(512)}, u32[]{:S(2)}) copy-start(s32[512]{0:T(512)} %param.21) | copy-start | bytes 6148
  11.3 22.9 %all-to-all-start.1 = ((f32[8,6,5,8,128]{4,3,2,1,0:T(8,128)}), f32[8,6,5,8,128]{4,3,2,1,0:T(8,128)S(1)}, u32[]{:S(2)}, u32[]{:S(2)}) async-start(f32[8,6,5,8,128]{4,3,2,1,0:T(8,128)} %get-tuple-element.28.refs_5_), calls=%async_computation.1 | async-start | bytes 1966080 | tf_op jit(solution)/shard_map/all_to_all | solution.py:611
  22.1 17.9 %collective-permute-start.2 = (f32[17,8,512]{2,1,0:T(8,128)}, f32[17,8,512]{2,1,0:T(8,128)S(1)}, u32[]{:S(2)}, u32[]{:S(2)}) collective-permute-start(f32[17,8,512]{2,1,0:T(8,128)} %get-tuple-element.34), channel_id=1, source_target_pairs={{0,1},{1,2},{2,3},{3,4},{4,5},{5,6},{6,7},{7,8},{8,9},{9,10},{10,1... | collective-permute-start | bytes 835592 | tf_op jit(solution)/shard_map/ppermute | solution.py:607
  22.6 18.1 %collective-permute-start.3 = (f32[17,8,512]{2,1,0:T(8,128)}, f32[17,8,512]{2,1,0:T(8,128)}, u32[]{:S(2)}, u32[]{:S(2)}) collective-permute-start(f32[17,8,512]{2,1,0:T(8,128)} %get-tuple-element.35), channel_id=1, source_target_pairs={{1,0},{2,1},{3,2},{4,3},{5,4},{6,5},{7,6},{8,7},{9,8},{10,9},{11,1... | collective-permute-start | bytes 835592 | tf_op jit(solution)/shard_map/ppermute | solution.py:607
  34.2 19.9 %all-to-all-start = ((f32[8,34,8,128]{3,2,1,0:T(8,128)}), f32[8,34,8,128]{3,2,1,0:T(8,128)S(1)}, u32[]{:S(2)}, u32[]{:S(2)}) async-start(f32[8,34,8,128]{3,2,1,0:T(8,128)} %get-tuple-element.31), calls=%async_computation | async-start | bytes 2228224 | tf_op jit(solution)/shard_map/all_to_all | solution.py:611
  41.7 12.4 %copy-start.1 = (bf16[384,1152]{1,0:T(8,128)(2,1)S(1)}, bf16[384,1152]{1,0:T(8,128)(2,1)}, u32[]{:S(2)}) copy-start(bf16[384,1152]{1,0:T(8,128)(2,1)} %constant.4.clone.refs_0_.refs_3_) | copy-start | bytes 2654212
  41.7 12.4 %copy-start.8 = (f32[8,1024]{1,0:T(8,128)S(1)}, f32[8,1024]{1,0:T(8,128)}, u32[]{:S(2)}) copy-start(f32[8,1024]{1,0:T(8,128)} %refs_4_.3) | copy-start | bytes 98308
  41.7 12.4 %copy-start.11 = (f32[8,8,512]{2,1,0:T(8,128)S(1)}, f32[8,8,512]{2,1,0:T(8,128)}, u32[]{:S(2)}) copy-start(f32[8,8,512]{2,1,0:T(8,128)} %get-tuple-element.32.refs_5_) | copy-start | bytes 393220
  57.6 3.9 %copy-start.22 = (f32[8,512]{1,0:T(8,128)S(1)}, f32[8,512]{1,0:T(8,128)}, u32[]{:S(2)}) copy-start(f32[8,512]{1,0:T(8,128)} %get-tuple-element.43) | copy-start | bytes 49156
  57.6 20.2 %copy-start.4 = (f32[6,5,8,1024]{3,2,1,0:T(8,128)S(1)}, f32[6,5,8,1024]{3,2,1,0:T(8,128)}, u32[]{:S(2)}) copy-start(f32[6,5,8,1024]{3,2,1,0:T(8,128)} %copy-done.3) | copy-start | bytes 2949124
  57.6 20.2 %copy-start.10 = (f32[6,8,1024]{2,1,0:T(8,128)S(1)}, f32[6,8,1024]{2,1,0:T(8,128)}, u32[]{:S(2)}) copy-start(f32[6,8,1024]{2,1,0:T(8,128)} %get-tuple-element.40.refs_2_) | copy-start | bytes 589828
  57.7 20.2 %copy-start.12 = (f32[8,8,512]{2,1,0:T(8,128)S(1)}, f32[8,8,512]{2,1,0:T(8,128)}, u32[]{:S(2)}) copy-start(f32[8,8,512]{2,1,0:T(8,128)} %get-tuple-element.41.refs_3_) | copy-start | bytes 393220
  57.7 20.2 %all-to-all-start.2 = ((f32[8,34,8,128]{3,2,1,0:T(8,128)}), f32[8,34,8,128]{3,2,1,0:T(8,128)S(1)}, u32[]{:S(2)}, u32[]{:S(2)}) async-start(f32[8,34,8,128]{3,2,1,0:T(8,128)} %get-tuple-element.38), calls=%async_computation.2 | async-start | bytes 2228224 | tf_op jit(solution)/shard_map/all_to_all | solution.py:611
  61.4 5.0 %collective-permute-start.4 = (f32[8,512]{1,0:T(8,128)S(1)}, f32[8,512]{1,0:T(8,128)S(1)}, u32[]{:S(2)}, u32[]{:S(2)}) collective-permute-start(f32[8,512]{1,0:T(8,128)S(1)} %copy-done.23), channel_id=1, source_target_pairs={{0,1},{1,2},{2,3},{3,4},{4,5},{5,6},{6,7},{7,8},{8,9},{9,10},{10,1... | collective-permute-start | bytes 49160 | tf_op jit(solution)/shard_map/ppermute | solution.py:607
  61.5 4.9 %collective-permute-start.5 = (f32[8,512]{1,0:T(8,128)S(1)}, f32[8,512]{1,0:T(8,128)S(1)}, u32[]{:S(2)}, u32[]{:S(2)}) collective-permute-start(f32[8,512]{1,0:T(8,128)S(1)} %copy-done.22), channel_id=1, source_target_pairs={{1,0},{2,1},{3,2},{4,3},{5,4},{6,5},{7,6},{8,7},{9,8},{10,9},{11,1... | collective-permute-start | bytes 49160 | tf_op jit(solution)/shard_map/ppermute | solution.py:607
  (9 other events, 13.4 us)

commit v9 on v8

--- a/solution.py
+++ b/solution.py
@@ -286,13 +286,14 @@
     pack_tile([get(4), get(5), extra, extra], 7, up_ref, down_ref)
 
 
-def prepare_kernel(a, ps, m_in, up, down, a_copy, ps_copy):
+def prepare_kernel(a, ps, m_in, up, down):
     for t in range(6):
-        ref = a.piece(t)
+        a.piece(2 * t)
+        ref = a.piece(2 * t + 1)
         pack_tile([ref[t, v] for v in range(4)], t, up.buffer, down.buffer)
         for x in (up, down):
             x.put(pl.ds(2 * t, 2))
-    pack_last(lambda t: a.buffer[t, NV - 1], ps.whole()[...], up.buffer, down.buffer)
+    pack_last(lambda t: a.buffer[t, NV - 1], ps[...], up.buffer, down.buffer)
     metal_edges(m_in.whole(), up.buffer.at[16], down.buffer.at[16])
     for x in (up, down):
         x.put(pl.ds(12, 5))
@@ -543,7 +544,8 @@
     v_ref = v.buffer
     near = local_step(ps_ref)
     x = turned(lambda j, t, u: q_ref[j, t * NV + u]) - g_ref[...]
-    for half in range(2):
+
+    def send(half):
         d = rotate_time(kron_ref[pl.ds(half * 192, 192), :], x)
         for j in range(4):
             for t in range(6):
@@ -551,26 +553,29 @@
                 for u in range(NV):
                     v_ref[half * 4 + j, t * NV + u] = -near * d[at : at + ROWS, u * CHUNK : (u + 1) * CHUNK]
         v.put((pl.ds(half * 4, 4), pl.ds(0, 30)))
+
     step = ps_ref[...]
     coeff = fc_ref[...]
     m_hot, m_row = metal_hots(mf_ref)
-    f_hot, f_row = fluid_hots(ff_ref)
     source = onto_cells(heat_sum(lambda j, k: q_ref[j, 30 + k]), m_hot, m_row)
     m = [m_ref[ch] + metal_step * source[ch] for ch in range(CH)]
+    send(0)
+    values = at_faces(jnp.stack(m), m_hot, m_row) * coeff
+    f_hot, f_row = fluid_hots(ff_ref)
+    cells = onto_cells(values, f_hot, f_row)
+    send(1)
     for ch in range(CH):
         m_out.buffer[ch] = m[ch]
-    m_out.put(slice(None))
     metal_edges(m, mup.buffer, mdown.buffer)
-    mup.put(slice(None))
-    mdown.put(slice(None))
-    cells = onto_cells(at_faces(jnp.stack(m), m_hot, m_row) * coeff, f_hot, f_row)
+    for result in (m_out, mup, mdown):
+        result.put(slice(None))
     for t in range(6):
         e.buffer[t] = step * combine(tab_ref, SYNTH, first + t, cells)
     e.put(slice(None))
     heat = []
     for ch in range(CH):
         total = hc_ref[ch]
-        for t in range(6):
+        for t in range(6 if ch != NH else 0):
             total += tab_ref[W0 + (first + t) * CH + ch] * e.buffer[t]
         heat.append(total)
     values = at_faces(jnp.stack(heat), f_hot, f_row) * coeff
@@ -639,17 +644,16 @@
     tab = jnp.asarray(FLAT)
     coeff, ff, mf = (x.reshape(1, NF) for x in (coeff, ff, mf))
     metal = metal.reshape(METAL)
-    up, down, a_here, ps_here = call(
-        prepare_kernel,
-        [(a0, Into(2, SIX)), (ps, Into(3, WHOLE))] + late(metal),
-        [(EDGES, 7), (EDGES, 7), (FLUID, 0), ((ROWS, SPAN), 0)],
-    )
+    ends = tuple(
+        (pl.ds(t, 1), slice(None), pl.ds(row, 2)) for t in range(6) for row in (0, ROWS - 2)
+    )
+    up, down = call(prepare_kernel, [(a0, ends)] + late(ps, metal), [(EDGES, 7), (EDGES, 7)])
     up, down = exchange(up, down)
     scalars = [(tab, "smem"), (jx, "smem"), (jz, "smem")]
     last_variable = (a0, ((slice(None), pl.ds(NV - 1, 1)),))
     b, q, blocks = call(
         inner_kernel,
-        scalars[1:] + plain(a_here, source, ps_here),
+        scalars[1:] + plain(a0, source, ps),
         [(FLUID, 6), (FLUID, 6), ((8, 6, NV, ROWS, CHUNK), -1)],
         scratch=[pltpu.VMEM((6, NV, ROWS, SPAN), F32), pltpu.SemaphoreType.DMA((8,))],
     )

time: 79.8 us -> 80.8 us (1.013)
  local copies, waits for them, and re-layouts: 3.94 us -> 5.15 us
    unnamed x48 -> x50, local copies, waits for them, and re-layouts: 3.94 us -> 5.15 us
where the time goes in v9:
time: 80.8 us; the launch traced here: 80.3 us
  waiting for transfers between devices  28.6 us (35%)
  Pallas kernels  22.8 us (28%)
  starting transfers between devices  22.6 us (28%)
  local copies, waits for them, and re-layouts  5.15 us (6%)
  between operations  1.15 us (1%)
    all_to_all x3, waiting for transfers between devices, turn(): return lax.all_to_all(x, 'inst', 0, 0, tiled=True)  26.9 us
    pallas_call x8, Pallas kernels, call(): pl.pallas_call(kernel, out_shape=[pltpu.HBM(dims, F32) if n else jax.Shap...  22.8 us
    all_to_all x3, starting transfers between devices, turn(): return lax.all_to_all(x, 'inst', 0, 0, tiled=True)  12.6 us
    ppermute x3, starting transfers between devices, exchange(): lax.ppermute(down, 'space', back)  9.31 us
    unnamed x50, local copies, waits for them, and re-layouts  5.15 us
    ppermute x3, waiting for transfers between devices, exchange(): lax.ppermute(up, 'space', forward)  1.66 us
  transfers between devices with their start and end apart: 9, of which 4 were waited for; matrix products, arithmetic and copies ran while one was open for 0% of the time, Pallas kernels for 20%

profile of v9, /device:TPU:112, one launch (start us, length us, event | category | flops | bytes accessed | tf_op | source)
XLA Modules:
  0.0 80.3 jit_solution(7522451522045549684)
XLA Ops:
  0.7 2.1 %shard_map.133 = (f32[17,8,512]{2,1,0:T(8,128)}, f32[17,8,512]{2,1,0:T(8,128)}) custom-call(f32[6,5,8,1024]{3,2,1,0:T(8,128)} %refs_8_.1, f32[8,1024]{1,0:T(8,128)} %refs_4_.5, f32[8,8,512]{2,1,0:T(8,128)} %bitcast.5), custom_call_target="tpu_custom_call" | custom-call | flops 1048576 | bytes 1048576 | tf_op jit(solution)/shard_map/pallas_call | solution.py:171
  2.9 3.2 %collective-permute-start.1 = (f32[17,8,512]{2,1,0:T(8,128)}, f32[17,8,512]{2,1,0:T(8,128)S(1)}, u32[]{:S(2)}, u32[]{:S(2)}) collective-permute-start(f32[17,8,512]{2,1,0:T(8,128)} %get-tuple-element.26), channel_id=1, source_target_pairs={{1,0},{2,1},{3,2},{4,3},{5,4},{6,5},{7,6},{8,7},{9,8},{10,9},{11,1... | collective-permute-start | bytes 835592 | tf_op jit(solution)/shard_map/ppermute | solution.py:612
  6.2 1.2 %copy-done.3 = f32[6,5,8,1024]{3,2,1,0:T(8,128)S(1)} copy-done((f32[6,5,8,1024]{3,2,1,0:T(8,128)S(1)}, f32[6,5,8,1024]{3,2,1,0:T(8,128)}, u32[]{:S(2)}) %copy-start.3) | copy-done | bytes 983064
  7.4 5.0 %shard_map.131 = (f32[6,5,8,1024]{3,2,1,0:T(8,128)}, f32[6,5,8,1024]{3,2,1,0:T(8,128)}, f32[8,6,5,8,128]{4,3,2,1,0:T(8,128)}) custom-call(f32[5,5]{1,0:T(8,128)S(1)} %copy-done.16, f32[5,5]{1,0:T(8,128)S(1)} %copy-done.17, f32[6,5,8,1024]{3,2,1,0:T(8,128)S(1)} %copy-done, f32[6,5,8,1024]{3,2,1,0:T(8,128)S(1)} %copy-done.3, f32[8,1024]{1,0:T(8,128)S(1)} %copy-done.8), custom_call_target="tpu_custom_call" | custom-call | flops 1048576 | bytes 1048576 | tf_op jit(solution)/shard_map/pallas_call | solution.py:171
  12.4 5.2 %all-to-all-start.1 = ((f32[8,6,5,8,128]{4,3,2,1,0:T(8,128)}), f32[8,6,5,8,128]{4,3,2,1,0:T(8,128)S(1)}, u32[]{:S(2)}, u32[]{:S(2)}) async-start(f32[8,6,5,8,128]{4,3,2,1,0:T(8,128)} %get-tuple-element.24.refs_5_), calls=%async_computation.1 | async-start | bytes 1966080 | tf_op jit(solution)/shard_map/all_to_all | solution.py:616
  17.6 1.4 %shard_map.132.refs_6_ = f32[6,8,1024]{2,1,0:T(8,128)S(1)} custom-call(f32[1536]{0:T(1024)S(1)} %copy-done.15, f32[8,8,512]{2,1,0:T(8,128)S(1)} %bitcast.6, f32[1,512]{1,0:T(1,128)S(1)} %bitcast.8, s32[1,512]{1,0:T(1,128)S(1)} %bitcast.11, s32[1,512]{1,0:T(1,128)S(1)} %bitcast.14, f32[8,6,5,8,128]{4,3,2,1,0:T(8,128)} %get-tuple-element.24.refs_5_), custom_call_target="tpu_custom_call" | custom-call | flops 68719476736 | bytes 1048576 | tf_op jit(solution)/shard_map/pallas_call | solution.py:171
  19.1 4.1 %shard_map.134 = (f32[8,34,8,128]{3,2,1,0:T(8,128)}, f32[6,5,8,1024]{3,2,1,0:T(8,128)}, f32[17,8,512]{2,1,0:T(8,128)}, f32[17,8,512]{2,1,0:T(8,128)}, f32[6,8,1024]{2,1,0:T(8,128)}, /*index=5*/f32[8,8,512]{2,1,0:T(8,128)}) custom-call(f32[1536]{0:T(1024)S(1)} %copy-done.15, f32[5,5]{1,0:T(8,128)S(1)} %copy-done.16, f32[5,5]{1,0:T(8,128)S(1)} %copy-done.17, ...), custom_call_target="tpu_custom_call" | custom-call | flops 1048576 | bytes 1048576 | tf_op jit(solution)/shard_map/pallas_call | solution.py:171
  23.2 0.5 collective-permute-start.2
  23.7 2.8 %collective-permute-start.3 = (f32[17,8,512]{2,1,0:T(8,128)}, f32[17,8,512]{2,1,0:T(8,128)}, u32[]{:S(2)}, u32[]{:S(2)}) collective-permute-start(f32[17,8,512]{2,1,0:T(8,128)} %get-tuple-element.31), channel_id=1, source_target_pairs={{1,0},{2,1},{3,2},{4,3},{5,4},{6,5},{7,6},{8,7},{9,8},{10,9},{11,1... | collective-permute-start | bytes 835592 | tf_op jit(solution)/shard_map/ppermute | solution.py:612
  26.6 8.7 %all-to-all-done.1.refs_1_ = f32[8,6,5,8,128]{4,3,2,1,0:T(8,128)S(1)} async-done(((f32[8,6,5,8,128]{4,3,2,1,0:T(8,128)}), f32[8,6,5,8,128]{4,3,2,1,0:T(8,128)S(1)}, u32[]{:S(2)}, u32[]{:S(2)}) %all-to-all-start.1) | async-done | bytes 983072 | tf_op jit(solution)/shard_map/all_to_all | solution.py:616
  35.3 3.7 %all-to-all-start = ((f32[8,34,8,128]{3,2,1,0:T(8,128)}), f32[8,34,8,128]{3,2,1,0:T(8,128)S(1)}, u32[]{:S(2)}, u32[]{:S(2)}) async-start(f32[8,34,8,128]{3,2,1,0:T(8,128)} %get-tuple-element.27), calls=%async_computation | async-start | bytes 2228224 | tf_op jit(solution)/shard_map/all_to_all | solution.py:616
  39.1 1.2 %copy-done.1 = bf16[384,1152]{1,0:T(8,128)(2,1)S(1)} copy-done((bf16[384,1152]{1,0:T(8,128)(2,1)S(1)}, bf16[384,1152]{1,0:T(8,128)(2,1)}, u32[]{:S(2)}) %copy-start.1) | copy-done | bytes 884760
  40.2 0.9 %shard_map.135.refs_10_.refs_2_ = f32[384,640]{1,0:T(8,128)S(1)} custom-call(bf16[384,1152]{1,0:T(8,128)(2,1)S(1)} %copy-done.1, f32[8,6,5,8,128]{4,3,2,1,0:T(8,128)S(1)} %all-to-all-done.1.refs_1_, f32[8,1024]{1,0:T(8,128)S(1)} %copy-done.8), custom_call_target="tpu_custom_call" | custom-call | flops 1048576 | bytes 1048576 | tf_op jit(solution)/shard_map/pallas_call | solution.py:171
  41.2 0.7 copy-done.21
  41.9 1.0 %copy-done.22 = f32[17,8,512]{2,1,0:T(8,128)S(1)} copy-done((f32[17,8,512]{2,1,0:T(8,128)S(1)}, f32[17,8,512]{2,1,0:T(8,128)}, u32[]{:S(2)}) %copy-start.22) | copy-done | bytes 278552
  42.8 4.6 %shard_map.136 = (f32[6,5,8,1024]{3,2,1,0:T(8,128)S(1)}, f32[8,8,1024]{2,1,0:T(8,128)S(1)}) custom-call(f32[1536]{0:T(1024)S(1)} %copy-done.15, f32[5,5]{1,0:T(8,128)S(1)} %copy-done.16, f32[5,5]{1,0:T(8,128)S(1)} %copy-done.17, f32[6,5,8,1024]{3,2,1,0:T(8,128)} %get-tuple-element.29.refs_3_, f32[6,5,8,1024]{3,2,1,0:T(8,128)} %refs_4_.4, f32[8,1024]{1,0:T(8,128)} %refs_4_.5, ...), custom_call_target="tpu_custom_call" | custom-call | flops 68719476736 | bytes 1048576 | tf_op jit(solution)/shard_map/pallas_call | solution.py:171
  47.5 0.9 %copy-done.4 = f32[6,5,8,1024]{3,2,1,0:T(8,128)} copy-done((f32[6,5,8,1024]{3,2,1,0:T(8,128)}, f32[6,5,8,1024]{3,2,1,0:T(8,128)S(1)}, u32[]{:S(2)}) %copy-start.4) | copy-done | bytes 983064
  48.4 6.8 %all-to-all-done.refs_1_ = f32[8,34,8,128]{3,2,1,0:T(8,128)S(1)} async-done(((f32[8,34,8,128]{3,2,1,0:T(8,128)}), f32[8,34,8,128]{3,2,1,0:T(8,128)S(1)}, u32[]{:S(2)}, u32[]{:S(2)}) %all-to-all-start) | async-done | bytes 1114144 | tf_op jit(solution)/shard_map/all_to_all | solution.py:616
  55.2 3.4 %shard_map.137 = (f32[8,34,8,128]{3,2,1,0:T(8,128)}, f32[8,8,512]{2,1,0:T(8,128)}, f32[8,512]{1,0:T(8,128)}, f32[8,512]{1,0:T(8,128)}, f32[6,8,1024]{2,1,0:T(8,128)}) custom-call(f32[1536]{0:T(1024)S(1)} %copy-done.15, f32[8,34,8,128]{3,2,1,0:T(8,128)S(1)} %all-to-all-done.refs_1_, f32[384,640]{1,0:T(8,128)S(1)} %shard_map.135.refs_10_.refs_2_, ...), custom_call_target="tpu_custom_call" | custom-call | flops 1048576 | bytes 1048576 | tf_op jit(solution)/shard_map/pallas_call | solution.py:171
  58.6 3.7 %all-to-all-start.2 = ((f32[8,34,8,128]{3,2,1,0:T(8,128)}), f32[8,34,8,128]{3,2,1,0:T(8,128)S(1)}, u32[]{:S(2)}, u32[]{:S(2)}) async-start(f32[8,34,8,128]{3,2,1,0:T(8,128)} %get-tuple-element.34), calls=%async_computation.2 | async-start | bytes 2228224 | tf_op jit(solution)/shard_map/all_to_all | solution.py:616
  62.4 3.2 %collective-permute-start.5 = (f32[8,512]{1,0:T(8,128)S(1)}, f32[8,512]{1,0:T(8,128)S(1)}, u32[]{:S(2)}, u32[]{:S(2)}) collective-permute-start(f32[8,512]{1,0:T(8,128)S(1)} %copy-done.23), channel_id=1, source_target_pairs={{1,0},{2,1},{3,2},{4,3},{5,4},{6,5},{7,6},{8,7},{9,8},{10,9},{11,1... | collective-permute-start | bytes 49160 | tf_op jit(solution)/shard_map/ppermute | solution.py:612
  65.7 1.7 %collective-permute-done.4.refs_4_ = f32[8,512]{1,0:T(8,128)S(1)} collective-permute-done((f32[8,512]{1,0:T(8,128)S(1)}, f32[8,512]{1,0:T(8,128)S(1)}, u32[]{:S(2)}, u32[]{:S(2)}) %collective-permute-start.4) | collective-permute-done | bytes 16416 | tf_op jit(solution)/shard_map/ppermute | solution.py:612
  67.3 11.4 %all-to-all-done.2.refs_0_ = f32[8,34,8,128]{3,2,1,0:T(8,128)S(1)} async-done(((f32[8,34,8,128]{3,2,1,0:T(8,128)}), f32[8,34,8,128]{3,2,1,0:T(8,128)S(1)}, u32[]{:S(2)}, u32[]{:S(2)}) %all-to-all-start.2) | async-done | bytes 1114144 | tf_op jit(solution)/shard_map/all_to_all | solution.py:616
  78.8 1.4 %shard_map.138 = (f32[6,5,8,1024]{3,2,1,0:T(8,128)}, f32[8,8,512]{2,1,0:T(8,128)}) custom-call(f32[8,34,8,128]{3,2,1,0:T(8,128)S(1)} %all-to-all-done.2.refs_0_, f32[6,5,8,1024]{3,2,1,0:T(8,128)S(1)} %copy-done.5, f32[6,8,1024]{2,1,0:T(8,128)S(1)} %copy-done.11, f32[8,8,512]{2,1,0:T(8,128)S(1)} %copy-done.13, f32[8,512]{1,0:T(8,128)S(1)} %collective-permute-done.4.refs_4_, ...), custom_call_target="tpu_custom_call" | custom-call | flops 1048576 | bytes 1048576 | tf_op jit(solution)/shard_map/pallas_call | solution.py:171
  (52 shorter events, 0.4 us)
Async XLA Ops:
  0.6 5.5 %copy-start.8 = (f32[8,1024]{1,0:T(8,128)S(1)}, f32[8,1024]{1,0:T(8,128)}, u32[]{:S(2)}) copy-start(f32[8,1024]{1,0:T(8,128)} %refs_4_.5) | copy-start | bytes 98308
  0.6 5.5 %copy-start = (f32[6,5,8,1024]{3,2,1,0:T(8,128)S(1)}, f32[6,5,8,1024]{3,2,1,0:T(8,128)}, u32[]{:S(2)}) copy-start(f32[6,5,8,1024]{3,2,1,0:T(8,128)} %refs_8_.1) | copy-start | bytes 2949124
  0.7 5.5 %copy-start.17 = (f32[5,5]{1,0:T(8,128)S(1)}, f32[5,5]{1,0:T(8,128)}, u32[]{:S(2)}) copy-start(f32[5,5]{1,0:T(8,128)} %refs_2_.7) | copy-start | bytes 304
  0.7 5.5 %copy-start.16 = (f32[5,5]{1,0:T(8,128)S(1)}, f32[5,5]{1,0:T(8,128)}, u32[]{:S(2)}) copy-start(f32[5,5]{1,0:T(8,128)} %refs_1_.7) | copy-start | bytes 304
  2.8 16.2 %collective-permute-start = (f32[17,8,512]{2,1,0:T(8,128)}, f32[17,8,512]{2,1,0:T(8,128)S(1)}, u32[]{:S(2)}, u32[]{:S(2)}) collective-permute-start(f32[17,8,512]{2,1,0:T(8,128)} %get-tuple-element.25), channel_id=1, source_target_pairs={{0,1},{1,2},{2,3},{3,4},{4,5},{5,6},{6,7},{7,8},{8,9},{9,10},{10,1... | collective-permute-start | bytes 835592 | tf_op jit(solution)/shard_map/ppermute | solution.py:612
  2.9 16.1 %collective-permute-start.1 = (f32[17,8,512]{2,1,0:T(8,128)}, f32[17,8,512]{2,1,0:T(8,128)S(1)}, u32[]{:S(2)}, u32[]{:S(2)}) collective-permute-start(f32[17,8,512]{2,1,0:T(8,128)} %get-tuple-element.26), channel_id=1, source_target_pairs={{1,0},{2,1},{3,2},{4,3},{5,4},{6,5},{7,6},{8,7},{9,8},{10,9},{11,1... | collective-permute-start | bytes 835592 | tf_op jit(solution)/shard_map/ppermute | solution.py:612
  12.3 5.2 %copy-start.10 = (f32[2,4,8,512]{3,2,1,0:T(8,128)S(1)}, f32[2,4,8,512]{3,2,1,0:T(8,128)}, u32[]{:S(2)}) copy-start(f32[2,4,8,512]{3,2,1,0:T(8,128)} %param.17) | copy-start | bytes 393220
  12.3 5.2 %copy-start.15 = (f32[1536]{0:T(1024)S(1)}, f32[1536]{0:T(1024)}, u32[]{:S(2)}) copy-start(f32[1536]{0:T(1024)} %constant.5.clone.refs_0_) | copy-start | bytes 18436
  12.4 5.2 %copy-start.18 = (f32[512]{0:T(512)S(1)}, f32[512]{0:T(512)}, u32[]{:S(2)}) copy-start(f32[512]{0:T(512)} %param.19) | copy-start | bytes 6148
  12.4 5.2 %copy-start.19 = (s32[512]{0:T(512)S(1)}, s32[512]{0:T(512)}, u32[]{:S(2)}) copy-start(s32[512]{0:T(512)} %param.20) | copy-start | bytes 6148
  12.4 5.2 %copy-start.20 = (s32[512]{0:T(512)S(1)}, s32[512]{0:T(512)}, u32[]{:S(2)}) copy-start(s32[512]{0:T(512)} %param.21) | copy-start | bytes 6148
  12.4 22.9 %all-to-all-start.1 = ((f32[8,6,5,8,128]{4,3,2,1,0:T(8,128)}), f32[8,6,5,8,128]{4,3,2,1,0:T(8,128)S(1)}, u32[]{:S(2)}, u32[]{:S(2)}) async-start(f32[8,6,5,8,128]{4,3,2,1,0:T(8,128)} %get-tuple-element.24.refs_5_), calls=%async_computation.1 | async-start | bytes 1966080 | tf_op jit(solution)/shard_map/all_to_all | solution.py:616
  23.2 17.9 %collective-permute-start.2 = (f32[17,8,512]{2,1,0:T(8,128)}, f32[17,8,512]{2,1,0:T(8,128)S(1)}, u32[]{:S(2)}, u32[]{:S(2)}) collective-permute-start(f32[17,8,512]{2,1,0:T(8,128)} %get-tuple-element.30), channel_id=1, source_target_pairs={{0,1},{1,2},{2,3},{3,4},{4,5},{5,6},{6,7},{7,8},{8,9},{9,10},{10,1... | collective-permute-start | bytes 835592 | tf_op jit(solution)/shard_map/ppermute | solution.py:612
  23.7 18.2 %collective-permute-start.3 = (f32[17,8,512]{2,1,0:T(8,128)}, f32[17,8,512]{2,1,0:T(8,128)}, u32[]{:S(2)}, u32[]{:S(2)}) collective-permute-start(f32[17,8,512]{2,1,0:T(8,128)} %get-tuple-element.31), channel_id=1, source_target_pairs={{1,0},{2,1},{3,2},{4,3},{5,4},{6,5},{7,6},{8,7},{9,8},{10,9},{11,1... | collective-permute-start | bytes 835592 | tf_op jit(solution)/shard_map/ppermute | solution.py:612
  35.3 19.9 %all-to-all-start = ((f32[8,34,8,128]{3,2,1,0:T(8,128)}), f32[8,34,8,128]{3,2,1,0:T(8,128)S(1)}, u32[]{:S(2)}, u32[]{:S(2)}) async-start(f32[8,34,8,128]{3,2,1,0:T(8,128)} %get-tuple-element.27), calls=%async_computation | async-start | bytes 2228224 | tf_op jit(solution)/shard_map/all_to_all | solution.py:616
  42.8 12.3 %copy-start.2 = (bf16[384,1152]{1,0:T(8,128)(2,1)S(1)}, bf16[384,1152]{1,0:T(8,128)(2,1)}, u32[]{:S(2)}) copy-start(bf16[384,1152]{1,0:T(8,128)(2,1)} %constant.4.clone.refs_0_.refs_3_) | copy-start | bytes 2654212
  42.8 12.3 %copy-start.9 = (f32[8,1024]{1,0:T(8,128)S(1)}, f32[8,1024]{1,0:T(8,128)}, u32[]{:S(2)}) copy-start(f32[8,1024]{1,0:T(8,128)} %refs_4_.5) | copy-start | bytes 98308
  42.8 12.3 %copy-start.12 = (f32[8,8,512]{2,1,0:T(8,128)S(1)}, f32[8,8,512]{2,1,0:T(8,128)}, u32[]{:S(2)}) copy-start(f32[8,8,512]{2,1,0:T(8,128)} %get-tuple-element.28.refs_5_) | copy-start | bytes 393220
  58.6 20.2 %copy-start.5 = (f32[6,5,8,1024]{3,2,1,0:T(8,128)S(1)}, f32[6,5,8,1024]{3,2,1,0:T(8,128)}, u32[]{:S(2)}) copy-start(f32[6,5,8,1024]{3,2,1,0:T(8,128)} %copy-done.4) | copy-start | bytes 2949124
  58.6 20.2 %copy-start.11 = (f32[6,8,1024]{2,1,0:T(8,128)S(1)}, f32[6,8,1024]{2,1,0:T(8,128)}, u32[]{:S(2)}) copy-start(f32[6,8,1024]{2,1,0:T(8,128)} %get-tuple-element.36.refs_2_) | copy-start | bytes 589828
  58.6 20.2 %copy-start.13 = (f32[8,8,512]{2,1,0:T(8,128)S(1)}, f32[8,8,512]{2,1,0:T(8,128)}, u32[]{:S(2)}) copy-start(f32[8,8,512]{2,1,0:T(8,128)} %get-tuple-element.37.refs_3_) | copy-start | bytes 393220
  58.6 20.2 %all-to-all-start.2 = ((f32[8,34,8,128]{3,2,1,0:T(8,128)}), f32[8,34,8,128]{3,2,1,0:T(8,128)S(1)}, u32[]{:S(2)}, u32[]{:S(2)}) async-start(f32[8,34,8,128]{3,2,1,0:T(8,128)} %get-tuple-element.34), calls=%async_computation.2 | async-start | bytes 2228224 | tf_op jit(solution)/shard_map/all_to_all | solution.py:616
  62.3 5.0 %collective-permute-start.4 = (f32[8,512]{1,0:T(8,128)S(1)}, f32[8,512]{1,0:T(8,128)S(1)}, u32[]{:S(2)}, u32[]{:S(2)}) collective-permute-start(f32[8,512]{1,0:T(8,128)S(1)} %copy-done.24), channel_id=1, source_target_pairs={{0,1},{1,2},{2,3},{3,4},{4,5},{5,6},{6,7},{7,8},{8,9},{9,10},{10,1... | collective-permute-start | bytes 49160 | tf_op jit(solution)/shard_map/ppermute | solution.py:612
  62.4 4.9 %collective-permute-start.5 = (f32[8,512]{1,0:T(8,128)S(1)}, f32[8,512]{1,0:T(8,128)S(1)}, u32[]{:S(2)}, u32[]{:S(2)}) collective-permute-start(f32[8,512]{1,0:T(8,128)S(1)} %copy-done.23), channel_id=1, source_target_pairs={{1,0},{2,1},{3,2},{4,3},{5,4},{6,5},{7,6},{8,7},{9,8},{10,9},{11,1... | collective-permute-start | bytes 49160 | tf_op jit(solution)/shard_map/ppermute | solution.py:612
  (10 other events, 17.0 us)

commit v10 on v8

--- a/solution.py
+++ b/solution.py
@@ -121,6 +121,8 @@
 
 
 def call(body, operands, results, scratch=(), flops=1 << 20, moved=1 << 20):
+    types = [r[2] if len(r) > 2 else F32 for r in results]
+    results = [r[:2] for r in results]
     space = {"idle": pltpu.HBM, "smem": pltpu.SMEM, "vmem": pltpu.VMEM, "held": pltpu.VMEM}
     modes = [mode for _, mode in operands]
     here = [isinstance(mode, str) for mode in modes]
@@ -170,7 +172,7 @@
 
     return pl.pallas_call(
         kernel,
-        out_shape=[pltpu.HBM(dims, F32) if n else jax.ShapeDtypeStruct(dims, kinds.get(k, F32)) for k, (dims, n) in enumerate(results)],
+        out_shape=[pltpu.HBM(dims, F32) if n else jax.ShapeDtypeStruct(dims, kinds.get(k, types[k])) for k, (dims, n) in enumerate(results)],
         in_specs=in_specs,
         out_specs=out_specs,
         scratch_shapes=buffers + list(scratch),
@@ -215,6 +217,10 @@
     both = jnp.concatenate(split(spread), axis=0)
     out = lax.dot_general(both, span_hot, (((1,), (1,)), ((), ())), preferred_element_type=F32)
     return (out[: CH * ROWS] + out[CH * ROWS :]).reshape(CH, ROWS, span_hot.shape[0])
+
+
+def rows_of(faces_ref, bits):
+    return jnp.where(row_index(NF) == (faces_ref[...] >> bits), 1.0, 0.0)
 
 
 def fluid_hots(ff_ref):
@@ -324,17 +330,9 @@
     return out
 
 
-def inner_kernel(jx_ref, jz_ref, a_ref, s_ref, ps_ref, b, q, blocks, parts, sems):
+def inner_steps(instances, jx_ref, jz_ref, a_ref, s_ref, ps_ref, b, q, parts):
     step = ps_ref[...]
-    copies = [
-        pltpu.make_async_copy(
-            a_ref.at[:, :, :, pl.ds(i * CHUNK, CHUNK)], blocks.at[i], sems.at[i]
-        )
-        for i in range(8)
-    ]
-    for copy in copies:
-        copy.start()
-    for t in range(6):
+    for at, t in enumerate(instances):
         for v in range(NV):
             a = a_ref[t, v]
             dx, dz, rest = stencil_parts(a, 0.0, 0.0)
@@ -352,12 +350,31 @@
                 space = convect(jx_ref, jz_ref, dx, dz, parts[2, u, :, cut], u)
                 source = s_ref[t, u, :, cut] + space
                 inner = a + ps_ref[:, cut] * source
-                b.buffer[t, u, :, cut] = inner
-                q.buffer[t, u, :, cut] = a + inner + convect(jx_ref, jz_ref, px, pz, parts[5, u, :, cut], u)
-        b.put(pl.ds(t, 1))
-        q.put(pl.ds(t, 1))
+                b.buffer[at, u, :, cut] = inner
+                q.buffer[at, u, :, cut] = a + inner + convect(jx_ref, jz_ref, px, pz, parts[5, u, :, cut], u)
+        b.put(pl.ds(at, 1))
+        q.put(pl.ds(at, 1))
+
+
+EARLY = 4
+
+
+def early_kernel(jx_ref, jz_ref, a_ref, s_ref, ps_ref, b, q, blocks, parts, sems):
+    copies = [
+        pltpu.make_async_copy(
+            a_ref.at[:, :, :, pl.ds(i * CHUNK, CHUNK)], blocks.at[i], sems.at[i]
+        )
+        for i in range(8)
+    ]
+    for copy in copies:
+        copy.start()
+    inner_steps(range(EARLY), jx_ref, jz_ref, a_ref, s_ref, ps_ref, b, q, parts)
     for copy in copies:
         copy.wait()
+
+
+def late_kernel(jx_ref, jz_ref, a_ref, s_ref, ps_ref, after, b, q, parts):
+    inner_steps(range(EARLY, 6), jx_ref, jz_ref, a_ref, s_ref, ps_ref, b, q, parts)
 
 
 def edge_terms(up_ref, down_ref, half, t, v):
@@ -373,7 +390,7 @@
 
 
 def first_kernel(
-    tab_ref, jx_ref, jz_ref, a_ref, bi_ref, qi_ref, e_ref, ps_ref, up_ref, down_ref, fc_ref, ff_ref, m_ref, cond_ref,
+    tab_ref, jx_ref, jz_ref, a_ref, b0_ref, q0_ref, b1_ref, q1_ref, e_ref, ps_ref, up_ref, down_ref, fc_ref, ff_ref, m_ref, cond_ref,
     q, b_out, bup, bdown, q4, m_out,
 ):
     first = lax.axis_index("inst") * 6
@@ -394,6 +411,8 @@
             here = ps_ref[:, wide]
             step_one, step_two = step_edges[half]
             edges = [edge_terms(up_ref, down_ref, half, t, v) for v in range(NV)]
+            bi_ref, qi_ref = (b0_ref, q0_ref) if t < EARLY else (b1_ref, q1_ref)
+            ti = t if t < EARLY else t - EARLY
             for u in range(NV):
                 total = jx_ref[u, 0] * edges[0][0]
                 for v in range(1, NV):
@@ -404,8 +423,8 @@
                 if u == NV - 1:
                     change = change + e_ref[t, :, wide]
                 change = here * change
-                b_ref[t, u, :, wide] = bi_ref[t, u, :, wide] + change
-                value = qi_ref[t, u, :, wide] + change + (step_one * one - step_two * two)
+                b_ref[t, u, :, wide] = bi_ref[ti, u, :, wide] + change
+                value = qi_ref[ti, u, :, wide] + change + (step_one * one - step_two * two)
                 for i in range(4):
                     q_ref[4 * half + i, t * NV + u] = value[:, i * CHUNK : (i + 1) * CHUNK]
                 if u == NV - 1:
@@ -467,8 +486,8 @@
 
 
 def middle_kernel(
-    tab_ref, jx_ref, jz_ref, b_in, s_in, ps_ref, up_ref, down_ref, a_ref, q4_ref, g_ref,
-    c_out, hc,
+    tab_ref, jx_ref, jz_ref, b_in, s_in, ps_ref, up_ref, down_ref, a_ref, q4_ref, ff_ref, mf_ref, g_ref,
+    c_out, hc, f_hot, m_hot,
     parts,
 ):
     first = lax.axis_index("inst") * 6
@@ -497,6 +516,8 @@
             h3 += tab_ref[W2 + at] * a_ref[t, NV - 1]
         hc.buffer[ch] = h0 + step * (step * h3 - h2)
     hc.put(slice(None))
+    f_hot.buffer[...] = fluid_hots(ff_ref)[0]
+    m_hot.buffer[...] = metal_hots(mf_ref)[0]
 
 
 def metal_update(m, before, after, cond):
@@ -536,41 +557,42 @@
 
 
 def second_kernel(
-    tab_ref, q_ref, g_ref, kron_ref, ps_ref, m_ref, fc_ref, ff_ref, mf_ref, hc_ref,
+    tab_ref, q_ref, g_ref, kron_ref, ps_ref, m_ref, fc_ref, ff_ref, mf_ref, hc_ref, f_hot_ref, m_hot_ref,
     v, m_out, mup, mdown, e,
 ):
     first = lax.axis_index("inst") * 6
     v_ref = v.buffer
     near = local_step(ps_ref)
     x = turned(lambda j, t, u: q_ref[j, t * NV + u]) - g_ref[...]
+
+    d = rotate_time(kron_ref[...], x)
     for half in range(2):
-        d = rotate_time(kron_ref[pl.ds(half * 192, 192), :], x)
-        for j in range(4):
+        for j in range(4 * half, 4 * half + 4):
             for t in range(6):
                 at = (j * 6 + t) * ROWS
                 for u in range(NV):
-                    v_ref[half * 4 + j, t * NV + u] = -near * d[at : at + ROWS, u * CHUNK : (u + 1) * CHUNK]
+                    v_ref[j, t * NV + u] = -near * d[at : at + ROWS, u * CHUNK : (u + 1) * CHUNK]
         v.put((pl.ds(half * 4, 4), pl.ds(0, 30)))
     step = ps_ref[...]
     coeff = fc_ref[...]
-    m_hot, m_row = metal_hots(mf_ref)
-    f_hot, f_row = fluid_hots(ff_ref)
+    m_hot, m_row = m_hot_ref[...], rows_of(mf_ref, 9)
     source = onto_cells(heat_sum(lambda j, k: q_ref[j, 30 + k]), m_hot, m_row)
     m = [m_ref[ch] + metal_step * source[ch] for ch in range(CH)]
+    values = at_faces(jnp.stack(m), m_hot, m_row) * coeff
+    f_hot, f_row = f_hot_ref[...], rows_of(ff_ref, 10)
+    cells = onto_cells(values, f_hot, f_row)
     for ch in range(CH):
         m_out.buffer[ch] = m[ch]
-    m_out.put(slice(None))
     metal_edges(m, mup.buffer, mdown.buffer)
-    mup.put(slice(None))
-    mdown.put(slice(None))
-    cells = onto_cells(at_faces(jnp.stack(m), m_hot, m_row) * coeff, f_hot, f_row)
+    for result in (m_out, mup, mdown):
+        result.put(slice(None))
     for t in range(6):
         e.buffer[t] = step * combine(tab_ref, SYNTH, first + t, cells)
     e.put(slice(None))
     heat = []
     for ch in range(CH):
         total = hc_ref[ch]
-        for t in range(6):
+        for t in range(6 if ch != NH else 0):
             total += tab_ref[W0 + (first + t) * CH + ch] * e.buffer[t]
         heat.append(total)
     values = at_faces(jnp.stack(heat), f_hot, f_row) * coeff
@@ -647,11 +669,12 @@
     up, down = exchange(up, down)
     scalars = [(tab, "smem"), (jx, "smem"), (jz, "smem")]
     last_variable = (a0, ((slice(None), pl.ds(NV - 1, 1)),))
+    parts = pltpu.VMEM((6, NV, ROWS, SPAN), F32)
     b, q, blocks = call(
-        inner_kernel,
+        early_kernel,
         scalars[1:] + plain(a_here, source, ps_here),
-        [(FLUID, 6), (FLUID, 6), ((8, 6, NV, ROWS, CHUNK), -1)],
-        scratch=[pltpu.VMEM((6, NV, ROWS, SPAN), F32), pltpu.SemaphoreType.DMA((8,))],
+        [((EARLY,) + FLUID[1:], EARLY), ((EARLY,) + FLUID[1:], EARLY), ((8, 6, NV, ROWS, CHUNK), -1)],
+        scratch=[parts, pltpu.SemaphoreType.DMA((8,))],
     )
     (e0,) = call(
         energy_kernel,
@@ -659,26 +682,33 @@
         [(ONE, 0)],
         flops=LONG,
     )
+    b_late, q_late = call(
+        late_kernel,
+        scalars[1:] + plain(a0, source, ps) + [(blocks, "idle")],
+        [((6 - EARLY,) + FLUID[1:], 0)] * 2,
+        scratch=[parts],
+        flops=LONG,
+    )
     a_turned = turn(blocks)
     q, b, bup, bdown, q4, metal = call(
         first_kernel,
-        scalars + [last_variable] + plain(b, q, e0, ps, up, down, coeff, ff, metal, cond),
+        scalars + [last_variable] + plain(b, q, b_late, q_late, e0, ps, up, down, coeff, ff, metal, cond),
         [(BLOCKS, 7), (FLUID, 6), (EDGES, 1), (EDGES, 1), (ONE, 1), (METAL, 1)],
     )
     q_turned = turn(q)
     bup, bdown = exchange(bup, bdown)
     (g,) = call(derive_kernel, plain(kron, a_turned, ps), [((NT * ROWS, NV * CHUNK), 0)])
-    c, hc = call(
+    c, hc, f_hot, m_hot = call(
         middle_kernel,
-        scalars + [(b, SIX), (source, SIX)] + late(ps) + plain(bup, bdown) + [last_variable] + late(q4)
+        scalars + [(b, SIX), (source, SIX)] + late(ps) + plain(bup, bdown) + [last_variable] + late(q4, ff, mf)
         + plain(g),
-        [(FLUID, 0), ((CH, ROWS, SPAN), 0)],
+        [(FLUID, 0), ((CH, ROWS, SPAN), 0), ((SPAN, NF), 0, BF16), ((MSPAN, NF), 0, BF16)],
         scratch=[pltpu.VMEM((3, NV, ROWS, SPAN), F32)],
         flops=LONG,
     )
     v, metal, mup, mdown, e1 = call(
         second_kernel,
-        scalars[:1] + plain(q_turned, g, kron, ps, metal, coeff, ff, mf, hc),
+        scalars[:1] + plain(q_turned, g, kron, ps, metal, coeff, ff, mf, hc, f_hot, m_hot),
         [(BLOCKS, 3), (METAL, 1), ((CH, MSPAN), 1), ((CH, MSPAN), 1), (ONE, 1)],
     )
     v = turn(v)

time: 79.8 us -> 84.6 us (1.060)
  local copies, waits for them, and re-layouts: 3.94 us -> 11.4 us
  waiting for transfers between devices: 28.7 us -> 24.9 us
  Pallas kernels: 23 us -> 23.9 us
    all_to_all x3, waiting for transfers between devices: 27 us -> 18.2 us  [turn(): return lax.all_to_all(x, 'inst', 0, 0, tiled=True)]
    unnamed x48 -> x74, local copies, waits for them, and re-layouts: 3.94 us -> 11.4 us
    ppermute x3, waiting for transfers between devices: 1.67 us -> 6.7 us  [exchange(): lax.ppermute(up, 'space', forward)]
    pallas_call x8 -> x9, Pallas kernels: 23 us -> 23.9 us  [call(): pl.pallas_call(kernel, out_shape=[pltpu.HBM(dims, F32) if n else jax.Shap...]
where the time goes in v10:
time: 84.6 us; the launch traced here: 84 us
  waiting for transfers between devices  24.9 us (29%)
  Pallas kernels  23.9 us (28%)
  starting transfers between devices  22.6 us (27%)
  local copies, waits for them, and re-layouts  11.4 us (13%)
  between operations  1.21 us (1%)
    pallas_call x9, Pallas kernels, call(): pl.pallas_call(kernel, out_shape=[pltpu.HBM(dims, F32) if n else jax.Shap...  23.9 us
    all_to_all x3, waiting for transfers between devices, turn(): return lax.all_to_all(x, 'inst', 0, 0, tiled=True)  18.2 us
    all_to_all x3, starting transfers between devices, turn(): return lax.all_to_all(x, 'inst', 0, 0, tiled=True)  12.6 us
    unnamed x74, local copies, waits for them, and re-layouts  11.4 us
    ppermute x3, starting transfers between devices, exchange(): lax.ppermute(down, 'space', back)  9.32 us
    ppermute x3, waiting for transfers between devices, exchange(): lax.ppermute(up, 'space', forward)  6.7 us
  transfers between devices with their start and end apart: 9, of which 4 were waited for; matrix products, arithmetic and copies ran while one was open for 0% of the time, Pallas kernels for 20%

profile of v10, /device:TPU:112, one launch (start us, length us, event | category | flops | bytes accessed | tf_op | source)
XLA Modules:
  0.0 84.0 jit_solution(14546208352835412806)
XLA Ops:
  0.7 2.3 %shard_map.131 = (f32[17,8,512]{2,1,0:T(8,128)}, f32[17,8,512]{2,1,0:T(8,128)}, f32[6,5,8,1024]{3,2,1,0:T(8,128)S(1)}, f32[8,1024]{1,0:T(8,128)S(1)}) custom-call(f32[6,5,8,1024]{3,2,1,0:T(8,128)} %refs_8_.1, f32[8,1024]{1,0:T(8,128)} %refs_4_.5, f32[8,8,512]{2,1,0:T(8,128)} %bitcast.5), custom_call_target="tpu_custom_call" | custom-call | flops 1048576 | bytes 1048576 | tf_op jit(solution)/shard_map/pallas_call | solution.py:173
  3.1 3.2 %collective-permute-start.1 = (f32[17,8,512]{2,1,0:T(8,128)}, f32[17,8,512]{2,1,0:T(8,128)}, u32[]{:S(2)}, u32[]{:S(2)}) collective-permute-start(f32[17,8,512]{2,1,0:T(8,128)} %get-tuple-element.36), channel_id=1, source_target_pairs={{1,0},{2,1},{3,2},{4,3},{5,4},{6,5},{7,6},{8,7},{9,8},{10,9},{11,1... | collective-permute-start | bytes 835592 | tf_op jit(solution)/shard_map/ppermute | solution.py:629
  6.3 3.8 %shard_map.132 = (f32[4,5,8,1024]{3,2,1,0:T(8,128)}, f32[4,5,8,1024]{3,2,1,0:T(8,128)}, f32[8,6,5,8,128]{4,3,2,1,0:T(8,128)}) custom-call(f32[5,5]{1,0:T(8,128)S(1)} %copy-done.22, f32[5,5]{1,0:T(8,128)S(1)} %copy-done.24, f32[6,5,8,1024]{3,2,1,0:T(8,128)S(1)} %get-tuple-element.28.refs_2_, f32[6,5,8,1024]{3,2,1,0:T(8,128)S(1)} %copy-done.5, ...), custom_call_target="tpu_custom_call" | custom-call | flops 1048576 | bytes 1048576 | tf_op jit(solution)/shard_map/pallas_call | solution.py:173
  10.2 5.2 %all-to-all-start.1 = ((f32[8,6,5,8,128]{4,3,2,1,0:T(8,128)}), f32[8,6,5,8,128]{4,3,2,1,0:T(8,128)S(1)}, u32[]{:S(2)}, u32[]{:S(2)}) async-start(f32[8,6,5,8,128]{4,3,2,1,0:T(8,128)} %get-tuple-element.32.refs_5_), calls=%async_computation.1 | async-start | bytes 1966080 | tf_op jit(solution)/shard_map/all_to_all | solution.py:633
  15.4 1.7 %shard_map.133 = (f32[2,5,8,1024]{3,2,1,0:T(8,128)S(1)}, f32[2,5,8,1024]{3,2,1,0:T(8,128)S(1)}) custom-call(f32[5,5]{1,0:T(8,128)S(1)} %copy-done.22, f32[5,5]{1,0:T(8,128)S(1)} %copy-done.24, f32[6,5,8,1024]{3,2,1,0:T(8,128)S(1)} %copy-done, f32[6,5,8,1024]{3,2,1,0:T(8,128)S(1)} %copy-done.5, f32[8,1024]{1,0:T(8,128)S(1)} %copy-done.10, ...), custom_call_target="tpu_custom_call" | custom-call | flops 68719476736 | bytes 1048576 | tf_op jit(solution)/shard_map/pallas_call | solution.py:173
  17.2 1.3 %shard_map.134.refs_8_ = f32[6,8,1024]{2,1,0:T(8,128)S(1)} custom-call(f32[1536]{0:T(1024)S(1)} %copy-done.19, f32[8,8,512]{2,1,0:T(8,128)S(1)} %bitcast.6, f32[1,512]{1,0:T(1,128)S(1)} %bitcast.8, s32[1,512]{1,0:T(1,128)S(1)} %bitcast.12, s32[1,512]{1,0:T(1,128)S(1)} %bitcast.16, f32[8,6,5,8,128]{4,3,2,1,0:T(8,128)} %get-tuple-element.32.refs_5_), custom_call_target="tpu_custom_call" | custom-call | flops 68719476736 | bytes 1048576 | tf_op jit(solution)/shard_map/pallas_call | solution.py:173
  18.6 4.3 %shard_map.135 = (f32[8,34,8,128]{3,2,1,0:T(8,128)}, f32[6,5,8,1024]{3,2,1,0:T(8,128)}, f32[17,8,512]{2,1,0:T(8,128)}, f32[17,8,512]{2,1,0:T(8,128)}, f32[6,8,1024]{2,1,0:T(8,128)}, /*index=5*/f32[8,8,512]{2,1,0:T(8,128)}) custom-call(f32[1536]{0:T(1024)S(1)} %copy-done.19, f32[5,5]{1,0:T(8,128)S(1)} %copy-done.22, f32[5,5]{1,0:T(8,128)S(1)} %copy-done.24, ...), custom_call_target="tpu_custom_call" | custom-call | flops 1048576 | bytes 1048576 | tf_op jit(solution)/shard_map/pallas_call | solution.py:173
  23.4 2.8 %collective-permute-start.3 = (f32[17,8,512]{2,1,0:T(8,128)}, f32[17,8,512]{2,1,0:T(8,128)}, u32[]{:S(2)}, u32[]{:S(2)}) collective-permute-start(f32[17,8,512]{2,1,0:T(8,128)} %get-tuple-element.41), channel_id=1, source_target_pairs={{1,0},{2,1},{3,2},{4,3},{5,4},{6,5},{7,6},{8,7},{9,8},{10,9},{11,1... | collective-permute-start | bytes 835592 | tf_op jit(solution)/shard_map/ppermute | solution.py:629
  26.3 6.5 %all-to-all-done.1.refs_1_ = f32[8,6,5,8,128]{4,3,2,1,0:T(8,128)S(1)} async-done(((f32[8,6,5,8,128]{4,3,2,1,0:T(8,128)}), f32[8,6,5,8,128]{4,3,2,1,0:T(8,128)S(1)}, u32[]{:S(2)}, u32[]{:S(2)}) %all-to-all-start.1) | async-done | bytes 983072 | tf_op jit(solution)/shard_map/all_to_all | solution.py:633
  32.8 3.7 %all-to-all-start = ((f32[8,34,8,128]{3,2,1,0:T(8,128)}), f32[8,34,8,128]{3,2,1,0:T(8,128)S(1)}, u32[]{:S(2)}, u32[]{:S(2)}) async-start(f32[8,34,8,128]{3,2,1,0:T(8,128)} %get-tuple-element.37), calls=%async_computation | async-start | bytes 2228224 | tf_op jit(solution)/shard_map/all_to_all | solution.py:633
  36.6 1.2 %copy-done.1 = bf16[384,1152]{1,0:T(8,128)(2,1)S(1)} copy-done((bf16[384,1152]{1,0:T(8,128)(2,1)S(1)}, bf16[384,1152]{1,0:T(8,128)(2,1)}, u32[]{:S(2)}) %copy-start.1) | copy-done | bytes 884760
  39.4 0.9 %copy-done.34 = f32[17,8,512]{2,1,0:T(8,128)S(1)} copy-done((f32[17,8,512]{2,1,0:T(8,128)S(1)}, f32[17,8,512]{2,1,0:T(8,128)}, u32[]{:S(2)}) %copy-start.34) | copy-done | bytes 278552
  40.4 4.8 %shard_map.137 = (f32[6,5,8,1024]{3,2,1,0:T(8,128)S(1)}, f32[8,8,1024]{2,1,0:T(8,128)S(1)}, bf16[1024,512]{1,0:T(8,128)(2,1)S(1)}, bf16[512,512]{1,0:T(8,128)(2,1)S(1)}) custom-call(f32[1536]{0:T(1024)S(1)} %copy-done.20, f32[5,5]{1,0:T(8,128)S(1)} %copy-done.23, f32[5,5]{1,0:T(8,128)S(1)} %copy-done.25, f32[6,5,8,1024]{3,2,1,0:T(8,128)} %get-tuple-element.39.refs_3_, ...), custom_call_target="tpu_custom_call" | custom-call | flops 68719476736 | bytes 1048576 | tf_op jit(solution)/shard_map/pallas_call | solution.py:173
  45.2 1.0 %copy-done.3 = bf16[1024,512]{1,0:T(8,128)(2,1)} copy-done((bf16[1024,512]{1,0:T(8,128)(2,1)}, bf16[1024,512]{1,0:T(8,128)(2,1)S(1)}, u32[]{:S(2)}) %copy-start.3) | copy-done | bytes 1048600
  46.2 0.9 %copy-done.6 = f32[6,5,8,1024]{3,2,1,0:T(8,128)} copy-done((f32[6,5,8,1024]{3,2,1,0:T(8,128)}, f32[6,5,8,1024]{3,2,1,0:T(8,128)S(1)}, u32[]{:S(2)}) %copy-start.6) | copy-done | bytes 983064
  47.8 4.8 %all-to-all-done.refs_1_ = f32[8,34,8,128]{3,2,1,0:T(8,128)S(1)} async-done(((f32[8,34,8,128]{3,2,1,0:T(8,128)}), f32[8,34,8,128]{3,2,1,0:T(8,128)S(1)}, u32[]{:S(2)}, u32[]{:S(2)}) %all-to-all-start) | async-done | bytes 1114144 | tf_op jit(solution)/shard_map/all_to_all | solution.py:633
  52.7 1.2 %copy-done.4 = bf16[1024,512]{1,0:T(8,128)(2,1)S(1)} copy-done((bf16[1024,512]{1,0:T(8,128)(2,1)S(1)}, bf16[1024,512]{1,0:T(8,128)(2,1)}, u32[]{:S(2)}) %copy-start.4) | copy-done | bytes 1048600
  53.9 0.9 %copy-done.14 = f32[8,8,1024]{2,1,0:T(8,128)S(1)} copy-done((f32[8,8,1024]{2,1,0:T(8,128)S(1)}, f32[8,8,1024]{2,1,0:T(8,128)}, u32[]{:S(2)}) %copy-start.14) | copy-done | bytes 262168
  58.5 3.3 %shard_map.138 = (f32[8,34,8,128]{3,2,1,0:T(8,128)}, f32[8,8,512]{2,1,0:T(8,128)}, f32[8,512]{1,0:T(8,128)}, f32[8,512]{1,0:T(8,128)}, f32[6,8,1024]{2,1,0:T(8,128)}) custom-call(f32[1536]{0:T(1024)S(1)} %copy-done.21, f32[8,34,8,128]{3,2,1,0:T(8,128)S(1)} %all-to-all-done.refs_1_, f32[384,640]{1,0:T(8,128)S(1)} %shard_map.136.refs_12_.refs_2_, ...), custom_call_target="tpu_custom_call" | custom-call | flops 1048576 | bytes 1048576 | tf_op jit(solution)/shard_map/pallas_call | solution.py:173
  61.9 3.7 %all-to-all-start.2 = ((f32[8,34,8,128]{3,2,1,0:T(8,128)}), f32[8,34,8,128]{3,2,1,0:T(8,128)S(1)}, u32[]{:S(2)}, u32[]{:S(2)}) async-start(f32[8,34,8,128]{3,2,1,0:T(8,128)} %get-tuple-element.46), calls=%async_computation.2 | async-start | bytes 2228224 | tf_op jit(solution)/shard_map/all_to_all | solution.py:633
  65.7 3.2 %collective-permute-start.5 = (f32[8,512]{1,0:T(8,128)S(1)}, f32[8,512]{1,0:T(8,128)S(1)}, u32[]{:S(2)}, u32[]{:S(2)}) collective-permute-start(f32[8,512]{1,0:T(8,128)S(1)} %copy-done.35), channel_id=1, source_target_pairs={{1,0},{2,1},{3,2},{4,3},{5,4},{6,5},{7,6},{8,7},{9,8},{10,9},{11,1... | collective-permute-start | bytes 49160 | tf_op jit(solution)/shard_map/ppermute | solution.py:629
  68.9 6.7 %collective-permute-done.4.refs_4_ = f32[8,512]{1,0:T(8,128)S(1)} collective-permute-done((f32[8,512]{1,0:T(8,128)S(1)}, f32[8,512]{1,0:T(8,128)S(1)}, u32[]{:S(2)}, u32[]{:S(2)}) %collective-permute-start.4) | collective-permute-done | bytes 16416 | tf_op jit(solution)/shard_map/ppermute | solution.py:629
  75.6 6.8 %all-to-all-done.2.refs_0_ = f32[8,34,8,128]{3,2,1,0:T(8,128)S(1)} async-done(((f32[8,34,8,128]{3,2,1,0:T(8,128)}), f32[8,34,8,128]{3,2,1,0:T(8,128)S(1)}, u32[]{:S(2)}, u32[]{:S(2)}) %all-to-all-start.2) | async-done | bytes 1114144 | tf_op jit(solution)/shard_map/all_to_all | solution.py:633
  82.5 1.3 %shard_map.139 = (f32[6,5,8,1024]{3,2,1,0:T(8,128)}, f32[8,8,512]{2,1,0:T(8,128)}) custom-call(f32[8,34,8,128]{3,2,1,0:T(8,128)S(1)} %all-to-all-done.2.refs_0_, f32[6,5,8,1024]{3,2,1,0:T(8,128)S(1)} %copy-done.7, f32[6,8,1024]{2,1,0:T(8,128)S(1)} %copy-done.15, f32[8,8,512]{2,1,0:T(8,128)S(1)} %copy-done.16, f32[8,512]{1,0:T(8,128)S(1)} %collective-permute-done.4.refs_4_, ...), custom_call_target="tpu_custom_call" | custom-call | flops 1048576 | bytes 1048576 | tf_op jit(solution)/shard_map/pallas_call | solution.py:173
  (77 shorter events, 6.8 us)
Async XLA Ops:
  0.6 5.7 %copy-start.24 = (f32[5,5]{1,0:T(8,128)S(1)}, f32[5,5]{1,0:T(8,128)}, u32[]{:S(2)}) copy-start(f32[5,5]{1,0:T(8,128)} %refs_2_.7) | copy-start | bytes 304
  0.6 5.7 %copy-start.22 = (f32[5,5]{1,0:T(8,128)S(1)}, f32[5,5]{1,0:T(8,128)}, u32[]{:S(2)}) copy-start(f32[5,5]{1,0:T(8,128)} %refs_1_.9) | copy-start | bytes 304
  0.7 5.7 %copy-start.5 = (f32[6,5,8,1024]{3,2,1,0:T(8,128)S(1)}, f32[6,5,8,1024]{3,2,1,0:T(8,128)}, u32[]{:S(2)}) copy-start(f32[6,5,8,1024]{3,2,1,0:T(8,128)} %refs_4_.4) | copy-start | bytes 2949124
  3.0 15.6 %collective-permute-start = (f32[17,8,512]{2,1,0:T(8,128)}, f32[17,8,512]{2,1,0:T(8,128)S(1)}, u32[]{:S(2)}, u32[]{:S(2)}) collective-permute-start(f32[17,8,512]{2,1,0:T(8,128)} %get-tuple-element.35), channel_id=1, source_target_pairs={{0,1},{1,2},{2,3},{3,4},{4,5},{5,6},{6,7},{7,8},{8,9},{9,10},{10,1... | collective-permute-start | bytes 835592 | tf_op jit(solution)/shard_map/ppermute | solution.py:629
  3.1 15.5 %collective-permute-start.1 = (f32[17,8,512]{2,1,0:T(8,128)}, f32[17,8,512]{2,1,0:T(8,128)}, u32[]{:S(2)}, u32[]{:S(2)}) collective-permute-start(f32[17,8,512]{2,1,0:T(8,128)} %get-tuple-element.36), channel_id=1, source_target_pairs={{1,0},{2,1},{3,2},{4,3},{5,4},{6,5},{7,6},{8,7},{9,8},{10,9},{11,1... | collective-permute-start | bytes 835592 | tf_op jit(solution)/shard_map/ppermute | solution.py:629
  10.2 5.2 %copy-start = (f32[6,5,8,1024]{3,2,1,0:T(8,128)S(1)}, f32[6,5,8,1024]{3,2,1,0:T(8,128)}, u32[]{:S(2)}) copy-start(f32[6,5,8,1024]{3,2,1,0:T(8,128)} %refs_8_.1) | copy-start | bytes 2949124
  10.2 5.2 %copy-start.10 = (f32[8,1024]{1,0:T(8,128)S(1)}, f32[8,1024]{1,0:T(8,128)}, u32[]{:S(2)}) copy-start(f32[8,1024]{1,0:T(8,128)} %refs_4_.5) | copy-start | bytes 98308
  10.2 22.6 %all-to-all-start.1 = ((f32[8,6,5,8,128]{4,3,2,1,0:T(8,128)}), f32[8,6,5,8,128]{4,3,2,1,0:T(8,128)S(1)}, u32[]{:S(2)}, u32[]{:S(2)}) async-start(f32[8,6,5,8,128]{4,3,2,1,0:T(8,128)} %get-tuple-element.32.refs_5_), calls=%async_computation.1 | async-start | bytes 1966080 | tf_op jit(solution)/shard_map/all_to_all | solution.py:633
  15.4 1.8 %copy-start.12 = (f32[2,4,8,512]{3,2,1,0:T(8,128)S(1)}, f32[2,4,8,512]{3,2,1,0:T(8,128)}, u32[]{:S(2)}) copy-start(f32[2,4,8,512]{3,2,1,0:T(8,128)} %param.17) | copy-start | bytes 393220
  15.4 1.8 %copy-start.19 = (f32[1536]{0:T(1024)S(1)}, f32[1536]{0:T(1024)}, u32[]{:S(2)}) copy-start(f32[1536]{0:T(1024)} %constant.5.clone.refs_0_) | copy-start | bytes 18436
  23.0 15.7 %collective-permute-start.2 = (f32[17,8,512]{2,1,0:T(8,128)}, f32[17,8,512]{2,1,0:T(8,128)S(1)}, u32[]{:S(2)}, u32[]{:S(2)}) collective-permute-start(f32[17,8,512]{2,1,0:T(8,128)} %get-tuple-element.40), channel_id=1, source_target_pairs={{0,1},{1,2},{2,3},{3,4},{4,5},{5,6},{6,7},{7,8},{8,9},{9,10},{10,1... | collective-permute-start | bytes 835592 | tf_op jit(solution)/shard_map/ppermute | solution.py:629
  23.4 15.9 %collective-permute-start.3 = (f32[17,8,512]{2,1,0:T(8,128)}, f32[17,8,512]{2,1,0:T(8,128)}, u32[]{:S(2)}, u32[]{:S(2)}) collective-permute-start(f32[17,8,512]{2,1,0:T(8,128)} %get-tuple-element.41), channel_id=1, source_target_pairs={{1,0},{2,1},{3,2},{4,3},{5,4},{6,5},{7,6},{8,7},{9,8},{10,9},{11,1... | collective-permute-start | bytes 835592 | tf_op jit(solution)/shard_map/ppermute | solution.py:629
  32.8 19.9 %all-to-all-start = ((f32[8,34,8,128]{3,2,1,0:T(8,128)}), f32[8,34,8,128]{3,2,1,0:T(8,128)S(1)}, u32[]{:S(2)}, u32[]{:S(2)}) async-start(f32[8,34,8,128]{3,2,1,0:T(8,128)} %get-tuple-element.37), calls=%async_computation | async-start | bytes 2228224 | tf_op jit(solution)/shard_map/all_to_all | solution.py:633
  40.4 12.3 %copy-start.2 = (bf16[384,1152]{1,0:T(8,128)(2,1)S(1)}, bf16[384,1152]{1,0:T(8,128)(2,1)}, u32[]{:S(2)}) copy-start(bf16[384,1152]{1,0:T(8,128)(2,1)} %constant.4.clone.refs_0_.refs_3_) | copy-start | bytes 2654212
  40.4 12.3 %copy-start.11 = (f32[8,1024]{1,0:T(8,128)S(1)}, f32[8,1024]{1,0:T(8,128)}, u32[]{:S(2)}) copy-start(f32[8,1024]{1,0:T(8,128)} %refs_4_.5) | copy-start | bytes 98308
  61.8 3.8 %copy-start.36 = (f32[8,512]{1,0:T(8,128)S(1)}, f32[8,512]{1,0:T(8,128)}, u32[]{:S(2)}) copy-start(f32[8,512]{1,0:T(8,128)} %get-tuple-element.50) | copy-start | bytes 49156
  61.8 3.9 %copy-start.35 = (f32[8,512]{1,0:T(8,128)S(1)}, f32[8,512]{1,0:T(8,128)}, u32[]{:S(2)}) copy-start(f32[8,512]{1,0:T(8,128)} %get-tuple-element.51) | copy-start | bytes 49156
  61.8 20.6 %copy-start.7 = (f32[6,5,8,1024]{3,2,1,0:T(8,128)S(1)}, f32[6,5,8,1024]{3,2,1,0:T(8,128)}, u32[]{:S(2)}) copy-start(f32[6,5,8,1024]{3,2,1,0:T(8,128)} %copy-done.6) | copy-start | bytes 2949124
  61.8 20.6 %copy-start.15 = (f32[6,8,1024]{2,1,0:T(8,128)S(1)}, f32[6,8,1024]{2,1,0:T(8,128)}, u32[]{:S(2)}) copy-start(f32[6,8,1024]{2,1,0:T(8,128)} %get-tuple-element.48.refs_2_) | copy-start | bytes 589828
  61.8 20.6 %copy-start.16 = (f32[8,8,512]{2,1,0:T(8,128)S(1)}, f32[8,8,512]{2,1,0:T(8,128)}, u32[]{:S(2)}) copy-start(f32[8,8,512]{2,1,0:T(8,128)} %get-tuple-element.49.refs_3_) | copy-start | bytes 393220
  61.8 20.6 %copy-start.32 = (s32[512]{0:T(512)S(1)}, s32[512]{0:T(512)}, u32[]{:S(2)}) copy-start(s32[512]{0:T(512)} %param.21) | copy-start | bytes 6148
  61.9 20.6 %all-to-all-start.2 = ((f32[8,34,8,128]{3,2,1,0:T(8,128)}), f32[8,34,8,128]{3,2,1,0:T(8,128)S(1)}, u32[]{:S(2)}, u32[]{:S(2)}) async-start(f32[8,34,8,128]{3,2,1,0:T(8,128)} %get-tuple-element.46), calls=%async_computation.2 | async-start | bytes 2228224 | tf_op jit(solution)/shard_map/all_to_all | solution.py:633
  65.6 10.0 %collective-permute-start.4 = (f32[8,512]{1,0:T(8,128)S(1)}, f32[8,512]{1,0:T(8,128)S(1)}, u32[]{:S(2)}, u32[]{:S(2)}) collective-permute-start(f32[8,512]{1,0:T(8,128)S(1)} %copy-done.36), channel_id=1, source_target_pairs={{0,1},{1,2},{2,3},{3,4},{4,5},{5,6},{6,7},{7,8},{8,9},{9,10},{10,1... | collective-permute-start | bytes 49160 | tf_op jit(solution)/shard_map/ppermute | solution.py:629
  65.7 9.9 %collective-permute-start.5 = (f32[8,512]{1,0:T(8,128)S(1)}, f32[8,512]{1,0:T(8,128)S(1)}, u32[]{:S(2)}, u32[]{:S(2)}) collective-permute-start(f32[8,512]{1,0:T(8,128)S(1)} %copy-done.35), channel_id=1, source_target_pairs={{1,0},{2,1},{3,2},{4,3},{5,4},{6,5},{7,6},{8,7},{9,8},{10,9},{11,1... | collective-permute-start | bytes 49160 | tf_op jit(solution)/shard_map/ppermute | solution.py:629
  (22 other events, 25.7 us)

commit v11 on v10

--- a/solution.py
+++ b/solution.py
@@ -390,11 +390,14 @@
 
 
 def first_kernel(
-    tab_ref, jx_ref, jz_ref, a_ref, b0_ref, q0_ref, b1_ref, q1_ref, e_ref, ps_ref, up_ref, down_ref, fc_ref, ff_ref, m_ref, cond_ref,
-    q, b_out, bup, bdown, q4, m_out,
+    tab_ref, jx_ref, jz_ref, a_ref, b0_ref, q0_ref, b1_ref, q1_ref, e_ref, ps_ref, up_ref, down_ref, fc_ref, ff_ref,
+    q, b_out, bup, bdown, q4, mup, mdown,
 ):
     first = lax.axis_index("inst") * 6
     step = ps_ref[...]
+    mup.buffer[...], mdown.buffer[...] = up_ref[16], down_ref[16]
+    mup.put(slice(None))
+    mdown.put(slice(None))
     q_ref, b_ref = q.buffer, b_out.buffer
     sign = jnp.where(row_index(512) == 0, 0.5, -0.5)
     step_edges = []
@@ -450,11 +453,6 @@
         for k in range(4):
             q_ref[i, 30 + k] = values[:, k * CHUNK : (k + 1) * CHUNK]
     q.put((slice(None), pl.ds(30, 4)))
-    before, after = metal_sides(up_ref.at[16], down_ref.at[16])
-    m = metal_update(m_ref, before, after, cond_ref[...])
-    for ch in range(CH):
-        m_out.buffer[ch] = m[ch]
-    m_out.put(slice(None))
 
 
 def rotate_time(kron, x):
@@ -486,8 +484,8 @@
 
 
 def middle_kernel(
-    tab_ref, jx_ref, jz_ref, b_in, s_in, ps_ref, up_ref, down_ref, a_ref, q4_ref, ff_ref, mf_ref, g_ref,
-    c_out, hc, f_hot, m_hot,
+    tab_ref, jx_ref, jz_ref, b_in, s_in, ps_ref, up_ref, down_ref, a_ref, q4_ref, m_ref, mup_ref, mdown_ref, cond_ref, g_ref,
+    c_out, hc, m_out,
     parts,
 ):
     first = lax.axis_index("inst") * 6
@@ -516,8 +514,10 @@
             h3 += tab_ref[W2 + at] * a_ref[t, NV - 1]
         hc.buffer[ch] = h0 + step * (step * h3 - h2)
     hc.put(slice(None))
-    f_hot.buffer[...] = fluid_hots(ff_ref)[0]
-    m_hot.buffer[...] = metal_hots(mf_ref)[0]
+    before, after = metal_sides(mup_ref, mdown_ref)
+    m = metal_update(m_ref, before, after, cond_ref[...])
+    for ch in range(CH):
+        m_out.buffer[ch] = m[ch]
 
 
 def metal_update(m, before, after, cond):
@@ -557,7 +557,7 @@
 
 
 def second_kernel(
-    tab_ref, q_ref, g_ref, kron_ref, ps_ref, m_ref, fc_ref, ff_ref, mf_ref, hc_ref, f_hot_ref, m_hot_ref,
+    tab_ref, q_ref, g_ref, kron_ref, ps_ref, m_ref, fc_ref, ff_ref, mf_ref, hc_ref,
     v, m_out, mup, mdown, e,
 ):
     first = lax.axis_index("inst") * 6
@@ -575,11 +575,11 @@
         v.put((pl.ds(half * 4, 4), pl.ds(0, 30)))
     step = ps_ref[...]
     coeff = fc_ref[...]
-    m_hot, m_row = m_hot_ref[...], rows_of(mf_ref, 9)
+    m_hot, m_row = metal_hots(mf_ref)
     source = onto_cells(heat_sum(lambda j, k: q_ref[j, 30 + k]), m_hot, m_row)
     m = [m_ref[ch] + metal_step * source[ch] for ch in range(CH)]
     values = at_faces(jnp.stack(m), m_hot, m_row) * coeff
-    f_hot, f_row = f_hot_ref[...], rows_of(ff_ref, 10)
+    f_hot, f_row = fluid_hots(ff_ref)
     cells = onto_cells(values, f_hot, f_row)
     for ch in range(CH):
         m_out.buffer[ch] = m[ch]
@@ -690,25 +690,25 @@
         flops=LONG,
     )
     a_turned = turn(blocks)
-    q, b, bup, bdown, q4, metal = call(
+    q, b, bup, bdown, q4, mup, mdown = call(
         first_kernel,
-        scalars + [last_variable] + plain(b, q, b_late, q_late, e0, ps, up, down, coeff, ff, metal, cond),
-        [(BLOCKS, 7), (FLUID, 6), (EDGES, 1), (EDGES, 1), (ONE, 1), (METAL, 1)],
+        scalars + [last_variable] + plain(b, q, b_late, q_late, e0, ps, up, down, coeff, ff),
+        [(BLOCKS, 7), (FLUID, 6), (EDGES, 1), (EDGES, 1), (ONE, 1), ((CH, MSPAN), 1), ((CH, MSPAN), 1)],
     )
     q_turned = turn(q)
     bup, bdown = exchange(bup, bdown)
     (g,) = call(derive_kernel, plain(kron, a_turned, ps), [((NT * ROWS, NV * CHUNK), 0)])
-    c, hc, f_hot, m_hot = call(
+    c, hc, metal = call(
         middle_kernel,
-        scalars + [(b, SIX), (source, SIX)] + late(ps) + plain(bup, bdown) + [last_variable] + late(q4, ff, mf)
+        scalars + [(b, SIX), (source, SIX)] + late(ps) + plain(bup, bdown) + [last_variable] + late(q4, metal, mup, mdown, cond)
         + plain(g),
-        [(FLUID, 0), ((CH, ROWS, SPAN), 0), ((SPAN, NF), 0, BF16), ((MSPAN, NF), 0, BF16)],
+        [(FLUID, 0), ((CH, ROWS, SPAN), 0), (METAL, 0)],
         scratch=[pltpu.VMEM((3, NV, ROWS, SPAN), F32)],
         flops=LONG,
     )
     v, metal, mup, mdown, e1 = call(
         second_kernel,
-        scalars[:1] + plain(q_turned, g, kron, ps, metal, coeff, ff, mf, hc, f_hot, m_hot),
+        scalars[:1] + plain(q_turned, g, kron, ps, metal, coeff, ff, mf, hc),
         [(BLOCKS, 3), (METAL, 1), ((CH, MSPAN), 1), ((CH, MSPAN), 1), (ONE, 1)],
     )
     v = turn(v)

time: 84.6 us -> 78.2 us (0.924)
  local copies, waits for them, and re-layouts: 11.4 us -> 3.87 us
  waiting for transfers between devices: 24.9 us -> 26 us
    unnamed x74 -> x48, local copies, waits for them, and re-layouts: 11.4 us -> 3.87 us
    all_to_all x3, waiting for transfers between devices: 18.2 us -> 19.2 us  [turn(): return lax.all_to_all(x, 'inst', 0, 0, tiled=True)]
  transfers between devices with their start and end apart: 9 -> 9, of which waited for: 4 -> 4; matrix products, arithmetic and copies ran while one was open for 0% -> 0% of each run, Pallas kernels for 20% -> 22%
where the time goes in v11:
time: 78.2 us; the launch traced here: 77.7 us
  waiting for transfers between devices  26 us (33%)
  Pallas kernels  24.1 us (31%)
  starting transfers between devices  22.6 us (29%)
  local copies, waits for them, and re-layouts  3.87 us (5%)
  between operations  1.17 us (1%)
    pallas_call x9, Pallas kernels, call(): pl.pallas_call(kernel, out_shape=[pltpu.HBM(dims, F32) if n else jax.Shap...  24.1 us
    all_to_all x3, waiting for transfers between devices, turn(): return lax.all_to_all(x, 'inst', 0, 0, tiled=True)  19.2 us
    all_to_all x3, starting transfers between devices, turn(): return lax.all_to_all(x, 'inst', 0, 0, tiled=True)  12.6 us
    ppermute x3, starting transfers between devices, exchange(): lax.ppermute(down, 'space', back)  9.32 us
    ppermute x3, waiting for transfers between devices, exchange(): lax.ppermute(up, 'space', forward)  6.8 us
    unnamed x48, local copies, waits for them, and re-layouts  3.87 us
  transfers between devices with their start and end apart: 9, of which 4 were waited for; matrix products, arithmetic and copies ran while one was open for 0% of the time, Pallas kernels for 22%

profile of v11, /device:TPU:112, one launch (start us, length us, event | category | flops | bytes accessed | tf_op | source)
XLA Modules:
  0.0 77.7 jit_solution(10511843078073953866)
XLA Ops:
  0.7 2.3 %shard_map.131 = (f32[17,8,512]{2,1,0:T(8,128)}, f32[17,8,512]{2,1,0:T(8,128)}, f32[6,5,8,1024]{3,2,1,0:T(8,128)S(1)}, f32[8,1024]{1,0:T(8,128)S(1)}) custom-call(f32[6,5,8,1024]{3,2,1,0:T(8,128)} %refs_8_.1, f32[8,1024]{1,0:T(8,128)} %refs_4_.5, f32[8,8,512]{2,1,0:T(8,128)} %bitcast.5), custom_call_target="tpu_custom_call" | custom-call | flops 1048576 | bytes 1048576 | tf_op jit(solution)/shard_map/pallas_call | solution.py:173
  3.1 3.2 %collective-permute-start.1 = (f32[17,8,512]{2,1,0:T(8,128)}, f32[17,8,512]{2,1,0:T(8,128)}, u32[]{:S(2)}, u32[]{:S(2)}) collective-permute-start(f32[17,8,512]{2,1,0:T(8,128)} %get-tuple-element.36), channel_id=1, source_target_pairs={{1,0},{2,1},{3,2},{4,3},{5,4},{6,5},{7,6},{8,7},{9,8},{10,9},{11,1... | collective-permute-start | bytes 835592 | tf_op jit(solution)/shard_map/ppermute | solution.py:629
  6.3 3.9 %shard_map.132 = (f32[4,5,8,1024]{3,2,1,0:T(8,128)}, f32[4,5,8,1024]{3,2,1,0:T(8,128)}, f32[8,6,5,8,128]{4,3,2,1,0:T(8,128)}) custom-call(f32[5,5]{1,0:T(8,128)S(1)} %copy-done.15, f32[5,5]{1,0:T(8,128)S(1)} %copy-done.16, f32[6,5,8,1024]{3,2,1,0:T(8,128)S(1)} %get-tuple-element.28.refs_2_, f32[6,5,8,1024]{3,2,1,0:T(8,128)S(1)} %copy-done.3, ...), custom_call_target="tpu_custom_call" | custom-call | flops 1048576 | bytes 1048576 | tf_op jit(solution)/shard_map/pallas_call | solution.py:173
  10.3 5.2 %all-to-all-start.1 = ((f32[8,6,5,8,128]{4,3,2,1,0:T(8,128)}), f32[8,6,5,8,128]{4,3,2,1,0:T(8,128)S(1)}, u32[]{:S(2)}, u32[]{:S(2)}) async-start(f32[8,6,5,8,128]{4,3,2,1,0:T(8,128)} %get-tuple-element.32.refs_5_), calls=%async_computation.1 | async-start | bytes 1966080 | tf_op jit(solution)/shard_map/all_to_all | solution.py:633
  15.5 1.7 %shard_map.133 = (f32[2,5,8,1024]{3,2,1,0:T(8,128)S(1)}, f32[2,5,8,1024]{3,2,1,0:T(8,128)S(1)}) custom-call(f32[5,5]{1,0:T(8,128)S(1)} %copy-done.15, f32[5,5]{1,0:T(8,128)S(1)} %copy-done.16, f32[6,5,8,1024]{3,2,1,0:T(8,128)S(1)} %copy-done, f32[6,5,8,1024]{3,2,1,0:T(8,128)S(1)} %copy-done.3, f32[8,1024]{1,0:T(8,128)S(1)} %copy-done.8, ...), custom_call_target="tpu_custom_call" | custom-call | flops 68719476736 | bytes 1048576 | tf_op jit(solution)/shard_map/pallas_call | solution.py:173
  17.3 1.4 %shard_map.134.refs_8_ = f32[6,8,1024]{2,1,0:T(8,128)S(1)} custom-call(f32[1536]{0:T(1024)S(1)} %copy-done.13, f32[8,8,512]{2,1,0:T(8,128)S(1)} %bitcast.7, f32[1,512]{1,0:T(1,128)S(1)} %bitcast.8, s32[1,512]{1,0:T(1,128)S(1)} %bitcast.11, s32[1,512]{1,0:T(1,128)S(1)} %bitcast.14, f32[8,6,5,8,128]{4,3,2,1,0:T(8,128)} %get-tuple-element.32.refs_5_), custom_call_target="tpu_custom_call" | custom-call | flops 68719476736 | bytes 1048576 | tf_op jit(solution)/shard_map/pallas_call | solution.py:173
  18.7 4.3 %shard_map.135 = (f32[8,34,8,128]{3,2,1,0:T(8,128)}, f32[6,5,8,1024]{3,2,1,0:T(8,128)}, f32[17,8,512]{2,1,0:T(8,128)}, f32[17,8,512]{2,1,0:T(8,128)}, f32[6,8,10...) custom-call(f32[1536]{0:T(1024)S(1)} %copy-done.13, f32[5,5]{1,0:T(8,128)S(1)} %copy-done.15, ...), custom_call_target="tpu_custom_call" | custom-call | flops 1048576 | bytes 1048576 | tf_op jit(solution)/shard_map/pallas_call | solution.py:173
  23.0 0.5 collective-permute-start.2
  23.5 2.8 %collective-permute-start.3 = (f32[17,8,512]{2,1,0:T(8,128)}, f32[17,8,512]{2,1,0:T(8,128)}, u32[]{:S(2)}, u32[]{:S(2)}) collective-permute-start(f32[17,8,512]{2,1,0:T(8,128)} %get-tuple-element.40), channel_id=1, source_target_pairs={{1,0},{2,1},{3,2},{4,3},{5,4},{6,5},{7,6},{8,7},{9,8},{10,9},{11,1... | collective-permute-start | bytes 835592 | tf_op jit(solution)/shard_map/ppermute | solution.py:629
  26.4 6.5 %all-to-all-done.1.refs_1_ = f32[8,6,5,8,128]{4,3,2,1,0:T(8,128)S(1)} async-done(((f32[8,6,5,8,128]{4,3,2,1,0:T(8,128)}), f32[8,6,5,8,128]{4,3,2,1,0:T(8,128)S(1)}, u32[]{:S(2)}, u32[]{:S(2)}) %all-to-all-start.1) | async-done | bytes 983072 | tf_op jit(solution)/shard_map/all_to_all | solution.py:633
  32.9 3.7 %all-to-all-start = ((f32[8,34,8,128]{3,2,1,0:T(8,128)}), f32[8,34,8,128]{3,2,1,0:T(8,128)S(1)}, u32[]{:S(2)}, u32[]{:S(2)}) async-start(f32[8,34,8,128]{3,2,1,0:T(8,128)} %get-tuple-element.37), calls=%async_computation | async-start | bytes 2228224 | tf_op jit(solution)/shard_map/all_to_all | solution.py:633
  36.6 1.2 %copy-done.1 = bf16[384,1152]{1,0:T(8,128)(2,1)S(1)} copy-done((bf16[384,1152]{1,0:T(8,128)(2,1)S(1)}, bf16[384,1152]{1,0:T(8,128)(2,1)}, u32[]{:S(2)}) %copy-start.1) | copy-done | bytes 884760
  37.8 0.9 %shard_map.136.refs_14_.refs_2_ = f32[384,640]{1,0:T(8,128)S(1)} custom-call(bf16[384,1152]{1,0:T(8,128)(2,1)S(1)} %copy-done.1, f32[8,6,5,8,128]{4,3,2,1,0:T(8,128)S(1)} %all-to-all-done.1.refs_1_, f32[8,1024]{1,0:T(8,128)S(1)} %copy-done.8), custom_call_target="tpu_custom_call" | custom-call | flops 1048576 | bytes 1048576 | tf_op jit(solution)/shard_map/pallas_call | solution.py:173
  38.7 0.7 copy-done.20
  39.4 1.0 %copy-done.21 = f32[17,8,512]{2,1,0:T(8,128)S(1)} copy-done((f32[17,8,512]{2,1,0:T(8,128)S(1)}, f32[17,8,512]{2,1,0:T(8,128)}, u32[]{:S(2)}) %copy-start.21) | copy-done | bytes 278552
  40.4 4.8 %shard_map.137 = (f32[6,5,8,1024]{3,2,1,0:T(8,128)S(1)}, f32[8,8,1024]{2,1,0:T(8,128)S(1)}, f32[8,8,512]{2,1,0:T(8,128)S(1)}) custom-call(f32[1536]{0:T(1024)S(1)} %copy-done.13, f32[5,5]{1,0:T(8,128)S(1)} %copy-done.15, f32[5,5]{1,0:T(8,128)S(1)} %copy-done.16, f32[6,5,8,1024]{3,2,1,0:T(8,128)} %get-tuple-element.38.refs_3_, f32[6,5,8,1024]{3,2,1,0:T(8,128)} %refs_4_.4, ...), custom_call_target="tpu_custom_call" | custom-call | flops 68719476736 | bytes 1048576 | tf_op jit(solution)/shard_map/pallas_call | solution.py:173
  45.3 0.9 %copy-done.4 = f32[6,5,8,1024]{3,2,1,0:T(8,128)} copy-done((f32[6,5,8,1024]{3,2,1,0:T(8,128)}, f32[6,5,8,1024]{3,2,1,0:T(8,128)S(1)}, u32[]{:S(2)}) %copy-start.4) | copy-done | bytes 983064
  46.2 6.4 %all-to-all-done.refs_1_ = f32[8,34,8,128]{3,2,1,0:T(8,128)S(1)} async-done(((f32[8,34,8,128]{3,2,1,0:T(8,128)}), f32[8,34,8,128]{3,2,1,0:T(8,128)S(1)}, u32[]{:S(2)}, u32[]{:S(2)}) %all-to-all-start) | async-done | bytes 1114144 | tf_op jit(solution)/shard_map/all_to_all | solution.py:633
  52.6 3.4 %shard_map.138 = (f32[8,34,8,128]{3,2,1,0:T(8,128)}, f32[8,8,512]{2,1,0:T(8,128)}, f32[8,512]{1,0:T(8,128)}, f32[8,512]{1,0:T(8,128)}, f32[6,8,1024]{2,1,0:T(8,128)}) custom-call(f32[1536]{0:T(1024)S(1)} %copy-done.13, f32[8,34,8,128]{3,2,1,0:T(8,128)S(1)} %all-to-all-done.refs_1_, f32[384,640]{1,0:T(8,128)S(1)} %shard_map.136.refs_14_.refs_2_, ...), custom_call_target="tpu_custom_call" | custom-call | flops 1048576 | bytes 1048576 | tf_op jit(solution)/shard_map/pallas_call | solution.py:173
  56.0 3.7 %all-to-all-start.2 = ((f32[8,34,8,128]{3,2,1,0:T(8,128)}), f32[8,34,8,128]{3,2,1,0:T(8,128)S(1)}, u32[]{:S(2)}, u32[]{:S(2)}) async-start(f32[8,34,8,128]{3,2,1,0:T(8,128)} %get-tuple-element.46), calls=%async_computation.2 | async-start | bytes 2228224 | tf_op jit(solution)/shard_map/all_to_all | solution.py:633
  59.8 3.2 %collective-permute-start.5 = (f32[8,512]{1,0:T(8,128)S(1)}, f32[8,512]{1,0:T(8,128)S(1)}, u32[]{:S(2)}, u32[]{:S(2)}) collective-permute-start(f32[8,512]{1,0:T(8,128)S(1)} %copy-done.22), channel_id=1, source_target_pairs={{1,0},{2,1},{3,2},{4,3},{5,4},{6,5},{7,6},{8,7},{9,8},{10,9},{11,1... | collective-permute-start | bytes 49160 | tf_op jit(solution)/shard_map/ppermute | solution.py:629
  63.1 6.8 %collective-permute-done.4.refs_4_ = f32[8,512]{1,0:T(8,128)S(1)} collective-permute-done((f32[8,512]{1,0:T(8,128)S(1)}, f32[8,512]{1,0:T(8,128)S(1)}, u32[]{:S(2)}, u32[]{:S(2)}) %collective-permute-start.4) | collective-permute-done | bytes 16416 | tf_op jit(solution)/shard_map/ppermute | solution.py:629
  69.9 6.3 %all-to-all-done.2.refs_0_ = f32[8,34,8,128]{3,2,1,0:T(8,128)S(1)} async-done(((f32[8,34,8,128]{3,2,1,0:T(8,128)}), f32[8,34,8,128]{3,2,1,0:T(8,128)S(1)}, u32[]{:S(2)}, u32[]{:S(2)}) %all-to-all-start.2) | async-done | bytes 1114144 | tf_op jit(solution)/shard_map/all_to_all | solution.py:633
  76.2 1.4 %shard_map.139 = (f32[6,5,8,1024]{3,2,1,0:T(8,128)}, f32[8,8,512]{2,1,0:T(8,128)}) custom-call(f32[8,34,8,128]{3,2,1,0:T(8,128)S(1)} %all-to-all-done.2.refs_0_, f32[6,5,8,1024]{3,2,1,0:T(8,128)S(1)} %copy-done.5, f32[6,8,1024]{2,1,0:T(8,128)S(1)} %copy-done.10, f32[8,8,512]{2,1,0:T(8,128)S(1)} %copy-done.12, f32[8,512]{1,0:T(8,128)S(1)} %collective-permute-done.4.refs_4_, ...), custom_call_target="tpu_custom_call" | custom-call | flops 1048576 | bytes 1048576 | tf_op jit(solution)/shard_map/pallas_call | solution.py:173
  (51 shorter events, 0.3 us)
Async XLA Ops:
  0.6 5.7 %copy-start.16 = (f32[5,5]{1,0:T(8,128)S(1)}, f32[5,5]{1,0:T(8,128)}, u32[]{:S(2)}) copy-start(f32[5,5]{1,0:T(8,128)} %refs_2_.7) | copy-start | bytes 304
  0.6 5.7 %copy-start.15 = (f32[5,5]{1,0:T(8,128)S(1)}, f32[5,5]{1,0:T(8,128)}, u32[]{:S(2)}) copy-start(f32[5,5]{1,0:T(8,128)} %refs_1_.9) | copy-start | bytes 304
  0.6 5.7 %copy-start.3 = (f32[6,5,8,1024]{3,2,1,0:T(8,128)S(1)}, f32[6,5,8,1024]{3,2,1,0:T(8,128)}, u32[]{:S(2)}) copy-start(f32[6,5,8,1024]{3,2,1,0:T(8,128)} %refs_4_.4) | copy-start | bytes 2949124
  3.0 15.6 %collective-permute-start = (f32[17,8,512]{2,1,0:T(8,128)}, f32[17,8,512]{2,1,0:T(8,128)S(1)}, u32[]{:S(2)}, u32[]{:S(2)}) collective-permute-start(f32[17,8,512]{2,1,0:T(8,128)} %get-tuple-element.35), channel_id=1, source_target_pairs={{0,1},{1,2},{2,3},{3,4},{4,5},{5,6},{6,7},{7,8},{8,9},{9,10},{10,1... | collective-permute-start | bytes 835592 | tf_op jit(solution)/shard_map/ppermute | solution.py:629
  3.1 15.6 %collective-permute-start.1 = (f32[17,8,512]{2,1,0:T(8,128)}, f32[17,8,512]{2,1,0:T(8,128)}, u32[]{:S(2)}, u32[]{:S(2)}) collective-permute-start(f32[17,8,512]{2,1,0:T(8,128)} %get-tuple-element.36), channel_id=1, source_target_pairs={{1,0},{2,1},{3,2},{4,3},{5,4},{6,5},{7,6},{8,7},{9,8},{10,9},{11,1... | collective-permute-start | bytes 835592 | tf_op jit(solution)/shard_map/ppermute | solution.py:629
  10.2 5.2 %copy-start = (f32[6,5,8,1024]{3,2,1,0:T(8,128)S(1)}, f32[6,5,8,1024]{3,2,1,0:T(8,128)}, u32[]{:S(2)}) copy-start(f32[6,5,8,1024]{3,2,1,0:T(8,128)} %refs_8_.1) | copy-start | bytes 2949124
  10.2 5.2 %copy-start.8 = (f32[8,1024]{1,0:T(8,128)S(1)}, f32[8,1024]{1,0:T(8,128)}, u32[]{:S(2)}) copy-start(f32[8,1024]{1,0:T(8,128)} %refs_4_.5) | copy-start | bytes 98308
  10.3 22.6 %all-to-all-start.1 = ((f32[8,6,5,8,128]{4,3,2,1,0:T(8,128)}), f32[8,6,5,8,128]{4,3,2,1,0:T(8,128)S(1)}, u32[]{:S(2)}, u32[]{:S(2)}) async-start(f32[8,6,5,8,128]{4,3,2,1,0:T(8,128)} %get-tuple-element.32.refs_5_), calls=%async_computation.1 | async-start | bytes 1966080 | tf_op jit(solution)/shard_map/all_to_all | solution.py:633
  15.4 1.8 %copy-start.11 = (f32[2,4,8,512]{3,2,1,0:T(8,128)S(1)}, f32[2,4,8,512]{3,2,1,0:T(8,128)}, u32[]{:S(2)}) copy-start(f32[2,4,8,512]{3,2,1,0:T(8,128)} %param.17) | copy-start | bytes 393220
  15.4 1.8 %copy-start.13 = (f32[1536]{0:T(1024)S(1)}, f32[1536]{0:T(1024)}, u32[]{:S(2)}) copy-start(f32[1536]{0:T(1024)} %constant.5.clone.refs_0_) | copy-start | bytes 18436
  23.0 15.7 %collective-permute-start.2 = (f32[17,8,512]{2,1,0:T(8,128)}, f32[17,8,512]{2,1,0:T(8,128)S(1)}, u32[]{:S(2)}, u32[]{:S(2)}) collective-permute-start(f32[17,8,512]{2,1,0:T(8,128)} %get-tuple-element.39), channel_id=1, source_target_pairs={{0,1},{1,2},{2,3},{3,4},{4,5},{5,6},{6,7},{7,8},{8,9},{9,10},{10,1... | collective-permute-start | bytes 835592 | tf_op jit(solution)/shard_map/ppermute | solution.py:629
  23.5 15.9 %collective-permute-start.3 = (f32[17,8,512]{2,1,0:T(8,128)}, f32[17,8,512]{2,1,0:T(8,128)}, u32[]{:S(2)}, u32[]{:S(2)}) collective-permute-start(f32[17,8,512]{2,1,0:T(8,128)} %get-tuple-element.40), channel_id=1, source_target_pairs={{1,0},{2,1},{3,2},{4,3},{5,4},{6,5},{7,6},{8,7},{9,8},{10,9},{11,1... | collective-permute-start | bytes 835592 | tf_op jit(solution)/shard_map/ppermute | solution.py:629
  32.9 19.7 %all-to-all-start = ((f32[8,34,8,128]{3,2,1,0:T(8,128)}), f32[8,34,8,128]{3,2,1,0:T(8,128)S(1)}, u32[]{:S(2)}, u32[]{:S(2)}) async-start(f32[8,34,8,128]{3,2,1,0:T(8,128)} %get-tuple-element.37), calls=%async_computation | async-start | bytes 2228224 | tf_op jit(solution)/shard_map/all_to_all | solution.py:633
  40.4 12.2 %copy-start.2 = (bf16[384,1152]{1,0:T(8,128)(2,1)S(1)}, bf16[384,1152]{1,0:T(8,128)(2,1)}, u32[]{:S(2)}) copy-start(bf16[384,1152]{1,0:T(8,128)(2,1)} %constant.4.clone.refs_0_.refs_3_) | copy-start | bytes 2654212
  40.4 12.2 %copy-start.9 = (f32[8,1024]{1,0:T(8,128)S(1)}, f32[8,1024]{1,0:T(8,128)}, u32[]{:S(2)}) copy-start(f32[8,1024]{1,0:T(8,128)} %refs_4_.5) | copy-start | bytes 98308
  56.0 3.8 %copy-start.23 = (f32[8,512]{1,0:T(8,128)S(1)}, f32[8,512]{1,0:T(8,128)}, u32[]{:S(2)}) copy-start(f32[8,512]{1,0:T(8,128)} %get-tuple-element.50) | copy-start | bytes 49156
  56.0 3.9 %copy-start.22 = (f32[8,512]{1,0:T(8,128)S(1)}, f32[8,512]{1,0:T(8,128)}, u32[]{:S(2)}) copy-start(f32[8,512]{1,0:T(8,128)} %get-tuple-element.51) | copy-start | bytes 49156
  56.0 20.2 %copy-start.5 = (f32[6,5,8,1024]{3,2,1,0:T(8,128)S(1)}, f32[6,5,8,1024]{3,2,1,0:T(8,128)}, u32[]{:S(2)}) copy-start(f32[6,5,8,1024]{3,2,1,0:T(8,128)} %copy-done.4) | copy-start | bytes 2949124
  56.0 20.2 %copy-start.10 = (f32[6,8,1024]{2,1,0:T(8,128)S(1)}, f32[6,8,1024]{2,1,0:T(8,128)}, u32[]{:S(2)}) copy-start(f32[6,8,1024]{2,1,0:T(8,128)} %get-tuple-element.48.refs_2_) | copy-start | bytes 589828
  56.0 20.2 %copy-start.12 = (f32[8,8,512]{2,1,0:T(8,128)S(1)}, f32[8,8,512]{2,1,0:T(8,128)}, u32[]{:S(2)}) copy-start(f32[8,8,512]{2,1,0:T(8,128)} %get-tuple-element.49.refs_3_) | copy-start | bytes 393220
  56.0 20.2 %copy-start.14 = (f32[8,512]{1,0:T(8,128)S(1)}, f32[8,512]{1,0:T(8,128)}, u32[]{:S(2)}) copy-start(f32[8,512]{1,0:T(8,128)} %refs_6_.1) | copy-start | bytes 49156
  56.0 20.2 %all-to-all-start.2 = ((f32[8,34,8,128]{3,2,1,0:T(8,128)}), f32[8,34,8,128]{3,2,1,0:T(8,128)S(1)}, u32[]{:S(2)}, u32[]{:S(2)}) async-start(f32[8,34,8,128]{3,2,1,0:T(8,128)} %get-tuple-element.46), calls=%async_computation.2 | async-start | bytes 2228224 | tf_op jit(solution)/shard_map/all_to_all | solution.py:633
  59.7 10.1 %collective-permute-start.4 = (f32[8,512]{1,0:T(8,128)S(1)}, f32[8,512]{1,0:T(8,128)S(1)}, u32[]{:S(2)}, u32[]{:S(2)}) collective-permute-start(f32[8,512]{1,0:T(8,128)S(1)} %copy-done.23), channel_id=1, source_target_pairs={{0,1},{1,2},{2,3},{3,4},{4,5},{5,6},{6,7},{7,8},{8,9},{9,10},{10,1... | collective-permute-start | bytes 49160 | tf_op jit(solution)/shard_map/ppermute | solution.py:629
  59.8 10.0 %collective-permute-start.5 = (f32[8,512]{1,0:T(8,128)S(1)}, f32[8,512]{1,0:T(8,128)S(1)}, u32[]{:S(2)}, u32[]{:S(2)}) collective-permute-start(f32[8,512]{1,0:T(8,128)S(1)} %copy-done.22), channel_id=1, source_target_pairs={{1,0},{2,1},{3,2},{4,3},{5,4},{6,5},{7,6},{8,7},{9,8},{10,9},{11,1... | collective-permute-start | bytes 49160 | tf_op jit(solution)/shard_map/ppermute | solution.py:629
  (9 other events, 11.9 us)

commit v12 on v11

--- a/solution.py
+++ b/solution.py
@@ -356,7 +356,7 @@
         q.put(pl.ds(at, 1))
 
 
-EARLY = 4
+EARLY = 3
 
 
 def early_kernel(jx_ref, jz_ref, a_ref, s_ref, ps_ref, b, q, blocks, parts, sems):

time: 78.2 us -> 77.9 us (level)
  waiting for transfers between devices: 26 us -> 25.2 us
    ppermute x3, waiting for transfers between devices: 6.8 us -> 1.51 us  [exchange(): lax.ppermute(up, 'space', forward)]
    all_to_all x3, waiting for transfers between devices: 19.2 us -> 23.6 us  [turn(): return lax.all_to_all(x, 'inst', 0, 0, tiled=True)]
where the time goes in v12:
time: 77.9 us; the launch traced here: 76.9 us
  waiting for transfers between devices  25.2 us (32%)
  Pallas kernels  24.1 us (31%)
  starting transfers between devices  22.6 us (29%)
  local copies, waits for them, and re-layouts  3.87 us (5%)
  between operations  1.17 us (2%)
    pallas_call x9, Pallas kernels, call(): pl.pallas_call(kernel, out_shape=[pltpu.HBM(dims, F32) if n else jax.Shap...  24.1 us
    all_to_all x3, waiting for transfers between devices, turn(): return lax.all_to_all(x, 'inst', 0, 0, tiled=True)  23.6 us
    all_to_all x3, starting transfers between devices, turn(): return lax.all_to_all(x, 'inst', 0, 0, tiled=True)  12.6 us
    ppermute x3, starting transfers between devices, exchange(): lax.ppermute(down, 'space', back)  9.32 us
    unnamed x48, local copies, waits for them, and re-layouts  3.87 us
  transfers between devices with their start and end apart: 9, of which 4 were waited for; matrix products, arithmetic and copies ran while one was open for 0% of the time, Pallas kernels for 22%

profile of v12, /device:TPU:112, one launch (start us, length us, event | category | flops | bytes accessed | tf_op | source)
XLA Modules:
  0.0 76.9 jit_solution(15373398594146628241)
XLA Ops:
  0.7 2.3 %shard_map.131 = (f32[17,8,512]{2,1,0:T(8,128)}, f32[17,8,512]{2,1,0:T(8,128)}, f32[6,5,8,1024]{3,2,1,0:T(8,128)S(1)}, f32[8,1024]{1,0:T(8,128)S(1)}) custom-call(f32[6,5,8,1024]{3,2,1,0:T(8,128)} %refs_8_.1, f32[8,1024]{1,0:T(8,128)} %refs_4_.5, f32[8,8,512]{2,1,0:T(8,128)} %bitcast.5), custom_call_target="tpu_custom_call" | custom-call | flops 1048576 | bytes 1048576 | tf_op jit(solution)/shard_map/pallas_call | solution.py:173
  3.1 3.2 %collective-permute-start.1 = (f32[17,8,512]{2,1,0:T(8,128)}, f32[17,8,512]{2,1,0:T(8,128)}, u32[]{:S(2)}, u32[]{:S(2)}) collective-permute-start(f32[17,8,512]{2,1,0:T(8,128)} %get-tuple-element.36), channel_id=1, source_target_pairs={{1,0},{2,1},{3,2},{4,3},{5,4},{6,5},{7,6},{8,7},{9,8},{10,9},{11,1... | collective-permute-start | bytes 835592 | tf_op jit(solution)/shard_map/ppermute | solution.py:629
  6.3 3.3 %shard_map.132 = (f32[3,5,8,1024]{3,2,1,0:T(8,128)}, f32[3,5,8,1024]{3,2,1,0:T(8,128)}, f32[8,6,5,8,128]{4,3,2,1,0:T(8,128)}) custom-call(f32[5,5]{1,0:T(8,128)S(1)} %copy-done.15, f32[5,5]{1,0:T(8,128)S(1)} %copy-done.16, f32[6,5,8,1024]{3,2,1,0:T(8,128)S(1)} %get-tuple-element.28.refs_2_, f32[6,5,8,1024]{3,2,1,0:T(8,128)S(1)} %copy-done.3, ...), custom_call_target="tpu_custom_call" | custom-call | flops 1048576 | bytes 1048576 | tf_op jit(solution)/shard_map/pallas_call | solution.py:173
  9.7 5.2 %all-to-all-start.1 = ((f32[8,6,5,8,128]{4,3,2,1,0:T(8,128)}), f32[8,6,5,8,128]{4,3,2,1,0:T(8,128)S(1)}, u32[]{:S(2)}, u32[]{:S(2)}) async-start(f32[8,6,5,8,128]{4,3,2,1,0:T(8,128)} %get-tuple-element.32.refs_5_), calls=%async_computation.1 | async-start | bytes 1966080 | tf_op jit(solution)/shard_map/all_to_all | solution.py:633
  14.9 2.3 %shard_map.133 = (f32[3,5,8,1024]{3,2,1,0:T(8,128)S(1)}, f32[3,5,8,1024]{3,2,1,0:T(8,128)S(1)}) custom-call(f32[5,5]{1,0:T(8,128)S(1)} %copy-done.15, f32[5,5]{1,0:T(8,128)S(1)} %copy-done.16, f32[6,5,8,1024]{3,2,1,0:T(8,128)S(1)} %copy-done, f32[6,5,8,1024]{3,2,1,0:T(8,128)S(1)} %copy-done.3, f32[8,1024]{1,0:T(8,128)S(1)} %copy-done.6, ...), custom_call_target="tpu_custom_call" | custom-call | flops 68719476736 | bytes 1048576 | tf_op jit(solution)/shard_map/pallas_call | solution.py:173
  17.3 1.4 %shard_map.134.refs_8_ = f32[6,8,1024]{2,1,0:T(8,128)S(1)} custom-call(f32[1536]{0:T(1024)S(1)} %copy-done.13, f32[8,8,512]{2,1,0:T(8,128)S(1)} %bitcast.7, f32[1,512]{1,0:T(1,128)S(1)} %bitcast.8, s32[1,512]{1,0:T(1,128)S(1)} %bitcast.11, s32[1,512]{1,0:T(1,128)S(1)} %bitcast.14, f32[8,6,5,8,128]{4,3,2,1,0:T(8,128)} %get-tuple-element.32.refs_5_), custom_call_target="tpu_custom_call" | custom-call | flops 68719476736 | bytes 1048576 | tf_op jit(solution)/shard_map/pallas_call | solution.py:173
  18.7 4.3 %shard_map.135 = (f32[8,34,8,128]{3,2,1,0:T(8,128)}, f32[6,5,8,1024]{3,2,1,0:T(8,128)}, f32[17,8,512]{2,1,0:T(8,128)}, f32[17,8,512]{2,1,0:T(8,128)}, f32[6,8,10...) custom-call(f32[1536]{0:T(1024)S(1)} %copy-done.13, f32[5,5]{1,0:T(8,128)S(1)} %copy-done.15, ...), custom_call_target="tpu_custom_call" | custom-call | flops 1048576 | bytes 1048576 | tf_op jit(solution)/shard_map/pallas_call | solution.py:173
  23.0 0.5 collective-permute-start.2
  23.5 2.8 %collective-permute-start.3 = (f32[17,8,512]{2,1,0:T(8,128)}, f32[17,8,512]{2,1,0:T(8,128)}, u32[]{:S(2)}, u32[]{:S(2)}) collective-permute-start(f32[17,8,512]{2,1,0:T(8,128)} %get-tuple-element.40), channel_id=1, source_target_pairs={{1,0},{2,1},{3,2},{4,3},{5,4},{6,5},{7,6},{8,7},{9,8},{10,9},{11,1... | collective-permute-start | bytes 835592 | tf_op jit(solution)/shard_map/ppermute | solution.py:629
  26.4 5.7 %all-to-all-done.1.refs_1_ = f32[8,6,5,8,128]{4,3,2,1,0:T(8,128)S(1)} async-done(((f32[8,6,5,8,128]{4,3,2,1,0:T(8,128)}), f32[8,6,5,8,128]{4,3,2,1,0:T(8,128)S(1)}, u32[]{:S(2)}, u32[]{:S(2)}) %all-to-all-start.1) | async-done | bytes 983072 | tf_op jit(solution)/shard_map/all_to_all | solution.py:633
  32.1 3.7 %all-to-all-start = ((f32[8,34,8,128]{3,2,1,0:T(8,128)}), f32[8,34,8,128]{3,2,1,0:T(8,128)S(1)}, u32[]{:S(2)}, u32[]{:S(2)}) async-start(f32[8,34,8,128]{3,2,1,0:T(8,128)} %get-tuple-element.37), calls=%async_computation | async-start | bytes 2228224 | tf_op jit(solution)/shard_map/all_to_all | solution.py:633
  35.8 1.2 %copy-done.1 = bf16[384,1152]{1,0:T(8,128)(2,1)S(1)} copy-done((bf16[384,1152]{1,0:T(8,128)(2,1)S(1)}, bf16[384,1152]{1,0:T(8,128)(2,1)}, u32[]{:S(2)}) %copy-start.1) | copy-done | bytes 884760
  37.0 0.9 %shard_map.136.refs_14_.refs_2_ = f32[384,640]{1,0:T(8,128)S(1)} custom-call(bf16[384,1152]{1,0:T(8,128)(2,1)S(1)} %copy-done.1, f32[8,6,5,8,128]{4,3,2,1,0:T(8,128)S(1)} %all-to-all-done.1.refs_1_, f32[8,1024]{1,0:T(8,128)S(1)} %copy-done.6), custom_call_target="tpu_custom_call" | custom-call | flops 1048576 | bytes 1048576 | tf_op jit(solution)/shard_map/pallas_call | solution.py:173
  37.9 0.7 copy-done.20
  38.6 1.0 %copy-done.21 = f32[17,8,512]{2,1,0:T(8,128)S(1)} copy-done((f32[17,8,512]{2,1,0:T(8,128)S(1)}, f32[17,8,512]{2,1,0:T(8,128)}, u32[]{:S(2)}) %copy-start.21) | copy-done | bytes 278552
  39.6 4.8 %shard_map.137 = (f32[6,5,8,1024]{3,2,1,0:T(8,128)S(1)}, f32[8,8,1024]{2,1,0:T(8,128)S(1)}, f32[8,8,512]{2,1,0:T(8,128)S(1)}) custom-call(f32[1536]{0:T(1024)S(1)} %copy-done.13, f32[5,5]{1,0:T(8,128)S(1)} %copy-done.15, f32[5,5]{1,0:T(8,128)S(1)} %copy-done.16, f32[6,5,8,1024]{3,2,1,0:T(8,128)} %get-tuple-element.38.refs_3_, f32[6,5,8,1024]{3,2,1,0:T(8,128)} %refs_4_.4, ...), custom_call_target="tpu_custom_call" | custom-call | flops 68719476736 | bytes 1048576 | tf_op jit(solution)/shard_map/pallas_call | solution.py:173
  44.4 0.9 %copy-done.4 = f32[6,5,8,1024]{3,2,1,0:T(8,128)} copy-done((f32[6,5,8,1024]{3,2,1,0:T(8,128)}, f32[6,5,8,1024]{3,2,1,0:T(8,128)S(1)}, u32[]{:S(2)}) %copy-start.4) | copy-done | bytes 983064
  45.4 6.4 %all-to-all-done.refs_1_ = f32[8,34,8,128]{3,2,1,0:T(8,128)S(1)} async-done(((f32[8,34,8,128]{3,2,1,0:T(8,128)}), f32[8,34,8,128]{3,2,1,0:T(8,128)S(1)}, u32[]{:S(2)}, u32[]{:S(2)}) %all-to-all-start) | async-done | bytes 1114144 | tf_op jit(solution)/shard_map/all_to_all | solution.py:633
  51.7 3.4 %shard_map.138 = (f32[8,34,8,128]{3,2,1,0:T(8,128)}, f32[8,8,512]{2,1,0:T(8,128)}, f32[8,512]{1,0:T(8,128)}, f32[8,512]{1,0:T(8,128)}, f32[6,8,1024]{2,1,0:T(8,128)}) custom-call(f32[1536]{0:T(1024)S(1)} %copy-done.13, f32[8,34,8,128]{3,2,1,0:T(8,128)S(1)} %all-to-all-done.refs_1_, f32[384,640]{1,0:T(8,128)S(1)} %shard_map.136.refs_14_.refs_2_, ...), custom_call_target="tpu_custom_call" | custom-call | flops 1048576 | bytes 1048576 | tf_op jit(solution)/shard_map/pallas_call | solution.py:173
  55.2 3.7 %all-to-all-start.2 = ((f32[8,34,8,128]{3,2,1,0:T(8,128)}), f32[8,34,8,128]{3,2,1,0:T(8,128)S(1)}, u32[]{:S(2)}, u32[]{:S(2)}) async-start(f32[8,34,8,128]{3,2,1,0:T(8,128)} %get-tuple-element.46), calls=%async_computation.2 | async-start | bytes 2228224 | tf_op jit(solution)/shard_map/all_to_all | solution.py:633
  59.0 3.2 %collective-permute-start.5 = (f32[8,512]{1,0:T(8,128)S(1)}, f32[8,512]{1,0:T(8,128)S(1)}, u32[]{:S(2)}, u32[]{:S(2)}) collective-permute-start(f32[8,512]{1,0:T(8,128)S(1)} %copy-done.22), channel_id=1, source_target_pairs={{1,0},{2,1},{3,2},{4,3},{5,4},{6,5},{7,6},{8,7},{9,8},{10,9},{11,1... | collective-permute-start | bytes 49160 | tf_op jit(solution)/shard_map/ppermute | solution.py:629
  62.3 1.5 %collective-permute-done.4.refs_4_ = f32[8,512]{1,0:T(8,128)S(1)} collective-permute-done((f32[8,512]{1,0:T(8,128)S(1)}, f32[8,512]{1,0:T(8,128)S(1)}, u32[]{:S(2)}, u32[]{:S(2)}) %collective-permute-start.4) | collective-permute-done | bytes 16416 | tf_op jit(solution)/shard_map/ppermute | solution.py:629
  63.8 11.6 %all-to-all-done.2.refs_0_ = f32[8,34,8,128]{3,2,1,0:T(8,128)S(1)} async-done(((f32[8,34,8,128]{3,2,1,0:T(8,128)}), f32[8,34,8,128]{3,2,1,0:T(8,128)S(1)}, u32[]{:S(2)}, u32[]{:S(2)}) %all-to-all-start.2) | async-done | bytes 1114144 | tf_op jit(solution)/shard_map/all_to_all | solution.py:633
  75.4 1.4 %shard_map.139 = (f32[6,5,8,1024]{3,2,1,0:T(8,128)}, f32[8,8,512]{2,1,0:T(8,128)}) custom-call(f32[8,34,8,128]{3,2,1,0:T(8,128)S(1)} %all-to-all-done.2.refs_0_, f32[6,5,8,1024]{3,2,1,0:T(8,128)S(1)} %copy-done.5, f32[6,8,1024]{2,1,0:T(8,128)S(1)} %copy-done.10, f32[8,8,512]{2,1,0:T(8,128)S(1)} %copy-done.12, f32[8,512]{1,0:T(8,128)S(1)} %collective-permute-done.4.refs_4_, ...), custom_call_target="tpu_custom_call" | custom-call | flops 1048576 | bytes 1048576 | tf_op jit(solution)/shard_map/pallas_call | solution.py:173
  (51 shorter events, 0.3 us)
Async XLA Ops:
  0.6 5.7 %copy-start.16 = (f32[5,5]{1,0:T(8,128)S(1)}, f32[5,5]{1,0:T(8,128)}, u32[]{:S(2)}) copy-start(f32[5,5]{1,0:T(8,128)} %refs_2_.7) | copy-start | bytes 304
  0.6 5.7 %copy-start.15 = (f32[5,5]{1,0:T(8,128)S(1)}, f32[5,5]{1,0:T(8,128)}, u32[]{:S(2)}) copy-start(f32[5,5]{1,0:T(8,128)} %refs_1_.9) | copy-start | bytes 304
  0.6 5.7 %copy-start.3 = (f32[6,5,8,1024]{3,2,1,0:T(8,128)S(1)}, f32[6,5,8,1024]{3,2,1,0:T(8,128)}, u32[]{:S(2)}) copy-start(f32[6,5,8,1024]{3,2,1,0:T(8,128)} %refs_4_.4) | copy-start | bytes 2949124
  3.0 15.6 %collective-permute-start = (f32[17,8,512]{2,1,0:T(8,128)}, f32[17,8,512]{2,1,0:T(8,128)S(1)}, u32[]{:S(2)}, u32[]{:S(2)}) collective-permute-start(f32[17,8,512]{2,1,0:T(8,128)} %get-tuple-element.35), channel_id=1, source_target_pairs={{0,1},{1,2},{2,3},{3,4},{4,5},{5,6},{6,7},{7,8},{8,9},{9,10},{10,1... | collective-permute-start | bytes 835592 | tf_op jit(solution)/shard_map/ppermute | solution.py:629
  3.1 15.5 %collective-permute-start.1 = (f32[17,8,512]{2,1,0:T(8,128)}, f32[17,8,512]{2,1,0:T(8,128)}, u32[]{:S(2)}, u32[]{:S(2)}) collective-permute-start(f32[17,8,512]{2,1,0:T(8,128)} %get-tuple-element.36), channel_id=1, source_target_pairs={{1,0},{2,1},{3,2},{4,3},{5,4},{6,5},{7,6},{8,7},{9,8},{10,9},{11,1... | collective-permute-start | bytes 835592 | tf_op jit(solution)/shard_map/ppermute | solution.py:629
  9.7 5.2 %copy-start = (f32[6,5,8,1024]{3,2,1,0:T(8,128)S(1)}, f32[6,5,8,1024]{3,2,1,0:T(8,128)}, u32[]{:S(2)}) copy-start(f32[6,5,8,1024]{3,2,1,0:T(8,128)} %refs_8_.1) | copy-start | bytes 2949124
  9.7 5.2 %copy-start.6 = (f32[8,1024]{1,0:T(8,128)S(1)}, f32[8,1024]{1,0:T(8,128)}, u32[]{:S(2)}) copy-start(f32[8,1024]{1,0:T(8,128)} %refs_4_.5) | copy-start | bytes 98308
  9.7 22.3 %all-to-all-start.1 = ((f32[8,6,5,8,128]{4,3,2,1,0:T(8,128)}), f32[8,6,5,8,128]{4,3,2,1,0:T(8,128)S(1)}, u32[]{:S(2)}, u32[]{:S(2)}) async-start(f32[8,6,5,8,128]{4,3,2,1,0:T(8,128)} %get-tuple-element.32.refs_5_), calls=%async_computation.1 | async-start | bytes 1966080 | tf_op jit(solution)/shard_map/all_to_all | solution.py:633
  14.9 2.3 %copy-start.11 = (f32[2,4,8,512]{3,2,1,0:T(8,128)S(1)}, f32[2,4,8,512]{3,2,1,0:T(8,128)}, u32[]{:S(2)}) copy-start(f32[2,4,8,512]{3,2,1,0:T(8,128)} %param.17) | copy-start | bytes 393220
  14.9 2.3 %copy-start.13 = (f32[1536]{0:T(1024)S(1)}, f32[1536]{0:T(1024)}, u32[]{:S(2)}) copy-start(f32[1536]{0:T(1024)} %constant.5.clone.refs_0_) | copy-start | bytes 18436
  23.0 14.9 %collective-permute-start.2 = (f32[17,8,512]{2,1,0:T(8,128)}, f32[17,8,512]{2,1,0:T(8,128)S(1)}, u32[]{:S(2)}, u32[]{:S(2)}) collective-permute-start(f32[17,8,512]{2,1,0:T(8,128)} %get-tuple-element.39), channel_id=1, source_target_pairs={{0,1},{1,2},{2,3},{3,4},{4,5},{5,6},{6,7},{7,8},{8,9},{9,10},{10,1... | collective-permute-start | bytes 835592 | tf_op jit(solution)/shard_map/ppermute | solution.py:629
  23.5 15.1 %collective-permute-start.3 = (f32[17,8,512]{2,1,0:T(8,128)}, f32[17,8,512]{2,1,0:T(8,128)}, u32[]{:S(2)}, u32[]{:S(2)}) collective-permute-start(f32[17,8,512]{2,1,0:T(8,128)} %get-tuple-element.40), channel_id=1, source_target_pairs={{1,0},{2,1},{3,2},{4,3},{5,4},{6,5},{7,6},{8,7},{9,8},{10,9},{11,1... | collective-permute-start | bytes 835592 | tf_op jit(solution)/shard_map/ppermute | solution.py:629
  32.1 19.7 %all-to-all-start = ((f32[8,34,8,128]{3,2,1,0:T(8,128)}), f32[8,34,8,128]{3,2,1,0:T(8,128)S(1)}, u32[]{:S(2)}, u32[]{:S(2)}) async-start(f32[8,34,8,128]{3,2,1,0:T(8,128)} %get-tuple-element.37), calls=%async_computation | async-start | bytes 2228224 | tf_op jit(solution)/shard_map/all_to_all | solution.py:633
  39.6 12.1 %copy-start.2 = (bf16[384,1152]{1,0:T(8,128)(2,1)S(1)}, bf16[384,1152]{1,0:T(8,128)(2,1)}, u32[]{:S(2)}) copy-start(bf16[384,1152]{1,0:T(8,128)(2,1)} %constant.4.clone.refs_0_.refs_3_) | copy-start | bytes 2654212
  39.6 12.1 %copy-start.7 = (f32[8,1024]{1,0:T(8,128)S(1)}, f32[8,1024]{1,0:T(8,128)}, u32[]{:S(2)}) copy-start(f32[8,1024]{1,0:T(8,128)} %refs_4_.5) | copy-start | bytes 98308
  55.1 3.8 %copy-start.23 = (f32[8,512]{1,0:T(8,128)S(1)}, f32[8,512]{1,0:T(8,128)}, u32[]{:S(2)}) copy-start(f32[8,512]{1,0:T(8,128)} %get-tuple-element.50) | copy-start | bytes 49156
  55.1 3.9 %copy-start.22 = (f32[8,512]{1,0:T(8,128)S(1)}, f32[8,512]{1,0:T(8,128)}, u32[]{:S(2)}) copy-start(f32[8,512]{1,0:T(8,128)} %get-tuple-element.51) | copy-start | bytes 49156
  55.2 20.2 %copy-start.5 = (f32[6,5,8,1024]{3,2,1,0:T(8,128)S(1)}, f32[6,5,8,1024]{3,2,1,0:T(8,128)}, u32[]{:S(2)}) copy-start(f32[6,5,8,1024]{3,2,1,0:T(8,128)} %copy-done.4) | copy-start | bytes 2949124
  55.2 20.2 %copy-start.10 = (f32[6,8,1024]{2,1,0:T(8,128)S(1)}, f32[6,8,1024]{2,1,0:T(8,128)}, u32[]{:S(2)}) copy-start(f32[6,8,1024]{2,1,0:T(8,128)} %get-tuple-element.48.refs_2_) | copy-start | bytes 589828
  55.2 20.2 %copy-start.12 = (f32[8,8,512]{2,1,0:T(8,128)S(1)}, f32[8,8,512]{2,1,0:T(8,128)}, u32[]{:S(2)}) copy-start(f32[8,8,512]{2,1,0:T(8,128)} %get-tuple-element.49.refs_3_) | copy-start | bytes 393220
  55.2 20.2 %copy-start.14 = (f32[8,512]{1,0:T(8,128)S(1)}, f32[8,512]{1,0:T(8,128)}, u32[]{:S(2)}) copy-start(f32[8,512]{1,0:T(8,128)} %refs_6_.1) | copy-start | bytes 49156
  55.2 20.2 %all-to-all-start.2 = ((f32[8,34,8,128]{3,2,1,0:T(8,128)}), f32[8,34,8,128]{3,2,1,0:T(8,128)S(1)}, u32[]{:S(2)}, u32[]{:S(2)}) async-start(f32[8,34,8,128]{3,2,1,0:T(8,128)} %get-tuple-element.46), calls=%async_computation.2 | async-start | bytes 2228224 | tf_op jit(solution)/shard_map/all_to_all | solution.py:633
  58.9 4.8 %collective-permute-start.4 = (f32[8,512]{1,0:T(8,128)S(1)}, f32[8,512]{1,0:T(8,128)S(1)}, u32[]{:S(2)}, u32[]{:S(2)}) collective-permute-start(f32[8,512]{1,0:T(8,128)S(1)} %copy-done.23), channel_id=1, source_target_pairs={{0,1},{1,2},{2,3},{3,4},{4,5},{5,6},{6,7},{7,8},{8,9},{9,10},{10,1... | collective-permute-start | bytes 49160 | tf_op jit(solution)/shard_map/ppermute | solution.py:629
  59.0 4.7 %collective-permute-start.5 = (f32[8,512]{1,0:T(8,128)S(1)}, f32[8,512]{1,0:T(8,128)S(1)}, u32[]{:S(2)}, u32[]{:S(2)}) collective-permute-start(f32[8,512]{1,0:T(8,128)S(1)} %copy-done.22), channel_id=1, source_target_pairs={{1,0},{2,1},{3,2},{4,3},{5,4},{6,5},{7,6},{8,7},{9,8},{10,9},{11,1... | collective-permute-start | bytes 49160 | tf_op jit(solution)/shard_map/ppermute | solution.py:629
  (9 other events, 13.5 us)
